TPU v7x, 32 devices: a whole 2x2x4 slice. The times are simulated.
32 devices in a mesh: band: 4 (over x, core), dom: 8 (over z, y).
Axes of the slice: x: 2, y: 2, z: 4, core: 2. Of those that a mesh axis runs over, the one named last changes fastest.
Arguments:
- orbitals: float32 [32, 32, 48, 512], P('dom', None, None, 'band'), may hold values from -6 to 6
- potential: float32 [32, 32, 48], P('dom'), may hold values from -1 to 2
- projectors: float32 [64, 4, 4608], P('dom'), may hold values from -0.09375 to 0.09375
- coupling: float32 [64, 4, 4], P('dom'), may hold values from -4 to 4
- atom_plane: int32 [64], P('dom'), may hold values from 0 to 31, as said below
- projector_count: int32 [64], P('dom'), may hold values from 1 to 4
Outputs:
- filtered: float32 [32, 32, 48, 512], P('dom', None, None, 'band')
- gram: float32 [512, 512], replicated
Inputs may be any that keep to these rules, and one draw needn't show every extreme that they name: `atom_plane`: atom a's first plane lies among the 4 planes of dom index a // 8, that is from (a // 8) * 4 to (a // 8) * 4 + 3; the last atom of each dom index starts on that index's last plane.
All inputs are finite; a program needn't handle non-finite values.
Results may differ from a plain program's by a relative error of at most 0.0003.
Values sent between devices are 32-bit elements; how exact they have to be, the bound alone decides.
No kernel may reach another device: no remote copies, remote signals or barrier semaphores. Data moves between devices by JAX's collectives and lax.ppermute only.
A program may use at most 192 MiB of HBM per device.

v0:
```python
import jax
import jax.numpy as jnp
from jax import lax
from jax.sharding import PartitionSpec as P

NORB = 512
HALO = 4
SPAN = 3
MAXPROJ = 4


center_weight = -205.0 / 72.0
side_weights = (8.0 / 5.0, -1.0 / 5.0, 8.0 / 315.0, -1.0 / 560.0)
HIGH = lax.Precision.HIGHEST


def with_halo(value, sides, width):
    for axis, dim in sides:
        peers, length = (lax.axis_size(axis), value.shape[dim])
        up = [(i, (i + 1) % peers) for i in range(peers)]
        down = [(j, i) for i, j in up]
        last = lax.slice_in_dim(value, length - width, length, axis=dim)
        first = lax.slice_in_dim(value, 0, width, axis=dim)
        before = lax.ppermute(last, axis, up)
        after = lax.ppermute(first, axis, down)
        value = jnp.concatenate([before, value, after], axis=dim)
    return value


def passed_along(value, axis, steps):
    count = lax.axis_size(axis)
    pairs = [(source, (source + steps) % count) for source in range(count)]
    return lax.ppermute(value, axis, pairs)


def laplacian(orbital_field, padded, planes):
    total = 3.0 * center_weight * orbital_field
    for offset in range(1, 5):
        weight = side_weights[offset - 1]
        total = total + weight * (
            padded[HALO + offset : HALO + offset + planes]
            + padded[HALO - offset : HALO - offset + planes]
        )
        total = total + weight * (
            jnp.roll(orbital_field, offset, 1) + jnp.roll(orbital_field, -offset, 1)
        )
        total = total + weight * (
            jnp.roll(orbital_field, offset, 2) + jnp.roll(orbital_field, -offset, 2)
        )
    return total


def apply_hamiltonian(orbital_field, potential, layout_pieces):
    planes, side_y, side_z, local_orbs = orbital_field.shape
    beta_full, live_mask, sym_coupling = layout_pieces
    padded = with_halo(orbital_field, (("dom", 0),), HALO)
    extended = padded[HALO : HALO + planes + SPAN - 1].reshape(
        planes + SPAN - 1, side_y * side_z, local_orbs
    )
    correlations = (
        jnp.einsum(
            "ajpc,pco->ajo", beta_full, extended, precision=HIGH, preferred_element_type=jnp.float32
        )
        * live_mask[:, :, None]
    )
    weighted = (
        jnp.einsum(
            "aij,ajo->aio",
            sym_coupling,
            correlations,
            precision=HIGH,
            preferred_element_type=jnp.float32,
        )
        * live_mask[:, :, None]
    )
    contrib = jnp.einsum(
        "ajpc,ajo->pco", beta_full, weighted, precision=HIGH, preferred_element_type=jnp.float32
    )
    contrib = contrib.reshape(planes + SPAN - 1, side_y, side_z, local_orbs)
    arrived = passed_along(contrib[planes:], "dom", 1)
    own_planes = contrib[:planes]
    own_planes = jnp.concatenate([own_planes[: SPAN - 1] + arrived, own_planes[SPAN - 1 :]], axis=0)
    kinetic = -0.5 * laplacian(orbital_field, padded, planes)
    return kinetic + potential[:, :, :, None] * orbital_field + own_planes


def shards(orbitals, potential, projectors, coupling, atom_plane, projector_count):
    planes, side_y, side_z, local_orbs = orbitals.shape
    atom_total = projectors.shape[0]
    first_plane = atom_plane - lax.axis_index("dom") * planes
    plane_ids = jnp.arange(planes + SPAN - 1, dtype=jnp.int32)
    span_ids = jnp.arange(SPAN, dtype=jnp.int32)
    onehot = (
        plane_ids[None, None, :] == first_plane[:, None, None] + span_ids[None, :, None]
    ).astype(jnp.float32)
    beta_split = projectors.reshape(atom_total, MAXPROJ, SPAN, side_y * side_z)
    beta_full = jnp.einsum(
        "akp,ajkc->ajpc", onehot, beta_split, precision=HIGH, preferred_element_type=jnp.float32
    )
    slots = jnp.arange(MAXPROJ, dtype=jnp.int32)
    live_mask = (slots[None, :] < projector_count[:, None]).astype(jnp.float32)
    sym_coupling = 0.5 * (coupling + jnp.transpose(coupling, (0, 2, 1)))
    layout_pieces = (beta_full, live_mask, sym_coupling)
    first = (apply_hamiltonian(orbitals, potential, layout_pieces) - 7.0 * orbitals) / 6.0
    second = (
        2.0 * (apply_hamiltonian(first, potential, layout_pieces) - 7.0 * first) / 6.0 - orbitals
    )
    cells = planes * side_y * side_z
    total_cells = cells * lax.axis_size("dom")
    flat = second.reshape(cells, local_orbs)
    identity = jnp.eye(NORB, dtype=jnp.float32)
    panels = lax.all_gather(flat, "band", axis=1, tiled=True)
    partial_gram = jnp.dot(panels.T, panels, precision=HIGH, preferred_element_type=jnp.float32)
    gram = lax.psum(partial_gram, "dom") * (1.0 / total_cells)
    lower = jnp.linalg.cholesky(gram)
    inverse = jax.scipy.linalg.solve_triangular(lower, identity, lower=True)
    own_rows = lax.dynamic_slice_in_dim(inverse, lax.axis_index("band") * local_orbs, local_orbs, 0)
    result = jnp.dot(panels, own_rows.T, precision=HIGH, preferred_element_type=jnp.float32)
    return (result.reshape(planes, side_y, side_z, local_orbs), gram)


def solution(mesh):
    placed = (
        P("dom", None, None, "band"),
        P("dom", None, None),
        P("dom", None, None),
        P("dom", None, None),
        P("dom"),
        P("dom"),
    )
    return jax.shard_map(
        shards,
        mesh=mesh,
        in_specs=placed,
        out_specs=(P("dom", None, None, "band"), P()),
        check_vma=False,
    )
```

profile of v0, /device:TPU:0, one launch (start us, length us, event | category | flops | bytes accessed | tf_op | source)
XLA Modules:
  0.0 795.9 jit_solution(17699913817623490107)
XLA Ops:
  41.5 103.9 %collective-permute-done.1 = f32[4,32,48,128]{3,2,1,0:T(8,128)} collective-permute-done((f32[4,32,48,128]{3,2,1,0:T(8,128)}, f32[4,32,48,128]{3,2,1,0:T(8,128)}, u32[]{:S(2)}, u32[]{:S(2)}) %collective-permute-start.1) | collective-permute-done | bytes 3145760 | tf_op jit(solution)/shard_map/ppermute | solution.py:24
  148.0 4.4 constant_dynamic-update-slice_fusion
  156.1 7.7 convolution_bitcast_fusion.1
  168.4 3.4 fusion.146
  175.0 3.4 fusion.154
  178.4 25.9 %collective-permute-done.2 = f32[2,32,48,128]{3,2,1,0:T(8,128)S(1)} collective-permute-done((f32[2,32,48,128]{3,2,1,0:T(8,128)S(1)}, f32[2,32,48,128]{3,2,1,0:T(8,128)S(1)}, u32[]{:S(2)}, u32[]{:S(2)}) %collective-permute-start.2) | collective-permute-done | bytes 1572896 | tf_op jit(solution)/shard_map/ppermute | solution.py:33
  205.6 29.0 %broadcast_multiply_fusion = (f32[4,32,48,128]{3,2,1,0:T(8,128)S(1)}, f32[4,32,48,128]{3,2,1,0:T(8,128)}) fusion(f32[4,32,48,128]{3,2,1,0:T(8,128)S(1)} %copy-done, f32[2,32,48,128]{3,2,1,0:T(8,128)} %bitcast.108, f32[2,32,48,128]{3,2,1,0:T(8,128)} %add.258, f32[4,32,48]{2,1,0:T(8,128)} %param.7, f32[4,32,4,128]{3,2,1,0:T(4,128)} %get-tuple-element.95, ...), kind=kLoop, calls=%fused_computation.99 | loop fusion | flops 47972352 | bytes 88104960 | tf_op jit(solution)/shard_map/div | solution.py:104
  258.2 112.3 %collective-permute-done.3 = f32[4,32,48,128]{3,2,1,0:T(8,128)S(1)} collective-permute-done((f32[4,32,48,128]{3,2,1,0:T(8,128)S(1)}, f32[4,32,48,128]{3,2,1,0:T(8,128)S(1)}, u32[]{:S(2)}, u32[]{:S(2)}) %collective-permute-start.3) | collective-permute-done | bytes 3145760 | tf_op jit(solution)/shard_map/ppermute | solution.py:25
  374.3 7.7 convolution_bitcast_fusion
  392.7 26.1 %collective-permute-done.5 = f32[2,32,48,128]{3,2,1,0:T(8,128)S(1)} collective-permute-done((f32[2,32,48,128]{3,2,1,0:T(8,128)S(1)}, f32[2,32,48,128]{3,2,1,0:T(8,128)S(1)}, u32[]{:S(2)}, u32[]{:S(2)}) %collective-permute-start.5) | collective-permute-done | bytes 1572896 | tf_op jit(solution)/shard_map/ppermute | solution.py:33
  421.7 25.2 %multiply_subtract_fusion = f32[4,32,48,128]{3,2,1,0:T(8,128)} fusion(f32[4,32,48,128]{3,2,1,0:T(8,128)S(1)} %copy-done, f32[4,32,48,128]{3,2,1,0:T(8,128)S(1)} %copy-done.2, f32[2,32,48,128]{3,2,1,0:T(8,128)S(1)} %bitcast.109, f32[2,32,48,128]{3,2,1,0:T(8,128)} %add.285, f32[4,32,4,128]{3,2,1,0:T(4,128)} %get-tuple-element.61, ...), kind=kLoop, calls=%fused_computation.97 | loop fusion | flops 53477376 | bytes 72376320 | tf_op jit(solution)/shard_map/sub | solution.py:106
  447.0 81.1 %all-gather.2.cloned.1.call-done = f32[6144,512]{1,0:T(8,128)} async-done(((f32[6144,128]{1,0:T(8,128)}), f32[6144,512]{1,0:T(8,128)}) %all-gather.2.cloned.1.call-update) | async-done | bytes 12582928 | tf_op jit(solution)/shard_map/all_gather | solution.py:112
  528.2 26.4 %fusion.155 = f32[512,512]{0,1:T(8,128)} fusion(f32[6144,512]{1,0:T(8,128)} %all-gather.2.cloned.1.call-done), kind=kOutput, calls=%fused_computation.243 | convolution fusion | flops 19327352832 | bytes 13631488 | tf_op jit(solution)/shard_map/dot_general | solution.py:113
  556.5 76.3 %all-reduce.3.cloned.1.call-done = f32[512,512]{0,1:T(8,128)} async-done(((f32[512,512]{0,1:T(8,128)}), f32[512,512]{0,1:T(8,128)}) %all-reduce.3.cloned.1.call-update) | async-done | bytes 1048592 | tf_op jit(solution)/shard_map/psum | solution.py:114
  634.9 11.7 %cholesky.104 = f32[128,128]{1,0:T(8,128)S(1)} custom-call(f32[128,128]{1,0:T(8,128)S(1)} %cholesky.266), custom_call_target="Cholesky" | custom-call | tf_op jit(solution)/shard_map/jit(cholesky)/cholesky | solution.py:115
  646.7 9.8 %custom-call.31 = f32[1,128,128]{1,2,0:T(8,128)S(1)} custom-call(f32[1,128,128]{2,1,0:T(8,128)S(1)} %get-tuple-element.107), custom_call_target="InvertDiagBlocksLowerTriangular" | custom-call | tf_op jit(solution)/shard_map/jit(cholesky)/cholesky | solution.py:115
  658.2 11.7 %cholesky.217 = f32[128,128]{1,0:T(8,128)S(1)} custom-call(f32[128,128]{1,0:T(8,128)S(1)} %cholesky.270), custom_call_target="Cholesky" | custom-call | tf_op jit(solution)/shard_map/jit(cholesky)/cholesky | solution.py:115
  670.0 10.0 %custom-call.32 = f32[1,128,128]{1,2,0:T(8,128)S(1)} custom-call(f32[1,128,128]{2,1,0:T(8,128)S(1)} %get-tuple-element.104), custom_call_target="InvertDiagBlocksLowerTriangular" | custom-call | tf_op jit(solution)/shard_map/jit(cholesky)/cholesky | solution.py:115
  681.5 11.7 %cholesky.238 = f32[128,128]{1,0:T(8,128)S(1)} custom-call(f32[128,128]{1,0:T(8,128)S(1)} %cholesky.275), custom_call_target="Cholesky" | custom-call | tf_op jit(solution)/shard_map/jit(cholesky)/cholesky | solution.py:115
  693.9 9.8 %custom-call.33 = f32[1,128,128]{1,2,0:T(8,128)S(1)} custom-call(f32[1,128,128]{2,1,0:T(8,128)S(1)} %get-tuple-element.101), custom_call_target="InvertDiagBlocksLowerTriangular" | custom-call | tf_op jit(solution)/shard_map/jit(cholesky)/cholesky | solution.py:115
  705.2 11.9 %cholesky.255 = f32[128,128]{1,0:T(8,128)S(1)} custom-call(f32[128,128]{1,0:T(8,128)S(1)} %convolution_subtract_fusion.5), custom_call_target="Cholesky" | custom-call | tf_op jit(solution)/shard_map/jit(cholesky)/cholesky | solution.py:115
  721.0 10.1 %while.1 = (s32[]{:T(128)}, f32[512,512]{1,0:T(8,128)S(1)}, s32[4,2]{0,1:T(2,128)S(1)}, f32[4,128,128]{2,1,0:T(8,128)}, s32[]{:T(128)}) while((s32[]{:T(128)}, f32[512,512]{1,0:T(8,128)S(1)}, s32[4,2]{0,1:T(2,128)S(1)}, f32[4,128,128]{2,1,0:T(8,128)}, s32[]{:T(128)}) %tuple.71), condition=%wide.while_cond, body=%wide.while_body.sunk | while | flops 2 | bytes 132705 | solution.py:116
  731.1 40.1 %custom-call.34 = f32[4,128,128]{1,2,0:T(8,128)S(1)} custom-call(f32[4,128,128]{2,1,0:T(8,128)} %get-tuple-element.9), custom_call_target="InvertDiagBlocksLowerTriangular" | custom-call | tf_op jit(solution)/shard_map/jit(_solve_triangular)/triangular_solve | solution.py:116
  775.1 13.8 %fusion.81 = f32[6144,128]{1,0:T(8,128)} fusion(f32[6144,512]{1,0:T(8,128)} %all-gather.2.cloned.1.call-done, s32[]{:T(128)S(6)} %select_n.8, f32[128,512]{1,0:T(8,128)S(1)} %fusion.84, f32[128,512]{1,0:T(8,128)S(1)} %fusion.96, f32[128,512]{1,0:T(8,128)S(1)} %fusion.94, f32[128,512]{1,0:T(8,128)S(1)} %fusion.93), kind=kOutput, calls=%fused_computation.138 | convolution fusion | flops 4832034816 | bytes 16777220 | tf_op jit(solution)/shard_map/dot_general | solution.py:118
  (135 shorter events, 115.5 us)
Async XLA Ops:
  7.2 12.4 %copy-start = (f32[4,32,48,128]{3,2,1,0:T(8,128)S(1)}, f32[4,32,48,128]{3,2,1,0:T(8,128)}, u32[]{:S(2)}) copy-start(f32[4,32,48,128]{3,2,1,0:T(8,128)} %param.6) | copy-start | bytes 9437188
  7.2 521.0 %all-gather.2.cloned.1.call-start = ((), (), s32[]{:S(2)}) async-start(), calls=%async_computation | async-start | bytes 15728640 | tf_op jit(solution)/shard_map/all_gather | solution.py:112
  7.2 138.1 %collective-permute-start.1 = (f32[4,32,48,128]{3,2,1,0:T(8,128)}, f32[4,32,48,128]{3,2,1,0:T(8,128)}, u32[]{:S(2)}, u32[]{:S(2)}) collective-permute-start(f32[4,32,48,128]{3,2,1,0:T(8,128)} %param.6), channel_id=1, source_target_pairs={{0,1},{1,2},{2,3},{3,4},{4,5},{5,6},{6,7},{7,0},{8,9},{9,10},{10,1... | collective-permute-start | bytes 9437192 | tf_op jit(solution)/shard_map/ppermute | solution.py:24
  10.2 137.7 %collective-permute-start = (f32[4,32,48,128]{3,2,1,0:T(8,128)}, f32[4,32,48,128]{3,2,1,0:T(8,128)}, u32[]{:S(2)}, u32[]{:S(2)}) collective-permute-start(f32[4,32,48,128]{3,2,1,0:T(8,128)} %param.6), channel_id=1, source_target_pairs={{1,0},{2,1},{3,2},{4,3},{5,4},{6,5},{7,6},{0,7},{9,8},{10,9},{11,1... | collective-permute-start | bytes 9437192 | tf_op jit(solution)/shard_map/ppermute | solution.py:25
  13.3 11.7 %copy-start.12 = (f32[8,4,4]{0,2,1:T(4,128)S(1)}, f32[8,4,4]{0,2,1:T(4,128)}, u32[]{:S(2)}) copy-start(f32[8,4,4]{0,2,1:T(4,128)} %param.9) | copy-start | bytes 1540
  13.4 11.8 %copy-start.13 = (s32[8]{0:T(128)S(1)}, s32[8]{0:T(128)}, u32[]{:S(2)}) copy-start(s32[8]{0:T(128)} %param.10) | copy-start | bytes 100
  28.9 127.1 %copy-start.3 = (f32[8,4,6,1536]{3,2,1,0:T(8,128)}, f32[8,4,6,1536]{3,2,1,0:T(8,128)S(1)}, u32[]{:S(2)}) copy-start(f32[8,4,6,1536]{3,2,1,0:T(8,128)S(1)} %convolution_bitcast_fusion.2) | copy-start | bytes 3538948
  147.9 7.9 copy-start.1
  163.8 3.9 copy-start.11
  165.3 39.0 %collective-permute-start.2 = (f32[2,32,48,128]{3,2,1,0:T(8,128)S(1)}, f32[2,32,48,128]{3,2,1,0:T(8,128)S(1)}, u32[]{:S(2)}, u32[]{:S(2)}) collective-permute-start(f32[2,32,48,128]{3,2,1,0:T(8,128)S(1)} %bitcast.112), channel_id=1, source_target_pairs={{0,1},{1,2},{2,3},{3,4},{4,5},{5,6},{6,7},{7,0},{8,9},{9,10},{10,1... | collective-permute-start | bytes 4718600 | tf_op jit(solution)/shard_map/ppermute | solution.py:33
  178.4 27.2 %copy-start.10 = (f32[4,1,48,128]{3,2,1,0:T(8,128)S(1)}, f32[4,1,48,128]{3,2,1,0:T(8,128)}, u32[]{:S(2)}) copy-start(f32[4,1,48,128]{3,2,1,0:T(8,128)} %get-tuple-element.64) | copy-start | bytes 294916
  234.7 135.8 %collective-permute-start.3 = (f32[4,32,48,128]{3,2,1,0:T(8,128)S(1)}, f32[4,32,48,128]{3,2,1,0:T(8,128)S(1)}, u32[]{:S(2)}, u32[]{:S(2)}) collective-permute-start(f32[4,32,48,128]{3,2,1,0:T(8,128)S(1)} %get-tuple-element.22), channel_id=1, source_target_pairs={{1,0},{2,1},{3,2},{4,3},{5,4},{6,5},{7,6},{0,7},{9,8},{10,9},{11,1... | collective-permute-start | bytes 9437192 | tf_op jit(solution)/shard_map/ppermute | solution.py:25
  238.9 181.2 %collective-permute-start.4 = (f32[4,32,48,128]{3,2,1,0:T(8,128)S(1)}, f32[4,32,48,128]{3,2,1,0:T(8,128)S(1)}, u32[]{:S(2)}, u32[]{:S(2)}) collective-permute-start(f32[4,32,48,128]{3,2,1,0:T(8,128)S(1)} %get-tuple-element.22), channel_id=1, source_target_pairs={{0,1},{1,2},{2,3},{3,4},{4,5},{5,6},{6,7},{7,0},{8,9},{9,10},{10,1... | collective-permute-start | bytes 9437192 | tf_op jit(solution)/shard_map/ppermute | solution.py:24
  258.1 112.9 %copy-start.4 = (f32[8,4,6,1536]{3,2,1,0:T(8,128)S(1)}, f32[8,4,6,1536]{3,2,1,0:T(8,128)}, u32[]{:S(2)}) copy-start(f32[8,4,6,1536]{3,2,1,0:T(8,128)} %copy-done.3) | copy-start | bytes 3538948
  382.3 36.4 %collective-permute-start.5 = (f32[2,32,48,128]{3,2,1,0:T(8,128)S(1)}, f32[2,32,48,128]{3,2,1,0:T(8,128)S(1)}, u32[]{:S(2)}, u32[]{:S(2)}) collective-permute-start(f32[2,32,48,128]{3,2,1,0:T(8,128)S(1)} %bitcast.111), channel_id=1, source_target_pairs={{0,1},{1,2},{2,3},{3,4},{4,5},{5,6},{6,7},{7,0},{8,9},{9,10},{10,1... | collective-permute-start | bytes 4718600 | tf_op jit(solution)/shard_map/ppermute | solution.py:33
  392.7 29.1 %copy-start.2 = (f32[4,32,48,128]{3,2,1,0:T(8,128)S(1)}, f32[4,32,48,128]{3,2,1,0:T(8,128)}, u32[]{:S(2)}) copy-start(f32[4,32,48,128]{3,2,1,0:T(8,128)} %get-tuple-element.23) | copy-start | bytes 9437188
  420.1 1.6 copy-start.8
  447.0 185.8 %all-reduce.3.cloned.1.call-start = ((), (), s32[]{:S(2)}) async-start(), calls=%async_computation.1 | async-start | bytes 2097152 | tf_op jit(solution)/shard_map/psum | solution.py:114
  632.8 1.8 copy-start.6
  634.6 45.7 %copy-start.5 = (f32[512,512]{1,0:T(8,128)}, f32[512,512]{1,0:T(8,128)S(1)}, u32[]{:S(2)}) copy-start(f32[512,512]{1,0:T(8,128)S(1)} %copy.20) | copy-start | bytes 3145732
  634.8 22.0 %copy-start.9 = (f32[512,512]{1,0:T(8,128)}, f32[512,512]{1,0:T(8,128)S(1)}, u32[]{:S(2)}) copy-start(f32[512,512]{1,0:T(8,128)S(1)} %fusion.64) | copy-start | bytes 3145732
  656.9 115.5 %copy-start.7 = (f32[512,512]{1,0:T(8,128)S(1)}, f32[512,512]{1,0:T(8,128)}, u32[]{:S(2)}) copy-start(f32[512,512]{1,0:T(8,128)} %fusion.77) | copy-start | bytes 3145732
Sparse Core Ops, SparseCore 0:
  447.1 81.0 all-gather.1
  554.7 77.9 all-reduce.2
where the time goes:
time: 806 us; the launch traced here: 796 us
  waiting for transfers between devices  426 us (53%)
  other arithmetic  181 us (22%)
  local copies, waits for them, and re-layouts  87.8 us (11%)
  matrix products  72.9 us (9%)
  between operations  17.2 us (2%)
  starting transfers between devices  11.2 us (1%)
    ppermute x2, waiting for transfers between devices, with_halo(): after = lax.ppermute(first, axis, down)  112 us
    ppermute x2, waiting for transfers between devices, with_halo(): before = lax.ppermute(last, axis, up)  104 us
    all_gather x1, waiting for transfers between devices, shards(): panels = lax.all_gather(flat, 'band', axis=1, tiled=True)  81.1 us
    another operation x14, other arithmetic, shards(): lower = jnp.linalg.cholesky(gram)  78.7 us
    psum x1, waiting for transfers between devices, shards(): gram = lax.psum(partial_gram, 'dom') * (1.0 / total_cells)  76.3 us
    ppermute x2, waiting for transfers between devices, passed_along(): return lax.ppermute(value, axis, pairs)  52 us
    another operation x3, other arithmetic, shards(): inverse = jax.scipy.linalg.solve_triangular(lower, identity, lower=True)  40.3 us
    slice x16, local copies, waits for them, and re-layouts, laplacian(): jnp.roll(orbital_field, offset, 2) + jnp.roll(orbital_field, -offset, 2)  32.4 us
  transfers between devices with their start and end apart: 8, of which 6 were waited for; matrix products, arithmetic and copies ran while one was open for 11% of the time, Pallas kernels for 0%

commit v1 on v0

v1 whole, which is shorter than its diff:
```python
import functools

import jax
import jax.numpy as jnp
from jax import lax
from jax.experimental import pallas as pl
from jax.experimental.pallas import tpu as pltpu
from jax.sharding import PartitionSpec as P

SPAN = 3
MAXPROJ = 4
PAD = 8
LANES = 128

center_weight = -205.0 / 72.0
side_weights = (8.0 / 5.0, -1.0 / 5.0, 8.0 / 315.0, -1.0 / 560.0)
HIGH = lax.Precision.HIGH
VMEM_LIMIT = 60 * 1024 * 1024


def halves(value):
    high = value.astype(jnp.bfloat16)
    return high, (value - high.astype(jnp.float32)).astype(jnp.bfloat16)


def dot3(left, right):
    dot = functools.partial(jnp.dot, preferred_element_type=jnp.float32)
    return dot(left[0], right[0]) + (dot(left[0], right[1]) + dot(left[1], right[0]))


def swapped(blocks, lane):
    count = len(blocks)
    width = LANES // count
    blocks = list(blocks)
    bit = 1
    while bit < count:
        clear = (lane // (bit * width)) % 2 == 0
        for low in range(count):
            if low & bit:
                continue
            first, second = blocks[low], blocks[low | bit]
            blocks[low] = jnp.where(clear, first, pltpu.roll(second, bit * width, 1))
            blocks[low | bit] = jnp.where(clear, pltpu.roll(first, LANES - bit * width, 1), second)
        bit *= 2
    return blocks


def swap_kernel(count, rows, in_ref, out_ref):
    lane = lax.broadcasted_iota(jnp.int32, (8, LANES), 1)

    def step(tile, carry):
        at = pl.ds(pl.multiple_of(tile * 8, 8), 8)
        in_blocks = [in_ref[index, at, :] for index in range(count)]
        for index, block in enumerate(swapped(in_blocks, lane)):
            out_ref[index, at, :] = block
        return carry

    lax.fori_loop(0, rows // 8, step, 0)


def swap_blocks(value, planes_first_in, planes_first_out):
    planes, count = value.shape[:2] if planes_first_in else value.shape[1::-1]
    rows = value.shape[2]

    def spec(planes_first):
        if planes_first:
            return pl.BlockSpec((None, count, rows, LANES), lambda p: (p, 0, 0, 0))
        return pl.BlockSpec((count, None, rows, LANES), lambda p: (0, p, 0, 0))

    lead = (planes, count) if planes_first_out else (count, planes)
    return pl.pallas_call(
        functools.partial(swap_kernel, count, rows),
        grid=(planes,),
        in_specs=[spec(planes_first_in)],
        out_specs=spec(planes_first_out),
        out_shape=jax.ShapeDtypeStruct((*lead, rows, LANES), jnp.float32),
        compiler_params=pltpu.CompilerParams(vmem_limit_bytes=VMEM_LIMIT),
    )(value)


def nonlocal_into(field, near, projector, coupling_ref, mask_ref, planes, width):
    inner = outer = None
    for plane in range(planes):
        parts = halves(field(plane))
        term = dot3(projector(plane), parts)
        inner = term if inner is None else inner + term
        if plane < SPAN - 1:
            term = dot3(projector(planes + plane), parts)
            outer = term if outer is None else outer + term
    correlations = (inner + pltpu.roll(outer, LANES - width, 1)) * mask_ref[...]
    weighted = dot3(halves(coupling_ref[...]), halves(correlations))
    moved = pltpu.roll(weighted, width, 1)
    here, next_block = halves(weighted.T), halves(moved.T)
    for plane in range(planes):
        total = dot3(here, projector(plane))
        if plane < SPAN - 1:
            total = total + dot3(next_block, projector(planes + plane))
        near[plane] = total.T


def filter_kernel(planes, side_y, side_z, width, field_ref, potential_ref, high_ref, low_ref, coupling_ref, mask_ref, out_ref, padded, first, near, *staged):
    cells = side_y * side_z
    tile = 16

    def projector(plane):
        at = pl.ds(plane * cells, cells)
        if not staged:
            return high_ref[:, at], low_ref[:, at]
        high_buffer, low_buffer, sems = staged
        copies = [
            pltpu.make_async_copy(high_ref.at[:, at], high_buffer, sems.at[0]),
            pltpu.make_async_copy(low_ref.at[:, at], low_buffer, sems.at[1]),
        ]
        for copy in copies:
            copy.start()
        for copy in copies:
            copy.wait()
        return high_buffer[...], low_buffer[...]

    def fill(y, carry):
        for plane in range(planes):
            row = field_ref[plane, pl.ds(pl.multiple_of(y * side_z, 8), side_z), :]
            padded[plane, y, pl.ds(PAD, side_z), :] = row
            padded[plane, y, pl.ds(PAD - 4, 4), :] = row[side_z - 4 :]
            padded[plane, y, pl.ds(PAD + side_z, 4), :] = row[:4]
        return carry

    lax.fori_loop(0, side_y, fill, 0)

    def apply(source, finish):
        def row(y, carry):
            for start in range(0, side_z, tile):
                def load(plane, y_at, shift):
                    return source[plane, y_at, pl.ds(PAD + start + shift, tile), :]

                inside = [load(plane, y, 0) for plane in range(planes)]
                before = [pltpu.roll(value, width, 1) for value in inside]
                after = [pltpu.roll(value, LANES - width, 1) for value in inside]
                line = before + inside + after
                at = pl.ds(pl.multiple_of(y * side_z + start, 8), tile)
                for plane in range(planes):
                    own = inside[plane]
                    total = (potential_ref[plane, at, :] - 1.5 * center_weight - 7.0) * own + near[plane, at, :]
                    for offset in range(1, 5):
                        around = line[planes + plane + offset] + line[planes + plane - offset]
                        around = around + (load(plane, y, offset) + load(plane, y, -offset))
                        up = lax.rem(y + offset, side_y)
                        down = lax.rem(y + side_y - offset, side_y)
                        around = around + (load(plane, up, 0) + load(plane, down, 0))
                        total = total - (0.5 * side_weights[offset - 1]) * around
                    finish(plane, y, start, at, total)
            return carry

        lax.fori_loop(0, side_y, row, 0)

    common = (projector, coupling_ref, mask_ref, planes, width)
    nonlocal_into(lambda plane: field_ref[plane], near, *common)

    def finish_first(plane, y, start, at, total):
        value = total * (1.0 / 6.0)
        first[plane, y, pl.ds(PAD + start, tile), :] = value
        out_ref[plane, at, :] = value
        if start == 0:
            first[plane, y, pl.ds(PAD + side_z, 4), :] = value[:4]
        if start == side_z - tile:
            first[plane, y, pl.ds(PAD - 4, 4), :] = value[tile - 4 :]

    apply(padded, finish_first)
    nonlocal_into(lambda plane: out_ref[plane], near, *common)

    def finish_second(plane, y, start, at, total):
        out_ref[plane, at, :] = total * (2.0 / 6.0) - field_ref[plane, at, :]

    apply(first, finish_second)


def filter_orbitals(field, potential, high, low, coupling, mask, side_y, side_z, width):
    planes, cells, _ = field.shape
    whole = pl.BlockSpec(memory_space=pltpu.VMEM)
    stay, staged = whole, []
    if high.size > 8 * 1024 * 1024:
        stay = pl.BlockSpec(memory_space=pl.ANY)
        staged = [pltpu.VMEM((high.shape[0], cells), jnp.bfloat16)] * 2 + [pltpu.SemaphoreType.DMA((2,))]
    return pl.pallas_call(
        functools.partial(filter_kernel, planes, side_y, side_z, width),
        in_specs=[whole, whole, stay, stay, whole, whole],
        out_specs=whole,
        out_shape=jax.ShapeDtypeStruct(field.shape, jnp.float32),
        scratch_shapes=[
            pltpu.VMEM((planes, side_y, side_z + 2 * PAD, LANES), jnp.float32),
            pltpu.VMEM((planes, side_y, side_z + 2 * PAD, LANES), jnp.float32),
            pltpu.VMEM((planes, cells, LANES), jnp.float32),
            *staged,
        ],
        compiler_params=pltpu.CompilerParams(vmem_limit_bytes=VMEM_LIMIT),
    )(field, potential, high, low, coupling, mask)


def gathered_projectors(projectors, coupling, atom_plane, projector_count, planes, cells, width):
    bands, blocks = lax.axis_size("band"), lax.axis_size("dom")
    share = projectors.shape[0] // bands
    slots = jnp.arange(MAXPROJ, dtype=jnp.int32)
    live = (slots[None, :] < projector_count[:, None]).astype(jnp.float32)
    coupled = 0.5 * (coupling + jnp.transpose(coupling, (0, 2, 1))) * live[:, :, None] * live[:, None, :]
    offset = (atom_plane - lax.axis_index("dom") * planes).astype(jnp.float32)
    extra = jnp.concatenate(
        [
            coupled,
            jnp.broadcast_to(offset[:, None, None], (*coupled.shape[:2], 1)),
            jnp.zeros((*coupled.shape[:2], LANES - MAXPROJ - 1), jnp.float32),
        ],
        axis=2,
    )
    packed = jnp.concatenate([projectors, extra], axis=2)
    mine = lax.dynamic_slice_in_dim(packed, lax.axis_index("band") * share, share, 0)
    mine = mine.reshape(share * MAXPROJ, -1)
    everyone = lax.all_gather(lax.all_gather(mine, "dom"), "band")
    count = bands * blocks * share * MAXPROJ
    everyone = everyone.reshape(count, -1)
    beta, extra = everyone[:, : SPAN * cells], everyone[:, SPAN * cells :]
    offset = extra[:, MAXPROJ]
    placed = []
    for plane in range(planes + SPAN - 1):
        value = 0.0
        for part in range(SPAN):
            value = value + jnp.where(
                (offset == plane - part)[:, None], beta[:, part * cells : (part + 1) * cells], 0.0
            )
        placed.append(value)
    high, low = halves(jnp.concatenate(placed, axis=1))
    row = jnp.arange(count, dtype=jnp.int32)
    same_atom = row[:, None] // MAXPROJ == row[None, :] // MAXPROJ
    matrix = jnp.where(same_atom, jnp.tile(extra[:, :MAXPROJ], (1, count // MAXPROJ)), 0.0)
    block_of = (row // (share * MAXPROJ)) % blocks
    lanes = jnp.arange(LANES, dtype=jnp.int32) // width
    mask = (block_of[:, None] == lanes[None, :]).astype(jnp.float32)
    return high, low, matrix, mask


def shards(orbitals, potential, projectors, coupling, atom_plane, projector_count):
    planes, side_y, side_z, local_orbs = orbitals.shape
    blocks, bands = lax.axis_size("dom"), lax.axis_size("band")
    cells = side_y * side_z
    rows = cells // blocks
    width = local_orbs // blocks
    norb = local_orbs * bands

    high, low, matrix, mask = gathered_projectors(
        projectors, coupling, atom_plane, projector_count, planes, cells, width
    )
    levels = lax.all_gather(potential.reshape(planes, cells), "dom")
    levels = jnp.transpose(levels, (1, 2, 0))
    levels = jnp.broadcast_to(levels[..., None], (planes, cells, blocks, width)).reshape(planes, cells, LANES)

    packed = swap_blocks(orbitals.reshape(planes, blocks, rows, local_orbs), True, False)
    arrived = lax.all_to_all(packed, "dom", 0, 0, tiled=True)
    field = swap_blocks(arrived, False, True).reshape(planes, cells, LANES)

    second = filter_orbitals(field, levels, high, low, matrix, mask, side_y, side_z, width)

    packed = swap_blocks(second.reshape(planes, blocks, rows, LANES), True, False)
    arrived = lax.all_to_all(packed, "dom", 0, 0, tiled=True)
    own = swap_blocks(arrived, False, True).reshape(planes * cells, local_orbs)

    panels = lax.all_gather(own, "band")
    part = jnp.einsum("co,bcq->obq", own, panels, precision=HIGH, preferred_element_type=jnp.float32)
    own_gram = lax.psum(part.reshape(local_orbs, norb), "dom")
    gram = lax.all_gather(own_gram, "band", axis=0, tiled=True) * (1.0 / (planes * cells * blocks))
    lower = jnp.linalg.cholesky(gram)
    inverse = jax.scipy.linalg.solve_triangular(lower, jnp.eye(norb, dtype=jnp.float32), lower=True)
    own_rows = lax.dynamic_slice_in_dim(inverse, lax.axis_index("band") * local_orbs, local_orbs, 0)
    result = jnp.einsum(
        "bcq,obq->co",
        panels,
        own_rows.reshape(local_orbs, bands, local_orbs),
        precision=HIGH,
        preferred_element_type=jnp.float32,
    )
    return (result.reshape(planes, side_y, side_z, local_orbs), gram)


def solution(mesh):
    placed = (
        P("dom", None, None, "band"),
        P("dom", None, None),
        P("dom", None, None),
        P("dom", None, None),
        P("dom"),
        P("dom"),
    )
    return jax.shard_map(
        shards,
        mesh=mesh,
        in_specs=placed,
        out_specs=(P("dom", None, None, "band"), P()),
        check_vma=False,
    )
```

time: 806 us -> 729 us (0.904)
  waiting for transfers between devices: 426 us -> 211 us
  blocking collectives: 0 us -> 160 us
  Pallas kernels: 0 us -> 125 us
  local copies, waits for them, and re-layouts: 87.8 us -> 37.1 us
  matrix products: 72.9 us -> 26.2 us
  other arithmetic: 181 us -> 139 us
    ppermute x6 -> x0, waiting for transfers between devices: 268 us -> none  [the longest x2 112 us: with_halo(): after = lax.ppermute(first, axis, down)]
    pallas_call x0 -> x5, Pallas kernels: none -> 125 us  [the longest x4 92.2 us: swap_blocks(): pl.pallas_call(functools.partial(swap_kernel, count, rows), grid=(planes,...]
    all_gather x0 -> x1, blocking collectives: none -> 89.9 us  [shards(): levels = lax.all_gather(potential.reshape(planes, cells), 'dom')]
    all_to_all x0 -> x1, blocking collectives: none -> 70.4 us  [shards(): arrived = lax.all_to_all(packed, 'dom', 0, 0, tiled=True)]
    slice x35 -> x2, local copies, waits for them, and re-layouts: 65.9 us -> 0.99 us  [gathered_projectors(): extra[:, :MAXPROJ]]
    all_gather x1 -> x4, waiting for transfers between devices: 81.1 us -> 141 us  [the longest x1 81 us: shards(): panels = lax.all_gather(own, 'band')]
    dot_general x9 -> x2, matrix products: 64.5 us -> 17.8 us  [the longest x1 9.08 us: shards(): jnp.einsum('bcq,obq->co', panels, own_rows.reshape(local_orbs, bands, loc...]
    div x1 -> x0, other arithmetic: 29 us -> none  [shards(): (apply_hamiltonian(orbitals, potential, layout_pieces) - 7.0 * orbitals)...]
  transfers between devices with their start and end apart: 8 -> 6, of which waited for: 6 -> 4; matrix products, arithmetic and copies ran while one was open for 11% -> 1% of each run, Pallas kernels for 0% -> 6%
where the time goes in v1:
time: 729 us; the launch traced here: 720 us
  waiting for transfers between devices  211 us (29%)
  blocking collectives  160 us (22%)
  other arithmetic  139 us (19%)
  Pallas kernels  125 us (17%)
  local copies, waits for them, and re-layouts  37.1 us (5%)
  matrix products  26.2 us (4%)
  between operations  17 us (2%)
    pallas_call x4, Pallas kernels, swap_blocks(): pl.pallas_call(functools.partial(swap_kernel, count, rows), grid=(planes,...  92.2 us
    all_gather x1, blocking collectives, shards(): levels = lax.all_gather(potential.reshape(planes, cells), 'dom')  89.9 us
    all_gather x1, waiting for transfers between devices, shards(): panels = lax.all_gather(own, 'band')  81 us
    another operation x15, other arithmetic, shards(): lower = jnp.linalg.cholesky(gram)  79.4 us
    psum x1, waiting for transfers between devices, shards(): own_gram = lax.psum(part.reshape(local_orbs, norb), 'dom')  70.5 us
    all_to_all x1, blocking collectives, shards(): arrived = lax.all_to_all(packed, 'dom', 0, 0, tiled=True)  70.4 us
    all_gather x2, waiting for transfers between devices, gathered_projectors(): everyone = lax.all_gather(lax.all_gather(mine, 'dom'), 'band')  44.1 us
    another operation x4, other arithmetic, shards(): jax.scipy.linalg.solve_triangular(lower, jnp.eye(norb, dtype=jnp.float32)...  40.4 us
  transfers between devices with their start and end apart: 6, of which 4 were waited for; matrix products, arithmetic and copies ran while one was open for 1% of the time, Pallas kernels for 6%

profile of v1, /device:TPU:0, one launch (start us, length us, event | category | flops | bytes accessed | tf_op | source)
XLA Modules:
  0.0 719.9 jit_solution(2468440101247017886)
XLA Ops:
  12.3 44.1 %all-gather.6.cloned.1.call-done = f32[8,8,4736]{2,1,0:T(8,128)} async-done(((f32[1,8,4736]{2,1,0:T(8,128)}), f32[8,8,4736]{2,1,0:T(8,128)}) %all-gather.6.cloned.1.call-update) | async-done | bytes 1212432 | tf_op jit(solution)/shard_map/all_gather | solution.py:217
  56.4 23.1 %shard_map.77 = f32[8,4,192,128]{3,2,1,0:T(8,128)} custom-call(f32[4,8,192,128]{3,2,1,0:T(8,128)} %bitcast.95), custom_call_target="tpu_custom_call" | custom-call | tf_op jit(solution)/shard_map/pallas_call | solution.py:71
  83.4 89.9 %all_gather.18 = f32[8,4,1536]{2,1,0:T(4,128)S(1)} all-gather(f32[1,4,1536]{2,1,0:T(4,128)S(1)} %all_gather_reshape.9), channel_id=1, replica_groups=mesh['band'=4,'dom'=8] {'dom'}, dimensions={0}, use_global_device_ids=true | all-gather | bytes 221184 | tf_op jit(solution)/shard_map/all_gather | solution.py:251
  181.4 23.1 %shard_map.78 = f32[4,8,192,128]{3,2,1,0:T(8,128)} custom-call(f32[8,4,192,128]{3,2,1,0:T(8,128)} %copy-done.2), custom_call_target="tpu_custom_call" | custom-call | tf_op jit(solution)/shard_map/pallas_call | solution.py:71
  212.4 4.9 subtract_convert_fusion
  218.5 32.8 %shard_map.79 = f32[4,1536,128]{2,1,0:T(8,128)} custom-call(f32[4,1536,128]{2,1,0:T(8,128)} %bitcast.92, f32[4,1536,128]{2,1,0:T(8,128)} %copy.32.potential_ref, bf16[256,9216]{1,0:T(8,128)(2,1)} %get-tuple-element.33.high_ref, bf16[256,9216]{1,0:T(8,128)(2,1)} %get-tuple-element.32.low_ref, f32[256,256]{1,0:T(8,128)} %compare_select_fusion.coupling_ref, ...), custom_call_target="tpu_custom_call" | custom-call | tf_op jit(solution)/shard_map/pallas_call | solution.py:184
  251.4 23.1 %shard_map.80 = f32[8,4,192,128]{3,2,1,0:T(8,128)} custom-call(f32[4,8,192,128]{3,2,1,0:T(8,128)} %bitcast.93), custom_call_target="tpu_custom_call" | custom-call | tf_op jit(solution)/shard_map/pallas_call | solution.py:71
  274.4 70.4 %all_to_all.10.in_ref = f32[8,4,192,128]{3,2,1,0:T(8,128)} all-to-all(f32[8,4,192,128]{3,2,1,0:T(8,128)} %shard_map.80), channel_id=1, replica_groups=mesh['band'=4,'dom'=8] {'dom'}, dimensions={0} | all-to-all | bytes 6291456 | tf_op jit(solution)/shard_map/all_to_all | solution.py:262
  344.8 23.0 %shard_map.81 = f32[4,8,192,128]{3,2,1,0:T(8,128)} custom-call(f32[8,4,192,128]{3,2,1,0:T(8,128)} %all_to_all.10.in_ref), custom_call_target="tpu_custom_call" | custom-call | tf_op jit(solution)/shard_map/pallas_call | solution.py:71
  367.9 81.0 %all-gather.8.cloned.1.call-done = f32[4,6144,128]{2,1,0:T(8,128)} async-done(((f32[1,6144,128]{2,1,0:T(8,128)}), f32[4,6144,128]{2,1,0:T(8,128)}) %all-gather.8.cloned.1.call-update) | async-done | bytes 12582928 | tf_op jit(solution)/shard_map/all_gather | solution.py:265
  449.0 12.6 %copy.33 = f32[4,6144,128]{1,2,0:T(8,128)} copy(f32[4,6144,128]{2,1,0:T(8,128)} %all-gather.8.cloned.1.call-done) | data formatting | bytes 25165824 | tf_op jit(solution)/shard_map/all_gather | solution.py:265
  461.6 8.7 %fusion.46 = f32[128,512]{0,1:T(8,128)} fusion(f32[6144,128]{1,0:T(8,128)S(1)} %bitcast.91, f32[512,6144]{1,0:T(8,128)} %bitcast.89), kind=kOutput, calls=%fused_computation.120 | convolution fusion | flops 2415919104 | bytes 15990784 | tf_op jit(solution)/shard_map/co,bcq->obq/dot_general | solution.py:266
  470.6 70.5 %all-reduce.3.cloned.1.call-done = f32[128,512]{0,1:T(8,128)} async-done(((f32[128,512]{0,1:T(8,128)}), f32[128,512]{0,1:T(8,128)}) %all-reduce.3.cloned.1.call-update) | async-done | bytes 262160 | tf_op jit(solution)/shard_map/psum | solution.py:267
  543.1 15.6 %all-gather.10.cloned.1.call-done = f32[512,512]{0,1:T(8,128)} async-done(((f32[128,512]{0,1:T(8,128)}), f32[512,512]{0,1:T(8,128)}) %all-gather.10.cloned.1.call-update) | async-done | bytes 1048592 | tf_op jit(solution)/shard_map/all_gather | solution.py:268
  560.8 11.7 %cholesky.104 = f32[128,128]{1,0:T(8,128)S(1)} custom-call(f32[128,128]{1,0:T(8,128)S(1)} %cholesky.266), custom_call_target="Cholesky" | custom-call | tf_op jit(solution)/shard_map/jit(cholesky)/cholesky | solution.py:269
  572.7 9.8 %custom-call.31 = f32[1,128,128]{1,2,0:T(8,128)S(1)} custom-call(f32[1,128,128]{2,1,0:T(8,128)S(1)} %get-tuple-element.45), custom_call_target="InvertDiagBlocksLowerTriangular" | custom-call | tf_op jit(solution)/shard_map/jit(cholesky)/cholesky | solution.py:269
  584.2 11.7 %cholesky.217 = f32[128,128]{1,0:T(8,128)S(1)} custom-call(f32[128,128]{1,0:T(8,128)S(1)} %cholesky.270), custom_call_target="Cholesky" | custom-call | tf_op jit(solution)/shard_map/jit(cholesky)/cholesky | solution.py:269
  597.2 10.0 %custom-call.32 = f32[1,128,128]{1,2,0:T(8,128)S(1)} custom-call(f32[1,128,128]{2,1,0:T(8,128)S(1)} %get-tuple-element.42), custom_call_target="InvertDiagBlocksLowerTriangular" | custom-call | tf_op jit(solution)/shard_map/jit(cholesky)/cholesky | solution.py:269
  608.7 11.7 %cholesky.238 = f32[128,128]{1,0:T(8,128)S(1)} custom-call(f32[128,128]{1,0:T(8,128)S(1)} %cholesky.275), custom_call_target="Cholesky" | custom-call | tf_op jit(solution)/shard_map/jit(cholesky)/cholesky | solution.py:269
  621.1 9.8 %custom-call.33 = f32[1,128,128]{1,2,0:T(8,128)S(1)} custom-call(f32[1,128,128]{2,1,0:T(8,128)S(1)} %get-tuple-element.39), custom_call_target="InvertDiagBlocksLowerTriangular" | custom-call | tf_op jit(solution)/shard_map/jit(cholesky)/cholesky | solution.py:269
  632.4 11.9 %cholesky.255 = f32[128,128]{1,0:T(8,128)S(1)} custom-call(f32[128,128]{1,0:T(8,128)S(1)} %convolution_subtract_fusion.5), custom_call_target="Cholesky" | custom-call | tf_op jit(solution)/shard_map/jit(cholesky)/cholesky | solution.py:269
  647.5 10.1 %while.1 = (s32[]{:T(128)}, f32[512,512]{1,0:T(8,128)S(1)}, s32[4,2]{0,1:T(2,128)S(1)}, f32[4,128,128]{2,1,0:T(8,128)}, s32[]{:T(128)}) while((s32[]{:T(128)}, f32[512,512]{1,0:T(8,128)S(1)}, s32[4,2]{0,1:T(2,128)S(1)}, f32[4,128,128]{2,1,0:T(8,128)}, s32[]{:T(128)}) %tuple.42), condition=%wide.while_cond, body=%wide.while_body.sunk | while | flops 2 | bytes 132705 | solution.py:270
  657.6 40.1 %custom-call.34 = f32[4,128,128]{1,2,0:T(8,128)S(1)} custom-call(f32[4,128,128]{2,1,0:T(8,128)} %get-tuple-element.9), custom_call_target="InvertDiagBlocksLowerTriangular" | custom-call | tf_op jit(solution)/shard_map/jit(_solve_triangular)/triangular_solve | solution.py:270
  701.9 9.1 %fusion.2 = f32[4,32,48,128]{3,2,0,1:T(8,128)S(1)} fusion(f32[128,4,128,1,1]{0,2,3,4,1:T(8,128)S(1)} %bitcast.96, f32[4,32,48,4,128]{4,2,1,0,3:T(8,128)} %bitcast.88), kind=kOutput, calls=%fused_computation.5 | convolution fusion | flops 2415919104 | bytes 15990784 | tf_op jit(solution)/shard_map/bcq,obq->co/dot_general | solution.py:272
  (108 shorter events, 54.1 us)
Async XLA Ops:
  7.2 49.2 %all-gather.6.cloned.1.call-start = ((), (), s32[]{:S(2)}) async-start(), calls=%async_computation.2 | async-start | bytes 1363968 | tf_op jit(solution)/shard_map/all_gather | solution.py:217
  12.3 192.2 %all-gather.12.cloned.1.call-start = ((), (), s32[]{:S(2)}) async-start(), calls=%async_computation.6 | async-start | bytes 6062080 | tf_op jit(solution)/shard_map/all_gather | solution.py:217
  79.5 3.9 copy-start.7
  79.5 100.3 %all-to-all-start = ((f32[8,4,192,128]{3,2,1,0:T(8,128)}), f32[8,4,192,128]{3,2,1,0:T(8,128)S(1)}, u32[]{:S(2)}, u32[]{:S(2)}) async-start(f32[8,4,192,128]{3,2,1,0:T(8,128)} %shard_map.77), calls=%async_computation | async-start | bytes 6291456 | tf_op jit(solution)/shard_map/all_to_all | solution.py:256
  83.3 365.7 %all-gather.8.cloned.1.call-start = ((), (), s32[]{:S(2)}) async-start(), calls=%async_computation.3 | async-start | bytes 15728640 | tf_op jit(solution)/shard_map/all_gather | solution.py:265
  179.7 1.7 copy-start.2
  206.7 3.8 copy-start
  367.9 93.7 %copy-start.1 = (f32[4,8,192,128]{3,2,1,0:T(8,128)S(1)}, f32[4,8,192,128]{3,2,1,0:T(8,128)}, u32[]{:S(2)}) copy-start(f32[4,8,192,128]{3,2,1,0:T(8,128)} %shard_map.81) | copy-start | bytes 9437188
  367.9 173.2 %all-reduce.3.cloned.1.call-start = ((), (), s32[]{:S(2)}) async-start(), calls=%async_computation.4 | async-start | bytes 524288 | tf_op jit(solution)/shard_map/psum | solution.py:267
  470.3 88.4 %all-gather.10.cloned.1.call-start = ((), (), s32[]{:S(2)}) async-start(), calls=%async_computation.5 | async-start | bytes 1310720 | tf_op jit(solution)/shard_map/all_gather | solution.py:268
  558.7 1.8 copy-start.4
  560.5 46.9 %copy-start.3 = (f32[512,512]{1,0:T(8,128)}, f32[512,512]{1,0:T(8,128)S(1)}, u32[]{:S(2)}) copy-start(f32[512,512]{1,0:T(8,128)S(1)} %copy.35) | copy-start | bytes 3145732
  560.7 22.0 %copy-start.6 = (f32[512,512]{1,0:T(8,128)}, f32[512,512]{1,0:T(8,128)S(1)}, u32[]{:S(2)}) copy-start(f32[512,512]{1,0:T(8,128)S(1)} %fusion.5) | copy-start | bytes 3145732
  582.8 116.1 %copy-start.5 = (f32[512,512]{1,0:T(8,128)S(1)}, f32[512,512]{1,0:T(8,128)}, u32[]{:S(2)}) copy-start(f32[512,512]{1,0:T(8,128)} %fusion.14) | copy-start | bytes 3145732
Sparse Core Ops, SparseCore 0:
  12.4 43.9 all-gather.5
  57.9 37.4 all-gather.11
  368.0 80.9 all-gather.7
  470.5 70.5 all-reduce.2
  542.5 16.1 all-gather.9

commit v2 on v1

v2 whole, which is shorter than its diff:
```python
import functools

import jax
import jax.numpy as jnp
from jax import lax
from jax.experimental import pallas as pl
from jax.experimental.pallas import tpu as pltpu
from jax.sharding import PartitionSpec as P

SPAN = 3
MAXPROJ = 4
PAD = 8
LANES = 128
GROUP = 8

center_weight = -205.0 / 72.0
side_weights = (8.0 / 5.0, -1.0 / 5.0, 8.0 / 315.0, -1.0 / 560.0)
HIGHEST = lax.Precision.HIGHEST
WHOLE = pl.BlockSpec(memory_space=pltpu.VMEM)
PARAMS = pltpu.CompilerParams(vmem_limit_bytes=60 * 1024 * 1024)


def cost(flops, bytes_accessed):
    return pl.CostEstimate(flops=int(flops), bytes_accessed=int(bytes_accessed), transcendentals=0)


def halves(value):
    high = value.astype(jnp.bfloat16)
    return high, (value - high.astype(jnp.float32)).astype(jnp.bfloat16)


def side_by_side(value):
    return jnp.concatenate(halves(value), axis=1)


def dot_halves(left, right):
    dot = functools.partial(jnp.dot, preferred_element_type=jnp.float32)
    return dot(left[0], right) + dot(left[1], right)


def folded(value):
    return value[:, :LANES] + value[:, LANES:]


def swapped(blocks, lane):
    count = len(blocks)
    width = LANES // count
    blocks = list(blocks)
    bit = 1
    while bit < count:
        clear = (lane // (bit * width)) % 2 == 0
        for low in range(count):
            if low & bit:
                continue
            first, second = blocks[low], blocks[low | bit]
            blocks[low] = jnp.where(clear, first, pltpu.roll(second, bit * width, 1))
            blocks[low | bit] = jnp.where(clear, pltpu.roll(first, LANES - bit * width, 1), second)
        bit *= 2
    return blocks


def swap_into(read, write, count, rows):
    tile = 8 * max(1, 32 // count)
    lane = lax.broadcasted_iota(jnp.int32, (tile, LANES), 1)

    def step(index, carry):
        start = pl.multiple_of(index * tile, 8)
        for block, value in enumerate(swapped([read(block, start, tile) for block in range(count)], lane)):
            write(block, start, tile, value)
        return carry

    lax.fori_loop(0, rows // tile, step, 0)


def swap_kernel(count, rows, in_ref, out_ref):
    def read(block, start, tile):
        return in_ref[block, pl.ds(start, tile), :]

    def write(block, start, tile, value):
        out_ref[block, pl.ds(start, tile), :] = value

    swap_into(read, write, count, rows)


def swap_in(value):
    planes, count, rows, _ = value.shape
    return pl.pallas_call(
        functools.partial(swap_kernel, count, rows),
        grid=(planes,),
        in_specs=[pl.BlockSpec((None, count, rows, LANES), lambda p: (p, 0, 0, 0))],
        out_specs=pl.BlockSpec((count, None, rows, LANES), lambda p: (0, p, 0, 0)),
        out_shape=jax.ShapeDtypeStruct((count, planes, rows, LANES), jnp.float32),
        compiler_params=PARAMS,
        cost_estimate=cost(0, 8 * value.size),
    )(value)


def swap_out(value):
    count, rows, _ = value.shape
    return pl.pallas_call(
        functools.partial(swap_kernel, count, rows),
        in_specs=[WHOLE],
        out_specs=WHOLE,
        out_shape=jax.ShapeDtypeStruct(value.shape, jnp.float32),
        compiler_params=PARAMS,
        cost_estimate=cost(0, 8 * value.size),
    )(value)


def nonlocal_into(field, near, projector, transposed, coupling_ref, mask_ref, planes, cells, width):
    inner = outer = None
    for plane in range(planes):
        parts = side_by_side(field(plane))
        term = dot_halves(projector(plane), parts)
        inner = term if inner is None else inner + term
        if plane < SPAN - 1:
            term = dot_halves(projector(planes + plane), parts)
            outer = term if outer is None else outer + term
    correlations = (folded(inner) + pltpu.roll(folded(outer), LANES - width, 1)) * mask_ref[...]
    weighted = folded(dot_halves(halves(coupling_ref[...]), side_by_side(correlations)))
    here, shifted = side_by_side(weighted), side_by_side(pltpu.roll(weighted, width, 1))
    tile = 256

    def add(plane, right, fresh):
        high, low, base = transposed(plane)

        def step(index, carry):
            start = pl.multiple_of(index * tile, tile)
            at, to = pl.ds(base + start, tile), pl.ds(start, tile)
            value = folded(dot_halves((high[at, :], low[at, :]), right))
            where = plane if fresh else plane - planes
            near[where, to, :] = value if fresh else near[where, to, :] + value
            return carry

        lax.fori_loop(0, cells // tile, step, 0)

    for plane in range(planes):
        add(plane, here, True)
        if plane < SPAN - 1:
            add(planes + plane, shifted, False)


def filter_kernel(
    planes, side_y, side_z, width, arrived_ref, potential_ref, high_ref, low_ref, high_t_ref, low_t_ref, coupling_ref, mask_ref, *rest
):
    outs, (field, padded, first, flat, near, *staged) = rest[:planes], rest[planes:]
    cells = side_y * side_z
    count, _, rows, _ = arrived_ref.shape
    tile = 16

    def copied(pairs):
        copies = [pltpu.make_async_copy(source, target, staged[4].at[at]) for at, (source, target) in enumerate(pairs)]
        for copy in copies:
            copy.start()
        for copy in copies:
            copy.wait()

    def projector(plane):
        at = pl.ds(plane * cells, cells)
        if not staged:
            return high_ref[:, at], low_ref[:, at]
        copied([(high_ref.at[:, at], staged[0]), (low_ref.at[:, at], staged[1])])
        return staged[0][...], staged[1][...]

    def transposed(plane):
        if not staged:
            return high_t_ref, low_t_ref, plane * cells
        at = pl.ds(plane * cells, cells)
        copied([(high_t_ref.at[at, :], staged[2]), (low_t_ref.at[at, :], staged[3])])
        return staged[2], staged[3], 0

    for plane in range(planes):
        swap_into(
            lambda block, start, size: arrived_ref[block, plane, pl.ds(start, size), :],
            lambda block, start, size, value: field.__setitem__(
                (plane, pl.ds(pl.multiple_of(block * rows + start, 8), size), slice(None)), value
            ),
            count,
            rows,
        )

    def fill(y, carry):
        for plane in range(planes):
            row = field[plane, pl.ds(pl.multiple_of(y * side_z, 8), side_z), :]
            padded[plane, y, pl.ds(PAD, side_z), :] = row
            padded[plane, y, pl.ds(PAD - 4, 4), :] = row[side_z - 4 :]
            padded[plane, y, pl.ds(PAD + side_z, 4), :] = row[:4]
        return carry

    lax.fori_loop(0, side_y, fill, 0)

    def apply(source, finish):
        def row(y, carry):
            for start in range(0, side_z, tile):
                def load(plane, y_at, shift):
                    return source[plane, y_at, pl.ds(PAD + start + shift, tile), :]

                inside = [load(plane, y, 0) for plane in range(planes)]
                before = [pltpu.roll(value, width, 1) for value in inside]
                after = [pltpu.roll(value, LANES - width, 1) for value in inside]
                line = before + inside + after
                at = pl.ds(pl.multiple_of(y * side_z + start, 8), tile)
                for plane in range(planes):
                    own = inside[plane]
                    total = (potential_ref[plane, at, :] - 1.5 * center_weight - 7.0) * own + near[plane, at, :]
                    for offset in range(1, 5):
                        around = line[planes + plane + offset] + line[planes + plane - offset]
                        around = around + (load(plane, y, offset) + load(plane, y, -offset))
                        up = lax.rem(y + offset, side_y)
                        down = lax.rem(y + side_y - offset, side_y)
                        around = around + (load(plane, up, 0) + load(plane, down, 0))
                        total = total - (0.5 * side_weights[offset - 1]) * around
                    finish(plane, y, start, at, total)
            return carry

        lax.fori_loop(0, side_y, row, 0)

    common = (projector, transposed, coupling_ref, mask_ref, planes, cells, width)
    nonlocal_into(lambda plane: field[plane], near, *common)

    def finish_first(plane, y, start, at, total):
        value = total * (1.0 / 6.0)
        first[plane, y, pl.ds(PAD + start, tile), :] = value
        flat[plane, at, :] = value
        if start == 0:
            first[plane, y, pl.ds(PAD + side_z, 4), :] = value[:4]
        if start == side_z - tile:
            first[plane, y, pl.ds(PAD - 4, 4), :] = value[tile - 4 :]

    apply(padded, finish_first)
    nonlocal_into(lambda plane: flat[plane], near, *common)

    def finish_second(plane, y, start, at, total):
        flat[plane, at, :] = total * (2.0 / 6.0) - field[plane, at, :]

    apply(first, finish_second)
    for plane in range(planes):
        swap_into(
            lambda block, start, size: flat[plane, pl.ds(pl.multiple_of(block * rows + start, 8), size), :],
            lambda block, start, size, value: outs[plane].__setitem__((block, pl.ds(start, size), slice(None)), value),
            count,
            rows,
        )


def filter_orbitals(arrived, potential, high, low, coupling, mask, side_y, side_z, width):
    count, planes, rows, _ = arrived.shape
    cells = side_y * side_z
    stay, staged = WHOLE, []
    if high.size > 8 * 1024 * 1024:
        stay = pl.BlockSpec(memory_space=pl.ANY)
        staged = [pltpu.VMEM((high.shape[0], cells), jnp.bfloat16)] * 2
        staged += [pltpu.VMEM((cells, high.shape[0]), jnp.bfloat16)] * 2
        staged += [pltpu.SemaphoreType.DMA((2,))]
    flat = pltpu.VMEM((planes, cells, LANES), jnp.float32)
    high_side = pltpu.VMEM((planes, side_y, side_z + 2 * PAD, LANES), jnp.float32)
    return pl.pallas_call(
        functools.partial(filter_kernel, planes, side_y, side_z, width),
        in_specs=[WHOLE, WHOLE, stay, stay, stay, stay, WHOLE, WHOLE],
        out_specs=[WHOLE] * planes,
        out_shape=[jax.ShapeDtypeStruct((count, rows, LANES), jnp.float32)] * planes,
        scratch_shapes=[flat, high_side, high_side, flat, flat, *staged],
        compiler_params=PARAMS,
        cost_estimate=cost(12 * high.size * LANES, 16 * high.size + 12 * arrived.size),
    )(arrived, potential, high, low, high.T, low.T, coupling, mask)


def gathered_parts(potential, projectors, coupling, atom_plane, projector_count, planes, cells, width):
    bands, blocks = lax.axis_size("band"), lax.axis_size("dom")
    band = lax.axis_index("band")
    share = projectors.shape[0] // bands
    lines = share * MAXPROJ
    slots = jnp.arange(MAXPROJ, dtype=jnp.int32)
    live = (slots[None, :] < projector_count[:, None]).astype(jnp.float32)
    coupled = 0.5 * (coupling + jnp.transpose(coupling, (0, 2, 1))) * live[:, :, None] * live[:, None, :]
    offset = (atom_plane - lax.axis_index("dom") * planes).astype(jnp.float32)
    offset = jnp.broadcast_to(offset[:, None, None], (*coupled.shape[:2], 1))
    extra = jnp.concatenate([coupled, offset], axis=2)
    piece = planes * cells // (bands * lines)
    levels = lax.dynamic_slice_in_dim(potential.reshape(bands * lines, piece), band * lines, lines, 0)
    mine = [
        lax.dynamic_slice_in_dim(projectors, band * share, share, 0).reshape(lines, -1),
        levels,
        lax.dynamic_slice_in_dim(extra, band * share, share, 0).reshape(lines, -1),
    ]
    mine.append(jnp.zeros((lines, -(piece + MAXPROJ + 1) % LANES), jnp.float32))
    everyone = lax.all_gather(jnp.concatenate(mine, axis=1), ("band", "dom"))
    count = bands * blocks * lines
    everyone = everyone.reshape(count, -1)
    beta = everyone[:, : SPAN * cells]
    levels = everyone[:, SPAN * cells : SPAN * cells + piece].reshape(bands, blocks, lines * piece)
    extra = everyone[:, SPAN * cells + piece :]
    levels = jnp.transpose(levels, (0, 2, 1)).reshape(planes, cells, blocks)
    levels = jnp.broadcast_to(levels[..., None], (*levels.shape, width)).reshape(planes, cells, LANES)
    offset = extra[:, MAXPROJ]
    placed = []
    for plane in range(planes + SPAN - 1):
        value = 0.0
        for part in range(SPAN):
            value = value + jnp.where(
                (offset == plane - part)[:, None], beta[:, part * cells : (part + 1) * cells], 0.0
            )
        placed.append(value)
    placed = jnp.concatenate(placed, axis=1)
    high = lax.reduce_precision(placed, 8, 7)
    low = (placed - high).astype(jnp.bfloat16)
    high = high.astype(jnp.bfloat16)
    row = jnp.arange(count, dtype=jnp.int32)
    same_atom = row[:, None] // MAXPROJ == row[None, :] // MAXPROJ
    matrix = jnp.where(same_atom, jnp.tile(extra[:, :MAXPROJ], (1, count // MAXPROJ)), 0.0)
    block_of = (row // lines) % blocks
    lanes = jnp.arange(LANES, dtype=jnp.int32) // width
    mask = (block_of[:, None] == lanes[None, :]).astype(jnp.float32)
    return levels, high, low, matrix, mask


def gram_kernel(own_ref, panels_ref, out_ref):
    @pl.when(pl.program_id(0) == 0)
    def _():
        out_ref[...] = jnp.zeros_like(out_ref)

    left = halves(own_ref[...].T)
    for band in range(panels_ref.shape[0]):
        at = pl.ds(band * LANES, LANES)
        out_ref[:, at] = out_ref[:, at] + folded(dot_halves(left, side_by_side(panels_ref[band])))


def gram_rows(own, panels):
    bands, cells, _ = panels.shape
    tile = cells // 4
    return pl.pallas_call(
        gram_kernel,
        grid=(cells // tile,),
        in_specs=[
            pl.BlockSpec((tile, LANES), lambda i: (i, 0)),
            pl.BlockSpec((bands, tile, LANES), lambda i: (0, i, 0)),
        ],
        out_specs=pl.BlockSpec((LANES, bands * LANES), lambda i: (0, 0)),
        out_shape=jax.ShapeDtypeStruct((LANES, bands * LANES), jnp.float32),
        compiler_params=PARAMS,
        cost_estimate=cost(8 * cells * LANES * LANES * bands, 4 * (own.size + panels.size)),
    )(own, panels)


def rotate_kernel(inverse_ref, *rest):
    panels, out_ref = rest[:-1], rest[-1]
    right = side_by_side(inverse_ref[...].T)
    for plane, panel in enumerate(panels):
        left = halves(jnp.concatenate([panel[band] for band in range(panel.shape[0])], axis=1))
        out_ref[plane] = folded(dot_halves(left, right))


def rotated(inverse_rows, panels):
    bands, cells, _ = panels[0].shape
    tile = cells // 4
    return pl.pallas_call(
        rotate_kernel,
        grid=(cells // tile,),
        in_specs=[pl.BlockSpec(inverse_rows.shape, lambda i: (0, 0))]
        + [pl.BlockSpec((bands, tile, LANES), lambda i: (0, i, 0))] * len(panels),
        out_specs=pl.BlockSpec((len(panels), tile, LANES), lambda i: (0, i, 0)),
        out_shape=jax.ShapeDtypeStruct((len(panels), cells, LANES), jnp.float32),
        compiler_params=PARAMS,
    )(inverse_rows, *panels)


def thirds(value):
    first = value.astype(jnp.bfloat16).astype(jnp.float32)
    rest = value - first
    second = rest.astype(jnp.bfloat16).astype(jnp.float32)
    return first, second, rest - second


def eliminate(work, result):
    sublane = lax.broadcasted_iota(jnp.int32, (GROUP, LANES), 0)
    for top in range(0, LANES, GROUP):
        left = [jnp.broadcast_to(work[pl.ds(top + i, 1), :LANES], (GROUP, LANES)) for i in range(GROUP)]
        right = [jnp.broadcast_to(work[pl.ds(top + i, 1), LANES:], (GROUP, LANES)) for i in range(GROUP)]
        entry = {
            (i, j): jnp.broadcast_to(left[i][:, top + j : top + j + 1], (GROUP, LANES))
            for i in range(GROUP)
            for j in range(i, GROUP)
        }
        for i in range(GROUP):
            scale = lax.rsqrt(entry[i, i])
            left[i] = left[i] * scale
            right[i] = right[i] * scale
            factor = {j: entry[i, j] * scale for j in range(i + 1, GROUP)}
            for m in range(i + 1, GROUP):
                for j in range(m, GROUP):
                    entry[m, j] = entry[m, j] - factor[m] * factor[j]
                left[m] = left[m] - factor[m] * left[i]
                right[m] = right[m] - factor[m] * right[i]
        upper, lower = left[0], right[0]
        for i in range(1, GROUP):
            upper = jnp.where(sublane == i, left[i], upper)
            lower = jnp.where(sublane == i, right[i], lower)
        result[pl.ds(top, GROUP), :] = lower
        below = top + GROUP
        if below < LANES:
            a, b, c = thirds(upper)
            x, y, z = thirds(lower)
            columns = jnp.concatenate([a, a, b, b, a, c], axis=0).T[below:].astype(jnp.bfloat16)
            rows = jnp.concatenate(
                [jnp.concatenate([a, b, a, b, c, a], axis=0), jnp.concatenate([x, y, x, y, z, x], axis=0)], axis=1
            ).astype(jnp.bfloat16)
            rest = pl.ds(below, LANES - below)
            work[rest, :] = work[rest, :] - jnp.dot(columns, rows, preferred_element_type=jnp.float32)


def cholesky_kernel(gram_ref, out_ref, matrix, work, corner, scaled):
    size = gram_ref.shape[0]
    dot = functools.partial(jnp.dot, precision=HIGHEST, preferred_element_type=jnp.float32)
    diagonal = lax.broadcasted_iota(jnp.int32, (LANES, LANES), 0) == lax.broadcasted_iota(jnp.int32, (LANES, LANES), 1)
    identity = diagonal.astype(jnp.float32)
    matrix[:, :size] = gram_ref[...]
    matrix[:, size:] = jnp.zeros((size, size), jnp.float32)
    for at in range(0, size, LANES):
        matrix[pl.ds(at, LANES), size + at : size + at + LANES] = identity

    def block(index, carry):
        start = pl.multiple_of(index * LANES, LANES)
        at = pl.ds(start, LANES)
        work[:, :LANES] = matrix[at, at]
        work[:, LANES:] = identity
        eliminate(work, corner)
        scaled[...] = dot(corner[...], matrix[at, :])
        out_ref[at, :] = scaled[:, size:]

        def below(other, carry):
            rows = pl.ds(pl.multiple_of(other * LANES, LANES), LANES)
            matrix[rows, :] = matrix[rows, :] - dot(scaled[:, rows].T, scaled[...])
            return carry

        lax.fori_loop(index + 1, size // LANES, below, 0)
        return carry

    lax.fori_loop(0, size // LANES, block, 0)


def cholesky_inverse(gram):
    size = gram.shape[0]
    whole = pl.BlockSpec(memory_space=pltpu.VMEM)
    return pl.pallas_call(
        cholesky_kernel,
        in_specs=[whole],
        out_specs=whole,
        out_shape=jax.ShapeDtypeStruct((size, size), jnp.float32),
        scratch_shapes=[
            pltpu.VMEM((size, 2 * size), jnp.float32),
            pltpu.VMEM((LANES, 2 * LANES), jnp.float32),
            pltpu.VMEM((LANES, LANES), jnp.float32),
            pltpu.VMEM((LANES, 2 * size), jnp.float32),
        ],
        compiler_params=PARAMS,
    )(gram)


def shards(orbitals, potential, projectors, coupling, atom_plane, projector_count):
    planes, side_y, side_z, local_orbs = orbitals.shape
    blocks, bands = lax.axis_size("dom"), lax.axis_size("band")
    cells = side_y * side_z
    rows = cells // blocks
    width = local_orbs // blocks
    norb = local_orbs * bands

    packed = swap_in(orbitals.reshape(planes, blocks, rows, local_orbs))
    arrived = lax.all_to_all(packed, "dom", 0, 0, tiled=True)
    parts = gathered_parts(potential, projectors, coupling, atom_plane, projector_count, planes, cells, width)
    seconds = filter_orbitals(arrived, *parts, side_y, side_z, width)

    panels, part = [], 0.0
    for packed in seconds:
        own = swap_out(lax.all_to_all(packed, "dom", 0, 0, tiled=True)).reshape(cells, local_orbs)
        panels.append(lax.all_gather(own, "band"))
        part = part + gram_rows(own, panels[-1])

    pieces = lax.all_to_all(part.reshape(blocks, width, norb), "dom", 0, 0, tiled=True)
    piece = jnp.sum(pieces, axis=0) * (1.0 / (planes * cells * blocks))
    gram = lax.all_gather(piece, ("band", "dom")).reshape(norb, norb)
    inverse = cholesky_inverse(gram)
    own_rows = lax.dynamic_slice_in_dim(inverse, lax.axis_index("band") * local_orbs, local_orbs, 0)
    result = rotated(own_rows, panels)
    return (result.reshape(planes, side_y, side_z, local_orbs), gram)


def solution(mesh):
    placed = (
        P("dom", None, None, "band"),
        P("dom", None, None),
        P("dom", None, None),
        P("dom", None, None),
        P("dom"),
        P("dom"),
    )
    return jax.shard_map(
        shards,
        mesh=mesh,
        in_specs=placed,
        out_specs=(P("dom", None, None, "band"), P()),
        check_vma=False,
    )
```

time: 729 us -> 490 us (0.67); the launches traced: 720 us -> 488 us
  other arithmetic: 139 us -> 16 us
  blocking collectives: 160 us -> 110 us
  waiting for transfers between devices: 211 us -> 169 us
  matrix products: 26.2 us -> 0 us
  Pallas kernels: 125 us -> 138 us
    another operation x19 -> x0, other arithmetic: 120 us -> none  [the longest x15 79.4 us: shards(): lower = jnp.linalg.cholesky(gram)]
    all_gather x1 -> x0, blocking collectives: 89.9 us -> none  [shards(): levels = lax.all_gather(potential.reshape(planes, cells), 'dom')]
    psum x1 -> x0, waiting for transfers between devices: 70.5 us -> none  [shards(): own_gram = lax.psum(part.reshape(local_orbs, norb), 'dom')]
    all_to_all x1 -> x5, blocking collectives: 70.4 us -> 110 us  [the longest x4 95.3 us: shards(): lax.all_to_all(packed, 'dom', 0, 0, tiled=True)]
    all_gather x4 -> x6, waiting for transfers between devices: 141 us -> 169 us  [the longest x1 93.9 us: gathered_parts(): everyone = lax.all_gather(jnp.concatenate(mine, axis=1), ('band', 'dom'))]
    pallas_call x1, Pallas kernels: 32.8 us -> 57 us  [filter_orbitals(): pl.pallas_call(functools.partial(filter_kernel, planes, side_y, side_z, w...]
    dot_general x2 -> x0, matrix products: 17.8 us -> none  [the longest x1 9.08 us: shards(): jnp.einsum('bcq,obq->co', panels, own_rows.reshape(local_orbs, bands, loc...]
    convert_element_type x0 -> x2, local copies, waits for them, and re-layouts: none -> 13.4 us  [the longest x1 6.7 us: gathered_parts(): low = (placed - high).astype(jnp.bfloat16)]
  transfers between devices with their start and end apart: 6 -> 7, of which waited for: 4 -> 3; matrix products, arithmetic and copies ran while one was open for 1% -> 8% of each run, Pallas kernels for 6% -> 7%
where the time goes in v2:
time: 490 us; the launch traced here: 488 us
  waiting for transfers between devices  169 us (34%)
  Pallas kernels  138 us (28%)
  blocking collectives  110 us (22%)
  local copies, waits for them, and re-layouts  33.5 us (7%)
  other arithmetic  16 us (3%)
  between operations  14.3 us (3%)
  starting transfers between devices  7.52 us (2%)
    all_to_all x4, blocking collectives, shards(): lax.all_to_all(packed, 'dom', 0, 0, tiled=True)  95.3 us
    all_gather x1, waiting for transfers between devices, gathered_parts(): everyone = lax.all_gather(jnp.concatenate(mine, axis=1), ('band', 'dom'))  93.9 us
    pallas_call x1, Pallas kernels, filter_orbitals(): pl.pallas_call(functools.partial(filter_kernel, planes, side_y, side_z, w...  57 us
    all_gather x1, waiting for transfers between devices, shards(): gram = lax.all_gather(piece, ('band', 'dom')).reshape(norb, norb)  52.1 us
    pallas_call x1, Pallas kernels, cholesky_inverse(): pl.pallas_call(cholesky_kernel, in_specs=[whole], out_specs=whole, out_sh...  30.2 us
    all_gather x4, waiting for transfers between devices, shards(): panels.append(lax.all_gather(own, 'band'))  22.9 us
    pallas_call x4, Pallas kernels, gram_rows(): pl.pallas_call(gram_kernel, grid=(cells // tile,), in_specs=[pl.BlockSpec...  19.3 us
    pallas_call x4, Pallas kernels, swap_out(): pl.pallas_call(functools.partial(swap_kernel, count, rows), in_specs=[WHO...  14.7 us
  transfers between devices with their start and end apart: 7, of which 3 were waited for; matrix products, arithmetic and copies ran while one was open for 8% of the time, Pallas kernels for 7%

profile of v2, /device:TPU:0, one launch (start us, length us, event | category | flops | bytes accessed | tf_op | source)
XLA Modules:
  0.0 488.4 jit_solution(7125774662285585588)
XLA Ops:
  12.0 8.4 %shard_map.77 = f32[8,4,192,128]{3,2,1,0:T(8,128)} custom-call(f32[4,8,192,128]{3,2,1,0:T(8,128)} %bitcast.35), custom_call_target="tpu_custom_call" | custom-call | bytes 6291456 | tf_op jit(solution)/shard_map/pallas_call | solution.py:87
  20.4 7.3 %all-to-all-start = ((f32[8,4,192,128]{3,2,1,0:T(8,128)}), f32[8,4,192,128]{3,2,1,0:T(8,128)}, u32[]{:S(2)}, u32[]{:S(2)}) async-start(f32[8,4,192,128]{3,2,1,0:T(8,128)} %shard_map.77), calls=%async_computation | async-start | bytes 6291456 | tf_op jit(solution)/shard_map/all_to_all | solution.py:468
  28.5 93.9 %all-gather.17.cloned.1.call-done = f32[256,4864]{1,0:T(8,128)} async-done(((f32[8,4864]{1,0:T(8,128)}), f32[256,4864]{1,0:T(8,128)}) %all-gather.17.cloned.1.call-update) | async-done | bytes 4980752 | tf_op jit(solution)/shard_map/all_gather | solution.py:287
  122.4 4.3 fusion.7
  137.4 4.6 fusion
  142.0 6.7 %copy.43.high_ref = bf16[256,9216]{1,0:T(8,128)(2,1)} copy(bf16[256,9216]{0,1:T(8,128)(2,1)} %get-tuple-element.19) | data formatting | bytes 9437184 | tf_op jit(solution)/shard_map/convert_element_type | solution.py:307
  148.7 6.7 %copy.44.low_ref = bf16[256,9216]{1,0:T(8,128)(2,1)} copy(bf16[256,9216]{0,1:T(8,128)(2,1)} %get-tuple-element.18) | data formatting | bytes 9437184 | tf_op jit(solution)/shard_map/convert_element_type | solution.py:306
  162.1 57.0 %shard_map.78 = (f32[8,192,128]{2,1,0:T(8,128)}, f32[8,192,128]{2,1,0:T(8,128)}, f32[8,192,128]{2,1,0:T(8,128)}, f32[8,192,128]{2,1,0:T(8,128)}) custom-call(f32[8,4,192,128]{3,2,1,0:T(8,128)} %all-to-all-done.arrived_ref, f32[4,1536,128]{2,1,0:T(8,128)} %copy.42.potential_ref, bf16[256,9216]{1,0:T(8,128)(2,1)} %copy.43.high_ref, ...), custom_call_target="tpu_custom_call" | custom-call | flops 3623878656 | bytes 47185920 | tf_op jit(solution)/shard_map/pallas_call | solution.py:257
  219.1 25.0 %all_to_all.30.in_ref = f32[8,192,128]{2,1,0:T(8,128)} all-to-all(f32[8,192,128]{2,1,0:T(8,128)} %get-tuple-element.7), channel_id=1, replica_groups=mesh['band'=4,'dom'=8] {'dom'}, dimensions={0} | all-to-all | bytes 1572864 | tf_op jit(solution)/shard_map/all_to_all | solution.py:474
  244.1 3.7 shard_map.81
  247.9 23.9 %all_to_all.31.in_ref = f32[8,192,128]{2,1,0:T(8,128)} all-to-all(f32[8,192,128]{2,1,0:T(8,128)S(1)} %copy-done.9), channel_id=1, replica_groups=mesh['band'=4,'dom'=8] {'dom'}, dimensions={0} | all-to-all | bytes 1572864 | tf_op jit(solution)/shard_map/all_to_all | solution.py:474
  271.7 3.7 shard_map.79
  275.5 23.3 %all_to_all.32.in_ref = f32[8,192,128]{2,1,0:T(8,128)} all-to-all(f32[8,192,128]{2,1,0:T(8,128)S(1)} %copy-done.8), channel_id=1, replica_groups=mesh['band'=4,'dom'=8] {'dom'}, dimensions={0} | all-to-all | bytes 1572864 | tf_op jit(solution)/shard_map/all_to_all | solution.py:474
  298.8 3.7 shard_map.83
  302.6 23.2 %all_to_all.33.in_ref = f32[8,192,128]{2,1,0:T(8,128)} all-to-all(f32[8,192,128]{2,1,0:T(8,128)S(1)} %copy-done.7), channel_id=1, replica_groups=mesh['band'=4,'dom'=8] {'dom'}, dimensions={0} | all-to-all | bytes 1572864 | tf_op jit(solution)/shard_map/all_to_all | solution.py:474
  329.4 5.0 %shard_map.82 = f32[128,512]{1,0:T(8,128)} custom-call(f32[1536,128]{1,0:T(8,128)} %bitcast.28, f32[4,1536,128]{2,1,0:T(8,128)} %all-gather.11.cloned.1.call-done.panels_ref.rest_1_), custom_call_target="tpu_custom_call" | custom-call | flops 805306368 | bytes 3932160 | tf_op jit(solution)/shard_map/pallas_call | solution.py:331
  334.4 4.8 shard_map.80
  339.2 4.8 shard_map.84
  343.9 22.9 %all-gather.15.cloned.1.call-done.panels_ref.rest_3_ = f32[4,1536,128]{2,1,0:T(8,128)} async-done(((f32[1,1536,128]{2,1,0:T(8,128)}), f32[4,1536,128]{2,1,0:T(8,128)}) %all-gather.15.cloned.1.call-update) | async-done | bytes 3145744 | tf_op jit(solution)/shard_map/all_gather | solution.py:475
  366.9 4.8 shard_map.86
  372.7 14.6 %all_to_all.34 = f32[8,16,512]{2,1,0:T(8,128)S(1)} all-to-all(f32[8,16,512]{2,1,0:T(8,128)S(1)} %bitcast.37), channel_id=1, replica_groups=mesh['band'=4,'dom'=8] {'dom'}, dimensions={0} | all-to-all | bytes 524288 | tf_op jit(solution)/shard_map/all_to_all | solution.py:478
  388.0 52.1 %all-gather.19.cloned.1.call-done.gram_ref = f32[512,512]{1,0:T(8,128)} async-done(((f32[16,512]{1,0:T(8,128)}), f32[512,512]{1,0:T(8,128)}) %all-gather.19.cloned.1.call-update) | async-done | bytes 1048592 | tf_op jit(solution)/shard_map/all_gather | solution.py:480
  440.0 30.2 %shard_map.87 = f32[512,512]{1,0:T(8,128)} custom-call(f32[512,512]{1,0:T(8,128)} %all-gather.19.cloned.1.call-done.gram_ref), custom_call_target="tpu_custom_call" | custom-call | tf_op jit(solution)/shard_map/pallas_call | solution.py:444
  471.9 8.6 %shard_map.88 = f32[4,1536,128]{2,1,0:T(8,128)} custom-call(f32[128,512]{1,0:T(8,128)} %constant_dynamic-slice_fusion.inverse_ref, f32[4,1536,128]{2,1,0:T(8,128)} %all-gather.9.cloned.1.call-done.panels_ref.rest_0_, f32[4,1536,128]{2,1,0:T(8,128)} %all-gather.11.cloned.1.call-done.panels_ref.rest_1_, ...), custom_call_target="tpu_custom_call" | custom-call | tf_op jit(solution)/shard_map/pallas_call | solution.py:356
  (79 shorter events, 31.0 us)
Async XLA Ops:
  7.2 3.1 copy-start
  7.2 115.2 %all-gather.17.cloned.1.call-start = ((), (), s32[]{:S(2)}) async-start(), calls=%async_computation.10 | async-start | bytes 5136384 | tf_op jit(solution)/shard_map/all_gather | solution.py:287
  20.4 141.7 %all-to-all-start = ((f32[8,4,192,128]{3,2,1,0:T(8,128)}), f32[8,4,192,128]{3,2,1,0:T(8,128)}, u32[]{:S(2)}, u32[]{:S(2)}) async-start(f32[8,4,192,128]{3,2,1,0:T(8,128)} %shard_map.77), calls=%async_computation | async-start | bytes 6291456 | tf_op jit(solution)/shard_map/all_to_all | solution.py:468
  27.7 301.7 %all-gather.11.cloned.1.call-start = ((), (), s32[]{:S(2)}) async-start(), calls=%async_computation.7 | async-start | bytes 3932160 | tf_op jit(solution)/shard_map/all_gather | solution.py:475
  133.4 1.9 copy-start.2
  155.4 1.4 slice-start
  244.1 3.8 copy-start.9
  247.8 86.6 %all-gather.9.cloned.1.call-start = ((), (), s32[]{:S(2)}) async-start(), calls=%async_computation.6 | async-start | bytes 3932160 | tf_op jit(solution)/shard_map/all_gather | solution.py:475
  271.7 3.8 copy-start.8
  275.4 63.7 %all-gather.13.cloned.1.call-start = ((), (), s32[]{:S(2)}) async-start(), calls=%async_computation.8 | async-start | bytes 3932160 | tf_op jit(solution)/shard_map/all_gather | solution.py:475
  298.8 3.7 copy-start.7
  302.5 64.3 %all-gather.15.cloned.1.call-start = ((), (), s32[]{:S(2)}) async-start(), calls=%async_computation.9 | async-start | bytes 3932160 | tf_op jit(solution)/shard_map/all_gather | solution.py:475
  329.3 110.7 %all-gather.19.cloned.1.call-start = ((), (), s32[]{:S(2)}) async-start(), calls=%async_computation.11 | async-start | bytes 1081344 | tf_op jit(solution)/shard_map/all_gather | solution.py:480
  366.9 4.8 copy-start.4
  366.9 4.8 copy-start.5
  366.9 4.8 copy-start.6
  471.9 8.6 %copy-start.3 = (f32[512,512]{1,0:T(8,128)S(1)}, f32[512,512]{1,0:T(8,128)}, u32[]{:S(2)}) copy-start(f32[512,512]{1,0:T(8,128)} %all-gather.19.cloned.1.call-done.gram_ref) | copy-start | bytes 3145732
  471.9 9.6 %copy-start.1 = (f32[8,4,4608]{2,1,0:T(4,128)S(1)}, f32[8,4,4608]{2,1,0:T(4,128)}, u32[]{:S(2)}) copy-start(f32[8,4,4608]{2,1,0:T(4,128)} %param.8) | copy-start | bytes 1769476
Sparse Core Ops, SparseCore 0:
  12.1 110.1 all-gather.16
  247.9 27.6 all-gather.10
  277.2 28.4 all-gather.8
  307.7 28.5 all-gather.12
  338.2 28.5 all-gather.14
  388.1 51.8 all-gather.18

commit v3 on v2

v3 whole, which is shorter than its diff:
```python
import functools

import jax
import jax.numpy as jnp
from jax import lax
from jax.experimental import pallas as pl
from jax.experimental.pallas import tpu as pltpu
from jax.sharding import PartitionSpec as P

SPAN = 3
MAXPROJ = 4
HALO = 4
PAD = 8
LANES = 128
GROUP = 8
BEFORE, AFTER = 2, 1
NEAR = BEFORE + 1 + AFTER

center_weight = -205.0 / 72.0
side_weights = (8.0 / 5.0, -1.0 / 5.0, 8.0 / 315.0, -1.0 / 560.0)
HIGHEST = lax.Precision.HIGHEST
WHOLE = pl.BlockSpec(memory_space=pltpu.VMEM)
PARAMS = pltpu.CompilerParams(vmem_limit_bytes=60 * 1024 * 1024)


def cost(flops, bytes_accessed):
    return pl.CostEstimate(flops=int(flops), bytes_accessed=int(bytes_accessed), transcendentals=0)


def halves(value):
    high = value.astype(jnp.bfloat16)
    return high, (value - high.astype(jnp.float32)).astype(jnp.bfloat16)


def side_by_side(value):
    return jnp.concatenate(halves(value), axis=1)


def dot_halves(left, right):
    dot = functools.partial(jnp.dot, preferred_element_type=jnp.float32)
    return dot(left[0], right) + dot(left[1], right)


def folded(value):
    return value[:, :LANES] + value[:, LANES:]


def swapped(blocks, lane):
    count = len(blocks)
    width = LANES // count
    blocks = [pltpu.roll(value, at * width, 1) if at else value for at, value in enumerate(blocks)]
    bit = 1
    while bit < count:
        chosen = (lane // (bit * width)) % 2 == 1
        blocks = [jnp.where(chosen, blocks[(at + bit) % count], blocks[at]) for at in range(count)]
        bit *= 2
    blocks = [blocks[-at % count] for at in range(count)]
    return [pltpu.roll(value, LANES - at * width, 1) if at else value for at, value in enumerate(blocks)]


def swap_into(read, write, count, rows):
    tile = 8 * max(1, 32 // count)
    lane = lax.broadcasted_iota(jnp.int32, (tile, LANES), 1)

    def step(index, carry):
        start = pl.multiple_of(index * tile, 8)
        for block, value in enumerate(swapped([read(block, start, tile) for block in range(count)], lane)):
            write(block, start, tile, value)
        return carry

    lax.fori_loop(0, rows // tile, step, 0)


def swap_in_kernel(count, rows, in_ref, out_ref):
    def read(block, start, size):
        return in_ref[block, pl.ds(start, size), :]

    def write(block, start, size, value):
        out_ref[block, pl.ds(start, size), :] = value

    swap_into(read, write, count, rows)


def swap_in(value):
    planes, count, rows, _ = value.shape
    return pl.pallas_call(
        functools.partial(swap_in_kernel, count, rows),
        grid=(planes,),
        in_specs=[pl.BlockSpec((None, count, rows, LANES), lambda p: (p, 0, 0, 0))],
        out_specs=pl.BlockSpec((count, None, rows, LANES), lambda p: (0, p, 0, 0)),
        out_shape=jax.ShapeDtypeStruct((count, planes, rows, LANES), jnp.float32),
        compiler_params=PARAMS,
        cost_estimate=cost(0, 8 * value.size),
    )(value)


def swap_out_kernel(count, rows, arrived_ref, high_ref, low_ref, weights_ref, out_ref):
    planes = out_ref.shape[0]
    weights = side_by_side(weights_ref[...] * (1.0 / 18.0))
    for plane in range(planes):

        def read(block, start, size):
            return arrived_ref[block, plane, pl.ds(start, size), :]

        def write(block, start, size, value):
            at = pl.ds(pl.multiple_of(block * rows + start, 8), size)
            out_ref[plane, at, :] = value

        swap_into(read, write, count, rows)
        tile = rows * count // 6

        def add(index, carry):
            at = pl.ds(pl.multiple_of(index * tile, 8), tile)
            term = folded(dot_halves((high_ref[plane, at, :], low_ref[plane, at, :]), weights))
            out_ref[plane, at, :] = out_ref[plane, at, :] + term
            return carry

        lax.fori_loop(0, 6, add, 0)


def swap_out(arrived, high, low, weights, first_plane):
    count, planes, rows, _ = arrived.shape
    cells = count * rows
    basis = pl.BlockSpec((planes, cells, 2 * LANES), lambda i: (first_plane // planes, 0, 0))
    return pl.pallas_call(
        functools.partial(swap_out_kernel, count, rows),
        grid=(1,),
        in_specs=[
            pl.BlockSpec(arrived.shape, lambda i: (0, 0, 0, 0)),
            basis,
            basis,
            pl.BlockSpec(weights.shape, lambda i: (0, 0)),
        ],
        out_specs=pl.BlockSpec((planes, cells, LANES), lambda i: (0, 0, 0)),
        out_shape=jax.ShapeDtypeStruct((planes, cells, LANES), jnp.float32),
        compiler_params=PARAMS,
        cost_estimate=cost(0, 24 * arrived.size),
    )(arrived, high, low, weights)


def fill_row(target, plane, y, row, side_z):
    target[plane, y, pl.ds(PAD, side_z), :] = row
    target[plane, y, pl.ds(PAD - HALO, HALO), :] = row[side_z - HALO :]
    target[plane, y, pl.ds(PAD + side_z, HALO), :] = row[:HALO]


def local_part(source, potential_ref, planes, first, side_y, side_z, line_of, finish):
    tile = 16

    def row(y, carry):
        for start in range(0, side_z, tile):

            def load(plane, y_at, shift):
                return source[plane, y_at, pl.ds(PAD + start + shift, tile), :]

            line = line_of(lambda plane: load(plane, y, 0))
            at = pl.ds(pl.multiple_of(y * side_z + start, 8), tile)
            for plane in range(planes):
                here = first + plane
                total = (potential_ref[plane, at, :] - 1.5 * center_weight - 7.0) * line[HALO + plane]
                for offset in range(1, HALO + 1):
                    around = line[HALO + plane + offset] + line[HALO + plane - offset]
                    around = around + (load(here, y, offset) + load(here, y, -offset))
                    up = lax.rem(y + offset, side_y)
                    down = lax.rem(y + side_y - offset, side_y)
                    around = around + (load(here, up, 0) + load(here, down, 0))
                    total = total - (0.5 * side_weights[offset - 1]) * around
                finish(plane, y, start, at, total)
        return carry

    lax.fori_loop(0, side_y, row, 0)


def filter_kernel(planes, side_y, side_z, width, chunks, arrived_ref, potential_ref, *rest):
    outs, (field, padded, first, flat) = rest[: len(chunks)], rest[len(chunks) :]
    count, _, rows, _ = arrived_ref.shape
    tile = 16

    for plane in range(planes):

        def read_in(block, start, size):
            return arrived_ref[block, plane, pl.ds(start, size), :]

        def write_in(block, start, size, value):
            field[plane, pl.ds(pl.multiple_of(block * rows + start, 8), size), :] = value

        swap_into(read_in, write_in, count, rows)

    def fill(y, carry):
        for plane in range(planes):
            fill_row(padded, plane, y, field[plane, pl.ds(pl.multiple_of(y * side_z, 8), side_z), :], side_z)
        return carry

    lax.fori_loop(0, side_y, fill, 0)

    def line_of(load):
        inside = [load(plane) for plane in range(planes)]
        before = [pltpu.roll(value, width, 1) for value in inside]
        after = [pltpu.roll(value, LANES - width, 1) for value in inside]
        return before[planes - HALO :] + inside + after[:HALO]

    def finish_first(plane, y, start, at, total):
        first[plane, y, pl.ds(PAD + start, tile), :] = total
        if start == 0:
            first[plane, y, pl.ds(PAD + side_z, HALO), :] = total[:HALO]
        if start == side_z - tile:
            first[plane, y, pl.ds(PAD - HALO, HALO), :] = total[tile - HALO :]

    def finish_second(plane, y, start, at, total):
        flat[plane, at, :] = total * (1.0 / 18.0) - field[plane, at, :]

    local_part(padded, potential_ref, planes, 0, side_y, side_z, line_of, finish_first)
    local_part(first, potential_ref, planes, 0, side_y, side_z, line_of, finish_second)

    for (begin, size_of), out_ref in zip(chunks, outs):
        for plane in range(size_of):

            def read_out(block, start, size):
                return flat[begin + plane, pl.ds(pl.multiple_of(block * rows + start, 8), size), :]

            def write_out(block, start, size, value):
                out_ref[block, plane, pl.ds(start, size), :] = value

            swap_into(read_out, write_out, count, rows)


def filter_orbitals(arrived, potential, side_y, side_z, width, chunks):
    count, planes, rows, _ = arrived.shape
    flat = pltpu.VMEM((planes, side_y * side_z, LANES), jnp.float32)
    padded = pltpu.VMEM((planes, side_y, side_z + 2 * PAD, LANES), jnp.float32)
    return pl.pallas_call(
        functools.partial(filter_kernel, planes, side_y, side_z, width, chunks),
        in_specs=[WHOLE, WHOLE],
        out_specs=[WHOLE] * len(chunks),
        out_shape=[jax.ShapeDtypeStruct((count, size, rows, LANES), jnp.float32) for _, size in chunks],
        scratch_shapes=[flat, padded, padded, flat],
        compiler_params=PARAMS,
        cost_estimate=cost(100 * arrived.size, 12 * arrived.size),
    )(arrived, potential)


def basis_kernel(planes, side_y, side_z, raw_ref, offset_ref, potential_ref, orbitals_ref, high_ref, low_ref, parts_ref, turned, placed):
    cells = side_y * side_z
    bands = raw_ref.shape[0]
    for part in range(SPAN):
        at = pl.ds(part * cells, cells)
        stack = [raw_ref[band, block, :, at] for block in range(NEAR) for band in range(bands)]
        turned[part] = jnp.concatenate(stack, axis=0).T
    offset = offset_ref[0:1, :]

    def place(y, carry):
        at = pl.ds(pl.multiple_of(y * side_z, 8), side_z)
        values = [turned[part, at, :] for part in range(SPAN)]
        for plane in range(planes + 2 * HALO):
            row = jnp.zeros((side_z, LANES), jnp.float32)
            for part in range(SPAN):
                row = jnp.where(offset == float(plane - HALO - part), values[part], row)
            fill_row(placed, plane, y, row, side_z)
        return carry

    lax.fori_loop(0, side_y, place, 0)

    def line_of(load):
        return [load(plane) for plane in range(planes + 2 * HALO)]

    def finish(plane, y, start, at, total):
        own = placed[HALO + plane, y, pl.ds(PAD + start, 16), :]
        high, low = halves(jnp.concatenate([total, own], axis=1))
        high_ref[plane, at, :] = high
        low_ref[plane, at, :] = low

    local_part(placed, potential_ref, planes, HALO, side_y, side_z, line_of, finish)

    dot = functools.partial(jnp.dot, preferred_element_type=jnp.float32)
    with_orbitals = with_basis = 0.0
    for plane in range(planes):
        high, low = high_ref[plane], low_ref[plane]
        left = halves(orbitals_ref[plane].T)
        with_orbitals = with_orbitals + (dot(left[0], high) + (dot(left[0], low) + dot(left[1], high)))
        own_high, own_low = high[:, LANES:], low[:, LANES:]
        turned_high = own_high.astype(jnp.float32).T.astype(jnp.bfloat16)
        turned_low = own_low.astype(jnp.float32).T.astype(jnp.bfloat16)
        both = jnp.concatenate([own_high, own_low], axis=1)
        with_basis = with_basis + (dot(turned_high, both) + dot(turned_low, both))
    parts_ref[0] = with_orbitals[:, LANES:].T
    parts_ref[1] = with_orbitals[:, :LANES].T
    parts_ref[2] = folded(with_basis)


def build_basis(raw, offset, potential, orbitals, side_y, side_z):
    planes, cells, _ = orbitals.shape
    pair = jax.ShapeDtypeStruct((planes, cells, 2 * LANES), jnp.bfloat16)
    return pl.pallas_call(
        functools.partial(basis_kernel, planes, side_y, side_z),
        in_specs=[WHOLE] * 4,
        out_specs=[WHOLE] * 3,
        out_shape=[pair, pair, jax.ShapeDtypeStruct((3, LANES, LANES), jnp.float32)],
        scratch_shapes=[
            pltpu.VMEM((SPAN, cells, LANES), jnp.float32),
            pltpu.VMEM((planes + 2 * HALO, side_y, side_z + 2 * PAD, LANES), jnp.float32),
        ],
        compiler_params=PARAMS,
        cost_estimate=cost(200 * orbitals.size, 24 * orbitals.size),
    )(raw, offset, potential, orbitals)


def weights_kernel(me_ref, parts_ref, coupling_ref, out_ref):
    count = parts_ref.shape[0]
    size = LANES // NEAR
    me = me_ref[0]
    dot = functools.partial(jnp.dot, precision=HIGHEST, preferred_element_type=jnp.float32)

    def device(step):
        return lax.rem(me + step % count, count)

    def total(pick, block):
        shares = [pick(block - (near - BEFORE), pl.ds(near * size, size)) for near in range(NEAR)]
        return (shares[0] + shares[1]) + (shares[2] + shares[3])

    def couple(block, value):
        return dot(coupling_ref[device(block)], value)

    def kept(function):
        known = {}

        def look(step):
            if step % count not in known:
                known[step % count] = function(step)
            return known[step % count]

        return look

    weight = kept(lambda block: couple(block, total(lambda step, at: parts_ref[device(step), 0, at, :], block)))
    near_weights = kept(lambda step: jnp.concatenate([weight(step + near - BEFORE) for near in range(NEAR)], axis=0))
    overlap = kept(lambda step: dot(parts_ref[device(step), 2], near_weights(step)))
    out_ref[pl.ds(0, LANES), :] = near_weights(0)
    for near in range(NEAR):
        block = near - BEFORE

        def share(step, at):
            return parts_ref[device(step), 1, at, :] + overlap(step)[at.start : at.start + size]

        out_ref[pl.ds(LANES + near * size, size), :] = couple(block, total(share, block))


def near_weights(parts, coupling):
    return pl.pallas_call(
        weights_kernel,
        in_specs=[pl.BlockSpec(memory_space=pltpu.SMEM), WHOLE, WHOLE],
        out_specs=WHOLE,
        out_shape=jax.ShapeDtypeStruct((2 * LANES, LANES), jnp.float32),
        compiler_params=PARAMS,
        cost_estimate=cost(0, 8 * parts.size),
    )(lax.axis_index("dom").astype(jnp.int32).reshape(1), parts, coupling)


def shifted(value, axis, step):
    count = lax.axis_size(axis)
    return lax.ppermute(value, axis, [(source, (source + step) % count) for source in range(count)])


def crossed(value, bit):
    return lax.ppermute(value, "band", [(source, source ^ bit) for source in range(lax.axis_size("band"))])


def gram_kernel(own_ref, *rest):
    panels, out_ref = (own_ref, *rest[:-1]), rest[-1]

    @pl.when(pl.program_id(0) == 0)
    def _():
        out_ref[...] = jnp.zeros_like(out_ref)

    for plane in range(own_ref.shape[0]):
        left = halves(own_ref[plane].T)
        for index, panel in enumerate(panels):
            at = pl.ds(index * LANES, LANES)
            out_ref[:, at] = out_ref[:, at] + folded(dot_halves(left, side_by_side(panel[plane])))


def gram_rows(panels):
    planes, cells, _ = panels[0].shape
    tile = cells // 4
    return pl.pallas_call(
        gram_kernel,
        grid=(cells // tile,),
        in_specs=[pl.BlockSpec((planes, tile, LANES), lambda i: (0, i, 0))] * len(panels),
        out_specs=pl.BlockSpec((LANES, len(panels) * LANES), lambda i: (0, 0)),
        out_shape=jax.ShapeDtypeStruct((LANES, len(panels) * LANES), jnp.float32),
        compiler_params=PARAMS,
        cost_estimate=cost(8 * panels[0].size * LANES * len(panels), 4 * panels[0].size * len(panels)),
    )(*panels)


def rotate_kernel(chunks, bands, inverse_ref, *rest):
    panels, out_ref = rest[:-1], rest[-1]
    right = side_by_side(inverse_ref[...].T)
    for index, (begin, size) in enumerate(chunks):
        group = panels[index * bands : (index + 1) * bands]
        for plane in range(size):
            left = halves(jnp.concatenate([panel[plane] for panel in group], axis=1))
            out_ref[begin + plane] = folded(dot_halves(left, right))


def rotated(inverse_rows, panels, chunks):
    bands = len(panels[0])
    planes = sum(size for _, size in chunks)
    cells = panels[0][0].shape[1]
    tile = cells // 4
    specs = [pl.BlockSpec((size, tile, LANES), lambda i: (0, i, 0)) for _, size in chunks for _ in range(bands)]
    return pl.pallas_call(
        functools.partial(rotate_kernel, chunks, bands),
        grid=(cells // tile,),
        in_specs=[pl.BlockSpec(inverse_rows.shape, lambda i: (0, 0)), *specs],
        out_specs=pl.BlockSpec((planes, tile, LANES), lambda i: (0, i, 0)),
        out_shape=jax.ShapeDtypeStruct((planes, cells, LANES), jnp.float32),
        compiler_params=PARAMS,
    )(inverse_rows, *[panel for group in panels for panel in group])


def thirds(value):
    first = value.astype(jnp.bfloat16).astype(jnp.float32)
    rest = value - first
    second = rest.astype(jnp.bfloat16).astype(jnp.float32)
    return first, second, rest - second


def eliminate(work, result):
    sublane = lax.broadcasted_iota(jnp.int32, (GROUP, LANES), 0)
    for top in range(0, LANES, GROUP):
        left = [jnp.broadcast_to(work[pl.ds(top + i, 1), :LANES], (GROUP, LANES)) for i in range(GROUP)]
        right = [jnp.broadcast_to(work[pl.ds(top + i, 1), LANES:], (GROUP, LANES)) for i in range(GROUP)]
        entry = {
            (i, j): jnp.broadcast_to(left[i][:, top + j : top + j + 1], (GROUP, LANES))
            for i in range(GROUP)
            for j in range(i, GROUP)
        }
        for i in range(GROUP):
            scale = lax.rsqrt(entry[i, i])
            left[i] = left[i] * scale
            right[i] = right[i] * scale
            factor = {j: entry[i, j] * scale for j in range(i + 1, GROUP)}
            for m in range(i + 1, GROUP):
                for j in range(m, GROUP):
                    entry[m, j] = entry[m, j] - factor[m] * factor[j]
                left[m] = left[m] - factor[m] * left[i]
                right[m] = right[m] - factor[m] * right[i]
        upper, lower = left[0], right[0]
        for i in range(1, GROUP):
            upper = jnp.where(sublane == i, left[i], upper)
            lower = jnp.where(sublane == i, right[i], lower)
        result[pl.ds(top, GROUP), :] = lower
        below = top + GROUP
        if below < LANES:
            a, b, c = thirds(upper)
            x, y, z = thirds(lower)
            columns = jnp.concatenate([a, a, b, b, a, c], axis=0).T[below:].astype(jnp.bfloat16)
            rows = jnp.concatenate(
                [jnp.concatenate([a, b, a, b, c, a], axis=0), jnp.concatenate([x, y, x, y, z, x], axis=0)], axis=1
            ).astype(jnp.bfloat16)
            rest = pl.ds(below, LANES - below)
            work[rest, :] = work[rest, :] - jnp.dot(columns, rows, preferred_element_type=jnp.float32)


def cholesky_kernel(gram_ref, out_ref, matrix, work, corner, scaled):
    size = gram_ref.shape[0]
    dot = functools.partial(jnp.dot, precision=HIGHEST, preferred_element_type=jnp.float32)
    diagonal = lax.broadcasted_iota(jnp.int32, (LANES, LANES), 0) == lax.broadcasted_iota(jnp.int32, (LANES, LANES), 1)
    identity = diagonal.astype(jnp.float32)
    matrix[:, :size] = gram_ref[...]
    matrix[:, size:] = jnp.zeros((size, size), jnp.float32)
    for at in range(0, size, LANES):
        matrix[pl.ds(at, LANES), size + at : size + at + LANES] = identity

    def block(index, carry):
        start = pl.multiple_of(index * LANES, LANES)
        at = pl.ds(start, LANES)
        work[:, :LANES] = matrix[at, at]
        work[:, LANES:] = identity
        eliminate(work, corner)
        scaled[...] = dot(corner[...], matrix[at, :])
        out_ref[at, :] = scaled[:, size:]

        def below(other, carry):
            rows = pl.ds(pl.multiple_of(other * LANES, LANES), LANES)
            matrix[rows, :] = matrix[rows, :] - dot(scaled[:, rows].T, scaled[...])
            return carry

        lax.fori_loop(index + 1, size // LANES, below, 0)
        return carry

    lax.fori_loop(0, size // LANES, block, 0)


def cholesky_inverse(gram):
    size = gram.shape[0]
    whole = pl.BlockSpec(memory_space=pltpu.VMEM)
    return pl.pallas_call(
        cholesky_kernel,
        in_specs=[whole],
        out_specs=whole,
        out_shape=jax.ShapeDtypeStruct((size, size), jnp.float32),
        scratch_shapes=[
            pltpu.VMEM((size, 2 * size), jnp.float32),
            pltpu.VMEM((LANES, 2 * LANES), jnp.float32),
            pltpu.VMEM((LANES, LANES), jnp.float32),
            pltpu.VMEM((LANES, 2 * size), jnp.float32),
        ],
        compiler_params=PARAMS,
    )(gram)


def near_projectors(projectors, atom_plane, planes):
    bands, band, block = lax.axis_size("band"), lax.axis_index("band"), lax.axis_index("dom")
    share = projectors.shape[0] // bands
    lines = share * MAXPROJ
    first = (atom_plane - block * planes).astype(jnp.float32)
    first = jnp.broadcast_to(first[:, None, None], (projectors.shape[0], MAXPROJ, LANES))
    packed = jnp.concatenate([projectors, first], axis=2)
    mine = lax.dynamic_slice_in_dim(packed, band * share, share, 0).reshape(lines, -1)
    near = [mine if step == BEFORE else shifted(mine, "dom", BEFORE - step) for step in range(NEAR)]
    raw = lax.all_gather(jnp.stack(near), "band")
    first = raw[:, :, :, -1] + (planes * (jnp.arange(NEAR, dtype=jnp.float32) - BEFORE))[None, :, None]
    first = jnp.transpose(first, (1, 0, 2)).reshape(1, LANES)
    return raw, jnp.broadcast_to(first, (GROUP, LANES))


def shards(orbitals, potential, projectors, coupling, atom_plane, projector_count):
    planes, side_y, side_z, local_orbs = orbitals.shape
    blocks, bands = lax.axis_size("dom"), lax.axis_size("band")
    band = lax.axis_index("band")
    cells = side_y * side_z
    rows = cells // blocks
    width = local_orbs // blocks
    norb = local_orbs * bands
    chunks = ((0, 2), (2, 1), (3, 1))

    raw, first = near_projectors(projectors, atom_plane, planes)
    levels = lax.all_gather(potential.reshape(planes, cells), "dom")
    levels = jnp.transpose(levels, (1, 2, 0))
    levels = jnp.broadcast_to(levels[..., None], (planes, cells, blocks, width)).reshape(planes, cells, LANES)

    packed = swap_in(orbitals.reshape(planes, blocks, rows, local_orbs))
    arrived = lax.all_to_all(packed, "dom", 0, 0, tiled=True)

    own_levels = jnp.broadcast_to(potential.reshape(planes, cells, 1), (planes, cells, LANES))
    high, low, parts = build_basis(raw, first, own_levels, orbitals.reshape(planes, cells, LANES), side_y, side_z)
    atoms = projectors.shape[0]
    slots = jnp.arange(MAXPROJ, dtype=jnp.int32)
    live = (slots[None, :] < projector_count[:, None]).astype(jnp.float32)
    coupled = 0.5 * (coupling + jnp.transpose(coupling, (0, 2, 1))) * live[:, :, None] * live[:, None, :]
    vectors = atoms * MAXPROJ
    row = jnp.arange(vectors, dtype=jnp.int32) // MAXPROJ
    matrix = jnp.tile(coupled.reshape(vectors, MAXPROJ), (1, atoms))
    matrix = jnp.where(row[:, None] == row[None, :], matrix, 0.0)
    matrix = jnp.pad(matrix, ((0, 0), (0, LANES - vectors)))
    everyone = lax.all_gather(jnp.concatenate([parts.reshape(3 * LANES, LANES), matrix], axis=0), "dom")
    weights = near_weights(
        everyone[:, : 3 * LANES].reshape(blocks, 3, LANES, LANES), everyone[:, 3 * LANES :, :vectors]
    )

    seconds = filter_orbitals(arrived, levels, side_y, side_z, width, chunks)

    panels, part = [], 0.0
    for (begin, size), packed in zip(chunks, seconds):
        own = swap_out(lax.all_to_all(packed, "dom", 0, 0, tiled=True), high, low, weights, begin)
        across = crossed(own, 2)
        panels.append([own, crossed(own, 1), across, crossed(across, 1)])
        part = part + gram_rows(panels[-1])

    order = jnp.arange(bands, dtype=jnp.int32) ^ band
    part = jnp.take(part.reshape(local_orbs, bands, local_orbs), order, axis=1)
    pieces = lax.all_to_all(part.reshape(blocks, width, norb), "dom", 0, 0, tiled=True)
    piece = jnp.sum(pieces, axis=0) * (1.0 / (planes * cells * blocks))
    own_gram = lax.all_to_all(jnp.broadcast_to(piece, (blocks, width, norb)), "dom", 0, 0, tiled=True)
    gram = lax.all_gather(own_gram.reshape(local_orbs, norb), "band", axis=0, tiled=True)
    inverse = cholesky_inverse(gram)
    own_rows = lax.dynamic_slice_in_dim(inverse, band * local_orbs, local_orbs, 0)
    own_rows = jnp.take(own_rows.reshape(local_orbs, bands, local_orbs), order, axis=1).reshape(local_orbs, norb)
    result = rotated(own_rows, panels, chunks)
    return (result.reshape(planes, side_y, side_z, local_orbs), gram)


def solution(mesh):
    placed = (
        P("dom", None, None, "band"),
        P("dom", None, None),
        P("dom", None, None),
        P("dom", None, None),
        P("dom"),
        P("dom"),
    )
    return jax.shard_map(
        shards,
        mesh=mesh,
        in_specs=placed,
        out_specs=(P("dom", None, None, "band"), P()),
        check_vma=False,
    )
```

time: 490 us -> 433 us (0.88)
  blocking collectives: 110 us -> 68 us
  starting transfers between devices: 7.52 us -> 28.3 us
  Pallas kernels: 138 us -> 123 us
  local copies, waits for them, and re-layouts: 33.5 us -> 20.4 us
  other arithmetic: 16 us -> 6.63 us
    all_gather x6 -> x3, waiting for transfers between devices: 169 us -> 52.7 us  [the longest x1 36.8 us: shards(): lax.all_gather(jnp.concatenate([parts.reshape(3 * LANES, LANES), matrix],...]
    ppermute x0 -> x12, waiting for transfers between devices: none -> 93.1 us  [the longest x3 54.9 us: shifted(): lax.ppermute(value, axis, [(source, (source + step) % count) for source i...]
    all_to_all x4 -> x1, blocking collectives: 95.3 us -> 12.6 us  [shards(): lax.all_to_all(jnp.broadcast_to(piece, (blocks, width, norb)), 'dom', 0,...]
    all_gather x0 -> x1, blocking collectives: none -> 43.1 us  [shards(): levels = lax.all_gather(potential.reshape(planes, cells), 'dom')]
    pallas_call x1, Pallas kernels: 57 us -> 25.2 us  [filter_orbitals(): pl.pallas_call(functools.partial(filter_kernel, planes, side_y, side_z, w...]
    all_to_all x0 -> x3, waiting for transfers between devices: none -> 26.3 us  [shards(): lax.all_to_all(packed, 'dom', 0, 0, tiled=True)]
    pallas_call x6 -> x7, Pallas kernels: 31.7 us -> 51.9 us  [the longest x3 18.8 us: swap_out(): pl.pallas_call(functools.partial(swap_out_kernel, count, rows), grid=(1,)...]
    convert_element_type x2 -> x0, local copies, waits for them, and re-layouts: 13.4 us -> none  [the longest x1 6.7 us: gathered_parts(): low = (placed - high).astype(jnp.bfloat16)]
  transfers between devices with their start and end apart: 7 -> 19, of which waited for: 3 -> 10; matrix products, arithmetic and copies ran while one was open for 8% -> 5% of each run, Pallas kernels for 7% -> 16%
where the time goes in v3:
time: 433 us; the launch traced here: 432 us
  waiting for transfers between devices  172 us (40%)
  Pallas kernels  123 us (28%)
  blocking collectives  68 us (16%)
  starting transfers between devices  28.3 us (7%)
  local copies, waits for them, and re-layouts  20.4 us (5%)
  between operations  14 us (3%)
  other arithmetic  6.63 us (2%)
    ppermute x3, waiting for transfers between devices, shifted(): lax.ppermute(value, axis, [(source, (source + step) % count) for source i...  54.9 us
    all_gather x1, blocking collectives, shards(): levels = lax.all_gather(potential.reshape(planes, cells), 'dom')  43.1 us
    ppermute x9, waiting for transfers between devices, crossed(): lax.ppermute(value, 'band', [(source, source ^ bit) for source in range(l...  38.1 us
    all_gather x1, waiting for transfers between devices, shards(): lax.all_gather(jnp.concatenate([parts.reshape(3 * LANES, LANES), matrix],...  36.8 us
    pallas_call x1, Pallas kernels, cholesky_inverse(): pl.pallas_call(cholesky_kernel, in_specs=[whole], out_specs=whole, out_sh...  30.2 us
    all_to_all x3, waiting for transfers between devices, shards(): lax.all_to_all(packed, 'dom', 0, 0, tiled=True)  26.3 us
    pallas_call x1, Pallas kernels, filter_orbitals(): pl.pallas_call(functools.partial(filter_kernel, planes, side_y, side_z, w...  25.2 us
    pallas_call x3, Pallas kernels, swap_out(): pl.pallas_call(functools.partial(swap_out_kernel, count, rows), grid=(1,)...  18.8 us
  transfers between devices with their start and end apart: 19, of which 10 were waited for; matrix products, arithmetic and copies ran while one was open for 5% of the time, Pallas kernels for 16%

profile of v3, /device:TPU:0, one launch (start us, length us, event | category | flops | bytes accessed | tf_op | source)
XLA Modules:
  0.0 432.0 jit_solution(9676678026224652561)
XLA Ops:
  7.2 7.0 %shard_map.77 = f32[8,4,192,128]{3,2,1,0:T(8,128)} custom-call(f32[4,8,192,128]{3,2,1,0:T(8,128)} %bitcast.40), custom_call_target="tpu_custom_call" | custom-call | bytes 6291456 | tf_op jit(solution)/shard_map/pallas_call | solution.py:86
  14.1 7.4 %all-to-all-start = ((f32[8,4,192,128]{3,2,1,0:T(8,128)}), f32[8,4,192,128]{3,2,1,0:T(8,128)S(1)}, u32[]{:S(2)}, u32[]{:S(2)}) async-start(f32[8,4,192,128]{3,2,1,0:T(8,128)} %shard_map.77), calls=%async_computation | async-start | bytes 6291456 | tf_op jit(solution)/shard_map/all_to_all | solution.py:543
  23.4 4.7 %collective-permute-start.2 = (f32[8,4736]{1,0:T(8,128)}, f32[8,4736]{1,0:T(8,128)}, u32[]{:S(2)}, u32[]{:S(2)}) collective-permute-start(f32[8,4736]{1,0:T(8,128)} %reshape.129), channel_id=1, source_target_pairs={{0,7},{1,0},{2,1},{3,2},{4,3},{5,4},{6,5},{7,6},{8,15},{9,8},{10,9... | collective-permute-start | bytes 454664 | tf_op jit(solution)/shard_map/ppermute | solution.py:359
  28.1 49.8 %collective-permute-done.2 = f32[8,4736]{1,0:T(8,128)} collective-permute-done((f32[8,4736]{1,0:T(8,128)}, f32[8,4736]{1,0:T(8,128)}, u32[]{:S(2)}, u32[]{:S(2)}) %collective-permute-start.2) | collective-permute-done | bytes 151584 | tf_op jit(solution)/shard_map/ppermute | solution.py:359
  85.1 43.1 %all_gather.18 = f32[8,4,1536]{2,1,0:T(4,128)S(1)} all-gather(f32[1,4,1536]{2,1,0:T(4,128)S(1)} %all_gather_reshape.3), channel_id=1, replica_groups=mesh['band'=4,'dom'=8] {'dom'}, dimensions={0}, use_global_device_ids=true | all-gather | bytes 221184 | tf_op jit(solution)/shard_map/all_gather | solution.py:538
  135.5 25.2 %shard_map.78 = (f32[8,2,192,128]{3,2,1,0:T(8,128)}, f32[8,1,192,128]{3,2,1,0:T(8,128)}, f32[8,1,192,128]{3,2,1,0:T(8,128)}) custom-call(f32[8,4,192,128]{3,2,1,0:T(8,128)} %copy-done.1, f32[4,1536,128]{2,1,0:T(8,128)} %copy.33.potential_ref), custom_call_target="tpu_custom_call" | custom-call | flops 78643200 | bytes 9437184 | tf_op jit(solution)/shard_map/pallas_call | solution.py:231
  169.8 13.5 %shard_map.79 = (bf16[4,1536,256]{2,1,0:T(8,128)(2,1)}, bf16[4,1536,256]{2,1,0:T(8,128)(2,1)}, f32[3,128,128]{2,1,0:T(8,128)}) custom-call(f32[4,4,8,4736]{3,2,1,0:T(8,128)} %bitcast.45, f32[8,128]{1,0:T(8,128)} %broadcast_in_dim.52.offset_ref, f32[4,1536,128]{2,1,0:T(8,128)} %broadcast_in_dim.54.potential_ref, f32[4,1536,128]{2,1,0:T(8,128)} %bitcast.41), custom_call_target="tpu_custom_call" | custom-call | flops 157286400 | bytes 18874368 | tf_op jit(solution)/shard_map/pallas_call | solution.py:293
  184.9 11.6 %all-to-all-done.1.arrived_ref = f32[8,2,192,128]{3,2,1,0:T(8,128)S(1)} async-done(((f32[8,2,192,128]{3,2,1,0:T(8,128)}), f32[8,2,192,128]{3,2,1,0:T(8,128)S(1)}, u32[]{:S(2)}, u32[]{:S(2)}) %all-to-all-start.1) | async-done | bytes 1572896 | tf_op jit(solution)/shard_map/all_to_all | solution.py:565
  200.8 36.8 %all-gather.10.cloned.1.call-done = f32[3328,128]{1,0:T(8,128)} async-done(((f32[416,128]{1,0:T(8,128)}), f32[3328,128]{1,0:T(8,128)}) %all-gather.10.cloned.1.call-update) | async-done | bytes 1703952 | tf_op jit(solution)/shard_map/all_gather | solution.py:556
  245.8 8.6 %shard_map.81.own_ref.rest_0_ = f32[2,1536,128]{2,1,0:T(8,128)} custom-call(f32[8,2,192,128]{3,2,1,0:T(8,128)} %copy-done.2, bf16[4,1536,256]{2,1,0:T(8,128)(2,1)} %get-tuple-element.10.high_ref, bf16[4,1536,256]{2,1,0:T(8,128)(2,1)} %get-tuple-element.11.low_ref, f32[256,128]{1,0:T(8,128)} %shard_map.80.weights_ref), custom_call_target="tpu_custom_call" | custom-call | bytes 9437184 | tf_op jit(solution)/shard_map/pallas_call | solution.py:125
  260.2 5.1 %shard_map.85.own_ref.rest_8_ = f32[1,1536,128]{2,1,0:T(8,128)} custom-call(f32[8,1,192,128]{3,2,1,0:T(8,128)} %all-to-all-done.3.arrived_ref, bf16[4,1536,256]{2,1,0:T(8,128)(2,1)} %get-tuple-element.10.high_ref, bf16[4,1536,256]{2,1,0:T(8,128)(2,1)} %get-tuple-element.11.low_ref, f32[256,128]{1,0:T(8,128)} %shard_map.80.weights_ref), custom_call_target="tpu_custom_call" | custom-call | bytes 4718592 | tf_op jit(solution)/shard_map/pallas_call | solution.py:125
  265.9 14.7 %all-to-all-done.2.arrived_ref = f32[8,1,192,128]{3,2,1,0:T(8,128)} async-done(((f32[8,1,192,128]{3,2,1,0:T(8,128)}), f32[8,1,192,128]{3,2,1,0:T(8,128)}, u32[]{:S(2)}, u32[]{:S(2)}) %all-to-all-start.2) | async-done | bytes 786464 | tf_op jit(solution)/shard_map/all_to_all | solution.py:565
  280.6 5.1 %shard_map.83.own_ref.rest_4_ = f32[1,1536,128]{2,1,0:T(8,128)} custom-call(f32[8,1,192,128]{3,2,1,0:T(8,128)} %all-to-all-done.2.arrived_ref, bf16[4,1536,256]{2,1,0:T(8,128)(2,1)} %get-tuple-element.10.high_ref, bf16[4,1536,256]{2,1,0:T(8,128)(2,1)} %get-tuple-element.11.low_ref, f32[256,128]{1,0:T(8,128)} %shard_map.80.weights_ref), custom_call_target="tpu_custom_call" | custom-call | bytes 4718592 | tf_op jit(solution)/shard_map/pallas_call | solution.py:125
  286.2 5.8 %collective-permute-done.4.rest_1_.rest_2_ = f32[2,1536,128]{2,1,0:T(8,128)S(1)} collective-permute-done((f32[2,1536,128]{2,1,0:T(8,128)}, f32[2,1536,128]{2,1,0:T(8,128)S(1)}, u32[]{:S(2)}, u32[]{:S(2)}) %collective-permute-start.4) | collective-permute-done | bytes 1572896 | tf_op jit(solution)/shard_map/ppermute | solution.py:363
  291.9 17.0 %collective-permute-done.10.rest_1_.rest_10_ = f32[1,1536,128]{2,1,0:T(8,128)} collective-permute-done((f32[1,1536,128]{2,1,0:T(8,128)}, f32[1,1536,128]{2,1,0:T(8,128)}, u32[]{:S(2)}, u32[]{:S(2)}) %collective-permute-start.10) | collective-permute-done | bytes 786464 | tf_op jit(solution)/shard_map/ppermute | solution.py:363
  309.4 15.4 %collective-permute-done.7.rest_1_.rest_6_ = f32[1,1536,128]{2,1,0:T(8,128)} collective-permute-done((f32[1,1536,128]{2,1,0:T(8,128)}, f32[1,1536,128]{2,1,0:T(8,128)}, u32[]{:S(2)}, u32[]{:S(2)}) %collective-permute-start.7) | collective-permute-done | bytes 786464 | tf_op jit(solution)/shard_map/ppermute | solution.py:363
  324.9 4.7 %shard_map.86 = f32[128,512]{1,0:T(8,128)} custom-call(f32[1,1536,128]{2,1,0:T(8,128)} %shard_map.85.own_ref.rest_8_, f32[1,1536,128]{2,1,0:T(8,128)} %collective-permute-done.9.rest_0_.rest_9_, f32[1,1536,128]{2,1,0:T(8,128)} %collective-permute-done.10.rest_1_.rest_10_, f32[1,1536,128]{2,1,0:T(8,128)} %collective-permute-done.11.rest_2_.rest_11_), custom_call_target="tpu_custom_call" | custom-call | flops 805306368 | bytes 3145728 | tf_op jit(solution)/shard_map/pallas_call | solution.py:383
  329.6 4.7 %shard_map.84 = f32[128,512]{1,0:T(8,128)} custom-call(f32[1,1536,128]{2,1,0:T(8,128)} %shard_map.83.own_ref.rest_4_, f32[1,1536,128]{2,1,0:T(8,128)} %collective-permute-done.6.rest_0_.rest_5_, f32[1,1536,128]{2,1,0:T(8,128)} %collective-permute-done.7.rest_1_.rest_6_, f32[1,1536,128]{2,1,0:T(8,128)} %collective-permute-done.8.rest_2_.rest_7_), custom_call_target="tpu_custom_call" | custom-call | flops 805306368 | bytes 3145728 | tf_op jit(solution)/shard_map/pallas_call | solution.py:383
  334.3 6.0 %shard_map.82 = f32[128,512]{1,0:T(8,128)} custom-call(f32[2,1536,128]{2,1,0:T(8,128)} %shard_map.81.own_ref.rest_0_, f32[2,1536,128]{2,1,0:T(8,128)} %collective-permute-done.3.rest_0_.rest_1_, f32[2,1536,128]{2,1,0:T(8,128)} %copy-done.3, f32[2,1536,128]{2,1,0:T(8,128)} %collective-permute-done.5.rest_2_.rest_3_), custom_call_target="tpu_custom_call" | custom-call | flops 1610612736 | bytes 6291456 | tf_op jit(solution)/shard_map/pallas_call | solution.py:383
  342.2 12.3 %all_to_all.30 = f32[8,16,512]{2,1,0:T(8,128)S(1)} all-to-all(f32[8,16,512]{2,1,0:T(8,128)S(1)} %reshape.135), channel_id=1, replica_groups=mesh['band'=4,'dom'=8] {'dom'}, dimensions={0} | all-to-all | bytes 524288 | tf_op jit(solution)/shard_map/all_to_all | solution.py:572
  354.6 12.6 %all_to_all.31 = f32[8,16,512]{2,1,0:T(8,128)} all-to-all(f32[8,16,512]{2,1,0:T(8,128)S(1)} %broadcast_in_dim.56), channel_id=1, replica_groups=mesh['band'=4,'dom'=8] {'dom'}, dimensions={0} | all-to-all | bytes 524288 | tf_op jit(solution)/shard_map/all_to_all | solution.py:574
  367.2 15.9 %all-gather.6.cloned.1.call-done.gram_ref = f32[512,512]{1,0:T(8,128)} async-done(((f32[128,512]{1,0:T(8,128)}), f32[512,512]{1,0:T(8,128)}) %all-gather.6.cloned.1.call-update) | async-done | bytes 1048592 | tf_op jit(solution)/shard_map/all_gather | solution.py:575
  383.1 30.2 %shard_map.87 = f32[512,512]{1,0:T(8,128)} custom-call(f32[512,512]{1,0:T(8,128)} %all-gather.6.cloned.1.call-done.gram_ref), custom_call_target="tpu_custom_call" | custom-call | tf_op jit(solution)/shard_map/pallas_call | solution.py:497
  415.9 8.6 %shard_map.88 = f32[4,1536,128]{2,1,0:T(8,128)} custom-call(f32[128,512]{1,0:T(8,128)} %copy_bitcast_fusion.inverse_ref, f32[2,1536,128]{2,1,0:T(8,128)} %shard_map.81.own_ref.rest_0_, f32[2,1536,128]{2,1,0:T(8,128)} %collective-permute-done.3.rest_0_.rest_1_, f32[2,1536,128]{2,1,0:T(8,128)} %copy-done.3, ...), custom_call_target="tpu_custom_call" | custom-call | tf_op jit(solution)/shard_map/pallas_call | solution.py:410
  (101 shorter events, 52.5 us)
Async XLA Ops:
  14.1 119.7 %all-to-all-start = ((f32[8,4,192,128]{3,2,1,0:T(8,128)}), f32[8,4,192,128]{3,2,1,0:T(8,128)S(1)}, u32[]{:S(2)}, u32[]{:S(2)}) async-start(f32[8,4,192,128]{3,2,1,0:T(8,128)} %shard_map.77), calls=%async_computation | async-start | bytes 6291456 | tf_op jit(solution)/shard_map/all_to_all | solution.py:543
  21.5 63.4 %copy-start.7 = (f32[4,32,48]{2,1,0:T(8,128)S(1)}, f32[4,32,48]{2,1,0:T(8,128)}, u32[]{:S(2)}) copy-start(f32[4,32,48]{2,1,0:T(8,128)} %param.9) | copy-start | bytes 73732
  21.5 144.3 %all-gather.8.cloned.1.call-start = ((), (), s32[]{:S(2)}) async-start(), calls=%async_computation.7 | async-start | bytes 3031040 | tf_op jit(solution)/shard_map/all_gather | solution.py:521
  23.4 54.5 %collective-permute-start.2 = (f32[8,4736]{1,0:T(8,128)}, f32[8,4736]{1,0:T(8,128)}, u32[]{:S(2)}, u32[]{:S(2)}) collective-permute-start(f32[8,4736]{1,0:T(8,128)} %reshape.129), channel_id=1, source_target_pairs={{0,7},{1,0},{2,1},{3,2},{4,3},{5,4},{6,5},{7,6},{8,15},{9,8},{10,9... | collective-permute-start | bytes 454664 | tf_op jit(solution)/shard_map/ppermute | solution.py:359
  28.0 54.1 %collective-permute-start.1 = (f32[8,4736]{1,0:T(8,128)}, f32[8,4736]{1,0:T(8,128)}, u32[]{:S(2)}, u32[]{:S(2)}) collective-permute-start(f32[8,4736]{1,0:T(8,128)} %reshape.129), channel_id=1, source_target_pairs={{0,1},{1,2},{2,3},{3,4},{4,5},{5,6},{6,7},{7,0},{8,9},{9,10},{10,1... | collective-permute-start | bytes 454664 | tf_op jit(solution)/shard_map/ppermute | solution.py:359
  28.0 55.0 %collective-permute-start = (f32[8,4736]{1,0:T(8,128)}, f32[8,4736]{1,0:T(8,128)}, u32[]{:S(2)}, u32[]{:S(2)}) collective-permute-start(f32[8,4736]{1,0:T(8,128)} %reshape.129), channel_id=1, source_target_pairs={{0,2},{1,3},{2,4},{3,5},{4,6},{5,7},{6,0},{7,1},{8,10},{9,11},{10,... | collective-permute-start | bytes 454664 | tf_op jit(solution)/shard_map/ppermute | solution.py:359
  160.8 35.8 %all-to-all-start.1 = ((f32[8,2,192,128]{3,2,1,0:T(8,128)}), f32[8,2,192,128]{3,2,1,0:T(8,128)S(1)}, u32[]{:S(2)}, u32[]{:S(2)}) async-start(f32[8,2,192,128]{3,2,1,0:T(8,128)} %get-tuple-element.9), calls=%async_computation.1 | async-start | bytes 3145728 | tf_op jit(solution)/shard_map/all_to_all | solution.py:565
  165.3 72.2 %all-gather.10.cloned.1.call-start = ((), (), s32[]{:S(2)}) async-start(), calls=%async_computation.8 | async-start | bytes 1916928 | tf_op jit(solution)/shard_map/all_gather | solution.py:556
  196.6 45.2 %copy-start.2 = (f32[8,2,192,128]{3,2,1,0:T(8,128)}, f32[8,2,192,128]{3,2,1,0:T(8,128)S(1)}, u32[]{:S(2)}) copy-start(f32[8,2,192,128]{3,2,1,0:T(8,128)S(1)} %all-to-all-done.1.arrived_ref) | copy-start | bytes 4718596
  196.6 59.4 %all-to-all-start.3 = ((f32[8,1,192,128]{3,2,1,0:T(8,128)}), f32[8,1,192,128]{3,2,1,0:T(8,128)}, u32[]{:S(2)}, u32[]{:S(2)}) async-start(f32[8,1,192,128]{3,2,1,0:T(8,128)} %get-tuple-element.14), calls=%async_computation.3 | async-start | bytes 1572864 | tf_op jit(solution)/shard_map/all_to_all | solution.py:565
  254.5 37.5 %collective-permute-start.4 = (f32[2,1536,128]{2,1,0:T(8,128)}, f32[2,1536,128]{2,1,0:T(8,128)S(1)}, u32[]{:S(2)}, u32[]{:S(2)}) collective-permute-start(f32[2,1536,128]{2,1,0:T(8,128)} %shard_map.81.own_ref.rest_0_), channel_id=1, source_target_pairs={{0,16},{8,24},{16,0},{24,8},{1,17},{9,25},{17,1},{25,9},{2,18},{10... | collective-permute-start | bytes 4718600 | tf_op jit(solution)/shard_map/ppermute | solution.py:363
  255.9 24.6 %all-to-all-start.2 = ((f32[8,1,192,128]{3,2,1,0:T(8,128)}), f32[8,1,192,128]{3,2,1,0:T(8,128)}, u32[]{:S(2)}, u32[]{:S(2)}) async-start(f32[8,1,192,128]{3,2,1,0:T(8,128)} %get-tuple-element.13), calls=%async_computation.2 | async-start | bytes 1572864 | tf_op jit(solution)/shard_map/all_to_all | solution.py:565
  260.2 122.9 %all-gather.6.cloned.1.call-start = ((), (), s32[]{:S(2)}) async-start(), calls=%async_computation.6 | async-start | bytes 1310720 | tf_op jit(solution)/shard_map/all_gather | solution.py:575
  265.4 20.8 %copy-start = (f32[2,1536,128]{2,1,0:T(8,128)S(1)}, f32[2,1536,128]{2,1,0:T(8,128)}, u32[]{:S(2)}) copy-start(f32[2,1536,128]{2,1,0:T(8,128)} %shard_map.81.own_ref.rest_0_) | copy-start | bytes 4718596
  265.4 43.5 %collective-permute-start.10 = (f32[1,1536,128]{2,1,0:T(8,128)}, f32[1,1536,128]{2,1,0:T(8,128)}, u32[]{:S(2)}, u32[]{:S(2)}) collective-permute-start(f32[1,1536,128]{2,1,0:T(8,128)} %shard_map.85.own_ref.rest_8_), channel_id=1, source_target_pairs={{0,16},{8,24},{16,0},{24,8},{1,17},{9,25},{17,1},{25,9},{2,18},{10... | collective-permute-start | bytes 2359304 | tf_op jit(solution)/shard_map/ppermute | solution.py:363
  265.9 43.0 %collective-permute-start.9 = (f32[1,1536,128]{2,1,0:T(8,128)}, f32[1,1536,128]{2,1,0:T(8,128)}, u32[]{:S(2)}, u32[]{:S(2)}) collective-permute-start(f32[1,1536,128]{2,1,0:T(8,128)} %shard_map.85.own_ref.rest_8_), channel_id=1, source_target_pairs={{0,8},{8,0},{16,24},{24,16},{1,9},{9,1},{17,25},{25,17},{2,10},{10... | collective-permute-start | bytes 2359304 | tf_op jit(solution)/shard_map/ppermute | solution.py:363
  285.6 39.2 %collective-permute-start.7 = (f32[1,1536,128]{2,1,0:T(8,128)}, f32[1,1536,128]{2,1,0:T(8,128)}, u32[]{:S(2)}, u32[]{:S(2)}) collective-permute-start(f32[1,1536,128]{2,1,0:T(8,128)} %shard_map.83.own_ref.rest_4_), channel_id=1, source_target_pairs={{0,16},{8,24},{16,0},{24,8},{1,17},{9,25},{17,1},{25,9},{2,18},{10... | collective-permute-start | bytes 2359304 | tf_op jit(solution)/shard_map/ppermute | solution.py:363
  286.2 48.1 %collective-permute-start.3 = (f32[2,1536,128]{2,1,0:T(8,128)S(1)}, f32[2,1536,128]{2,1,0:T(8,128)}, u32[]{:S(2)}, u32[]{:S(2)}) collective-permute-start(f32[2,1536,128]{2,1,0:T(8,128)S(1)} %copy-done), channel_id=1, source_target_pairs={{0,8},{8,0},{16,24},{24,16},{1,9},{9,1},{17,25},{25,17},{2,10},{10... | collective-permute-start | bytes 4718600 | tf_op jit(solution)/shard_map/ppermute | solution.py:363
  291.9 42.3 %copy-start.3 = (f32[2,1536,128]{2,1,0:T(8,128)}, f32[2,1536,128]{2,1,0:T(8,128)S(1)}, u32[]{:S(2)}) copy-start(f32[2,1536,128]{2,1,0:T(8,128)S(1)} %collective-permute-done.4.rest_1_.rest_2_) | copy-start | bytes 4718596
  291.9 42.3 %collective-permute-start.5 = (f32[2,1536,128]{2,1,0:T(8,128)S(1)}, f32[2,1536,128]{2,1,0:T(8,128)}, u32[]{:S(2)}, u32[]{:S(2)}) collective-permute-start(f32[2,1536,128]{2,1,0:T(8,128)S(1)} %collective-permute-done.4.rest_1_.rest_2_), channel_id=1, source_target_pairs={{0,8},{8,0},{16,24},{24,16},{1,9},{9,1},{17,25},{25,17},{2,10},{10... | collective-permute-start | bytes 4718600 | tf_op jit(solution)/shard_map/ppermute | solution.py:363
  308.9 16.0 %collective-permute-start.11 = (f32[1,1536,128]{2,1,0:T(8,128)}, f32[1,1536,128]{2,1,0:T(8,128)}, u32[]{:S(2)}, u32[]{:S(2)}) collective-permute-start(f32[1,1536,128]{2,1,0:T(8,128)} %collective-permute-done.10.rest_1_.rest_10_), channel_id=1, source_target_pairs={{0,8},{8,0},{16,24},{24,16},{1,9},{9,1},{17,25},{25,17},{2,10},{10... | collective-permute-start | bytes 2359304 | tf_op jit(solution)/shard_map/ppermute | solution.py:363
  308.9 20.7 %collective-permute-start.6 = (f32[1,1536,128]{2,1,0:T(8,128)}, f32[1,1536,128]{2,1,0:T(8,128)}, u32[]{:S(2)}, u32[]{:S(2)}) collective-permute-start(f32[1,1536,128]{2,1,0:T(8,128)} %shard_map.83.own_ref.rest_4_), channel_id=1, source_target_pairs={{0,8},{8,0},{16,24},{24,16},{1,9},{9,1},{17,25},{25,17},{2,10},{10... | collective-permute-start | bytes 2359304 | tf_op jit(solution)/shard_map/ppermute | solution.py:363
  324.8 4.7 %collective-permute-start.8 = (f32[1,1536,128]{2,1,0:T(8,128)}, f32[1,1536,128]{2,1,0:T(8,128)}, u32[]{:S(2)}, u32[]{:S(2)}) collective-permute-start(f32[1,1536,128]{2,1,0:T(8,128)} %collective-permute-done.7.rest_1_.rest_6_), channel_id=1, source_target_pairs={{0,8},{8,0},{16,24},{24,16},{1,9},{9,1},{17,25},{25,17},{2,10},{10... | collective-permute-start | bytes 2359304 | tf_op jit(solution)/shard_map/ppermute | solution.py:363
  415.9 8.6 %copy-start.4 = (f32[512,512]{1,0:T(8,128)S(1)}, f32[512,512]{1,0:T(8,128)}, u32[]{:S(2)}) copy-start(f32[512,512]{1,0:T(8,128)} %all-gather.6.cloned.1.call-done.gram_ref) | copy-start | bytes 3145732
  (6 other events, 29.4 us)
Sparse Core Ops, SparseCore 0:
  85.1 38.6 all-gather.7
  185.1 52.4 all-gather.9
  367.3 15.7 all-gather.5

commit v4 on v3

--- a/solution.py
+++ b/solution.py
@@ -68,10 +68,10 @@
             write(block, start, tile, value)
         return carry
 
-    lax.fori_loop(0, rows // tile, step, 0)
-
-
-def swap_in_kernel(count, rows, in_ref, out_ref):
+    lax.fori_loop(0, rows // tile, step, 0, unroll=True)
+
+
+def swap_in_kernel(count, rows, levels_ref, in_ref, out_ref):
     def read(block, start, size):
         return in_ref[block, pl.ds(start, size), :]
 
@@ -79,19 +79,25 @@
         out_ref[block, pl.ds(start, size), :] = value
 
     swap_into(read, write, count, rows)
-
-
-def swap_in(value):
+    for block in range(count):
+        out_ref[block, pl.ds(rows, levels_ref.shape[0]), :] = levels_ref[...]
+
+
+def swap_in(levels, value):
     planes, count, rows, _ = value.shape
+    extra = levels.shape[1]
     return pl.pallas_call(
         functools.partial(swap_in_kernel, count, rows),
         grid=(planes,),
-        in_specs=[pl.BlockSpec((None, count, rows, LANES), lambda p: (p, 0, 0, 0))],
-        out_specs=pl.BlockSpec((count, None, rows, LANES), lambda p: (0, p, 0, 0)),
-        out_shape=jax.ShapeDtypeStruct((count, planes, rows, LANES), jnp.float32),
+        in_specs=[
+            pl.BlockSpec((None, extra, LANES), lambda p: (p, 0, 0)),
+            pl.BlockSpec((None, count, rows, LANES), lambda p: (p, 0, 0, 0)),
+        ],
+        out_specs=pl.BlockSpec((count, None, rows + extra, LANES), lambda p: (0, p, 0, 0)),
+        out_shape=jax.ShapeDtypeStruct((count, planes, rows + extra, LANES), jnp.float32),
         compiler_params=PARAMS,
         cost_estimate=cost(0, 8 * value.size),
-    )(value)
+    )(levels, value)
 
 
 def swap_out_kernel(count, rows, arrived_ref, high_ref, low_ref, weights_ref, out_ref):
@@ -171,10 +177,21 @@
     lax.fori_loop(0, side_y, row, 0)
 
 
-def filter_kernel(planes, side_y, side_z, width, chunks, arrived_ref, potential_ref, *rest):
-    outs, (field, padded, first, flat) = rest[: len(chunks)], rest[len(chunks) :]
-    count, _, rows, _ = arrived_ref.shape
+def filter_kernel(planes, side_y, side_z, width, chunks, arrived_ref, *rest):
+    outs, (field, padded, first, flat, potential) = rest[: len(chunks)], rest[len(chunks) :]
+    count = arrived_ref.shape[0]
+    cells = side_y * side_z
+    rows = cells // count
     tile = 16
+
+    line = lax.broadcasted_iota(jnp.int32, (2 * count, LANES), 0) % count
+    lane = lax.broadcasted_iota(jnp.int32, (2 * count, LANES), 1) // width
+    spread = (line == lane).astype(jnp.bfloat16)
+    for plane in range(planes):
+        lines = [arrived_ref[:, plane, rows + at, :] for at in range(cells // LANES)]
+        high, low = halves(jnp.concatenate(lines, axis=1))
+        both = jnp.concatenate([high.astype(jnp.float32), low.astype(jnp.float32)], axis=0)
+        potential[plane] = jnp.dot(both.T.astype(jnp.bfloat16), spread, preferred_element_type=jnp.float32)
 
     for plane in range(planes):
 
@@ -209,8 +226,8 @@
     def finish_second(plane, y, start, at, total):
         flat[plane, at, :] = total * (1.0 / 18.0) - field[plane, at, :]
 
-    local_part(padded, potential_ref, planes, 0, side_y, side_z, line_of, finish_first)
-    local_part(first, potential_ref, planes, 0, side_y, side_z, line_of, finish_second)
+    local_part(padded, potential, planes, 0, side_y, side_z, line_of, finish_first)
+    local_part(first, potential, planes, 0, side_y, side_z, line_of, finish_second)
 
     for (begin, size_of), out_ref in zip(chunks, outs):
         for plane in range(size_of):
@@ -224,27 +241,29 @@
             swap_into(read_out, write_out, count, rows)
 
 
-def filter_orbitals(arrived, potential, side_y, side_z, width, chunks):
-    count, planes, rows, _ = arrived.shape
+def filter_orbitals(arrived, side_y, side_z, width, chunks):
+    count, planes = arrived.shape[:2]
+    rows = side_y * side_z // count
     flat = pltpu.VMEM((planes, side_y * side_z, LANES), jnp.float32)
     padded = pltpu.VMEM((planes, side_y, side_z + 2 * PAD, LANES), jnp.float32)
     return pl.pallas_call(
         functools.partial(filter_kernel, planes, side_y, side_z, width, chunks),
-        in_specs=[WHOLE, WHOLE],
+        in_specs=[WHOLE],
         out_specs=[WHOLE] * len(chunks),
         out_shape=[jax.ShapeDtypeStruct((count, size, rows, LANES), jnp.float32) for _, size in chunks],
-        scratch_shapes=[flat, padded, padded, flat],
+        scratch_shapes=[flat, padded, padded, flat, flat],
         compiler_params=PARAMS,
         cost_estimate=cost(100 * arrived.size, 12 * arrived.size),
-    )(arrived, potential)
-
-
-def basis_kernel(planes, side_y, side_z, raw_ref, offset_ref, potential_ref, orbitals_ref, high_ref, low_ref, parts_ref, turned, placed):
+    )(arrived)
+
+
+def basis_kernel(planes, side_y, side_z, bands, *refs):
+    raw_refs = refs[:bands]
+    offset_ref, potential_ref, orbitals_ref, high_ref, low_ref, parts_ref, turned, placed = refs[bands:]
     cells = side_y * side_z
-    bands = raw_ref.shape[0]
     for part in range(SPAN):
         at = pl.ds(part * cells, cells)
-        stack = [raw_ref[band, block, :, at] for block in range(NEAR) for band in range(bands)]
+        stack = [raw_ref[block, :, at] for raw_ref in raw_refs for block in range(NEAR)]
         turned[part] = jnp.concatenate(stack, axis=0).T
     offset = offset_ref[0:1, :]
 
@@ -291,8 +310,8 @@
     planes, cells, _ = orbitals.shape
     pair = jax.ShapeDtypeStruct((planes, cells, 2 * LANES), jnp.bfloat16)
     return pl.pallas_call(
-        functools.partial(basis_kernel, planes, side_y, side_z),
-        in_specs=[WHOLE] * 4,
+        functools.partial(basis_kernel, planes, side_y, side_z, len(raw)),
+        in_specs=[WHOLE] * (len(raw) + 3),
         out_specs=[WHOLE] * 3,
         out_shape=[pair, pair, jax.ShapeDtypeStruct((3, LANES, LANES), jnp.float32)],
         scratch_shapes=[
@@ -301,12 +320,13 @@
         ],
         compiler_params=PARAMS,
         cost_estimate=cost(200 * orbitals.size, 24 * orbitals.size),
-    )(raw, offset, potential, orbitals)
-
-
-def weights_kernel(me_ref, parts_ref, coupling_ref, out_ref):
+    )(*raw, offset, potential, orbitals)
+
+
+def weights_kernel(bands, me_ref, parts_ref, coupling_ref, out_ref):
     count = parts_ref.shape[0]
     size = LANES // NEAR
+    lines = size // bands
     me = me_ref[0]
     dot = functools.partial(jnp.dot, precision=HIGHEST, preferred_element_type=jnp.float32)
 
@@ -314,8 +334,17 @@
         return lax.rem(me + step % count, count)
 
     def total(pick, block):
-        shares = [pick(block - (near - BEFORE), pl.ds(near * size, size)) for near in range(NEAR)]
+        shares = [pick(block - (near - BEFORE), near) for near in range(NEAR)]
         return (shares[0] + shares[1]) + (shares[2] + shares[3])
+
+    def of_block(value, near):
+        starts = [(band * NEAR + near) * lines for band in range(bands)]
+        return jnp.concatenate([value[start : start + lines] for start in starts], axis=0)
+
+    def joined(values):
+        return jnp.concatenate(
+            [values[near][band * lines : (band + 1) * lines] for band in range(bands) for near in range(NEAR)], axis=0
+        )
 
     def couple(block, value):
         return dot(coupling_ref[device(block)], value)
@@ -330,22 +359,23 @@
 
         return look
 
-    weight = kept(lambda block: couple(block, total(lambda step, at: parts_ref[device(step), 0, at, :], block)))
-    near_weights = kept(lambda step: jnp.concatenate([weight(step + near - BEFORE) for near in range(NEAR)], axis=0))
-    overlap = kept(lambda step: dot(parts_ref[device(step), 2], near_weights(step)))
-    out_ref[pl.ds(0, LANES), :] = near_weights(0)
-    for near in range(NEAR):
-        block = near - BEFORE
-
-        def share(step, at):
-            return parts_ref[device(step), 1, at, :] + overlap(step)[at.start : at.start + size]
-
-        out_ref[pl.ds(LANES + near * size, size), :] = couple(block, total(share, block))
+    weight = kept(
+        lambda block: couple(block, total(lambda step, near: of_block(parts_ref[device(step), 0], near), block))
+    )
+    weights = kept(lambda step: joined([weight(step + near - BEFORE) for near in range(NEAR)]))
+    second = kept(lambda step: parts_ref[device(step), 1] + dot(parts_ref[device(step), 2], weights(step)))
+    out_ref[pl.ds(0, LANES), :] = weights(0)
+    out_ref[pl.ds(LANES, LANES), :] = joined(
+        [
+            couple(near - BEFORE, total(lambda step, at: of_block(second(step), at), near - BEFORE))
+            for near in range(NEAR)
+        ]
+    )
 
 
 def near_weights(parts, coupling):
     return pl.pallas_call(
-        weights_kernel,
+        functools.partial(weights_kernel, lax.axis_size("band")),
         in_specs=[pl.BlockSpec(memory_space=pltpu.SMEM), WHOLE, WHOLE],
         out_specs=WHOLE,
         out_shape=jax.ShapeDtypeStruct((2 * LANES, LANES), jnp.float32),
@@ -461,8 +491,18 @@
             work[rest, :] = work[rest, :] - jnp.dot(columns, rows, preferred_element_type=jnp.float32)
 
 
-def cholesky_kernel(gram_ref, out_ref, matrix, work, corner, scaled):
+def cholesky_kernel(band_ref, *refs):
+    rows_refs, (gram_ref, own_ref, inverse, matrix, work, corner, scaled) = refs[:-7], refs[-7:]
     size = gram_ref.shape[0]
+    bands = len(rows_refs)
+    band = band_ref[0]
+
+    def block_of(member):
+        return pl.ds(pl.multiple_of((band ^ member) * LANES, LANES), LANES)
+
+    for member, rows_ref in enumerate(rows_refs):
+        for other in range(bands):
+            gram_ref[block_of(member), block_of(member ^ other)] = rows_ref[:, other * LANES : (other + 1) * LANES]
     dot = functools.partial(jnp.dot, precision=HIGHEST, preferred_element_type=jnp.float32)
     diagonal = lax.broadcasted_iota(jnp.int32, (LANES, LANES), 0) == lax.broadcasted_iota(jnp.int32, (LANES, LANES), 1)
     identity = diagonal.astype(jnp.float32)
@@ -478,7 +518,7 @@
         work[:, LANES:] = identity
         eliminate(work, corner)
         scaled[...] = dot(corner[...], matrix[at, :])
-        out_ref[at, :] = scaled[:, size:]
+        inverse[at, :] = scaled[:, size:]
 
         def below(other, carry):
             rows = pl.ds(pl.multiple_of(other * LANES, LANES), LANES)
@@ -489,38 +529,48 @@
         return carry
 
     lax.fori_loop(0, size // LANES, block, 0)
-
-
-def cholesky_inverse(gram):
-    size = gram.shape[0]
+    for member in range(bands):
+        own_ref[:, member * LANES : (member + 1) * LANES] = inverse[block_of(0), block_of(member)]
+
+
+def cholesky_inverse(band, rows):
+    size = rows[0].shape[1]
     whole = pl.BlockSpec(memory_space=pltpu.VMEM)
     return pl.pallas_call(
         cholesky_kernel,
-        in_specs=[whole],
-        out_specs=whole,
-        out_shape=jax.ShapeDtypeStruct((size, size), jnp.float32),
+        in_specs=[pl.BlockSpec(memory_space=pltpu.SMEM)] + [whole] * len(rows),
+        out_specs=[whole] * 2,
+        out_shape=[
+            jax.ShapeDtypeStruct((size, size), jnp.float32),
+            jax.ShapeDtypeStruct((LANES, size), jnp.float32),
+        ],
         scratch_shapes=[
+            pltpu.VMEM((size, size), jnp.float32),
             pltpu.VMEM((size, 2 * size), jnp.float32),
             pltpu.VMEM((LANES, 2 * LANES), jnp.float32),
             pltpu.VMEM((LANES, LANES), jnp.float32),
             pltpu.VMEM((LANES, 2 * size), jnp.float32),
         ],
         compiler_params=PARAMS,
-    )(gram)
-
-
-def near_projectors(projectors, atom_plane, planes):
-    bands, band, block = lax.axis_size("band"), lax.axis_index("band"), lax.axis_index("dom")
-    share = projectors.shape[0] // bands
-    lines = share * MAXPROJ
-    first = (atom_plane - block * planes).astype(jnp.float32)
+    )(band.astype(jnp.int32).reshape(1), *rows)
+
+
+def packed_projectors(projectors, atom_plane, planes):
+    share = projectors.shape[0] // lax.axis_size("band")
+    first = (atom_plane - lax.axis_index("dom") * planes).astype(jnp.float32)
     first = jnp.broadcast_to(first[:, None, None], (projectors.shape[0], MAXPROJ, LANES))
     packed = jnp.concatenate([projectors, first], axis=2)
-    mine = lax.dynamic_slice_in_dim(packed, band * share, share, 0).reshape(lines, -1)
+    mine = lax.dynamic_slice_in_dim(packed, lax.axis_index("band") * share, share, 0)
+    return mine.reshape(share * MAXPROJ, -1)
+
+
+def near_projectors(mine, planes):
     near = [mine if step == BEFORE else shifted(mine, "dom", BEFORE - step) for step in range(NEAR)]
-    raw = lax.all_gather(jnp.stack(near), "band")
-    first = raw[:, :, :, -1] + (planes * (jnp.arange(NEAR, dtype=jnp.float32) - BEFORE))[None, :, None]
-    first = jnp.transpose(first, (1, 0, 2)).reshape(1, LANES)
+    near = jnp.stack(near)
+    across = crossed(near, 2)
+    raw = [near, crossed(near, 1), across, crossed(across, 1)]
+    moved = (planes * (jnp.arange(NEAR, dtype=jnp.float32) - BEFORE))[:, None]
+    first = jnp.stack([member[:, :, -1] + moved for member in raw]).reshape(1, LANES)
     return raw, jnp.broadcast_to(first, (GROUP, LANES))
 
 
@@ -534,12 +584,13 @@
     norb = local_orbs * bands
     chunks = ((0, 2), (2, 1), (3, 1))
 
-    raw, first = near_projectors(projectors, atom_plane, planes)
-    levels = lax.all_gather(potential.reshape(planes, cells), "dom")
-    levels = jnp.transpose(levels, (1, 2, 0))
-    levels = jnp.broadcast_to(levels[..., None], (planes, cells, blocks, width)).reshape(planes, cells, LANES)
-
-    packed = swap_in(orbitals.reshape(planes, blocks, rows, local_orbs))
+    order = jnp.arange(bands, dtype=jnp.int32) ^ band
+
+    mine = packed_projectors(projectors, atom_plane, planes)
+    mine, levels = lax.optimization_barrier((mine, potential.reshape(planes, cells // LANES, LANES)))
+    raw, first = near_projectors(mine, planes)
+    levels = jnp.pad(levels, ((0, 0), (0, -levels.shape[1] % GROUP), (0, 0)))
+    packed = swap_in(levels, orbitals.reshape(planes, blocks, rows, local_orbs))
     arrived = lax.all_to_all(packed, "dom", 0, 0, tiled=True)
 
     own_levels = jnp.broadcast_to(potential.reshape(planes, cells, 1), (planes, cells, LANES))
@@ -548,6 +599,7 @@
     slots = jnp.arange(MAXPROJ, dtype=jnp.int32)
     live = (slots[None, :] < projector_count[:, None]).astype(jnp.float32)
     coupled = 0.5 * (coupling + jnp.transpose(coupling, (0, 2, 1))) * live[:, :, None] * live[:, None, :]
+    coupled = jnp.take(coupled.reshape(bands, -1, MAXPROJ, MAXPROJ), order, axis=0)
     vectors = atoms * MAXPROJ
     row = jnp.arange(vectors, dtype=jnp.int32) // MAXPROJ
     matrix = jnp.tile(coupled.reshape(vectors, MAXPROJ), (1, atoms))
@@ -558,7 +610,7 @@
         everyone[:, : 3 * LANES].reshape(blocks, 3, LANES, LANES), everyone[:, 3 * LANES :, :vectors]
     )
 
-    seconds = filter_orbitals(arrived, levels, side_y, side_z, width, chunks)
+    seconds = filter_orbitals(arrived, side_y, side_z, width, chunks)
 
     panels, part = [], 0.0
     for (begin, size), packed in zip(chunks, seconds):
@@ -567,15 +619,12 @@
         panels.append([own, crossed(own, 1), across, crossed(across, 1)])
         part = part + gram_rows(panels[-1])
 
-    order = jnp.arange(bands, dtype=jnp.int32) ^ band
-    part = jnp.take(part.reshape(local_orbs, bands, local_orbs), order, axis=1)
     pieces = lax.all_to_all(part.reshape(blocks, width, norb), "dom", 0, 0, tiled=True)
     piece = jnp.sum(pieces, axis=0) * (1.0 / (planes * cells * blocks))
     own_gram = lax.all_to_all(jnp.broadcast_to(piece, (blocks, width, norb)), "dom", 0, 0, tiled=True)
-    gram = lax.all_gather(own_gram.reshape(local_orbs, norb), "band", axis=0, tiled=True)
-    inverse = cholesky_inverse(gram)
-    own_rows = lax.dynamic_slice_in_dim(inverse, band * local_orbs, local_orbs, 0)
-    own_rows = jnp.take(own_rows.reshape(local_orbs, bands, local_orbs), order, axis=1).reshape(local_orbs, norb)
+    own_gram = own_gram.reshape(local_orbs, norb)
+    across = crossed(own_gram, 2)
+    gram, own_rows = cholesky_inverse(band, [own_gram, crossed(own_gram, 1), across, crossed(across, 1)])
     result = rotated(own_rows, panels, chunks)
     return (result.reshape(planes, side_y, side_z, local_orbs), gram)
 

time: 433 us -> 415 us (0.958)
  blocking collectives: 68 us -> 24.8 us
  starting transfers between devices: 28.3 us -> 48.3 us
  waiting for transfers between devices: 172 us -> 187 us
  Pallas kernels: 123 us -> 116 us
    all_gather x1 -> x0, blocking collectives: 43.1 us -> none  [shards(): levels = lax.all_gather(potential.reshape(planes, cells), 'dom')]
    ppermute x9 -> x15, waiting for transfers between devices: 38.1 us -> 56.4 us  [crossed(): lax.ppermute(value, 'band', [(source, source ^ bit) for source in range(l...]
    all_to_all x3, starting transfers between devices: 13 us -> 29.9 us  [shards(): lax.all_to_all(packed, 'dom', 0, 0, tiled=True)]
    all_gather x2 -> x0, waiting for transfers between devices: 15.9 us -> none  [the longest x1 15.9 us: shards(): lax.all_gather(own_gram.reshape(local_orbs, norb), 'band', axis=0, tiled=...]
    all_to_all x3, waiting for transfers between devices: 26.3 us -> 35.9 us  [shards(): lax.all_to_all(packed, 'dom', 0, 0, tiled=True)]
    ppermute x3, waiting for transfers between devices: 54.9 us -> 60.7 us  [shifted(): lax.ppermute(value, axis, [(source, (source + step) % count) for source i...]
  transfers between devices with their start and end apart: 19 -> 23, of which waited for: 10 -> 12; matrix products, arithmetic and copies ran while one was open for 5% -> 4% of each run, Pallas kernels for 16% -> 16%
where the time goes in v4:
time: 415 us; the launch traced here: 414 us
  waiting for transfers between devices  187 us (45%)
  Pallas kernels  116 us (28%)
  starting transfers between devices  48.3 us (12%)
  blocking collectives  24.8 us (6%)
  local copies, waits for them, and re-layouts  16.8 us (4%)
  between operations  14.2 us (3%)
  other arithmetic  6.48 us (2%)
    ppermute x3, waiting for transfers between devices, shifted(): lax.ppermute(value, axis, [(source, (source + step) % count) for source i...  60.7 us
    ppermute x15, waiting for transfers between devices, crossed(): lax.ppermute(value, 'band', [(source, source ^ bit) for source in range(l...  56.4 us
    all_to_all x3, waiting for transfers between devices, shards(): lax.all_to_all(packed, 'dom', 0, 0, tiled=True)  35.9 us
    all_gather x1, waiting for transfers between devices, shards(): lax.all_gather(jnp.concatenate([parts.reshape(3 * LANES, LANES), matrix],...  34.2 us
    pallas_call x1, Pallas kernels, cholesky_inverse(): pl.pallas_call(cholesky_kernel, in_specs=[pl.BlockSpec(memory_space=pltpu...  30.4 us
    all_to_all x3, starting transfers between devices, shards(): lax.all_to_all(packed, 'dom', 0, 0, tiled=True)  29.9 us
    pallas_call x1, Pallas kernels, filter_orbitals(): pl.pallas_call(functools.partial(filter_kernel, planes, side_y, side_z, w...  21.2 us
    pallas_call x3, Pallas kernels, swap_out(): pl.pallas_call(functools.partial(swap_out_kernel, count, rows), grid=(1,)...  17.3 us
  transfers between devices with their start and end apart: 23, of which 12 were waited for; matrix products, arithmetic and copies ran while one was open for 4% of the time, Pallas kernels for 16%

profile of v4, /device:TPU:0, one launch (start us, length us, event | category | flops | bytes accessed | tf_op | source)
XLA Modules:
  0.0 413.7 jit_solution(15010049624965370414)
XLA Ops:
  11.1 6.0 %shard_map.77 = f32[8,4,208,128]{3,2,1,0:T(8,128)} custom-call(f32[4,16,128]{2,1,0:T(8,128)} %pad.8.levels_ref, f32[4,8,192,128]{3,2,1,0:T(8,128)} %bitcast.34), custom_call_target="tpu_custom_call" | custom-call | bytes 6291456 | tf_op jit(solution)/shard_map/pallas_call | solution.py:89
  17.1 7.4 %all-to-all-start = ((f32[8,4,208,128]{3,2,1,0:T(8,128)}), f32[8,4,208,128]{3,2,1,0:T(8,128)S(1)}, u32[]{:S(2)}, u32[]{:S(2)}) async-start(f32[8,4,208,128]{3,2,1,0:T(8,128)} %shard_map.77), calls=%async_computation | async-start | bytes 6815744 | tf_op jit(solution)/shard_map/all_to_all | solution.py:594
  24.5 4.7 %collective-permute-start.2 = (f32[8,4736]{1,0:T(8,128)}, f32[8,4736]{1,0:T(8,128)S(1)}, u32[]{:S(2)}, u32[]{:S(2)}) collective-permute-start(f32[8,4736]{1,0:T(8,128)} %reshape.267), channel_id=1, source_target_pairs={{0,7},{1,0},{2,1},{3,2},{4,3},{5,4},{6,5},{7,6},{8,15},{9,8},{10,9... | collective-permute-start | bytes 454664 | tf_op jit(solution)/shard_map/ppermute | solution.py:389
  29.4 55.6 %collective-permute-done.2 = f32[8,4736]{1,0:T(8,128)S(1)} collective-permute-done((f32[8,4736]{1,0:T(8,128)}, f32[8,4736]{1,0:T(8,128)S(1)}, u32[]{:S(2)}, u32[]{:S(2)}) %collective-permute-start.2) | collective-permute-done | bytes 151584 | tf_op jit(solution)/shard_map/ppermute | solution.py:389
  94.9 11.5 %collective-permute-done.4.refs_2_ = f32[4,8,4736]{2,1,0:T(8,128)} collective-permute-done((f32[4,8,4736]{2,1,0:T(8,128)}, f32[4,8,4736]{2,1,0:T(8,128)}, u32[]{:S(2)}, u32[]{:S(2)}) %collective-permute-start.4) | collective-permute-done | bytes 606240 | tf_op jit(solution)/shard_map/ppermute | solution.py:393
  108.4 21.2 %shard_map.78 = (f32[8,2,192,128]{3,2,1,0:T(8,128)}, f32[8,1,192,128]{3,2,1,0:T(8,128)}, f32[8,1,192,128]{3,2,1,0:T(8,128)}) custom-call(f32[8,4,208,128]{3,2,1,0:T(8,128)} %copy-done.1), custom_call_target="tpu_custom_call" | custom-call | flops 85196800 | bytes 10223616 | tf_op jit(solution)/shard_map/pallas_call | solution.py:249
  129.6 21.3 %all-to-all-start.1 = ((f32[8,2,192,128]{3,2,1,0:T(8,128)}), f32[8,2,192,128]{3,2,1,0:T(8,128)S(1)}, u32[]{:S(2)}, u32[]{:S(2)}) async-start(f32[8,2,192,128]{3,2,1,0:T(8,128)} %get-tuple-element.13), calls=%async_computation.1 | async-start | bytes 3145728 | tf_op jit(solution)/shard_map/all_to_all | solution.py:617
  157.4 13.5 %shard_map.79 = (bf16[4,1536,256]{2,1,0:T(8,128)(2,1)}, bf16[4,1536,256]{2,1,0:T(8,128)(2,1)}, f32[3,128,128]{2,1,0:T(8,128)}) custom-call(f32[4,8,4736]{2,1,0:T(8,128)} %pad_maximum_fusion.refs_0_, f32[4,8,4736]{2,1,0:T(8,128)} %collective-permute-done.3.refs_1_, f32[4,8,4736]{2,1,0:T(8,128)} %collective-permute-done.4.refs_2_, ...), custom_call_target="tpu_custom_call" | custom-call | flops 157286400 | bytes 18874368 | tf_op jit(solution)/shard_map/pallas_call | solution.py:312
  172.5 20.5 %all-to-all-done.1.arrived_ref = f32[8,2,192,128]{3,2,1,0:T(8,128)S(1)} async-done(((f32[8,2,192,128]{3,2,1,0:T(8,128)}), f32[8,2,192,128]{3,2,1,0:T(8,128)S(1)}, u32[]{:S(2)}, u32[]{:S(2)}) %all-to-all-start.1) | async-done | bytes 1572896 | tf_op jit(solution)/shard_map/all_to_all | solution.py:617
  197.5 34.2 %all-gather.3.cloned.1.call-done = f32[3328,128]{1,0:T(8,128)} async-done(((f32[416,128]{1,0:T(8,128)}), f32[3328,128]{1,0:T(8,128)}) %all-gather.3.cloned.1.call-update) | async-done | bytes 1703952 | tf_op jit(solution)/shard_map/all_gather | solution.py:608
  239.7 7.9 %shard_map.81.own_ref.rest_0_ = f32[2,1536,128]{2,1,0:T(8,128)} custom-call(f32[8,2,192,128]{3,2,1,0:T(8,128)} %copy-done.2, bf16[4,1536,256]{2,1,0:T(8,128)(2,1)} %get-tuple-element.15.high_ref, bf16[4,1536,256]{2,1,0:T(8,128)(2,1)} %get-tuple-element.16.low_ref, f32[256,128]{1,0:T(8,128)} %shard_map.80.weights_ref), custom_call_target="tpu_custom_call" | custom-call | bytes 9437184 | tf_op jit(solution)/shard_map/pallas_call | solution.py:131
  253.6 4.7 %shard_map.85.own_ref.rest_8_ = f32[1,1536,128]{2,1,0:T(8,128)} custom-call(f32[8,1,192,128]{3,2,1,0:T(8,128)} %all-to-all-done.3.arrived_ref, bf16[4,1536,256]{2,1,0:T(8,128)(2,1)} %get-tuple-element.15.high_ref, bf16[4,1536,256]{2,1,0:T(8,128)(2,1)} %get-tuple-element.16.low_ref, f32[256,128]{1,0:T(8,128)} %shard_map.80.weights_ref), custom_call_target="tpu_custom_call" | custom-call | bytes 4718592 | tf_op jit(solution)/shard_map/pallas_call | solution.py:131
  258.6 15.3 %all-to-all-done.2.arrived_ref = f32[8,1,192,128]{3,2,1,0:T(8,128)} async-done(((f32[8,1,192,128]{3,2,1,0:T(8,128)}), f32[8,1,192,128]{3,2,1,0:T(8,128)}, u32[]{:S(2)}, u32[]{:S(2)}) %all-to-all-start.2) | async-done | bytes 786464 | tf_op jit(solution)/shard_map/all_to_all | solution.py:617
  273.9 4.7 %shard_map.83.own_ref.rest_4_ = f32[1,1536,128]{2,1,0:T(8,128)} custom-call(f32[8,1,192,128]{3,2,1,0:T(8,128)} %all-to-all-done.2.arrived_ref, bf16[4,1536,256]{2,1,0:T(8,128)(2,1)} %get-tuple-element.15.high_ref, bf16[4,1536,256]{2,1,0:T(8,128)(2,1)} %get-tuple-element.16.low_ref, f32[256,128]{1,0:T(8,128)} %shard_map.80.weights_ref), custom_call_target="tpu_custom_call" | custom-call | bytes 4718592 | tf_op jit(solution)/shard_map/pallas_call | solution.py:131
  278.9 6.1 %collective-permute-done.7.rest_1_.rest_2_ = f32[2,1536,128]{2,1,0:T(8,128)S(1)} collective-permute-done((f32[2,1536,128]{2,1,0:T(8,128)}, f32[2,1536,128]{2,1,0:T(8,128)S(1)}, u32[]{:S(2)}, u32[]{:S(2)}) %collective-permute-start.7) | collective-permute-done | bytes 1572896 | tf_op jit(solution)/shard_map/ppermute | solution.py:393
  285.1 17.0 %collective-permute-done.13.rest_1_.rest_10_ = f32[1,1536,128]{2,1,0:T(8,128)} collective-permute-done((f32[1,1536,128]{2,1,0:T(8,128)}, f32[1,1536,128]{2,1,0:T(8,128)}, u32[]{:S(2)}, u32[]{:S(2)}) %collective-permute-start.13) | collective-permute-done | bytes 786464 | tf_op jit(solution)/shard_map/ppermute | solution.py:393
  302.6 15.4 %collective-permute-done.10.rest_1_.rest_6_ = f32[1,1536,128]{2,1,0:T(8,128)} collective-permute-done((f32[1,1536,128]{2,1,0:T(8,128)}, f32[1,1536,128]{2,1,0:T(8,128)}, u32[]{:S(2)}, u32[]{:S(2)}) %collective-permute-start.10) | collective-permute-done | bytes 786464 | tf_op jit(solution)/shard_map/ppermute | solution.py:393
  322.7 4.7 %shard_map.84 = f32[128,512]{1,0:T(8,128)} custom-call(f32[1,1536,128]{2,1,0:T(8,128)} %shard_map.83.own_ref.rest_4_, f32[1,1536,128]{2,1,0:T(8,128)} %collective-permute-done.9.rest_0_.rest_5_, f32[1,1536,128]{2,1,0:T(8,128)} %collective-permute-done.10.rest_1_.rest_6_, f32[1,1536,128]{2,1,0:T(8,128)} %collective-permute-done.11.rest_2_.rest_7_), custom_call_target="tpu_custom_call" | custom-call | flops 805306368 | bytes 3145728 | tf_op jit(solution)/shard_map/pallas_call | solution.py:413
  327.4 6.0 %shard_map.82 = f32[128,512]{1,0:T(8,128)} custom-call(f32[2,1536,128]{2,1,0:T(8,128)} %shard_map.81.own_ref.rest_0_, f32[2,1536,128]{2,1,0:T(8,128)} %collective-permute-done.6.rest_0_.rest_1_, f32[2,1536,128]{2,1,0:T(8,128)} %copy-done.3, f32[2,1536,128]{2,1,0:T(8,128)} %collective-permute-done.8.rest_2_.rest_3_), custom_call_target="tpu_custom_call" | custom-call | flops 1610612736 | bytes 6291456 | tf_op jit(solution)/shard_map/pallas_call | solution.py:413
  334.5 12.3 %all_to_all.30 = f32[8,16,512]{2,1,0:T(8,128)S(1)} all-to-all(f32[8,16,512]{2,1,0:T(8,128)S(1)} %bitcast.43), channel_id=1, replica_groups=mesh['band'=4,'dom'=8] {'dom'}, dimensions={0} | all-to-all | bytes 524288 | tf_op jit(solution)/shard_map/all_to_all | solution.py:622
  346.8 12.5 %all_to_all.31 = f32[8,16,512]{2,1,0:T(8,128)S(1)} all-to-all(f32[8,16,512]{2,1,0:T(8,128)S(1)} %broadcast_in_dim.58), channel_id=1, replica_groups=mesh['band'=4,'dom'=8] {'dom'}, dimensions={0} | all-to-all | bytes 524288 | tf_op jit(solution)/shard_map/all_to_all | solution.py:624
  361.0 4.7 %collective-permute-done.16.refs_2_ = f32[128,512]{1,0:T(8,128)S(1)} collective-permute-done((f32[128,512]{1,0:T(8,128)S(1)}, f32[128,512]{1,0:T(8,128)S(1)}, u32[]{:S(2)}, u32[]{:S(2)}) %collective-permute-start.16) | collective-permute-done | bytes 262176 | tf_op jit(solution)/shard_map/ppermute | solution.py:393
  368.0 30.4 %shard_map.87 = (f32[512,512]{1,0:T(8,128)}, f32[128,512]{1,0:T(8,128)}) custom-call(s32[1]{0:T(128)} %bitcast.band_ref, f32[128,512]{1,0:T(8,128)} %bitcast.42, f32[128,512]{1,0:T(8,128)} %copy-done.9, f32[128,512]{1,0:T(8,128)} %copy-done.8, f32[128,512]{1,0:T(8,128)} %copy-done.10), custom_call_target="tpu_custom_call" | custom-call | tf_op jit(solution)/shard_map/pallas_call | solution.py:539
  398.3 8.5 %shard_map.88 = f32[4,1536,128]{2,1,0:T(8,128)} custom-call(f32[128,512]{1,0:T(8,128)} %get-tuple-element.20.inverse_ref, f32[2,1536,128]{2,1,0:T(8,128)} %shard_map.81.own_ref.rest_0_, f32[2,1536,128]{2,1,0:T(8,128)} %collective-permute-done.6.rest_0_.rest_1_, f32[2,1536,128]{2,1,0:T(8,128)} %copy-done.3, ...), custom_call_target="tpu_custom_call" | custom-call | tf_op jit(solution)/shard_map/pallas_call | solution.py:440
  (107 shorter events, 53.1 us)
Async XLA Ops:
  17.1 77.7 %copy-start.7 = (f32[4,32,48]{2,1,0:T(8,128)S(1)}, f32[4,32,48]{2,1,0:T(8,128)}, u32[]{:S(2)}) copy-start(f32[4,32,48]{2,1,0:T(8,128)} %param.7) | copy-start | bytes 73732
  17.1 89.6 %all-to-all-start = ((f32[8,4,208,128]{3,2,1,0:T(8,128)}), f32[8,4,208,128]{3,2,1,0:T(8,128)S(1)}, u32[]{:S(2)}, u32[]{:S(2)}) async-start(f32[8,4,208,128]{3,2,1,0:T(8,128)} %shard_map.77), calls=%async_computation | async-start | bytes 6815744 | tf_op jit(solution)/shard_map/all_to_all | solution.py:594
  24.5 60.5 %collective-permute-start.2 = (f32[8,4736]{1,0:T(8,128)}, f32[8,4736]{1,0:T(8,128)S(1)}, u32[]{:S(2)}, u32[]{:S(2)}) collective-permute-start(f32[8,4736]{1,0:T(8,128)} %reshape.267), channel_id=1, source_target_pairs={{0,7},{1,0},{2,1},{3,2},{4,3},{5,4},{6,5},{7,6},{8,15},{9,8},{10,9... | collective-permute-start | bytes 454664 | tf_op jit(solution)/shard_map/ppermute | solution.py:389
  29.2 60.0 %collective-permute-start.1 = (f32[8,4736]{1,0:T(8,128)}, f32[8,4736]{1,0:T(8,128)S(1)}, u32[]{:S(2)}, u32[]{:S(2)}) collective-permute-start(f32[8,4736]{1,0:T(8,128)} %reshape.267), channel_id=1, source_target_pairs={{0,1},{1,2},{2,3},{3,4},{4,5},{5,6},{6,7},{7,0},{8,9},{9,10},{10,1... | collective-permute-start | bytes 454664 | tf_op jit(solution)/shard_map/ppermute | solution.py:389
  29.2 60.8 %collective-permute-start = (f32[8,4736]{1,0:T(8,128)}, f32[8,4736]{1,0:T(8,128)S(1)}, u32[]{:S(2)}, u32[]{:S(2)}) collective-permute-start(f32[8,4736]{1,0:T(8,128)} %reshape.267), channel_id=1, source_target_pairs={{0,2},{1,3},{2,4},{3,5},{4,6},{5,7},{6,0},{7,1},{8,10},{9,11},{10,... | collective-permute-start | bytes 454664 | tf_op jit(solution)/shard_map/ppermute | solution.py:389
  91.9 14.6 %collective-permute-start.4 = (f32[4,8,4736]{2,1,0:T(8,128)}, f32[4,8,4736]{2,1,0:T(8,128)}, u32[]{:S(2)}, u32[]{:S(2)}) collective-permute-start(f32[4,8,4736]{2,1,0:T(8,128)} %pad_maximum_fusion.refs_0_), channel_id=1, source_target_pairs={{0,16},{8,24},{16,0},{24,8},{1,17},{9,25},{17,1},{25,9},{2,18},{10... | collective-permute-start | bytes 1818632 | tf_op jit(solution)/shard_map/ppermute | solution.py:393
  94.7 58.0 %collective-permute-start.3 = (f32[4,8,4736]{2,1,0:T(8,128)}, f32[4,8,4736]{2,1,0:T(8,128)}, u32[]{:S(2)}, u32[]{:S(2)}) collective-permute-start(f32[4,8,4736]{2,1,0:T(8,128)} %pad_maximum_fusion.refs_0_), channel_id=1, source_target_pairs={{0,8},{8,0},{16,24},{24,16},{1,9},{9,1},{17,25},{25,17},{2,10},{10... | collective-permute-start | bytes 1818632 | tf_op jit(solution)/shard_map/ppermute | solution.py:393
  106.5 47.1 %collective-permute-start.5 = (f32[4,8,4736]{2,1,0:T(8,128)}, f32[4,8,4736]{2,1,0:T(8,128)}, u32[]{:S(2)}, u32[]{:S(2)}) collective-permute-start(f32[4,8,4736]{2,1,0:T(8,128)} %collective-permute-done.4.refs_2_), channel_id=1, source_target_pairs={{0,8},{8,0},{16,24},{24,16},{1,9},{9,1},{17,25},{25,17},{2,10},{10... | collective-permute-start | bytes 1818632 | tf_op jit(solution)/shard_map/ppermute | solution.py:393
  129.6 63.5 %all-to-all-start.1 = ((f32[8,2,192,128]{3,2,1,0:T(8,128)}), f32[8,2,192,128]{3,2,1,0:T(8,128)S(1)}, u32[]{:S(2)}, u32[]{:S(2)}) async-start(f32[8,2,192,128]{3,2,1,0:T(8,128)} %get-tuple-element.13), calls=%async_computation.1 | async-start | bytes 3145728 | tf_op jit(solution)/shard_map/all_to_all | solution.py:617
  150.9 80.8 %all-gather.3.cloned.1.call-start = ((), (), s32[]{:S(2)}) async-start(), calls=%async_computation.6 | async-start | bytes 1916928 | tf_op jit(solution)/shard_map/all_gather | solution.py:608
  193.1 56.2 %all-to-all-start.3 = ((f32[8,1,192,128]{3,2,1,0:T(8,128)}), f32[8,1,192,128]{3,2,1,0:T(8,128)}, u32[]{:S(2)}, u32[]{:S(2)}) async-start(f32[8,1,192,128]{3,2,1,0:T(8,128)} %get-tuple-element.19), calls=%async_computation.3 | async-start | bytes 1572864 | tf_op jit(solution)/shard_map/all_to_all | solution.py:617
  247.6 37.5 %collective-permute-start.7 = (f32[2,1536,128]{2,1,0:T(8,128)}, f32[2,1536,128]{2,1,0:T(8,128)S(1)}, u32[]{:S(2)}, u32[]{:S(2)}) collective-permute-start(f32[2,1536,128]{2,1,0:T(8,128)} %shard_map.81.own_ref.rest_0_), channel_id=1, source_target_pairs={{0,16},{8,24},{16,0},{24,8},{1,17},{9,25},{17,1},{25,9},{2,18},{10... | collective-permute-start | bytes 4718600 | tf_op jit(solution)/shard_map/ppermute | solution.py:393
  249.3 24.6 %all-to-all-start.2 = ((f32[8,1,192,128]{3,2,1,0:T(8,128)}), f32[8,1,192,128]{3,2,1,0:T(8,128)}, u32[]{:S(2)}, u32[]{:S(2)}) async-start(f32[8,1,192,128]{3,2,1,0:T(8,128)} %get-tuple-element.18), calls=%async_computation.2 | async-start | bytes 1572864 | tf_op jit(solution)/shard_map/all_to_all | solution.py:617
  258.3 43.7 %collective-permute-start.13 = (f32[1,1536,128]{2,1,0:T(8,128)}, f32[1,1536,128]{2,1,0:T(8,128)}, u32[]{:S(2)}, u32[]{:S(2)}) collective-permute-start(f32[1,1536,128]{2,1,0:T(8,128)} %shard_map.85.own_ref.rest_8_), channel_id=1, source_target_pairs={{0,16},{8,24},{16,0},{24,8},{1,17},{9,25},{17,1},{25,9},{2,18},{10... | collective-permute-start | bytes 2359304 | tf_op jit(solution)/shard_map/ppermute | solution.py:393
  258.6 43.4 %collective-permute-start.12 = (f32[1,1536,128]{2,1,0:T(8,128)}, f32[1,1536,128]{2,1,0:T(8,128)}, u32[]{:S(2)}, u32[]{:S(2)}) collective-permute-start(f32[1,1536,128]{2,1,0:T(8,128)} %shard_map.85.own_ref.rest_8_), channel_id=1, source_target_pairs={{0,8},{8,0},{16,24},{24,16},{1,9},{9,1},{17,25},{25,17},{2,10},{10... | collective-permute-start | bytes 2359304 | tf_op jit(solution)/shard_map/ppermute | solution.py:393
  278.6 39.4 %collective-permute-start.10 = (f32[1,1536,128]{2,1,0:T(8,128)}, f32[1,1536,128]{2,1,0:T(8,128)}, u32[]{:S(2)}, u32[]{:S(2)}) collective-permute-start(f32[1,1536,128]{2,1,0:T(8,128)} %shard_map.83.own_ref.rest_4_), channel_id=1, source_target_pairs={{0,16},{8,24},{16,0},{24,8},{1,17},{9,25},{17,1},{25,9},{2,18},{10... | collective-permute-start | bytes 2359304 | tf_op jit(solution)/shard_map/ppermute | solution.py:393
  278.9 48.5 %collective-permute-start.6 = (f32[2,1536,128]{2,1,0:T(8,128)S(1)}, f32[2,1536,128]{2,1,0:T(8,128)}, u32[]{:S(2)}, u32[]{:S(2)}) collective-permute-start(f32[2,1536,128]{2,1,0:T(8,128)S(1)} %copy-done), channel_id=1, source_target_pairs={{0,8},{8,0},{16,24},{24,16},{1,9},{9,1},{17,25},{25,17},{2,10},{10... | collective-permute-start | bytes 4718600 | tf_op jit(solution)/shard_map/ppermute | solution.py:393
  285.1 42.3 %collective-permute-start.8 = (f32[2,1536,128]{2,1,0:T(8,128)S(1)}, f32[2,1536,128]{2,1,0:T(8,128)}, u32[]{:S(2)}, u32[]{:S(2)}) collective-permute-start(f32[2,1536,128]{2,1,0:T(8,128)S(1)} %collective-permute-done.7.rest_1_.rest_2_), channel_id=1, source_target_pairs={{0,8},{8,0},{16,24},{24,16},{1,9},{9,1},{17,25},{25,17},{2,10},{10... | collective-permute-start | bytes 4718600 | tf_op jit(solution)/shard_map/ppermute | solution.py:393
  302.0 16.0 %collective-permute-start.14 = (f32[1,1536,128]{2,1,0:T(8,128)}, f32[1,1536,128]{2,1,0:T(8,128)}, u32[]{:S(2)}, u32[]{:S(2)}) collective-permute-start(f32[1,1536,128]{2,1,0:T(8,128)} %collective-permute-done.13.rest_1_.rest_10_), channel_id=1, source_target_pairs={{0,8},{8,0},{16,24},{24,16},{1,9},{9,1},{17,25},{25,17},{2,10},{10... | collective-permute-start | bytes 2359304 | tf_op jit(solution)/shard_map/ppermute | solution.py:393
  302.0 20.6 %collective-permute-start.9 = (f32[1,1536,128]{2,1,0:T(8,128)}, f32[1,1536,128]{2,1,0:T(8,128)}, u32[]{:S(2)}, u32[]{:S(2)}) collective-permute-start(f32[1,1536,128]{2,1,0:T(8,128)} %shard_map.83.own_ref.rest_4_), channel_id=1, source_target_pairs={{0,8},{8,0},{16,24},{24,16},{1,9},{9,1},{17,25},{25,17},{2,10},{10... | collective-permute-start | bytes 2359304 | tf_op jit(solution)/shard_map/ppermute | solution.py:393
  318.0 4.7 %collective-permute-start.11 = (f32[1,1536,128]{2,1,0:T(8,128)}, f32[1,1536,128]{2,1,0:T(8,128)}, u32[]{:S(2)}, u32[]{:S(2)}) collective-permute-start(f32[1,1536,128]{2,1,0:T(8,128)} %collective-permute-done.10.rest_1_.rest_6_), channel_id=1, source_target_pairs={{0,8},{8,0},{16,24},{24,16},{1,9},{9,1},{17,25},{25,17},{2,10},{10... | collective-permute-start | bytes 2359304 | tf_op jit(solution)/shard_map/ppermute | solution.py:393
  359.3 6.5 %collective-permute-start.16 = (f32[128,512]{1,0:T(8,128)S(1)}, f32[128,512]{1,0:T(8,128)S(1)}, u32[]{:S(2)}, u32[]{:S(2)}) collective-permute-start(f32[128,512]{1,0:T(8,128)S(1)} %bitcast.40), channel_id=1, source_target_pairs={{0,16},{8,24},{16,0},{24,8},{1,17},{9,25},{17,1},{25,9},{2,18},{10... | collective-permute-start | bytes 786440 | tf_op jit(solution)/shard_map/ppermute | solution.py:393
  361.0 4.7 %collective-permute-start.15 = (f32[128,512]{1,0:T(8,128)S(1)}, f32[128,512]{1,0:T(8,128)S(1)}, u32[]{:S(2)}, u32[]{:S(2)}) collective-permute-start(f32[128,512]{1,0:T(8,128)S(1)} %bitcast.41), channel_id=1, source_target_pairs={{0,8},{8,0},{16,24},{24,16},{1,9},{9,1},{17,25},{25,17},{2,10},{10... | collective-permute-start | bytes 786440 | tf_op jit(solution)/shard_map/ppermute | solution.py:393
  365.7 1.5 collective-permute-start.17
  (12 other events, 215.1 us)
Sparse Core Ops, SparseCore 0:
  172.7 59.0 all-gather.2

commit v5 on v4

--- a/solution.py
+++ b/solution.py
@@ -20,7 +20,10 @@
 side_weights = (8.0 / 5.0, -1.0 / 5.0, 8.0 / 315.0, -1.0 / 560.0)
 HIGHEST = lax.Precision.HIGHEST
 WHOLE = pl.BlockSpec(memory_space=pltpu.VMEM)
-PARAMS = pltpu.CompilerParams(vmem_limit_bytes=60 * 1024 * 1024)
+
+
+def params(mebibytes):
+    return pltpu.CompilerParams(vmem_limit_bytes=mebibytes * 1024 * 1024)
 
 
 def cost(flops, bytes_accessed):
@@ -95,7 +98,7 @@
         ],
         out_specs=pl.BlockSpec((count, None, rows + extra, LANES), lambda p: (0, p, 0, 0)),
         out_shape=jax.ShapeDtypeStruct((count, planes, rows + extra, LANES), jnp.float32),
-        compiler_params=PARAMS,
+        compiler_params=params(12),
         cost_estimate=cost(0, 8 * value.size),
     )(levels, value)
 
@@ -139,7 +142,7 @@
         ],
         out_specs=pl.BlockSpec((planes, cells, LANES), lambda i: (0, 0, 0)),
         out_shape=jax.ShapeDtypeStruct((planes, cells, LANES), jnp.float32),
-        compiler_params=PARAMS,
+        compiler_params=params(24),
         cost_estimate=cost(0, 24 * arrived.size),
     )(arrived, high, low, weights)
 
@@ -252,7 +255,7 @@
         out_specs=[WHOLE] * len(chunks),
         out_shape=[jax.ShapeDtypeStruct((count, size, rows, LANES), jnp.float32) for _, size in chunks],
         scratch_shapes=[flat, padded, padded, flat, flat],
-        compiler_params=PARAMS,
+        compiler_params=params(56),
         cost_estimate=cost(100 * arrived.size, 12 * arrived.size),
     )(arrived)
 
@@ -318,7 +321,7 @@
             pltpu.VMEM((SPAN, cells, LANES), jnp.float32),
             pltpu.VMEM((planes + 2 * HALO, side_y, side_z + 2 * PAD, LANES), jnp.float32),
         ],
-        compiler_params=PARAMS,
+        compiler_params=params(56),
         cost_estimate=cost(200 * orbitals.size, 24 * orbitals.size),
     )(*raw, offset, potential, orbitals)
 
@@ -379,7 +382,7 @@
         in_specs=[pl.BlockSpec(memory_space=pltpu.SMEM), WHOLE, WHOLE],
         out_specs=WHOLE,
         out_shape=jax.ShapeDtypeStruct((2 * LANES, LANES), jnp.float32),
-        compiler_params=PARAMS,
+        compiler_params=params(24),
         cost_estimate=cost(0, 8 * parts.size),
     )(lax.axis_index("dom").astype(jnp.int32).reshape(1), parts, coupling)
 
@@ -402,21 +405,23 @@
 
     for plane in range(own_ref.shape[0]):
         left = halves(own_ref[plane].T)
-        for index, panel in enumerate(panels):
+        both = jnp.concatenate([side_by_side(panel[plane]) for panel in panels], axis=1)
+        value = dot_halves(left, both)
+        for index in range(len(panels)):
             at = pl.ds(index * LANES, LANES)
-            out_ref[:, at] = out_ref[:, at] + folded(dot_halves(left, side_by_side(panel[plane])))
+            out_ref[:, at] = out_ref[:, at] + folded(value[:, 2 * index * LANES : 2 * (index + 1) * LANES])
 
 
 def gram_rows(panels):
     planes, cells, _ = panels[0].shape
-    tile = cells // 4
+    tile = cells // 2
     return pl.pallas_call(
         gram_kernel,
         grid=(cells // tile,),
         in_specs=[pl.BlockSpec((planes, tile, LANES), lambda i: (0, i, 0))] * len(panels),
         out_specs=pl.BlockSpec((LANES, len(panels) * LANES), lambda i: (0, 0)),
         out_shape=jax.ShapeDtypeStruct((LANES, len(panels) * LANES), jnp.float32),
-        compiler_params=PARAMS,
+        compiler_params=params(16),
         cost_estimate=cost(8 * panels[0].size * LANES * len(panels), 4 * panels[0].size * len(panels)),
     )(*panels)
 
@@ -443,7 +448,7 @@
         in_specs=[pl.BlockSpec(inverse_rows.shape, lambda i: (0, 0)), *specs],
         out_specs=pl.BlockSpec((planes, tile, LANES), lambda i: (0, i, 0)),
         out_shape=jax.ShapeDtypeStruct((planes, cells, LANES), jnp.float32),
-        compiler_params=PARAMS,
+        compiler_params=params(24),
     )(inverse_rows, *[panel for group in panels for panel in group])
 
 
@@ -456,14 +461,17 @@
 
 def eliminate(work, result):
     sublane = lax.broadcasted_iota(jnp.int32, (GROUP, LANES), 0)
-    for top in range(0, LANES, GROUP):
+
+    def splat(row, column):
+        return jnp.broadcast_to(row[:, column : column + 1], (GROUP, LANES))
+
+    def load(top):
         left = [jnp.broadcast_to(work[pl.ds(top + i, 1), :LANES], (GROUP, LANES)) for i in range(GROUP)]
         right = [jnp.broadcast_to(work[pl.ds(top + i, 1), LANES:], (GROUP, LANES)) for i in range(GROUP)]
-        entry = {
-            (i, j): jnp.broadcast_to(left[i][:, top + j : top + j + 1], (GROUP, LANES))
-            for i in range(GROUP)
-            for j in range(i, GROUP)
-        }
+        return left, right
+
+    def factored(top, left, right):
+        entry = {(i, j): splat(left[i], top + j) for i in range(GROUP) for j in range(i, GROUP)}
         for i in range(GROUP):
             scale = lax.rsqrt(entry[i, i])
             left[i] = left[i] * scale
@@ -474,12 +482,28 @@
                     entry[m, j] = entry[m, j] - factor[m] * factor[j]
                 left[m] = left[m] - factor[m] * left[i]
                 right[m] = right[m] - factor[m] * right[i]
-        upper, lower = left[0], right[0]
+
+    def gathered(rows):
+        value = rows[0]
         for i in range(1, GROUP):
-            upper = jnp.where(sublane == i, left[i], upper)
-            lower = jnp.where(sublane == i, right[i], lower)
-        result[pl.ds(top, GROUP), :] = lower
-        below = top + GROUP
+            value = jnp.where(sublane == i, rows[i], value)
+        return value
+
+    for top in range(0, LANES, 2 * GROUP):
+        left, right = load(top)
+        factored(top, left, right)
+        middle = top + GROUP
+        next_left, next_right = load(middle)
+        for m in range(GROUP):
+            for i in range(GROUP):
+                factor = splat(left[i], middle + m)
+                next_left[m] = next_left[m] - factor * left[i]
+                next_right[m] = next_right[m] - factor * right[i]
+        factored(middle, next_left, next_right)
+        upper = jnp.concatenate([gathered(left), gathered(next_left)], axis=0)
+        lower = jnp.concatenate([gathered(right), gathered(next_right)], axis=0)
+        result[pl.ds(top, 2 * GROUP), :] = lower
+        below = middle + GROUP
         if below < LANES:
             a, b, c = thirds(upper)
             x, y, z = thirds(lower)
@@ -535,11 +559,10 @@
 
 def cholesky_inverse(band, rows):
     size = rows[0].shape[1]
-    whole = pl.BlockSpec(memory_space=pltpu.VMEM)
     return pl.pallas_call(
         cholesky_kernel,
-        in_specs=[pl.BlockSpec(memory_space=pltpu.SMEM)] + [whole] * len(rows),
-        out_specs=[whole] * 2,
+        in_specs=[pl.BlockSpec(memory_space=pltpu.SMEM)] + [WHOLE] * len(rows),
+        out_specs=[WHOLE] * 2,
         out_shape=[
             jax.ShapeDtypeStruct((size, size), jnp.float32),
             jax.ShapeDtypeStruct((LANES, size), jnp.float32),
@@ -551,7 +574,7 @@
             pltpu.VMEM((LANES, LANES), jnp.float32),
             pltpu.VMEM((LANES, 2 * size), jnp.float32),
         ],
-        compiler_params=PARAMS,
+        compiler_params=params(14),
     )(band.astype(jnp.int32).reshape(1), *rows)
 
 
@@ -564,9 +587,11 @@
     return mine.reshape(share * MAXPROJ, -1)
 
 
-def near_projectors(mine, planes):
-    near = [mine if step == BEFORE else shifted(mine, "dom", BEFORE - step) for step in range(NEAR)]
-    near = jnp.stack(near)
+def near_shares(mine):
+    return jnp.stack([mine if step == BEFORE else shifted(mine, "dom", BEFORE - step) for step in range(NEAR)])
+
+
+def near_projectors(near, planes):
     across = crossed(near, 2)
     raw = [near, crossed(near, 1), across, crossed(across, 1)]
     moved = (planes * (jnp.arange(NEAR, dtype=jnp.float32) - BEFORE))[:, None]
@@ -588,9 +613,11 @@
 
     mine = packed_projectors(projectors, atom_plane, planes)
     mine, levels = lax.optimization_barrier((mine, potential.reshape(planes, cells // LANES, LANES)))
-    raw, first = near_projectors(mine, planes)
+    near = near_shares(mine)
     levels = jnp.pad(levels, ((0, 0), (0, -levels.shape[1] % GROUP), (0, 0)))
     packed = swap_in(levels, orbitals.reshape(planes, blocks, rows, local_orbs))
+    packed, near = lax.optimization_barrier((packed, near))
+    raw, first = near_projectors(near, planes)
     arrived = lax.all_to_all(packed, "dom", 0, 0, tiled=True)
 
     own_levels = jnp.broadcast_to(potential.reshape(planes, cells, 1), (planes, cells, LANES))
@@ -616,6 +643,8 @@
     for (begin, size), packed in zip(chunks, seconds):
         own = swap_out(lax.all_to_all(packed, "dom", 0, 0, tiled=True), high, low, weights, begin)
         across = crossed(own, 2)
+        if panels:
+            across, part = lax.optimization_barrier((across, part))
         panels.append([own, crossed(own, 1), across, crossed(across, 1)])
         part = part + gram_rows(panels[-1])
 

time: 415 us -> 356 us (0.86)
  waiting for transfers between devices: 187 us -> 160 us
  Pallas kernels: 116 us -> 96.6 us
  starting transfers between devices: 48.3 us -> 31.8 us
    ppermute x3, waiting for transfers between devices: 60.7 us -> 3.34 us  [shifted(): lax.ppermute(value, axis, [(source, (source + step) % count) for source i...]
    all_to_all x1, waiting for transfers between devices: 0.01 us -> 45.8 us  [shards(): arrived = lax.all_to_all(packed, 'dom', 0, 0, tiled=True)]
    all_gather x1, waiting for transfers between devices: 34.2 us -> 0.02 us  [shards(): lax.all_gather(jnp.concatenate([parts.reshape(3 * LANES, LANES), matrix],...]
    ppermute x15, waiting for transfers between devices: 56.4 us -> 78.9 us  [crossed(): lax.ppermute(value, 'band', [(source, source ^ bit) for source in range(l...]
    all_to_all x3, starting transfers between devices: 29.9 us -> 14 us  [shards(): lax.all_to_all(packed, 'dom', 0, 0, tiled=True)]
    pallas_call x3, Pallas kernels: 15.4 us -> 8.05 us  [gram_rows(): pl.pallas_call(gram_kernel, grid=(cells // tile,), in_specs=[pl.BlockSpec...]
    unnamed x29 -> x25, local copies, waits for them, and re-layouts: 2.72 us -> 9.67 us
    pallas_call x1, Pallas kernels: 30.4 us -> 25.5 us  [cholesky_inverse(): pl.pallas_call(cholesky_kernel, in_specs=[pl.BlockSpec(memory_space=pltpu...]
  transfers between devices with their start and end apart: 23 -> 23, of which waited for: 12 -> 10; matrix products, arithmetic and copies ran while one was open for 4% -> 4% of each run, Pallas kernels for 16% -> 15%
where the time goes in v5:
time: 356 us; the launch traced here: 355 us
  waiting for transfers between devices  160 us (45%)
  Pallas kernels  96.6 us (27%)
  starting transfers between devices  31.8 us (9%)
  blocking collectives  26.8 us (8%)
  local copies, waits for them, and re-layouts  20.9 us (6%)
  between operations  14.3 us (4%)
  other arithmetic  4.62 us (1%)
    ppermute x15, waiting for transfers between devices, crossed(): lax.ppermute(value, 'band', [(source, source ^ bit) for source in range(l...  78.9 us
    all_to_all x1, waiting for transfers between devices, shards(): arrived = lax.all_to_all(packed, 'dom', 0, 0, tiled=True)  45.8 us
    all_to_all x3, waiting for transfers between devices, shards(): lax.all_to_all(packed, 'dom', 0, 0, tiled=True)  32.1 us
    pallas_call x1, Pallas kernels, cholesky_inverse(): pl.pallas_call(cholesky_kernel, in_specs=[pl.BlockSpec(memory_space=pltpu...  25.5 us
    pallas_call x1, Pallas kernels, filter_orbitals(): pl.pallas_call(functools.partial(filter_kernel, planes, side_y, side_z, w...  21.2 us
    all_to_all x1, blocking collectives, shards(): lax.all_to_all(part.reshape(blocks, width, norb), 'dom', 0, 0, tiled=True)  14.8 us
    pallas_call x3, Pallas kernels, swap_out(): pl.pallas_call(functools.partial(swap_out_kernel, count, rows), grid=(1,)...  14.5 us
    all_to_all x3, starting transfers between devices, shards(): lax.all_to_all(packed, 'dom', 0, 0, tiled=True)  14 us
  transfers between devices with their start and end apart: 23, of which 10 were waited for; matrix products, arithmetic and copies ran while one was open for 4% of the time, Pallas kernels for 15%

profile of v5, /device:TPU:0, one launch (start us, length us, event | category | flops | bytes accessed | tf_op | source)
XLA Modules:
  0.0 355.1 jit_solution(2026725763029094499)
XLA Ops:
  9.8 6.1 %collective-permute-start.2 = (f32[8,4736]{1,0:T(8,128)S(1)}, f32[8,4736]{1,0:T(8,128)S(1)}, u32[]{:S(2)}, u32[]{:S(2)}) collective-permute-start(f32[8,4736]{1,0:T(8,128)S(1)} %reshape.267), channel_id=1, source_target_pairs={{0,7},{1,0},{2,1},{3,2},{4,3},{5,4},{6,5},{7,6},{8,15},{9,8},{10,9... | collective-permute-start | bytes 454664 | tf_op jit(solution)/shard_map/ppermute | solution.py:392
  17.8 4.3 %shard_map.77 = f32[8,4,208,128]{3,2,1,0:T(8,128)} custom-call(f32[4,16,128]{2,1,0:T(8,128)S(1)} %pad.8.levels_ref, f32[4,8,192,128]{3,2,1,0:T(8,128)S(1)} %bitcast.35), custom_call_target="tpu_custom_call" | custom-call | bytes 6291456 | tf_op jit(solution)/shard_map/pallas_call | solution.py:92
  22.1 3.3 collective-permute-done.1
  26.3 3.8 %all-to-all-start = ((f32[8,4,208,128]{3,2,1,0:T(8,128)}), f32[8,4,208,128]{3,2,1,0:T(8,128)S(1)}, u32[]{:S(2)}, u32[]{:S(2)}) async-start(f32[8,4,208,128]{3,2,1,0:T(8,128)} %shard_map.77), calls=%async_computation | async-start | bytes 6815744 | tf_op jit(solution)/shard_map/all_to_all | solution.py:621
  33.4 11.2 %collective-permute-done.4.refs_2_ = f32[4,8,4736]{2,1,0:T(8,128)} collective-permute-done((f32[4,8,4736]{2,1,0:T(8,128)}, f32[4,8,4736]{2,1,0:T(8,128)}, u32[]{:S(2)}, u32[]{:S(2)}) %collective-permute-start.4) | collective-permute-done | bytes 606240 | tf_op jit(solution)/shard_map/ppermute | solution.py:396
  51.2 13.5 %shard_map.79 = (bf16[4,1536,256]{2,1,0:T(8,128)(2,1)}, bf16[4,1536,256]{2,1,0:T(8,128)(2,1)}, f32[3,128,128]{2,1,0:T(8,128)}) custom-call(f32[4,8,4736]{2,1,0:T(8,128)} %pad_maximum_fusion.refs_0_, f32[4,8,4736]{2,1,0:T(8,128)} %collective-permute-done.3.refs_1_, f32[4,8,4736]{2,1,0:T(8,128)} %collective-permute-done.4.refs_2_, ...), custom_call_target="tpu_custom_call" | custom-call | flops 157286400 | bytes 18874368 | tf_op jit(solution)/shard_map/pallas_call | solution.py:315
  66.4 45.8 %all-to-all-done.arrived_ref = f32[8,4,208,128]{3,2,1,0:T(8,128)S(1)} async-done(((f32[8,4,208,128]{3,2,1,0:T(8,128)}), f32[8,4,208,128]{3,2,1,0:T(8,128)S(1)}, u32[]{:S(2)}, u32[]{:S(2)}) %all-to-all-start) | async-done | bytes 3407904 | tf_op jit(solution)/shard_map/all_to_all | solution.py:621
  114.0 21.2 %shard_map.78 = (f32[8,2,192,128]{3,2,1,0:T(8,128)}, f32[8,1,192,128]{3,2,1,0:T(8,128)}, f32[8,1,192,128]{3,2,1,0:T(8,128)}) custom-call(f32[8,4,208,128]{3,2,1,0:T(8,128)} %copy-done.7), custom_call_target="tpu_custom_call" | custom-call | flops 85196800 | bytes 10223616 | tf_op jit(solution)/shard_map/pallas_call | solution.py:252
  135.2 4.5 %all-to-all-start.3 = ((f32[8,2,192,128]{3,2,1,0:T(8,128)}), f32[8,2,192,128]{3,2,1,0:T(8,128)}, u32[]{:S(2)}, u32[]{:S(2)}) async-start(f32[8,2,192,128]{3,2,1,0:T(8,128)} %get-tuple-element.27), calls=%async_computation.3 | async-start | bytes 3145728 | tf_op jit(solution)/shard_map/all_to_all | solution.py:644
  144.0 32.1 %all-to-all-done.3.arrived_ref = f32[8,2,192,128]{3,2,1,0:T(8,128)} async-done(((f32[8,2,192,128]{3,2,1,0:T(8,128)}), f32[8,2,192,128]{3,2,1,0:T(8,128)}, u32[]{:S(2)}, u32[]{:S(2)}) %all-to-all-start.3) | async-done | bytes 1572896 | tf_op jit(solution)/shard_map/all_to_all | solution.py:644
  178.0 7.0 %shard_map.83.own_ref.rest_0_ = f32[2,1536,128]{2,1,0:T(8,128)} custom-call(f32[8,2,192,128]{3,2,1,0:T(8,128)} %all-to-all-done.3.arrived_ref, bf16[4,1536,256]{2,1,0:T(8,128)(2,1)S(1)} %copy-done, bf16[4,1536,256]{2,1,0:T(8,128)(2,1)S(1)} %copy-done.1, f32[256,128]{1,0:T(8,128)S(1)} %shard_map.80.weights_ref), custom_call_target="tpu_custom_call" | custom-call | bytes 9437184 | tf_op jit(solution)/shard_map/pallas_call | solution.py:134
  186.5 4.2 %all-to-all-start.2 = ((f32[8,1,192,128]{3,2,1,0:T(8,128)}), f32[8,1,192,128]{3,2,1,0:T(8,128)}, u32[]{:S(2)}, u32[]{:S(2)}) async-start(f32[8,1,192,128]{3,2,1,0:T(8,128)} %get-tuple-element.26), calls=%async_computation.2 | async-start | bytes 1572864 | tf_op jit(solution)/shard_map/all_to_all | solution.py:644
  190.8 29.0 %collective-permute-done.9.rest_1_.rest_2_ = f32[2,1536,128]{2,1,0:T(8,128)} collective-permute-done((f32[2,1536,128]{2,1,0:T(8,128)}, f32[2,1536,128]{2,1,0:T(8,128)}, u32[]{:S(2)}, u32[]{:S(2)}) %collective-permute-start.9) | collective-permute-done | bytes 1572896 | tf_op jit(solution)/shard_map/ppermute | solution.py:396
  219.8 5.3 %all-to-all-start.1 = ((f32[8,1,192,128]{3,2,1,0:T(8,128)}), f32[8,1,192,128]{3,2,1,0:T(8,128)}, u32[]{:S(2)}, u32[]{:S(2)}) async-start(f32[8,1,192,128]{3,2,1,0:T(8,128)} %get-tuple-element.21), calls=%async_computation.1 | async-start | bytes 1572864 | tf_op jit(solution)/shard_map/all_to_all | solution.py:644
  227.0 4.2 %shard_map.82.own_ref.rest_4_ = f32[1,1536,128]{2,1,0:T(8,128)} custom-call(f32[8,1,192,128]{3,2,1,0:T(8,128)} %all-to-all-done.2.arrived_ref, bf16[4,1536,256]{2,1,0:T(8,128)(2,1)S(1)} %copy-done, bf16[4,1536,256]{2,1,0:T(8,128)(2,1)S(1)} %copy-done.2, f32[256,128]{1,0:T(8,128)S(1)} %shard_map.80.weights_ref), custom_call_target="tpu_custom_call" | custom-call | bytes 4718592 | tf_op jit(solution)/shard_map/pallas_call | solution.py:134
  232.7 4.0 %shard_map.84 = f32[128,512]{1,0:T(8,128)S(1)} custom-call(f32[2,1536,128]{2,1,0:T(8,128)} %shard_map.83.own_ref.rest_0_, f32[2,1536,128]{2,1,0:T(8,128)} %collective-permute-done.8.rest_0_.rest_1_, f32[2,1536,128]{2,1,0:T(8,128)} %collective-permute-done.9.rest_1_.rest_2_, f32[2,1536,128]{2,1,0:T(8,128)} %collective-permute-done.10.rest_2_.rest_3_), custom_call_target="tpu_custom_call" | custom-call | flops 1610612736 | bytes 6291456 | tf_op jit(solution)/shard_map/pallas_call | solution.py:418
  236.8 14.5 %collective-permute-done.7.rest_1_.rest_6_ = f32[1,1536,128]{2,1,0:T(8,128)} collective-permute-done((f32[1,1536,128]{2,1,0:T(8,128)}, f32[1,1536,128]{2,1,0:T(8,128)}, u32[]{:S(2)}, u32[]{:S(2)}) %collective-permute-start.7) | collective-permute-done | bytes 786464 | tf_op jit(solution)/shard_map/ppermute | solution.py:396
  253.1 3.3 shard_map.81.own_ref.rest_8_
  261.0 15.5 %collective-permute-done.6.rest_1_.rest_10_ = f32[1,1536,128]{2,1,0:T(8,128)S(1)} collective-permute-done((f32[1,1536,128]{2,1,0:T(8,128)S(1)}, f32[1,1536,128]{2,1,0:T(8,128)S(1)}, u32[]{:S(2)}, u32[]{:S(2)}) %collective-permute-start.6) | collective-permute-done | bytes 786464 | tf_op jit(solution)/shard_map/ppermute | solution.py:396
  280.1 14.8 %all_to_all.30 = f32[8,16,512]{2,1,0:T(8,128)S(1)} all-to-all(f32[8,16,512]{2,1,0:T(8,128)S(1)} %bitcast.43), channel_id=1, replica_groups=mesh['band'=4,'dom'=8] {'dom'}, dimensions={0} | all-to-all | bytes 524288 | tf_op jit(solution)/shard_map/all_to_all | solution.py:651
  295.0 12.0 %all_to_all.31 = f32[8,16,512]{2,1,0:T(8,128)S(1)} all-to-all(f32[8,16,512]{2,1,0:T(8,128)S(1)} %broadcast_in_dim.58), channel_id=1, replica_groups=mesh['band'=4,'dom'=8] {'dom'}, dimensions={0} | all-to-all | bytes 524288 | tf_op jit(solution)/shard_map/all_to_all | solution.py:653
  308.5 4.9 %collective-permute-done.16.refs_2_ = f32[128,512]{1,0:T(8,128)S(1)} collective-permute-done((f32[128,512]{1,0:T(8,128)S(1)}, f32[128,512]{1,0:T(8,128)S(1)}, u32[]{:S(2)}, u32[]{:S(2)}) %collective-permute-start.16) | collective-permute-done | bytes 262176 | tf_op jit(solution)/shard_map/ppermute | solution.py:396
  314.9 25.5 %shard_map.87 = (f32[512,512]{1,0:T(8,128)}, f32[128,512]{1,0:T(8,128)S(1)}) custom-call(s32[1]{0:T(128)} %bitcast.band_ref, f32[128,512]{1,0:T(8,128)S(1)} %bitcast.39, f32[128,512]{1,0:T(8,128)S(1)} %collective-permute-done.15.refs_1_, f32[128,512]{1,0:T(8,128)S(1)} %collective-permute-done.16.refs_2_, f32[128,512]{1,0:T(8,128)S(1)} %collective-permute-done.17.refs_3_), custom_call_target="tpu_custom_call" | custom-call | tf_op jit(solution)/shard_map/pallas_call | solution.py:562
  340.4 7.8 %shard_map.88 = f32[4,1536,128]{2,1,0:T(8,128)} custom-call(f32[128,512]{1,0:T(8,128)S(1)} %get-tuple-element.32.inverse_ref, f32[2,1536,128]{2,1,0:T(8,128)} %shard_map.83.own_ref.rest_0_, f32[2,1536,128]{2,1,0:T(8,128)} %collective-permute-done.8.rest_0_.rest_1_, f32[2,1536,128]{2,1,0:T(8,128)} %collective-permute-done.9.rest_1_.rest_2_, ...), custom_call_target="tpu_custom_call" | custom-call | tf_op jit(solution)/shard_map/pallas_call | solution.py:445
  (104 shorter events, 43.0 us)
Async XLA Ops:
  9.8 12.3 %collective-permute-start.2 = (f32[8,4736]{1,0:T(8,128)S(1)}, f32[8,4736]{1,0:T(8,128)S(1)}, u32[]{:S(2)}, u32[]{:S(2)}) collective-permute-start(f32[8,4736]{1,0:T(8,128)S(1)} %reshape.267), channel_id=1, source_target_pairs={{0,7},{1,0},{2,1},{3,2},{4,3},{5,4},{6,5},{7,6},{8,15},{9,8},{10,9... | collective-permute-start | bytes 454664 | tf_op jit(solution)/shard_map/ppermute | solution.py:392
  15.9 9.6 %collective-permute-start.1 = (f32[8,4736]{1,0:T(8,128)S(1)}, f32[8,4736]{1,0:T(8,128)S(1)}, u32[]{:S(2)}, u32[]{:S(2)}) collective-permute-start(f32[8,4736]{1,0:T(8,128)S(1)} %reshape.267), channel_id=1, source_target_pairs={{0,1},{1,2},{2,3},{3,4},{4,5},{5,6},{6,7},{7,0},{8,9},{9,10},{10,1... | collective-permute-start | bytes 454664 | tf_op jit(solution)/shard_map/ppermute | solution.py:392
  15.9 9.6 %collective-permute-start = (f32[8,4736]{1,0:T(8,128)S(1)}, f32[8,4736]{1,0:T(8,128)S(1)}, u32[]{:S(2)}, u32[]{:S(2)}) collective-permute-start(f32[8,4736]{1,0:T(8,128)S(1)} %reshape.267), channel_id=1, source_target_pairs={{0,2},{1,3},{2,4},{3,5},{4,6},{5,7},{6,0},{7,1},{8,10},{9,11},{10,... | collective-permute-start | bytes 454664 | tf_op jit(solution)/shard_map/ppermute | solution.py:392
  26.3 85.8 %all-to-all-start = ((f32[8,4,208,128]{3,2,1,0:T(8,128)}), f32[8,4,208,128]{3,2,1,0:T(8,128)S(1)}, u32[]{:S(2)}, u32[]{:S(2)}) async-start(f32[8,4,208,128]{3,2,1,0:T(8,128)} %shard_map.77), calls=%async_computation | async-start | bytes 6815744 | tf_op jit(solution)/shard_map/all_to_all | solution.py:621
  30.1 109.5 %all-gather.3.cloned.1.call-start = ((), (), s32[]{:S(2)}) async-start(), calls=%async_computation.6 | async-start | bytes 1916928 | tf_op jit(solution)/shard_map/all_gather | solution.py:635
  30.4 14.2 %collective-permute-start.4 = (f32[4,8,4736]{2,1,0:T(8,128)}, f32[4,8,4736]{2,1,0:T(8,128)}, u32[]{:S(2)}, u32[]{:S(2)}) collective-permute-start(f32[4,8,4736]{2,1,0:T(8,128)} %pad_maximum_fusion.refs_0_), channel_id=1, source_target_pairs={{0,16},{8,24},{16,0},{24,8},{1,17},{9,25},{17,1},{25,9},{2,18},{10... | collective-permute-start | bytes 1818632 | tf_op jit(solution)/shard_map/ppermute | solution.py:396
  33.2 13.3 %collective-permute-start.3 = (f32[4,8,4736]{2,1,0:T(8,128)}, f32[4,8,4736]{2,1,0:T(8,128)}, u32[]{:S(2)}, u32[]{:S(2)}) collective-permute-start(f32[4,8,4736]{2,1,0:T(8,128)} %pad_maximum_fusion.refs_0_), channel_id=1, source_target_pairs={{0,8},{8,0},{16,24},{24,16},{1,9},{9,1},{17,25},{25,17},{2,10},{10... | collective-permute-start | bytes 1818632 | tf_op jit(solution)/shard_map/ppermute | solution.py:396
  44.6 2.8 collective-permute-start.5
  135.2 40.9 %all-to-all-start.3 = ((f32[8,2,192,128]{3,2,1,0:T(8,128)}), f32[8,2,192,128]{3,2,1,0:T(8,128)}, u32[]{:S(2)}, u32[]{:S(2)}) async-start(f32[8,2,192,128]{3,2,1,0:T(8,128)} %get-tuple-element.27), calls=%async_computation.3 | async-start | bytes 3145728 | tf_op jit(solution)/shard_map/all_to_all | solution.py:644
  185.0 34.8 %collective-permute-start.9 = (f32[2,1536,128]{2,1,0:T(8,128)}, f32[2,1536,128]{2,1,0:T(8,128)}, u32[]{:S(2)}, u32[]{:S(2)}) collective-permute-start(f32[2,1536,128]{2,1,0:T(8,128)} %shard_map.83.own_ref.rest_0_), channel_id=1, source_target_pairs={{0,16},{8,24},{16,0},{24,8},{1,17},{9,25},{17,1},{25,9},{2,18},{10... | collective-permute-start | bytes 4718600 | tf_op jit(solution)/shard_map/ppermute | solution.py:396
  186.5 33.3 %all-to-all-start.2 = ((f32[8,1,192,128]{3,2,1,0:T(8,128)}), f32[8,1,192,128]{3,2,1,0:T(8,128)}, u32[]{:S(2)}, u32[]{:S(2)}) async-start(f32[8,1,192,128]{3,2,1,0:T(8,128)} %get-tuple-element.26), calls=%async_computation.2 | async-start | bytes 1572864 | tf_op jit(solution)/shard_map/all_to_all | solution.py:644
  190.7 42.0 %collective-permute-start.8 = (f32[2,1536,128]{2,1,0:T(8,128)}, f32[2,1536,128]{2,1,0:T(8,128)}, u32[]{:S(2)}, u32[]{:S(2)}) collective-permute-start(f32[2,1536,128]{2,1,0:T(8,128)} %shard_map.83.own_ref.rest_0_), channel_id=1, source_target_pairs={{0,8},{8,0},{16,24},{24,16},{1,9},{9,1},{17,25},{25,17},{2,10},{10... | collective-permute-start | bytes 4718600 | tf_op jit(solution)/shard_map/ppermute | solution.py:396
  219.8 12.9 %collective-permute-start.10 = (f32[2,1536,128]{2,1,0:T(8,128)}, f32[2,1536,128]{2,1,0:T(8,128)}, u32[]{:S(2)}, u32[]{:S(2)}) collective-permute-start(f32[2,1536,128]{2,1,0:T(8,128)} %collective-permute-done.9.rest_1_.rest_2_), channel_id=1, source_target_pairs={{0,8},{8,0},{16,24},{24,16},{1,9},{9,1},{17,25},{25,17},{2,10},{10... | collective-permute-start | bytes 4718600 | tf_op jit(solution)/shard_map/ppermute | solution.py:396
  219.8 31.5 %all-to-all-start.1 = ((f32[8,1,192,128]{3,2,1,0:T(8,128)}), f32[8,1,192,128]{3,2,1,0:T(8,128)}, u32[]{:S(2)}, u32[]{:S(2)}) async-start(f32[8,1,192,128]{3,2,1,0:T(8,128)} %get-tuple-element.21), calls=%async_computation.1 | async-start | bytes 1572864 | tf_op jit(solution)/shard_map/all_to_all | solution.py:644
  231.2 20.0 %collective-permute-start.7 = (f32[1,1536,128]{2,1,0:T(8,128)}, f32[1,1536,128]{2,1,0:T(8,128)}, u32[]{:S(2)}, u32[]{:S(2)}) collective-permute-start(f32[1,1536,128]{2,1,0:T(8,128)} %shard_map.82.own_ref.rest_4_), channel_id=1, source_target_pairs={{0,16},{8,24},{16,0},{24,8},{1,17},{9,25},{17,1},{25,9},{2,18},{10... | collective-permute-start | bytes 2359304 | tf_op jit(solution)/shard_map/ppermute | solution.py:396
  232.7 25.5 %collective-permute-start.11 = (f32[1,1536,128]{2,1,0:T(8,128)}, f32[1,1536,128]{2,1,0:T(8,128)}, u32[]{:S(2)}, u32[]{:S(2)}) collective-permute-start(f32[1,1536,128]{2,1,0:T(8,128)} %shard_map.82.own_ref.rest_4_), channel_id=1, source_target_pairs={{0,8},{8,0},{16,24},{24,16},{1,9},{9,1},{17,25},{25,17},{2,10},{10... | collective-permute-start | bytes 2359304 | tf_op jit(solution)/shard_map/ppermute | solution.py:396
  251.2 7.0 %collective-permute-start.12 = (f32[1,1536,128]{2,1,0:T(8,128)}, f32[1,1536,128]{2,1,0:T(8,128)}, u32[]{:S(2)}, u32[]{:S(2)}) collective-permute-start(f32[1,1536,128]{2,1,0:T(8,128)} %collective-permute-done.7.rest_1_.rest_6_), channel_id=1, source_target_pairs={{0,8},{8,0},{16,24},{24,16},{1,9},{9,1},{17,25},{25,17},{2,10},{10... | collective-permute-start | bytes 2359304 | tf_op jit(solution)/shard_map/ppermute | solution.py:396
  256.5 20.0 %collective-permute-start.6 = (f32[1,1536,128]{2,1,0:T(8,128)S(1)}, f32[1,1536,128]{2,1,0:T(8,128)S(1)}, u32[]{:S(2)}, u32[]{:S(2)}) collective-permute-start(f32[1,1536,128]{2,1,0:T(8,128)S(1)} %shard_map.81.own_ref.rest_8_), channel_id=1, source_target_pairs={{0,16},{8,24},{16,0},{24,8},{1,17},{9,25},{17,1},{25,9},{2,18},{10... | collective-permute-start | bytes 2359304 | tf_op jit(solution)/shard_map/ppermute | solution.py:396
  258.0 18.5 %collective-permute-start.13 = (f32[1,1536,128]{2,1,0:T(8,128)S(1)}, f32[1,1536,128]{2,1,0:T(8,128)S(1)}, u32[]{:S(2)}, u32[]{:S(2)}) collective-permute-start(f32[1,1536,128]{2,1,0:T(8,128)S(1)} %shard_map.81.own_ref.rest_8_), channel_id=1, source_target_pairs={{0,8},{8,0},{16,24},{24,16},{1,9},{9,1},{17,25},{25,17},{2,10},{10... | collective-permute-start | bytes 2359304 | tf_op jit(solution)/shard_map/ppermute | solution.py:396
  276.5 2.3 collective-permute-start.14
  280.1 60.3 %copy-start.6 = (f32[1,1536,128]{2,1,0:T(8,128)S(1)}, f32[1,1536,128]{2,1,0:T(8,128)}, u32[]{:S(2)}) copy-start(f32[1,1536,128]{2,1,0:T(8,128)} %copy-done.5) | copy-start | bytes 2359300
  307.0 6.4 %collective-permute-start.16 = (f32[128,512]{1,0:T(8,128)S(1)}, f32[128,512]{1,0:T(8,128)S(1)}, u32[]{:S(2)}, u32[]{:S(2)}) collective-permute-start(f32[128,512]{1,0:T(8,128)S(1)} %bitcast.37), channel_id=1, source_target_pairs={{0,16},{8,24},{16,0},{24,8},{1,17},{9,25},{17,1},{25,9},{2,18},{10... | collective-permute-start | bytes 786440 | tf_op jit(solution)/shard_map/ppermute | solution.py:396
  308.5 4.9 %collective-permute-start.15 = (f32[128,512]{1,0:T(8,128)S(1)}, f32[128,512]{1,0:T(8,128)S(1)}, u32[]{:S(2)}, u32[]{:S(2)}) collective-permute-start(f32[128,512]{1,0:T(8,128)S(1)} %bitcast.38), channel_id=1, source_target_pairs={{0,8},{8,0},{16,24},{24,16},{1,9},{9,1},{17,25},{25,17},{2,10},{10... | collective-permute-start | bytes 786440 | tf_op jit(solution)/shard_map/ppermute | solution.py:396
  313.4 1.5 collective-permute-start.17
  (10 other events, 83.6 us)
Sparse Core Ops, SparseCore 0:
  66.5 69.5 all-gather.2

commit v6 on v5

--- a/solution.py
+++ b/solution.py
@@ -142,7 +142,7 @@
         ],
         out_specs=pl.BlockSpec((planes, cells, LANES), lambda i: (0, 0, 0)),
         out_shape=jax.ShapeDtypeStruct((planes, cells, LANES), jnp.float32),
-        compiler_params=params(24),
+        compiler_params=params(18),
         cost_estimate=cost(0, 24 * arrived.size),
     )(arrived, high, low, weights)
 
@@ -255,7 +255,7 @@
         out_specs=[WHOLE] * len(chunks),
         out_shape=[jax.ShapeDtypeStruct((count, size, rows, LANES), jnp.float32) for _, size in chunks],
         scratch_shapes=[flat, padded, padded, flat, flat],
-        compiler_params=params(56),
+        compiler_params=params(30),
         cost_estimate=cost(100 * arrived.size, 12 * arrived.size),
     )(arrived)
 
@@ -321,7 +321,7 @@
             pltpu.VMEM((SPAN, cells, LANES), jnp.float32),
             pltpu.VMEM((planes + 2 * HALO, side_y, side_z + 2 * PAD, LANES), jnp.float32),
         ],
-        compiler_params=params(56),
+        compiler_params=params(40),
         cost_estimate=cost(200 * orbitals.size, 24 * orbitals.size),
     )(*raw, offset, potential, orbitals)
 
@@ -382,7 +382,7 @@
         in_specs=[pl.BlockSpec(memory_space=pltpu.SMEM), WHOLE, WHOLE],
         out_specs=WHOLE,
         out_shape=jax.ShapeDtypeStruct((2 * LANES, LANES), jnp.float32),
-        compiler_params=params(24),
+        compiler_params=params(18),
         cost_estimate=cost(0, 8 * parts.size),
     )(lax.axis_index("dom").astype(jnp.int32).reshape(1), parts, coupling)
 
@@ -448,7 +448,7 @@
         in_specs=[pl.BlockSpec(inverse_rows.shape, lambda i: (0, 0)), *specs],
         out_specs=pl.BlockSpec((planes, tile, LANES), lambda i: (0, i, 0)),
         out_shape=jax.ShapeDtypeStruct((planes, cells, LANES), jnp.float32),
-        compiler_params=params(24),
+        compiler_params=params(18),
     )(inverse_rows, *[panel for group in panels for panel in group])
 
 
@@ -639,14 +639,15 @@
 
     seconds = filter_orbitals(arrived, side_y, side_z, width, chunks)
 
-    panels, part = [], 0.0
+    sent = []
     for (begin, size), packed in zip(chunks, seconds):
         own = swap_out(lax.all_to_all(packed, "dom", 0, 0, tiled=True), high, low, weights, begin)
-        across = crossed(own, 2)
-        if panels:
-            across, part = lax.optimization_barrier((across, part))
-        panels.append([own, crossed(own, 1), across, crossed(across, 1)])
-        part = part + gram_rows(panels[-1])
+        sent.append((own, crossed(own, 1), crossed(own, 2)))
+    panels, part = [], sent[-1][0]
+    for own, beside, across in sent:
+        across, part = lax.optimization_barrier((across, part))
+        panels.append([own, beside, across, crossed(across, 1)])
+        part = gram_rows(panels[-1]) + (part if len(panels) > 1 else 0.0)
 
     pieces = lax.all_to_all(part.reshape(blocks, width, norb), "dom", 0, 0, tiled=True)
     piece = jnp.sum(pieces, axis=0) * (1.0 / (planes * cells * blocks))

time: 356 us -> 380 us (1.067)
  waiting for transfers between devices: 160 us -> 191 us
  Pallas kernels: 96.6 us -> 90.6 us
    all_gather x1, waiting for transfers between devices: 0.02 us -> 27.3 us  [shards(): lax.all_gather(jnp.concatenate([parts.reshape(3 * LANES, LANES), matrix],...]
    all_to_all x3, waiting for transfers between devices: 32.1 us -> 42.6 us  [shards(): lax.all_to_all(packed, 'dom', 0, 0, tiled=True)]
    unnamed x25 -> x65, local copies, waits for them, and re-layouts: 9.67 us -> 17.1 us
    all_to_all x1, waiting for transfers between devices: 45.8 us -> 41.5 us  [shards(): arrived = lax.all_to_all(packed, 'dom', 0, 0, tiled=True)]
  transfers between devices with their start and end apart: 23 -> 23, of which waited for: 10 -> 13; matrix products, arithmetic and copies ran while one was open for 4% -> 2% of each run, Pallas kernels for 15% -> 10%
where the time goes in v6:
time: 380 us; the launch traced here: 379 us
  waiting for transfers between devices  191 us (50%)
  Pallas kernels  90.6 us (24%)
  starting transfers between devices  31.6 us (8%)
  blocking collectives  24.6 us (6%)
  local copies, waits for them, and re-layouts  23.5 us (6%)
  between operations  14.5 us (4%)
    ppermute x15, waiting for transfers between devices, crossed(): lax.ppermute(value, 'band', [(source, source ^ bit) for source in range(l...  76.1 us
    all_to_all x3, waiting for transfers between devices, shards(): lax.all_to_all(packed, 'dom', 0, 0, tiled=True)  42.6 us
    all_to_all x1, waiting for transfers between devices, shards(): arrived = lax.all_to_all(packed, 'dom', 0, 0, tiled=True)  41.5 us
    all_gather x1, waiting for transfers between devices, shards(): lax.all_gather(jnp.concatenate([parts.reshape(3 * LANES, LANES), matrix],...  27.3 us
    pallas_call x1, Pallas kernels, cholesky_inverse(): pl.pallas_call(cholesky_kernel, in_specs=[pl.BlockSpec(memory_space=pltpu...  25.5 us
    pallas_call x1, Pallas kernels, filter_orbitals(): pl.pallas_call(functools.partial(filter_kernel, planes, side_y, side_z, w...  20.3 us
    unnamed x65, local copies, waits for them, and re-layouts  17.1 us
    pallas_call x3, Pallas kernels, swap_out(): pl.pallas_call(functools.partial(swap_out_kernel, count, rows), grid=(1,)...  13.6 us
  transfers between devices with their start and end apart: 23, of which 13 were waited for; matrix products, arithmetic and copies ran while one was open for 2% of the time, Pallas kernels for 10%

profile of v6, /device:TPU:0, one launch (start us, length us, event | category | flops | bytes accessed | tf_op | source)
XLA Modules:
  0.0 378.6 jit_solution(14417426316625567762)
XLA Ops:
  9.8 6.1 %collective-permute-start.2 = (f32[8,4736]{1,0:T(8,128)S(1)}, f32[8,4736]{1,0:T(8,128)S(1)}, u32[]{:S(2)}, u32[]{:S(2)}) collective-permute-start(f32[8,4736]{1,0:T(8,128)S(1)} %reshape.267), channel_id=1, source_target_pairs={{0,7},{1,0},{2,1},{3,2},{4,3},{5,4},{6,5},{7,6},{8,15},{9,8},{10,9... | collective-permute-start | bytes 454664 | tf_op jit(solution)/shard_map/ppermute | solution.py:392
  17.8 4.3 %shard_map.77 = f32[8,4,208,128]{3,2,1,0:T(8,128)} custom-call(f32[4,16,128]{2,1,0:T(8,128)S(1)} %pad.8.levels_ref, f32[4,8,192,128]{3,2,1,0:T(8,128)S(1)} %bitcast.35), custom_call_target="tpu_custom_call" | custom-call | bytes 6291456 | tf_op jit(solution)/shard_map/pallas_call | solution.py:92
  22.1 3.4 collective-permute-done.1
  25.6 4.6 %all-to-all-start = ((f32[8,4,208,128]{3,2,1,0:T(8,128)}), f32[8,4,208,128]{3,2,1,0:T(8,128)}, u32[]{:S(2)}, u32[]{:S(2)}) async-start(f32[8,4,208,128]{3,2,1,0:T(8,128)} %shard_map.77), calls=%async_computation | async-start | bytes 6815744 | tf_op jit(solution)/shard_map/all_to_all | solution.py:621
  33.4 10.0 %collective-permute-done.4.refs_2_ = f32[4,8,4736]{2,1,0:T(8,128)S(1)} collective-permute-done((f32[4,8,4736]{2,1,0:T(8,128)S(1)}, f32[4,8,4736]{2,1,0:T(8,128)S(1)}, u32[]{:S(2)}, u32[]{:S(2)}) %collective-permute-start.4) | collective-permute-done | bytes 606240 | tf_op jit(solution)/shard_map/ppermute | solution.py:396
  50.1 11.3 %shard_map.79 = (bf16[4,1536,256]{2,1,0:T(8,128)(2,1)S(1)}, bf16[4,1536,256]{2,1,0:T(8,128)(2,1)S(1)}, f32[3,128,128]{2,1,0:T(8,128)S(1)}) custom-call(f32[4,8,4736]{2,1,0:T(8,128)S(1)} %copy-done.18, f32[4,8,4736]{2,1,0:T(8,128)S(1)} %copy-done.25, f32[4,8,4736]{2,1,0:T(8,128)S(1)} %copy-done.23, f32[4,8,4736]{2,1,0:T(8,128)S(1)} %copy-done.27, ...), custom_call_target="tpu_custom_call" | custom-call | flops 157286400 | bytes 18874368 | tf_op jit(solution)/shard_map/pallas_call | solution.py:315
  63.1 41.5 %all-to-all-done.arrived_ref = f32[8,4,208,128]{3,2,1,0:T(8,128)} async-done(((f32[8,4,208,128]{3,2,1,0:T(8,128)}), f32[8,4,208,128]{3,2,1,0:T(8,128)}, u32[]{:S(2)}, u32[]{:S(2)}) %all-to-all-start) | async-done | bytes 3407904 | tf_op jit(solution)/shard_map/all_to_all | solution.py:621
  104.6 20.3 %shard_map.78 = (f32[8,2,192,128]{3,2,1,0:T(8,128)S(1)}, f32[8,1,192,128]{3,2,1,0:T(8,128)S(1)}, f32[8,1,192,128]{3,2,1,0:T(8,128)S(1)}) custom-call(f32[8,4,208,128]{3,2,1,0:T(8,128)} %all-to-all-done.arrived_ref), custom_call_target="tpu_custom_call" | custom-call | flops 85196800 | bytes 10223616 | tf_op jit(solution)/shard_map/pallas_call | solution.py:252
  127.8 4.3 %all-to-all-start.3 = ((f32[8,2,192,128]{3,2,1,0:T(8,128)}), f32[8,2,192,128]{3,2,1,0:T(8,128)}, u32[]{:S(2)}, u32[]{:S(2)}) async-start(f32[8,2,192,128]{3,2,1,0:T(8,128)} %copy-done.19), calls=%async_computation.3 | async-start | bytes 3145728 | tf_op jit(solution)/shard_map/all_to_all | solution.py:644
  132.9 42.6 %all-to-all-done.3.arrived_ref = f32[8,2,192,128]{3,2,1,0:T(8,128)} async-done(((f32[8,2,192,128]{3,2,1,0:T(8,128)}), f32[8,2,192,128]{3,2,1,0:T(8,128)}, u32[]{:S(2)}, u32[]{:S(2)}) %all-to-all-start.3) | async-done | bytes 1572896 | tf_op jit(solution)/shard_map/all_to_all | solution.py:644
  175.5 4.4 %all-to-all-start.1 = ((f32[8,1,192,128]{3,2,1,0:T(8,128)}), f32[8,1,192,128]{3,2,1,0:T(8,128)}, u32[]{:S(2)}, u32[]{:S(2)}) async-start(f32[8,1,192,128]{3,2,1,0:T(8,128)} %copy-done.21), calls=%async_computation.1 | async-start | bytes 1572864 | tf_op jit(solution)/shard_map/all_to_all | solution.py:644
  179.9 27.3 %all-gather.3.cloned.1.call-done = f32[3328,128]{1,0:T(8,128)} async-done(((f32[416,128]{1,0:T(8,128)}), f32[3328,128]{1,0:T(8,128)}) %all-gather.3.cloned.1.call-update) | async-done | bytes 1703952 | tf_op jit(solution)/shard_map/all_gather | solution.py:635
  211.5 7.0 %shard_map.83.own_ref.rest_0_ = f32[2,1536,128]{2,1,0:T(8,128)} custom-call(f32[8,2,192,128]{3,2,1,0:T(8,128)} %all-to-all-done.3.arrived_ref, bf16[4,1536,256]{2,1,0:T(8,128)(2,1)S(1)} %get-tuple-element.24.high_ref, bf16[4,1536,256]{2,1,0:T(8,128)(2,1)S(1)} %copy-done.1, f32[256,128]{1,0:T(8,128)S(1)} %shard_map.80.weights_ref), custom_call_target="tpu_custom_call" | custom-call | bytes 9437184 | tf_op jit(solution)/shard_map/pallas_call | solution.py:134
  220.0 4.2 %all-to-all-start.2 = ((f32[8,1,192,128]{3,2,1,0:T(8,128)}), f32[8,1,192,128]{3,2,1,0:T(8,128)}, u32[]{:S(2)}, u32[]{:S(2)}) async-start(f32[8,1,192,128]{3,2,1,0:T(8,128)} %copy-done.20), calls=%async_computation.2 | async-start | bytes 1572864 | tf_op jit(solution)/shard_map/all_to_all | solution.py:644
  226.1 3.3 shard_map.81.own_ref.rest_8_
  230.3 24.9 %collective-permute-done.11.rest_1_.rest_2_ = f32[2,1536,128]{2,1,0:T(8,128)} collective-permute-done((f32[2,1536,128]{2,1,0:T(8,128)}, f32[2,1536,128]{2,1,0:T(8,128)}, u32[]{:S(2)}, u32[]{:S(2)}) %collective-permute-start.11) | collective-permute-done | bytes 1572896 | tf_op jit(solution)/shard_map/ppermute | solution.py:396
  262.2 4.0 %shard_map.84 = f32[128,512]{1,0:T(8,128)S(1)} custom-call(f32[2,1536,128]{2,1,0:T(8,128)} %shard_map.83.own_ref.rest_0_, f32[2,1536,128]{2,1,0:T(8,128)} %collective-permute-done.10.rest_0_.rest_1_, f32[2,1536,128]{2,1,0:T(8,128)} %collective-permute-done.11.rest_1_.rest_2_, f32[2,1536,128]{2,1,0:T(8,128)} %collective-permute-done.12.rest_2_.rest_3_), custom_call_target="tpu_custom_call" | custom-call | flops 1610612736 | bytes 6291456 | tf_op jit(solution)/shard_map/pallas_call | solution.py:418
  266.2 14.2 %collective-permute-done.9.rest_1_.rest_6_ = f32[1,1536,128]{2,1,0:T(8,128)S(1)} collective-permute-done((f32[1,1536,128]{2,1,0:T(8,128)S(1)}, f32[1,1536,128]{2,1,0:T(8,128)S(1)}, u32[]{:S(2)}, u32[]{:S(2)}) %collective-permute-start.9) | collective-permute-done | bytes 786464 | tf_op jit(solution)/shard_map/ppermute | solution.py:396
  284.1 16.3 %collective-permute-done.7.rest_1_.rest_10_ = f32[1,1536,128]{2,1,0:T(8,128)S(1)} collective-permute-done((f32[1,1536,128]{2,1,0:T(8,128)S(1)}, f32[1,1536,128]{2,1,0:T(8,128)S(1)}, u32[]{:S(2)}, u32[]{:S(2)}) %collective-permute-start.7) | collective-permute-done | bytes 786464 | tf_op jit(solution)/shard_map/ppermute | solution.py:396
  304.1 12.1 %all_to_all.30 = f32[8,16,512]{2,1,0:T(8,128)S(1)} all-to-all(f32[8,16,512]{2,1,0:T(8,128)S(1)} %bitcast.44), channel_id=1, replica_groups=mesh['band'=4,'dom'=8] {'dom'}, dimensions={0} | all-to-all | bytes 524288 | tf_op jit(solution)/shard_map/all_to_all | solution.py:652
  316.2 12.6 %all_to_all.31 = f32[8,16,512]{2,1,0:T(8,128)S(1)} all-to-all(f32[8,16,512]{2,1,0:T(8,128)S(1)} %broadcast_in_dim.58), channel_id=1, replica_groups=mesh['band'=4,'dom'=8] {'dom'}, dimensions={0} | all-to-all | bytes 524288 | tf_op jit(solution)/shard_map/all_to_all | solution.py:654
  330.3 4.9 %collective-permute-done.16.refs_2_ = f32[128,512]{1,0:T(8,128)S(1)} collective-permute-done((f32[128,512]{1,0:T(8,128)S(1)}, f32[128,512]{1,0:T(8,128)S(1)}, u32[]{:S(2)}, u32[]{:S(2)}) %collective-permute-start.16) | collective-permute-done | bytes 262176 | tf_op jit(solution)/shard_map/ppermute | solution.py:396
  336.7 25.5 %shard_map.87 = (f32[512,512]{1,0:T(8,128)}, f32[128,512]{1,0:T(8,128)S(1)}) custom-call(s32[1]{0:T(128)} %bitcast.band_ref, f32[128,512]{1,0:T(8,128)S(1)} %bitcast.39, f32[128,512]{1,0:T(8,128)S(1)} %collective-permute-done.15.refs_1_, f32[128,512]{1,0:T(8,128)S(1)} %collective-permute-done.16.refs_2_, f32[128,512]{1,0:T(8,128)S(1)} %collective-permute-done.17.refs_3_), custom_call_target="tpu_custom_call" | custom-call | tf_op jit(solution)/shard_map/pallas_call | solution.py:562
  364.5 7.3 %shard_map.88 = f32[4,1536,128]{2,1,0:T(8,128)} custom-call(f32[128,512]{1,0:T(8,128)S(1)} %get-tuple-element.34.inverse_ref, f32[2,1536,128]{2,1,0:T(8,128)} %shard_map.83.own_ref.rest_0_, f32[2,1536,128]{2,1,0:T(8,128)} %collective-permute-done.10.rest_0_.rest_1_, f32[2,1536,128]{2,1,0:T(8,128)} %collective-permute-done.11.rest_1_.rest_2_, ...), custom_call_target="tpu_custom_call" | custom-call | tf_op jit(solution)/shard_map/pallas_call | solution.py:445
  (144 shorter events, 47.8 us)
Async XLA Ops:
  9.8 12.2 %collective-permute-start.2 = (f32[8,4736]{1,0:T(8,128)S(1)}, f32[8,4736]{1,0:T(8,128)S(1)}, u32[]{:S(2)}, u32[]{:S(2)}) collective-permute-start(f32[8,4736]{1,0:T(8,128)S(1)} %reshape.267), channel_id=1, source_target_pairs={{0,7},{1,0},{2,1},{3,2},{4,3},{5,4},{6,5},{7,6},{8,15},{9,8},{10,9... | collective-permute-start | bytes 454664 | tf_op jit(solution)/shard_map/ppermute | solution.py:392
  15.9 9.6 %collective-permute-start.1 = (f32[8,4736]{1,0:T(8,128)S(1)}, f32[8,4736]{1,0:T(8,128)S(1)}, u32[]{:S(2)}, u32[]{:S(2)}) collective-permute-start(f32[8,4736]{1,0:T(8,128)S(1)} %reshape.267), channel_id=1, source_target_pairs={{0,1},{1,2},{2,3},{3,4},{4,5},{5,6},{6,7},{7,0},{8,9},{9,10},{10,1... | collective-permute-start | bytes 454664 | tf_op jit(solution)/shard_map/ppermute | solution.py:392
  15.9 9.6 %collective-permute-start = (f32[8,4736]{1,0:T(8,128)S(1)}, f32[8,4736]{1,0:T(8,128)S(1)}, u32[]{:S(2)}, u32[]{:S(2)}) collective-permute-start(f32[8,4736]{1,0:T(8,128)S(1)} %reshape.267), channel_id=1, source_target_pairs={{0,2},{1,3},{2,4},{3,5},{4,6},{5,7},{6,0},{7,1},{8,10},{9,11},{10,... | collective-permute-start | bytes 454664 | tf_op jit(solution)/shard_map/ppermute | solution.py:392
  25.6 79.0 %all-to-all-start = ((f32[8,4,208,128]{3,2,1,0:T(8,128)}), f32[8,4,208,128]{3,2,1,0:T(8,128)}, u32[]{:S(2)}, u32[]{:S(2)}) async-start(f32[8,4,208,128]{3,2,1,0:T(8,128)} %shard_map.77), calls=%async_computation | async-start | bytes 6815744 | tf_op jit(solution)/shard_map/all_to_all | solution.py:621
  30.4 13.1 %collective-permute-start.4 = (f32[4,8,4736]{2,1,0:T(8,128)S(1)}, f32[4,8,4736]{2,1,0:T(8,128)S(1)}, u32[]{:S(2)}, u32[]{:S(2)}) collective-permute-start(f32[4,8,4736]{2,1,0:T(8,128)S(1)} %pad_maximum_fusion.refs_0_), channel_id=1, source_target_pairs={{0,16},{8,24},{16,0},{24,8},{1,17},{9,25},{17,1},{25,9},{2,18},{10... | collective-permute-start | bytes 1818632 | tf_op jit(solution)/shard_map/ppermute | solution.py:396
  33.2 10.7 %collective-permute-start.3 = (f32[4,8,4736]{2,1,0:T(8,128)S(1)}, f32[4,8,4736]{2,1,0:T(8,128)S(1)}, u32[]{:S(2)}, u32[]{:S(2)}) collective-permute-start(f32[4,8,4736]{2,1,0:T(8,128)S(1)} %pad_maximum_fusion.refs_0_), channel_id=1, source_target_pairs={{0,8},{8,0},{16,24},{24,16},{1,9},{9,1},{17,25},{25,17},{2,10},{10... | collective-permute-start | bytes 1818632 | tf_op jit(solution)/shard_map/ppermute | solution.py:396
  43.5 2.0 collective-permute-start.5
  127.8 47.7 %all-to-all-start.3 = ((f32[8,2,192,128]{3,2,1,0:T(8,128)}), f32[8,2,192,128]{3,2,1,0:T(8,128)}, u32[]{:S(2)}, u32[]{:S(2)}) async-start(f32[8,2,192,128]{3,2,1,0:T(8,128)} %copy-done.19), calls=%async_computation.3 | async-start | bytes 3145728 | tf_op jit(solution)/shard_map/all_to_all | solution.py:644
  132.1 75.1 %all-gather.3.cloned.1.call-start = ((), (), s32[]{:S(2)}) async-start(), calls=%async_computation.6 | async-start | bytes 1916928 | tf_op jit(solution)/shard_map/all_gather | solution.py:635
  175.5 44.4 %all-to-all-start.1 = ((f32[8,1,192,128]{3,2,1,0:T(8,128)}), f32[8,1,192,128]{3,2,1,0:T(8,128)}, u32[]{:S(2)}, u32[]{:S(2)}) async-start(f32[8,1,192,128]{3,2,1,0:T(8,128)} %copy-done.21), calls=%async_computation.1 | async-start | bytes 1572864 | tf_op jit(solution)/shard_map/all_to_all | solution.py:644
  218.5 36.7 %collective-permute-start.11 = (f32[2,1536,128]{2,1,0:T(8,128)}, f32[2,1536,128]{2,1,0:T(8,128)}, u32[]{:S(2)}, u32[]{:S(2)}) collective-permute-start(f32[2,1536,128]{2,1,0:T(8,128)} %shard_map.83.own_ref.rest_0_), channel_id=1, source_target_pairs={{0,16},{8,24},{16,0},{24,8},{1,17},{9,25},{17,1},{25,9},{2,18},{10... | collective-permute-start | bytes 4718600 | tf_op jit(solution)/shard_map/ppermute | solution.py:396
  220.0 35.2 %all-to-all-start.2 = ((f32[8,1,192,128]{3,2,1,0:T(8,128)}), f32[8,1,192,128]{3,2,1,0:T(8,128)}, u32[]{:S(2)}, u32[]{:S(2)}) async-start(f32[8,1,192,128]{3,2,1,0:T(8,128)} %copy-done.20), calls=%async_computation.2 | async-start | bytes 1572864 | tf_op jit(solution)/shard_map/all_to_all | solution.py:644
  230.3 31.9 %collective-permute-start.10 = (f32[2,1536,128]{2,1,0:T(8,128)}, f32[2,1536,128]{2,1,0:T(8,128)}, u32[]{:S(2)}, u32[]{:S(2)}) collective-permute-start(f32[2,1536,128]{2,1,0:T(8,128)} %shard_map.83.own_ref.rest_0_), channel_id=1, source_target_pairs={{0,8},{8,0},{16,24},{24,16},{1,9},{9,1},{17,25},{25,17},{2,10},{10... | collective-permute-start | bytes 4718600 | tf_op jit(solution)/shard_map/ppermute | solution.py:396
  255.2 7.0 %collective-permute-start.12 = (f32[2,1536,128]{2,1,0:T(8,128)}, f32[2,1536,128]{2,1,0:T(8,128)}, u32[]{:S(2)}, u32[]{:S(2)}) collective-permute-start(f32[2,1536,128]{2,1,0:T(8,128)} %collective-permute-done.11.rest_1_.rest_2_), channel_id=1, source_target_pairs={{0,8},{8,0},{16,24},{24,16},{1,9},{9,1},{17,25},{25,17},{2,10},{10... | collective-permute-start | bytes 4718600 | tf_op jit(solution)/shard_map/ppermute | solution.py:396
  260.4 20.0 %collective-permute-start.9 = (f32[1,1536,128]{2,1,0:T(8,128)S(1)}, f32[1,1536,128]{2,1,0:T(8,128)S(1)}, u32[]{:S(2)}, u32[]{:S(2)}) collective-permute-start(f32[1,1536,128]{2,1,0:T(8,128)S(1)} %shard_map.82.own_ref.rest_4_), channel_id=1, source_target_pairs={{0,16},{8,24},{16,0},{24,8},{1,17},{9,25},{17,1},{25,9},{2,18},{10... | collective-permute-start | bytes 2359304 | tf_op jit(solution)/shard_map/ppermute | solution.py:396
  261.9 20.2 %collective-permute-start.8 = (f32[1,1536,128]{2,1,0:T(8,128)S(1)}, f32[1,1536,128]{2,1,0:T(8,128)S(1)}, u32[]{:S(2)}, u32[]{:S(2)}) collective-permute-start(f32[1,1536,128]{2,1,0:T(8,128)S(1)} %shard_map.82.own_ref.rest_4_), channel_id=1, source_target_pairs={{0,8},{8,0},{16,24},{24,16},{1,9},{9,1},{17,25},{25,17},{2,10},{10... | collective-permute-start | bytes 2359304 | tf_op jit(solution)/shard_map/ppermute | solution.py:396
  280.4 2.3 collective-permute-start.13
  280.4 20.0 %collective-permute-start.7 = (f32[1,1536,128]{2,1,0:T(8,128)S(1)}, f32[1,1536,128]{2,1,0:T(8,128)S(1)}, u32[]{:S(2)}, u32[]{:S(2)}) collective-permute-start(f32[1,1536,128]{2,1,0:T(8,128)S(1)} %copy-done.6), channel_id=1, source_target_pairs={{0,16},{8,24},{16,0},{24,8},{1,17},{9,25},{17,1},{25,9},{2,18},{10... | collective-permute-start | bytes 2359304 | tf_op jit(solution)/shard_map/ppermute | solution.py:396
  281.9 18.5 %collective-permute-start.6 = (f32[1,1536,128]{2,1,0:T(8,128)S(1)}, f32[1,1536,128]{2,1,0:T(8,128)S(1)}, u32[]{:S(2)}, u32[]{:S(2)}) collective-permute-start(f32[1,1536,128]{2,1,0:T(8,128)S(1)} %copy-done.6), channel_id=1, source_target_pairs={{0,8},{8,0},{16,24},{24,16},{1,9},{9,1},{17,25},{25,17},{2,10},{10... | collective-permute-start | bytes 2359304 | tf_op jit(solution)/shard_map/ppermute | solution.py:396
  300.4 2.3 collective-permute-start.14
  304.0 58.2 %copy-start.8 = (f32[1,1536,128]{2,1,0:T(8,128)S(1)}, f32[1,1536,128]{2,1,0:T(8,128)}, u32[]{:S(2)}) copy-start(f32[1,1536,128]{2,1,0:T(8,128)} %copy-done.7) | copy-start | bytes 2359300
  328.8 6.4 %collective-permute-start.16 = (f32[128,512]{1,0:T(8,128)S(1)}, f32[128,512]{1,0:T(8,128)S(1)}, u32[]{:S(2)}, u32[]{:S(2)}) collective-permute-start(f32[128,512]{1,0:T(8,128)S(1)} %bitcast.37), channel_id=1, source_target_pairs={{0,16},{8,24},{16,0},{24,8},{1,17},{9,25},{17,1},{25,9},{2,18},{10... | collective-permute-start | bytes 786440 | tf_op jit(solution)/shard_map/ppermute | solution.py:396
  330.3 4.9 %collective-permute-start.15 = (f32[128,512]{1,0:T(8,128)S(1)}, f32[128,512]{1,0:T(8,128)S(1)}, u32[]{:S(2)}, u32[]{:S(2)}) collective-permute-start(f32[128,512]{1,0:T(8,128)S(1)} %bitcast.38), channel_id=1, source_target_pairs={{0,8},{8,0},{16,24},{24,16},{1,9},{9,1},{17,25},{25,17},{2,10},{10... | collective-permute-start | bytes 786440 | tf_op jit(solution)/shard_map/ppermute | solution.py:396
  335.2 1.5 collective-permute-start.17
  (30 other events, 209.6 us)
Sparse Core Ops, SparseCore 0:
  135.1 72.0 all-gather.2

commit v7 on v6

--- a/solution.py
+++ b/solution.py
@@ -48,26 +48,32 @@
     return value[:, :LANES] + value[:, LANES:]
 
 
-def swapped(blocks, lane):
+def swapped(blocks, lane, before=None, after=None):
     count = len(blocks)
     width = LANES // count
-    blocks = [pltpu.roll(value, at * width, 1) if at else value for at, value in enumerate(blocks)]
+
+    def turned(value, at, extra):
+        if extra is None:
+            return pltpu.roll(value, at % count * width, 1) if at else value
+        return pltpu.roll(value, lax.rem((at % count + extra) * width, LANES), 1)
+
+    blocks = [turned(value, at, None if before is None else count - before) for at, value in enumerate(blocks)]
     bit = 1
     while bit < count:
         chosen = (lane // (bit * width)) % 2 == 1
         blocks = [jnp.where(chosen, blocks[(at + bit) % count], blocks[at]) for at in range(count)]
         bit *= 2
-    blocks = [blocks[-at % count] for at in range(count)]
-    return [pltpu.roll(value, LANES - at * width, 1) if at else value for at, value in enumerate(blocks)]
-
-
-def swap_into(read, write, count, rows):
+    return [turned(blocks[-at % count], -at, after) for at in range(count)]
+
+
+def swap_into(read, write, count, rows, before=None, after=None):
     tile = 8 * max(1, 32 // count)
     lane = lax.broadcasted_iota(jnp.int32, (tile, LANES), 1)
 
     def step(index, carry):
         start = pl.multiple_of(index * tile, 8)
-        for block, value in enumerate(swapped([read(block, start, tile) for block in range(count)], lane)):
+        blocks = [read(block, start, tile) for block in range(count)]
+        for block, value in enumerate(swapped(blocks, lane, before, after)):
             write(block, start, tile, value)
         return carry
 
@@ -103,19 +109,21 @@
     )(levels, value)
 
 
-def swap_out_kernel(count, rows, arrived_ref, high_ref, low_ref, weights_ref, out_ref):
-    planes = out_ref.shape[0]
+def swap_out_kernel(me_ref, high_ref, low_ref, weights_ref, *refs):
+    arrived_refs, out_ref = refs[:-1], refs[-1]
+    count = len(arrived_refs)
+    planes, rows, _ = arrived_refs[0].shape
     weights = side_by_side(weights_ref[...] * (1.0 / 18.0))
     for plane in range(planes):
 
         def read(block, start, size):
-            return arrived_ref[block, plane, pl.ds(start, size), :]
+            return arrived_refs[-block % count][plane, pl.ds(start, size), :]
 
         def write(block, start, size, value):
             at = pl.ds(pl.multiple_of(block * rows + start, 8), size)
             out_ref[plane, at, :] = value
 
-        swap_into(read, write, count, rows)
+        swap_into(read, write, count, rows, after=me_ref[0])
         tile = rows * count // 6
 
         def add(index, carry):
@@ -127,24 +135,26 @@
         lax.fori_loop(0, 6, add, 0)
 
 
-def swap_out(arrived, high, low, weights, first_plane):
-    count, planes, rows, _ = arrived.shape
+def swap_out(me, arrived, high, low, weights, first_plane):
+    count = len(arrived)
+    planes, rows, _ = arrived[0].shape
     cells = count * rows
     basis = pl.BlockSpec((planes, cells, 2 * LANES), lambda i: (first_plane // planes, 0, 0))
     return pl.pallas_call(
-        functools.partial(swap_out_kernel, count, rows),
+        swap_out_kernel,
         grid=(1,),
         in_specs=[
-            pl.BlockSpec(arrived.shape, lambda i: (0, 0, 0, 0)),
+            pl.BlockSpec(memory_space=pltpu.SMEM),
             basis,
             basis,
             pl.BlockSpec(weights.shape, lambda i: (0, 0)),
-        ],
+        ]
+        + [pl.BlockSpec(arrived[0].shape, lambda i: (0, 0, 0))] * count,
         out_specs=pl.BlockSpec((planes, cells, LANES), lambda i: (0, 0, 0)),
         out_shape=jax.ShapeDtypeStruct((planes, cells, LANES), jnp.float32),
-        compiler_params=params(18),
-        cost_estimate=cost(0, 24 * arrived.size),
-    )(arrived, high, low, weights)
+        compiler_params=params(24),
+        cost_estimate=cost(0, 24 * cells * planes * LANES),
+    )(me, high, low, weights, *arrived)
 
 
 def fill_row(target, plane, y, row, side_z):
@@ -180,8 +190,8 @@
     lax.fori_loop(0, side_y, row, 0)
 
 
-def filter_kernel(planes, side_y, side_z, width, chunks, arrived_ref, *rest):
-    outs, (field, padded, first, flat, potential) = rest[: len(chunks)], rest[len(chunks) :]
+def filter_kernel(planes, side_y, side_z, width, chunks, me_ref, arrived_ref, *rest):
+    outs, (field, padded, first, flat, potential) = rest[:-5], rest[-5:]
     count = arrived_ref.shape[0]
     cells = side_y * side_z
     rows = cells // count
@@ -232,32 +242,35 @@
     local_part(padded, potential, planes, 0, side_y, side_z, line_of, finish_first)
     local_part(first, potential, planes, 0, side_y, side_z, line_of, finish_second)
 
-    for (begin, size_of), out_ref in zip(chunks, outs):
+    for index, (begin, size_of) in enumerate(chunks):
+        group = outs[index * count : (index + 1) * count]
         for plane in range(size_of):
 
             def read_out(block, start, size):
                 return flat[begin + plane, pl.ds(pl.multiple_of(block * rows + start, 8), size), :]
 
             def write_out(block, start, size, value):
-                out_ref[block, plane, pl.ds(start, size), :] = value
-
-            swap_into(read_out, write_out, count, rows)
-
-
-def filter_orbitals(arrived, side_y, side_z, width, chunks):
+                group[block][plane, pl.ds(start, size), :] = value
+
+            swap_into(read_out, write_out, count, rows, before=me_ref[0])
+
+
+def filter_orbitals(me, arrived, side_y, side_z, width, chunks):
     count, planes = arrived.shape[:2]
     rows = side_y * side_z // count
     flat = pltpu.VMEM((planes, side_y * side_z, LANES), jnp.float32)
     padded = pltpu.VMEM((planes, side_y, side_z + 2 * PAD, LANES), jnp.float32)
-    return pl.pallas_call(
+    shapes = [jax.ShapeDtypeStruct((size, rows, LANES), jnp.float32) for _, size in chunks for _ in range(count)]
+    outs = pl.pallas_call(
         functools.partial(filter_kernel, planes, side_y, side_z, width, chunks),
-        in_specs=[WHOLE],
-        out_specs=[WHOLE] * len(chunks),
-        out_shape=[jax.ShapeDtypeStruct((count, size, rows, LANES), jnp.float32) for _, size in chunks],
+        in_specs=[pl.BlockSpec(memory_space=pltpu.SMEM), WHOLE],
+        out_specs=[WHOLE] * len(shapes),
+        out_shape=shapes,
         scratch_shapes=[flat, padded, padded, flat, flat],
-        compiler_params=params(30),
+        compiler_params=params(56),
         cost_estimate=cost(100 * arrived.size, 12 * arrived.size),
-    )(arrived)
+    )(me, arrived)
+    return [outs[index * count : (index + 1) * count] for index in range(len(chunks))]
 
 
 def basis_kernel(planes, side_y, side_z, bands, *refs):
@@ -321,7 +334,7 @@
             pltpu.VMEM((SPAN, cells, LANES), jnp.float32),
             pltpu.VMEM((planes + 2 * HALO, side_y, side_z + 2 * PAD, LANES), jnp.float32),
         ],
-        compiler_params=params(40),
+        compiler_params=params(56),
         cost_estimate=cost(200 * orbitals.size, 24 * orbitals.size),
     )(*raw, offset, potential, orbitals)
 
@@ -376,20 +389,24 @@
     )
 
 
-def near_weights(parts, coupling):
+def near_weights(me, parts, coupling):
     return pl.pallas_call(
         functools.partial(weights_kernel, lax.axis_size("band")),
         in_specs=[pl.BlockSpec(memory_space=pltpu.SMEM), WHOLE, WHOLE],
         out_specs=WHOLE,
         out_shape=jax.ShapeDtypeStruct((2 * LANES, LANES), jnp.float32),
-        compiler_params=params(18),
+        compiler_params=params(24),
         cost_estimate=cost(0, 8 * parts.size),
-    )(lax.axis_index("dom").astype(jnp.int32).reshape(1), parts, coupling)
+    )(me, parts, coupling)
 
 
 def shifted(value, axis, step):
     count = lax.axis_size(axis)
     return lax.ppermute(value, axis, [(source, (source + step) % count) for source in range(count)])
+
+
+def exchanged(values):
+    return [shifted(value, "dom", step) if step else value for step, value in enumerate(values)]
 
 
 def crossed(value, bit):
@@ -448,7 +465,7 @@
         in_specs=[pl.BlockSpec(inverse_rows.shape, lambda i: (0, 0)), *specs],
         out_specs=pl.BlockSpec((planes, tile, LANES), lambda i: (0, i, 0)),
         out_shape=jax.ShapeDtypeStruct((planes, cells, LANES), jnp.float32),
-        compiler_params=params(18),
+        compiler_params=params(24),
     )(inverse_rows, *[panel for group in panels for panel in group])
 
 
@@ -607,7 +624,8 @@
     rows = cells // blocks
     width = local_orbs // blocks
     norb = local_orbs * bands
-    chunks = ((0, 2), (2, 1), (3, 1))
+    chunks = tuple((plane, 1) for plane in range(planes))
+    me = lax.axis_index("dom").astype(jnp.int32).reshape(1)
 
     order = jnp.arange(bands, dtype=jnp.int32) ^ band
 
@@ -632,16 +650,23 @@
     matrix = jnp.tile(coupled.reshape(vectors, MAXPROJ), (1, atoms))
     matrix = jnp.where(row[:, None] == row[None, :], matrix, 0.0)
     matrix = jnp.pad(matrix, ((0, 0), (0, LANES - vectors)))
-    everyone = lax.all_gather(jnp.concatenate([parts.reshape(3 * LANES, LANES), matrix], axis=0), "dom")
+    payload = jnp.concatenate([parts.reshape(3 * LANES, LANES), matrix], axis=0)
+    everyone = lax.all_gather(payload, "dom")
     weights = near_weights(
-        everyone[:, : 3 * LANES].reshape(blocks, 3, LANES, LANES), everyone[:, 3 * LANES :, :vectors]
+        me,
+        everyone[:, : 3 * LANES].reshape(blocks, 3, LANES, LANES), everyone[:, 3 * LANES :, :vectors],
     )
 
-    seconds = filter_orbitals(arrived, side_y, side_z, width, chunks)
-
-    sent = []
+    arrived, _ = lax.optimization_barrier((arrived, payload))
+    seconds = filter_orbitals(me, arrived, side_y, side_z, width, chunks)
+
+    sent, came = [], None
     for (begin, size), packed in zip(chunks, seconds):
-        own = swap_out(lax.all_to_all(packed, "dom", 0, 0, tiled=True), high, low, weights, begin)
+        if came is not None:
+            packed, _ = lax.optimization_barrier((packed, came))
+        arrived = exchanged(packed)
+        came = arrived[1]
+        own = swap_out(me, arrived, high, low, weights, begin)
         sent.append((own, crossed(own, 1), crossed(own, 2)))
     panels, part = [], sent[-1][0]
     for own, beside, across in sent:

time: 380 us -> 364 us (0.958)
  waiting for transfers between devices: 191 us -> 128 us
  starting transfers between devices: 31.6 us -> 68.8 us
  local copies, waits for them, and re-layouts: 23.5 us -> 32.4 us
    ppermute x3 -> x31, starting transfers between devices: 6.06 us -> 54.8 us  [shifted(): lax.ppermute(value, axis, [(source, (source + step) % count) for source i...]
    all_to_all x3 -> x0, waiting for transfers between devices: 42.6 us -> none  [shards(): lax.all_to_all(packed, 'dom', 0, 0, tiled=True)]
    all_gather x1, waiting for transfers between devices: 27.3 us -> 0.01 us  [shards(): everyone = lax.all_gather(payload, 'dom')]
    ppermute x3 -> x31, waiting for transfers between devices: 3.39 us -> 24.4 us  [shifted(): lax.ppermute(value, axis, [(source, (source + step) % count) for source i...]
    ppermute x15 -> x18, waiting for transfers between devices: 76.1 us -> 58.1 us  [crossed(): lax.ppermute(value, 'band', [(source, source ^ bit) for source in range(l...]
    all_to_all x3 -> x0, starting transfers between devices: 12.9 us -> none  [shards(): lax.all_to_all(packed, 'dom', 0, 0, tiled=True)]
    all_to_all x1, waiting for transfers between devices: 41.5 us -> 45.8 us  [shards(): arrived = lax.all_to_all(packed, 'dom', 0, 0, tiled=True)]
    unnamed x65 -> x131, local copies, waits for them, and re-layouts: 17.1 us -> 21.3 us
  transfers between devices with their start and end apart: 23 -> 51, of which waited for: 13 -> 21; matrix products, arithmetic and copies ran while one was open for 2% -> 3% of each run, Pallas kernels for 10% -> 14%
where the time goes in v7:
time: 364 us; the launch traced here: 363 us
  waiting for transfers between devices  128 us (35%)
  Pallas kernels  87.5 us (24%)
  starting transfers between devices  68.8 us (19%)
  local copies, waits for them, and re-layouts  32.4 us (9%)
  blocking collectives  26.5 us (7%)
  between operations  14.8 us (4%)
  other arithmetic  4.64 us (1%)
    ppermute x18, waiting for transfers between devices, crossed(): lax.ppermute(value, 'band', [(source, source ^ bit) for source in range(l...  58.1 us
    ppermute x31, starting transfers between devices, shifted(): lax.ppermute(value, axis, [(source, (source + step) % count) for source i...  54.8 us
    all_to_all x1, waiting for transfers between devices, shards(): arrived = lax.all_to_all(packed, 'dom', 0, 0, tiled=True)  45.8 us
    pallas_call x1, Pallas kernels, cholesky_inverse(): pl.pallas_call(cholesky_kernel, in_specs=[pl.BlockSpec(memory_space=pltpu...  25.5 us
    ppermute x31, waiting for transfers between devices, shifted(): lax.ppermute(value, axis, [(source, (source + step) % count) for source i...  24.4 us
    pallas_call x1, Pallas kernels, filter_orbitals(): pl.pallas_call(functools.partial(filter_kernel, planes, side_y, side_z, w...  22 us
    unnamed x131, local copies, waits for them, and re-layouts  21.3 us
    all_to_all x1, blocking collectives, shards(): lax.all_to_all(part.reshape(blocks, width, norb), 'dom', 0, 0, tiled=True)  14.6 us
  transfers between devices with their start and end apart: 51, of which 21 were waited for; matrix products, arithmetic and copies ran while one was open for 3% of the time, Pallas kernels for 14%

profile of v7, /device:TPU:0, one launch (start us, length us, event | category | flops | bytes accessed | tf_op | source)
XLA Modules:
  0.0 362.9 jit_solution(1686424980462118056)
XLA Ops:
  9.8 6.1 %collective-permute-start.2 = (f32[8,4736]{1,0:T(8,128)S(1)}, f32[8,4736]{1,0:T(8,128)S(1)}, u32[]{:S(2)}, u32[]{:S(2)}) collective-permute-start(f32[8,4736]{1,0:T(8,128)S(1)} %reshape.268), channel_id=1, source_target_pairs={{0,7},{1,0},{2,1},{3,2},{4,3},{5,4},{6,5},{7,6},{8,15},{9,8},{10,9... | collective-permute-start | bytes 454664 | tf_op jit(solution)/shard_map/ppermute | solution.py:405
  17.8 4.2 %shard_map.77 = f32[8,4,208,128]{3,2,1,0:T(8,128)} custom-call(f32[4,16,128]{2,1,0:T(8,128)S(1)} %pad.8.levels_ref, f32[4,8,192,128]{3,2,1,0:T(8,128)S(1)} %bitcast.35), custom_call_target="tpu_custom_call" | custom-call | bytes 6291456 | tf_op jit(solution)/shard_map/pallas_call | solution.py:98
  22.1 3.4 collective-permute-done.1
  26.3 3.8 %all-to-all-start = ((f32[8,4,208,128]{3,2,1,0:T(8,128)}), f32[8,4,208,128]{3,2,1,0:T(8,128)S(1)}, u32[]{:S(2)}, u32[]{:S(2)}) async-start(f32[8,4,208,128]{3,2,1,0:T(8,128)} %shard_map.77), calls=%async_computation | async-start | bytes 6815744 | tf_op jit(solution)/shard_map/all_to_all | solution.py:639
  33.4 11.2 %collective-permute-done.4.refs_2_ = f32[4,8,4736]{2,1,0:T(8,128)} collective-permute-done((f32[4,8,4736]{2,1,0:T(8,128)}, f32[4,8,4736]{2,1,0:T(8,128)}, u32[]{:S(2)}, u32[]{:S(2)}) %collective-permute-start.4) | collective-permute-done | bytes 606240 | tf_op jit(solution)/shard_map/ppermute | solution.py:413
  51.2 13.5 %shard_map.78 = (bf16[4,1536,256]{2,1,0:T(8,128)(2,1)}, bf16[4,1536,256]{2,1,0:T(8,128)(2,1)}, f32[3,128,128]{2,1,0:T(8,128)}) custom-call(f32[4,8,4736]{2,1,0:T(8,128)} %pad_maximum_fusion.refs_0_, f32[4,8,4736]{2,1,0:T(8,128)} %collective-permute-done.3.refs_1_, f32[4,8,4736]{2,1,0:T(8,128)} %collective-permute-done.4.refs_2_, ...), custom_call_target="tpu_custom_call" | custom-call | flops 157286400 | bytes 18874368 | tf_op jit(solution)/shard_map/pallas_call | solution.py:328
  66.4 45.8 %all-to-all-done.arrived_ref = f32[8,4,208,128]{3,2,1,0:T(8,128)S(1)} async-done(((f32[8,4,208,128]{3,2,1,0:T(8,128)}), f32[8,4,208,128]{3,2,1,0:T(8,128)S(1)}, u32[]{:S(2)}, u32[]{:S(2)}) %all-to-all-start) | async-done | bytes 3407904 | tf_op jit(solution)/shard_map/all_to_all | solution.py:639
  113.9 22.0 %shard_map.80 = (f32[1,192,128]{2,1,0:T(8,128)}, f32[1,192,128]{2,1,0:T(8,128)}, f32[1,192,128]{2,1,0:T(8,128)}, f32[1,192,128]{2,1,0:T(8,128)}, f32[1,192,128]{...) custom-call(s32[1]{0:T(128)} %bitcast.1.me_ref, ...), custom_call_target="tpu_custom_call" | custom-call | flops 85196800 | bytes 10223616 | tf_op jit(solution)/shard_map/pallas_call | solution.py:264
  153.6 3.4 shard_map.84.own_ref.rest_0_
  158.6 4.3 %collective-permute-start.7 = (f32[1,192,128]{2,1,0:T(8,128)S(1)}, f32[1,192,128]{2,1,0:T(8,128)S(1)}, u32[]{:S(2)}, u32[]{:S(2)}) collective-permute-start(f32[1,192,128]{2,1,0:T(8,128)S(1)} %copy-done.63), channel_id=1, source_target_pairs={{0,1},{1,2},{2,3},{3,4},{4,5},{5,6},{6,7},{7,0},{8,9},{9,10},{10,1... | collective-permute-start | bytes 294920 | tf_op jit(solution)/shard_map/ppermute | solution.py:405
  162.9 3.9 %collective-permute-start.26 = (f32[1,192,128]{2,1,0:T(8,128)S(1)}, f32[1,192,128]{2,1,0:T(8,128)S(1)}, u32[]{:S(2)}, u32[]{:S(2)}) collective-permute-start(f32[1,192,128]{2,1,0:T(8,128)S(1)} %copy-done.62), channel_id=1, source_target_pairs={{0,2},{1,3},{2,4},{3,5},{4,6},{5,7},{6,0},{7,1},{8,10},{9,11},{10,... | collective-permute-start | bytes 294920 | tf_op jit(solution)/shard_map/ppermute | solution.py:405
  169.5 3.4 collective-permute-start.27
  178.0 3.4 collective-permute-done.27.refs_3_
  184.0 3.7 %collective-permute-start.10 = (f32[1,192,128]{2,1,0:T(8,128)S(1)}, f32[1,192,128]{2,1,0:T(8,128)S(1)}, u32[]{:S(2)}, u32[]{:S(2)}) collective-permute-start(f32[1,192,128]{2,1,0:T(8,128)S(1)} %copy-done.54), channel_id=1, source_target_pairs={{0,2},{1,3},{2,4},{3,5},{4,6},{5,7},{6,0},{7,1},{8,10},{9,11},{10,... | collective-permute-start | bytes 294920 | tf_op jit(solution)/shard_map/ppermute | solution.py:405
  199.0 4.7 %collective-permute-start.15 = (f32[1,192,128]{2,1,0:T(8,128)S(1)}, f32[1,192,128]{2,1,0:T(8,128)S(1)}, u32[]{:S(2)}, u32[]{:S(2)}) collective-permute-start(f32[1,192,128]{2,1,0:T(8,128)S(1)} %copy-done.49), channel_id=1, source_target_pairs={{0,7},{1,0},{2,1},{3,2},{4,3},{5,4},{6,5},{7,6},{8,15},{9,8},{10,9... | collective-permute-start | bytes 294920 | tf_op jit(solution)/shard_map/ppermute | solution.py:405
  212.0 5.5 %collective-permute-done.18.refs_2_ = f32[1,192,128]{2,1,0:T(8,128)S(1)} collective-permute-done((f32[1,192,128]{2,1,0:T(8,128)S(1)}, f32[1,192,128]{2,1,0:T(8,128)S(1)}, u32[]{:S(2)}, u32[]{:S(2)}) %collective-permute-start.18) | collective-permute-done | bytes 98336 | tf_op jit(solution)/shard_map/ppermute | solution.py:405
  220.1 5.9 %collective-permute-done.33.rest_1_.rest_6_ = f32[1,1536,128]{2,1,0:T(8,128)S(1)} collective-permute-done((f32[1,1536,128]{2,1,0:T(8,128)S(1)}, f32[1,1536,128]{2,1,0:T(8,128)S(1)}, u32[]{:S(2)}, u32[]{:S(2)}) %collective-permute-start.33) | collective-permute-done | bytes 786464 | tf_op jit(solution)/shard_map/ppermute | solution.py:413
  236.7 15.9 %collective-permute-done.25.rest_1_.rest_10_ = f32[1,1536,128]{2,1,0:T(8,128)S(1)} collective-permute-done((f32[1,1536,128]{2,1,0:T(8,128)S(1)}, f32[1,1536,128]{2,1,0:T(8,128)S(1)}, u32[]{:S(2)}, u32[]{:S(2)}) %collective-permute-start.25) | collective-permute-done | bytes 786464 | tf_op jit(solution)/shard_map/ppermute | solution.py:413
  256.3 16.2 %collective-permute-done.17.rest_1_.rest_14_ = f32[1,1536,128]{2,1,0:T(8,128)S(1)} collective-permute-done((f32[1,1536,128]{2,1,0:T(8,128)S(1)}, f32[1,1536,128]{2,1,0:T(8,128)S(1)}, u32[]{:S(2)}, u32[]{:S(2)}) %collective-permute-start.17) | collective-permute-done | bytes 786464 | tf_op jit(solution)/shard_map/ppermute | solution.py:413
  277.1 14.6 %all_to_all.15 = f32[8,16,512]{2,1,0:T(8,128)S(1)} all-to-all(f32[8,16,512]{2,1,0:T(8,128)S(1)} %bitcast.43), channel_id=1, replica_groups=mesh['band'=4,'dom'=8] {'dom'}, dimensions={0} | all-to-all | bytes 524288 | tf_op jit(solution)/shard_map/all_to_all | solution.py:677
  291.8 12.0 %all_to_all.16 = f32[8,16,512]{2,1,0:T(8,128)S(1)} all-to-all(f32[8,16,512]{2,1,0:T(8,128)S(1)} %broadcast_in_dim.58), channel_id=1, replica_groups=mesh['band'=4,'dom'=8] {'dom'}, dimensions={0} | all-to-all | bytes 524288 | tf_op jit(solution)/shard_map/all_to_all | solution.py:679
  305.5 4.6 %collective-permute-done.47.refs_2_ = f32[128,512]{1,0:T(8,128)S(1)} collective-permute-done((f32[128,512]{1,0:T(8,128)S(1)}, f32[128,512]{1,0:T(8,128)S(1)}, u32[]{:S(2)}, u32[]{:S(2)}) %collective-permute-start.47) | collective-permute-done | bytes 262176 | tf_op jit(solution)/shard_map/ppermute | solution.py:413
  311.7 25.5 %shard_map.89 = (f32[512,512]{1,0:T(8,128)}, f32[128,512]{1,0:T(8,128)S(1)}) custom-call(s32[1]{0:T(128)} %bitcast.band_ref, f32[128,512]{1,0:T(8,128)S(1)} %bitcast.39, f32[128,512]{1,0:T(8,128)S(1)} %collective-permute-done.46.refs_1_, f32[128,512]{1,0:T(8,128)S(1)} %collective-permute-done.47.refs_2_, f32[128,512]{1,0:T(8,128)S(1)} %collective-permute-done.48.refs_3_), custom_call_target="tpu_custom_call" | custom-call | tf_op jit(solution)/shard_map/pallas_call | solution.py:579
  350.8 5.3 %shard_map.90 = f32[4,1536,128]{2,1,0:T(8,128)} custom-call(f32[128,512]{1,0:T(8,128)S(1)} %get-tuple-element.146.inverse_ref, f32[1,1536,128]{2,1,0:T(8,128)S(1)} %copy-done.4, f32[1,1536,128]{2,1,0:T(8,128)S(1)} %copy-done.14, f32[1,1536,128]{2,1,0:T(8,128)S(1)} %copy-done.12, f32[1,1536,128]{2,1,0:T(8,128)S(1)} %copy-done.18, ...), custom_call_target="tpu_custom_call" | custom-call | tf_op jit(solution)/shard_map/pallas_call | solution.py:462
  (269 shorter events, 105.8 us)
Async XLA Ops:
  9.8 12.2 %collective-permute-start.2 = (f32[8,4736]{1,0:T(8,128)S(1)}, f32[8,4736]{1,0:T(8,128)S(1)}, u32[]{:S(2)}, u32[]{:S(2)}) collective-permute-start(f32[8,4736]{1,0:T(8,128)S(1)} %reshape.268), channel_id=1, source_target_pairs={{0,7},{1,0},{2,1},{3,2},{4,3},{5,4},{6,5},{7,6},{8,15},{9,8},{10,9... | collective-permute-start | bytes 454664 | tf_op jit(solution)/shard_map/ppermute | solution.py:405
  26.3 85.8 %all-to-all-start = ((f32[8,4,208,128]{3,2,1,0:T(8,128)}), f32[8,4,208,128]{3,2,1,0:T(8,128)S(1)}, u32[]{:S(2)}, u32[]{:S(2)}) async-start(f32[8,4,208,128]{3,2,1,0:T(8,128)} %shard_map.77), calls=%async_computation | async-start | bytes 6815744 | tf_op jit(solution)/shard_map/all_to_all | solution.py:639
  30.1 116.7 %all-gather.3.cloned.1.call-start = ((), (), s32[]{:S(2)}) async-start(), calls=%async_computation.3 | async-start | bytes 1916928 | tf_op jit(solution)/shard_map/all_gather | solution.py:654
  30.4 14.2 %collective-permute-start.4 = (f32[4,8,4736]{2,1,0:T(8,128)}, f32[4,8,4736]{2,1,0:T(8,128)}, u32[]{:S(2)}, u32[]{:S(2)}) collective-permute-start(f32[4,8,4736]{2,1,0:T(8,128)} %pad_maximum_fusion.refs_0_), channel_id=1, source_target_pairs={{0,16},{8,24},{16,0},{24,8},{1,17},{9,25},{17,1},{25,9},{2,18},{10... | collective-permute-start | bytes 1818632 | tf_op jit(solution)/shard_map/ppermute | solution.py:413
  33.2 13.3 %collective-permute-start.3 = (f32[4,8,4736]{2,1,0:T(8,128)}, f32[4,8,4736]{2,1,0:T(8,128)}, u32[]{:S(2)}, u32[]{:S(2)}) collective-permute-start(f32[4,8,4736]{2,1,0:T(8,128)} %pad_maximum_fusion.refs_0_), channel_id=1, source_target_pairs={{0,8},{8,0},{16,24},{24,16},{1,9},{9,1},{17,25},{25,17},{2,10},{10... | collective-permute-start | bytes 1818632 | tf_op jit(solution)/shard_map/ppermute | solution.py:413
  137.4 13.5 %collective-permute-start.35 = (f32[1,192,128]{2,1,0:T(8,128)}, f32[1,192,128]{2,1,0:T(8,128)S(1)}, u32[]{:S(2)}, u32[]{:S(2)}) collective-permute-start(f32[1,192,128]{2,1,0:T(8,128)} %get-tuple-element.134), channel_id=1, source_target_pairs={{0,3},{1,4},{2,5},{3,6},{4,7},{5,0},{6,1},{7,2},{8,11},{9,12},{10,... | collective-permute-start | bytes 294920 | tf_op jit(solution)/shard_map/ppermute | solution.py:405
  157.0 52.9 %collective-permute-start.41 = (f32[1,1536,128]{2,1,0:T(8,128)S(1)}, f32[1,1536,128]{2,1,0:T(8,128)S(1)}, u32[]{:S(2)}, u32[]{:S(2)}) collective-permute-start(f32[1,1536,128]{2,1,0:T(8,128)S(1)} %shard_map.84.own_ref.rest_0_), channel_id=1, source_target_pairs={{0,16},{8,24},{16,0},{24,8},{1,17},{9,25},{17,1},{25,9},{2,18},{10... | collective-permute-start | bytes 2359304 | tf_op jit(solution)/shard_map/ppermute | solution.py:413
  162.9 11.9 %collective-permute-start.26 = (f32[1,192,128]{2,1,0:T(8,128)S(1)}, f32[1,192,128]{2,1,0:T(8,128)S(1)}, u32[]{:S(2)}, u32[]{:S(2)}) collective-permute-start(f32[1,192,128]{2,1,0:T(8,128)S(1)} %copy-done.62), channel_id=1, source_target_pairs={{0,2},{1,3},{2,4},{3,5},{4,6},{5,7},{6,0},{7,1},{8,10},{9,11},{10,... | collective-permute-start | bytes 294920 | tf_op jit(solution)/shard_map/ppermute | solution.py:405
  169.5 11.9 %collective-permute-start.27 = (f32[1,192,128]{2,1,0:T(8,128)S(1)}, f32[1,192,128]{2,1,0:T(8,128)S(1)}, u32[]{:S(2)}, u32[]{:S(2)}) collective-permute-start(f32[1,192,128]{2,1,0:T(8,128)S(1)} %copy-done.60), channel_id=1, source_target_pairs={{0,3},{1,4},{2,5},{3,6},{4,7},{5,0},{6,1},{7,2},{8,11},{9,12},{10,... | collective-permute-start | bytes 294920 | tf_op jit(solution)/shard_map/ppermute | solution.py:405
  181.7 12.0 %collective-permute-start.9 = (f32[1,192,128]{2,1,0:T(8,128)S(1)}, f32[1,192,128]{2,1,0:T(8,128)S(1)}, u32[]{:S(2)}, u32[]{:S(2)}) collective-permute-start(f32[1,192,128]{2,1,0:T(8,128)S(1)} %copy-done.55), channel_id=1, source_target_pairs={{0,1},{1,2},{2,3},{3,4},{4,5},{5,6},{6,7},{7,0},{8,9},{9,10},{10,1... | collective-permute-start | bytes 294920 | tf_op jit(solution)/shard_map/ppermute | solution.py:405
  187.7 11.3 %collective-permute-start.11 = (f32[1,192,128]{2,1,0:T(8,128)S(1)}, f32[1,192,128]{2,1,0:T(8,128)S(1)}, u32[]{:S(2)}, u32[]{:S(2)}) collective-permute-start(f32[1,192,128]{2,1,0:T(8,128)S(1)} %copy-done.53), channel_id=1, source_target_pairs={{0,3},{1,4},{2,5},{3,6},{4,7},{5,0},{6,1},{7,2},{8,11},{9,12},{10,... | collective-permute-start | bytes 294920 | tf_op jit(solution)/shard_map/ppermute | solution.py:405
  190.5 15.4 %collective-permute-start.12 = (f32[1,192,128]{2,1,0:T(8,128)S(1)}, f32[1,192,128]{2,1,0:T(8,128)S(1)}, u32[]{:S(2)}, u32[]{:S(2)}) collective-permute-start(f32[1,192,128]{2,1,0:T(8,128)S(1)} %copy-done.52), channel_id=1, source_target_pairs={{0,4},{1,5},{2,6},{3,7},{4,0},{5,1},{6,2},{7,3},{8,12},{9,13},{10,... | collective-permute-start | bytes 294920 | tf_op jit(solution)/shard_map/ppermute | solution.py:405
  193.7 12.3 %collective-permute-start.13 = (f32[1,192,128]{2,1,0:T(8,128)S(1)}, f32[1,192,128]{2,1,0:T(8,128)S(1)}, u32[]{:S(2)}, u32[]{:S(2)}) collective-permute-start(f32[1,192,128]{2,1,0:T(8,128)S(1)} %copy-done.51), channel_id=1, source_target_pairs={{0,5},{1,6},{2,7},{3,0},{4,1},{5,2},{6,3},{7,4},{8,13},{9,14},{10,... | collective-permute-start | bytes 294920 | tf_op jit(solution)/shard_map/ppermute | solution.py:405
  194.9 12.7 %collective-permute-start.14 = (f32[1,192,128]{2,1,0:T(8,128)S(1)}, f32[1,192,128]{2,1,0:T(8,128)S(1)}, u32[]{:S(2)}, u32[]{:S(2)}) collective-permute-start(f32[1,192,128]{2,1,0:T(8,128)S(1)} %copy-done.50), channel_id=1, source_target_pairs={{0,6},{1,7},{2,0},{3,1},{4,2},{5,3},{6,4},{7,5},{8,14},{9,15},{10,... | collective-permute-start | bytes 294920 | tf_op jit(solution)/shard_map/ppermute | solution.py:405
  205.9 11.6 %collective-permute-start.40 = (f32[1,1536,128]{2,1,0:T(8,128)S(1)}, f32[1,1536,128]{2,1,0:T(8,128)S(1)}, u32[]{:S(2)}, u32[]{:S(2)}) collective-permute-start(f32[1,1536,128]{2,1,0:T(8,128)S(1)} %shard_map.84.own_ref.rest_0_), channel_id=1, source_target_pairs={{0,8},{8,0},{16,24},{24,16},{1,9},{9,1},{17,25},{25,17},{2,10},{10... | collective-permute-start | bytes 2359304 | tf_op jit(solution)/shard_map/ppermute | solution.py:413
  206.0 20.0 %collective-permute-start.33 = (f32[1,1536,128]{2,1,0:T(8,128)S(1)}, f32[1,1536,128]{2,1,0:T(8,128)S(1)}, u32[]{:S(2)}, u32[]{:S(2)}) collective-permute-start(f32[1,1536,128]{2,1,0:T(8,128)S(1)} %shard_map.83.own_ref.rest_4_), channel_id=1, source_target_pairs={{0,16},{8,24},{16,0},{24,8},{1,17},{9,25},{17,1},{25,9},{2,18},{10... | collective-permute-start | bytes 2359304 | tf_op jit(solution)/shard_map/ppermute | solution.py:413
  209.9 17.4 %collective-permute-start.42 = (f32[1,1536,128]{2,1,0:T(8,128)S(1)}, f32[1,1536,128]{2,1,0:T(8,128)S(1)}, u32[]{:S(2)}, u32[]{:S(2)}) collective-permute-start(f32[1,1536,128]{2,1,0:T(8,128)S(1)} %collective-permute-done.41.rest_1_.rest_2_), channel_id=1, source_target_pairs={{0,8},{8,0},{16,24},{24,16},{1,9},{9,1},{17,25},{25,17},{2,10},{10... | collective-permute-start | bytes 2359304 | tf_op jit(solution)/shard_map/ppermute | solution.py:413
  210.2 20.1 %collective-permute-start.19 = (f32[1,192,128]{2,1,0:T(8,128)S(1)}, f32[1,192,128]{2,1,0:T(8,128)S(1)}, u32[]{:S(2)}, u32[]{:S(2)}) collective-permute-start(f32[1,192,128]{2,1,0:T(8,128)S(1)} %copy-done.47), channel_id=1, source_target_pairs={{0,3},{1,4},{2,5},{3,6},{4,7},{5,0},{6,1},{7,2},{8,11},{9,12},{10,... | collective-permute-start | bytes 294920 | tf_op jit(solution)/shard_map/ppermute | solution.py:405
  217.6 12.7 %collective-permute-start.20 = (f32[1,192,128]{2,1,0:T(8,128)S(1)}, f32[1,192,128]{2,1,0:T(8,128)S(1)}, u32[]{:S(2)}, u32[]{:S(2)}) collective-permute-start(f32[1,192,128]{2,1,0:T(8,128)S(1)} %copy-done.46), channel_id=1, source_target_pairs={{0,4},{1,5},{2,6},{3,7},{4,0},{5,1},{6,2},{7,3},{8,12},{9,13},{10,... | collective-permute-start | bytes 294920 | tf_op jit(solution)/shard_map/ppermute | solution.py:405
  217.6 13.1 %collective-permute-start.21 = (f32[1,192,128]{2,1,0:T(8,128)S(1)}, f32[1,192,128]{2,1,0:T(8,128)S(1)}, u32[]{:S(2)}, u32[]{:S(2)}) collective-permute-start(f32[1,192,128]{2,1,0:T(8,128)S(1)} %copy-done.45), channel_id=1, source_target_pairs={{0,5},{1,6},{2,7},{3,0},{4,1},{5,2},{6,3},{7,4},{8,13},{9,14},{10,... | collective-permute-start | bytes 294920 | tf_op jit(solution)/shard_map/ppermute | solution.py:405
  234.2 18.4 %collective-permute-start.25 = (f32[1,1536,128]{2,1,0:T(8,128)S(1)}, f32[1,1536,128]{2,1,0:T(8,128)S(1)}, u32[]{:S(2)}, u32[]{:S(2)}) collective-permute-start(f32[1,1536,128]{2,1,0:T(8,128)S(1)} %shard_map.82.own_ref.rest_8_), channel_id=1, source_target_pairs={{0,16},{8,24},{16,0},{24,8},{1,17},{9,25},{17,1},{25,9},{2,18},{10... | collective-permute-start | bytes 2359304 | tf_op jit(solution)/shard_map/ppermute | solution.py:413
  235.3 19.1 %collective-permute-start.24 = (f32[1,1536,128]{2,1,0:T(8,128)S(1)}, f32[1,1536,128]{2,1,0:T(8,128)S(1)}, u32[]{:S(2)}, u32[]{:S(2)}) collective-permute-start(f32[1,1536,128]{2,1,0:T(8,128)S(1)} %shard_map.82.own_ref.rest_8_), channel_id=1, source_target_pairs={{0,8},{8,0},{16,24},{24,16},{1,9},{9,1},{17,25},{25,17},{2,10},{10... | collective-permute-start | bytes 2359304 | tf_op jit(solution)/shard_map/ppermute | solution.py:413
  252.6 20.0 %collective-permute-start.17 = (f32[1,1536,128]{2,1,0:T(8,128)S(1)}, f32[1,1536,128]{2,1,0:T(8,128)S(1)}, u32[]{:S(2)}, u32[]{:S(2)}) collective-permute-start(f32[1,1536,128]{2,1,0:T(8,128)S(1)} %shard_map.81.own_ref.rest_12_), channel_id=1, source_target_pairs={{0,16},{8,24},{16,0},{24,8},{1,17},{9,25},{17,1},{25,9},{2,18},{10... | collective-permute-start | bytes 2359304 | tf_op jit(solution)/shard_map/ppermute | solution.py:413
  254.2 18.4 %collective-permute-start.16 = (f32[1,1536,128]{2,1,0:T(8,128)S(1)}, f32[1,1536,128]{2,1,0:T(8,128)S(1)}, u32[]{:S(2)}, u32[]{:S(2)}) collective-permute-start(f32[1,1536,128]{2,1,0:T(8,128)S(1)} %shard_map.81.own_ref.rest_12_), channel_id=1, source_target_pairs={{0,8},{8,0},{16,24},{24,16},{1,9},{9,1},{17,25},{25,17},{2,10},{10... | collective-permute-start | bytes 2359304 | tf_op jit(solution)/shard_map/ppermute | solution.py:413
  (91 other events, 1482.5 us)
Sparse Core Ops, SparseCore 0:
  66.5 69.4 all-gather.2

commit v8 on v7

--- a/solution.py
+++ b/solution.py
@@ -465,7 +465,7 @@
         in_specs=[pl.BlockSpec(inverse_rows.shape, lambda i: (0, 0)), *specs],
         out_specs=pl.BlockSpec((planes, tile, LANES), lambda i: (0, i, 0)),
         out_shape=jax.ShapeDtypeStruct((planes, cells, LANES), jnp.float32),
-        compiler_params=params(24),
+        compiler_params=params(56),
     )(inverse_rows, *[panel for group in panels for panel in group])
 
 
@@ -657,22 +657,28 @@
         everyone[:, : 3 * LANES].reshape(blocks, 3, LANES, LANES), everyone[:, 3 * LANES :, :vectors],
     )
 
-    arrived, _ = lax.optimization_barrier((arrived, payload))
     seconds = filter_orbitals(me, arrived, side_y, side_z, width, chunks)
 
-    sent, came = [], None
-    for (begin, size), packed in zip(chunks, seconds):
-        if came is not None:
-            packed, _ = lax.optimization_barrier((packed, came))
-        arrived = exchanged(packed)
-        came = arrived[1]
-        own = swap_out(me, arrived, high, low, weights, begin)
-        sent.append((own, crossed(own, 1), crossed(own, 2)))
-    panels, part = [], sent[-1][0]
-    for own, beside, across in sent:
-        across, part = lax.optimization_barrier((across, part))
-        panels.append([own, beside, across, crossed(across, 1)])
-        part = gram_rows(panels[-1]) + (part if len(panels) > 1 else 0.0)
+    came, owns, besides, acrosses = exchanged(seconds[0]), [], [], []
+    for index, (begin, size) in enumerate(chunks):
+        if index + 1 < len(chunks):
+            tied = (seconds[index + 1], came[1:3], acrosses[-1:])
+            packed, came[1:3], acrosses[-1:] = lax.optimization_barrier(tied)
+            coming = exchanged(packed)
+        own = swap_out(me, came, high, low, weights, begin)
+        owns.append(own)
+        besides.append(crossed(own, 1))
+        acrosses.append(crossed(own, 2))
+        came = coming
+    panels, part = [], None
+    for index, across in enumerate(acrosses):
+        if index + 1 < len(acrosses):
+            across, owns[index + 1] = lax.optimization_barrier((across, owns[index + 1]))
+        else:
+            across, part = lax.optimization_barrier((across, part))
+        panels.append([owns[index], besides[index], across, crossed(across, 1)])
+        rows_of = gram_rows(panels[-1])
+        part = rows_of if part is None else part + rows_of
 
     pieces = lax.all_to_all(part.reshape(blocks, width, norb), "dom", 0, 0, tiled=True)
     piece = jnp.sum(pieces, axis=0) * (1.0 / (planes * cells * blocks))

time: 364 us -> 350 us (0.962)
  waiting for transfers between devices: 128 us -> 110 us
  starting transfers between devices: 68.8 us -> 83.8 us
  local copies, waits for them, and re-layouts: 32.4 us -> 17.6 us
    ppermute x18, waiting for transfers between devices: 58.1 us -> 37.1 us  [crossed(): lax.ppermute(value, 'band', [(source, source ^ bit) for source in range(l...]
    unnamed x131 -> x101, local copies, waits for them, and re-layouts: 21.3 us -> 6.63 us
    ppermute x31, starting transfers between devices: 54.8 us -> 69.4 us  [shifted(): lax.ppermute(value, axis, [(source, (source + step) % count) for source i...]
  transfers between devices with their start and end apart: 51 -> 51, of which waited for: 21 -> 19; matrix products, arithmetic and copies ran while one was open for 3% -> 4% of each run, Pallas kernels for 14% -> 14%
where the time goes in v8:
time: 350 us; the launch traced here: 349 us
  waiting for transfers between devices  110 us (31%)
  Pallas kernels  91 us (26%)
  starting transfers between devices  83.8 us (24%)
  blocking collectives  27.3 us (8%)
  local copies, waits for them, and re-layouts  17.6 us (5%)
  between operations  14.7 us (4%)
  other arithmetic  4.62 us (1%)
    ppermute x31, starting transfers between devices, shifted(): lax.ppermute(value, axis, [(source, (source + step) % count) for source i...  69.4 us
    all_to_all x1, waiting for transfers between devices, shards(): arrived = lax.all_to_all(packed, 'dom', 0, 0, tiled=True)  45.8 us
    ppermute x18, waiting for transfers between devices, crossed(): lax.ppermute(value, 'band', [(source, source ^ bit) for source in range(l...  37.1 us
    ppermute x31, waiting for transfers between devices, shifted(): lax.ppermute(value, axis, [(source, (source + step) % count) for source i...  27 us
    pallas_call x1, Pallas kernels, cholesky_inverse(): pl.pallas_call(cholesky_kernel, in_specs=[pl.BlockSpec(memory_space=pltpu...  25.5 us
    pallas_call x1, Pallas kernels, filter_orbitals(): pl.pallas_call(functools.partial(filter_kernel, planes, side_y, side_z, w...  22 us
    all_to_all x1, blocking collectives, shards(): lax.all_to_all(part.reshape(blocks, width, norb), 'dom', 0, 0, tiled=True)  15.4 us
    pallas_call x1, Pallas kernels, build_basis(): pl.pallas_call(functools.partial(basis_kernel, planes, side_y, side_z, le...  13.5 us
  transfers between devices with their start and end apart: 51, of which 19 were waited for; matrix products, arithmetic and copies ran while one was open for 4% of the time, Pallas kernels for 14%

profile of v8, /device:TPU:0, one launch (start us, length us, event | category | flops | bytes accessed | tf_op | source)
XLA Modules:
  0.0 349.0 jit_solution(11649186159563579915)
XLA Ops:
  9.8 6.1 %collective-permute-start.2 = (f32[8,4736]{1,0:T(8,128)S(1)}, f32[8,4736]{1,0:T(8,128)S(1)}, u32[]{:S(2)}, u32[]{:S(2)}) collective-permute-start(f32[8,4736]{1,0:T(8,128)S(1)} %reshape.268), channel_id=1, source_target_pairs={{0,7},{1,0},{2,1},{3,2},{4,3},{5,4},{6,5},{7,6},{8,15},{9,8},{10,9... | collective-permute-start | bytes 454664 | tf_op jit(solution)/shard_map/ppermute | solution.py:405
  17.8 4.3 %shard_map.77 = f32[8,4,208,128]{3,2,1,0:T(8,128)} custom-call(f32[4,16,128]{2,1,0:T(8,128)S(1)} %pad.8.levels_ref, f32[4,8,192,128]{3,2,1,0:T(8,128)S(1)} %bitcast.35), custom_call_target="tpu_custom_call" | custom-call | bytes 6291456 | tf_op jit(solution)/shard_map/pallas_call | solution.py:98
  22.1 3.4 collective-permute-done.1
  26.3 3.8 %all-to-all-start = ((f32[8,4,208,128]{3,2,1,0:T(8,128)}), f32[8,4,208,128]{3,2,1,0:T(8,128)S(1)}, u32[]{:S(2)}, u32[]{:S(2)}) async-start(f32[8,4,208,128]{3,2,1,0:T(8,128)} %shard_map.77), calls=%async_computation | async-start | bytes 6815744 | tf_op jit(solution)/shard_map/all_to_all | solution.py:639
  33.4 11.2 %collective-permute-done.4.refs_2_ = f32[4,8,4736]{2,1,0:T(8,128)} collective-permute-done((f32[4,8,4736]{2,1,0:T(8,128)}, f32[4,8,4736]{2,1,0:T(8,128)}, u32[]{:S(2)}, u32[]{:S(2)}) %collective-permute-start.4) | collective-permute-done | bytes 606240 | tf_op jit(solution)/shard_map/ppermute | solution.py:413
  51.2 13.5 %shard_map.78 = (bf16[4,1536,256]{2,1,0:T(8,128)(2,1)}, bf16[4,1536,256]{2,1,0:T(8,128)(2,1)}, f32[3,128,128]{2,1,0:T(8,128)}) custom-call(f32[4,8,4736]{2,1,0:T(8,128)} %pad_maximum_fusion.refs_0_, f32[4,8,4736]{2,1,0:T(8,128)} %collective-permute-done.3.refs_1_, f32[4,8,4736]{2,1,0:T(8,128)} %collective-permute-done.4.refs_2_, ...), custom_call_target="tpu_custom_call" | custom-call | flops 157286400 | bytes 18874368 | tf_op jit(solution)/shard_map/pallas_call | solution.py:328
  66.3 45.8 %all-to-all-done.arrived_ref = f32[8,4,208,128]{3,2,1,0:T(8,128)S(1)} async-done(((f32[8,4,208,128]{3,2,1,0:T(8,128)}), f32[8,4,208,128]{3,2,1,0:T(8,128)S(1)}, u32[]{:S(2)}, u32[]{:S(2)}) %all-to-all-start) | async-done | bytes 3407904 | tf_op jit(solution)/shard_map/all_to_all | solution.py:639
  113.8 22.0 %shard_map.80 = (f32[1,192,128]{2,1,0:T(8,128)}, f32[1,192,128]{2,1,0:T(8,128)}, f32[1,192,128]{2,1,0:T(8,128)}, f32[1,192,128]{2,1,0:T(8,128)}, f32[1,192,128]{...) custom-call(s32[1]{0:T(128)} %bitcast.1.me_ref, ...), custom_call_target="tpu_custom_call" | custom-call | flops 85196800 | bytes 10223616 | tf_op jit(solution)/shard_map/pallas_call | solution.py:264
  153.5 3.3 shard_map.81.own_ref.rest_0_
  158.4 4.3 %collective-permute-start.8 = (f32[1,192,128]{2,1,0:T(8,128)S(1)}, f32[1,192,128]{2,1,0:T(8,128)S(1)}, u32[]{:S(2)}, u32[]{:S(2)}) collective-permute-start(f32[1,192,128]{2,1,0:T(8,128)S(1)} %copy-done.48), channel_id=1, source_target_pairs={{0,1},{1,2},{2,3},{3,4},{4,5},{5,6},{6,7},{7,0},{8,9},{9,10},{10,1... | collective-permute-start | bytes 294920 | tf_op jit(solution)/shard_map/ppermute | solution.py:405
  162.7 3.9 %collective-permute-start.9 = (f32[1,192,128]{2,1,0:T(8,128)S(1)}, f32[1,192,128]{2,1,0:T(8,128)S(1)}, u32[]{:S(2)}, u32[]{:S(2)}) collective-permute-start(f32[1,192,128]{2,1,0:T(8,128)S(1)} %copy-done.47), channel_id=1, source_target_pairs={{0,2},{1,3},{2,4},{3,5},{4,6},{5,7},{6,0},{7,1},{8,10},{9,11},{10,... | collective-permute-start | bytes 294920 | tf_op jit(solution)/shard_map/ppermute | solution.py:405
  176.0 7.3 %collective-permute-start.22 = (f32[1,192,128]{2,1,0:T(8,128)S(1)}, f32[1,192,128]{2,1,0:T(8,128)S(1)}, u32[]{:S(2)}, u32[]{:S(2)}) collective-permute-start(f32[1,192,128]{2,1,0:T(8,128)S(1)} %copy-done.42), channel_id=1, source_target_pairs={{0,7},{1,0},{2,1},{3,2},{4,3},{5,4},{6,5},{7,6},{8,15},{9,8},{10,9... | collective-permute-start | bytes 294920 | tf_op jit(solution)/shard_map/ppermute | solution.py:405
  189.1 4.8 %collective-permute-start.17 = (f32[1,192,128]{2,1,0:T(8,128)S(1)}, f32[1,192,128]{2,1,0:T(8,128)S(1)}, u32[]{:S(2)}, u32[]{:S(2)}) collective-permute-start(f32[1,192,128]{2,1,0:T(8,128)S(1)} %copy-done.40), channel_id=1, source_target_pairs={{0,2},{1,3},{2,4},{3,5},{4,6},{5,7},{6,0},{7,1},{8,10},{9,11},{10,... | collective-permute-start | bytes 294920 | tf_op jit(solution)/shard_map/ppermute | solution.py:405
  202.1 7.5 %collective-permute-start.39 = (f32[1,192,128]{2,1,0:T(8,128)S(1)}, f32[1,192,128]{2,1,0:T(8,128)S(1)}, u32[]{:S(2)}, u32[]{:S(2)}) collective-permute-start(f32[1,192,128]{2,1,0:T(8,128)S(1)} %copy-done.35), channel_id=1, source_target_pairs={{0,7},{1,0},{2,1},{3,2},{4,3},{5,4},{6,5},{7,6},{8,15},{9,8},{10,9... | collective-permute-start | bytes 294920 | tf_op jit(solution)/shard_map/ppermute | solution.py:405
  215.2 4.1 %collective-permute-start.25 = (f32[1,192,128]{2,1,0:T(8,128)S(1)}, f32[1,192,128]{2,1,0:T(8,128)S(1)}, u32[]{:S(2)}, u32[]{:S(2)}) collective-permute-start(f32[1,192,128]{2,1,0:T(8,128)S(1)} %copy-done.33), channel_id=1, source_target_pairs={{0,2},{1,3},{2,4},{3,5},{4,6},{5,7},{6,0},{7,1},{8,10},{9,11},{10,... | collective-permute-start | bytes 294920 | tf_op jit(solution)/shard_map/ppermute | solution.py:405
  219.3 4.1 %collective-permute-done.24.refs_1_ = f32[1,192,128]{2,1,0:T(8,128)S(1)} collective-permute-done((f32[1,192,128]{2,1,0:T(8,128)S(1)}, f32[1,192,128]{2,1,0:T(8,128)S(1)}, u32[]{:S(2)}, u32[]{:S(2)}) %collective-permute-start.24) | collective-permute-done | bytes 98336 | tf_op jit(solution)/shard_map/ppermute | solution.py:405
  225.5 6.9 %collective-permute-done.26.refs_3_ = f32[1,192,128]{2,1,0:T(8,128)S(1)} collective-permute-done((f32[1,192,128]{2,1,0:T(8,128)S(1)}, f32[1,192,128]{2,1,0:T(8,128)S(1)}, u32[]{:S(2)}, u32[]{:S(2)}) %collective-permute-start.26) | collective-permute-done | bytes 98336 | tf_op jit(solution)/shard_map/ppermute | solution.py:405
  232.4 3.3 collective-permute-start.29
  254.5 13.7 %collective-permute-done.31.rest_1_.rest_14_ = f32[1,1536,128]{2,1,0:T(8,128)S(1)} collective-permute-done((f32[1,1536,128]{2,1,0:T(8,128)S(1)}, f32[1,1536,128]{2,1,0:T(8,128)S(1)}, u32[]{:S(2)}, u32[]{:S(2)}) %collective-permute-start.31) | collective-permute-done | bytes 786464 | tf_op jit(solution)/shard_map/ppermute | solution.py:413
  271.9 15.4 %all_to_all.15 = f32[8,16,512]{2,1,0:T(8,128)S(1)} all-to-all(f32[8,16,512]{2,1,0:T(8,128)S(1)} %bitcast.43), channel_id=1, replica_groups=mesh['band'=4,'dom'=8] {'dom'}, dimensions={0} | all-to-all | bytes 524288 | tf_op jit(solution)/shard_map/all_to_all | solution.py:683
  287.3 12.0 %all_to_all.16 = f32[8,16,512]{2,1,0:T(8,128)S(1)} all-to-all(f32[8,16,512]{2,1,0:T(8,128)S(1)} %broadcast_in_dim.58), channel_id=1, replica_groups=mesh['band'=4,'dom'=8] {'dom'}, dimensions={0} | all-to-all | bytes 524288 | tf_op jit(solution)/shard_map/all_to_all | solution.py:685
  301.0 4.6 %collective-permute-done.47.refs_2_ = f32[128,512]{1,0:T(8,128)S(1)} collective-permute-done((f32[128,512]{1,0:T(8,128)S(1)}, f32[128,512]{1,0:T(8,128)S(1)}, u32[]{:S(2)}, u32[]{:S(2)}) %collective-permute-start.47) | collective-permute-done | bytes 262176 | tf_op jit(solution)/shard_map/ppermute | solution.py:413
  307.2 25.5 %shard_map.89 = (f32[512,512]{1,0:T(8,128)}, f32[128,512]{1,0:T(8,128)S(1)}) custom-call(s32[1]{0:T(128)} %bitcast.band_ref, f32[128,512]{1,0:T(8,128)S(1)} %bitcast.39, f32[128,512]{1,0:T(8,128)S(1)} %collective-permute-done.46.refs_1_, f32[128,512]{1,0:T(8,128)S(1)} %collective-permute-done.47.refs_2_, f32[128,512]{1,0:T(8,128)S(1)} %collective-permute-done.48.refs_3_), custom_call_target="tpu_custom_call" | custom-call | tf_op jit(solution)/shard_map/pallas_call | solution.py:579
  333.4 8.7 %shard_map.90 = f32[4,1536,128]{2,1,0:T(8,128)} custom-call(f32[128,512]{1,0:T(8,128)} %copy-done.19, f32[1,1536,128]{2,1,0:T(8,128)} %copy-done.3, f32[1,1536,128]{2,1,0:T(8,128)} %copy-done.10, f32[1,1536,128]{2,1,0:T(8,128)} %copy-done.7, f32[1,1536,128]{2,1,0:T(8,128)} %copy-done.11, f32[1,1536,128]{2,1,0:T(8,128)} %copy-done.4, ...), custom_call_target="tpu_custom_call" | custom-call | tf_op jit(solution)/shard_map/pallas_call | solution.py:462
  (238 shorter events, 94.9 us)
Async XLA Ops:
  9.8 12.2 %collective-permute-start.2 = (f32[8,4736]{1,0:T(8,128)S(1)}, f32[8,4736]{1,0:T(8,128)S(1)}, u32[]{:S(2)}, u32[]{:S(2)}) collective-permute-start(f32[8,4736]{1,0:T(8,128)S(1)} %reshape.268), channel_id=1, source_target_pairs={{0,7},{1,0},{2,1},{3,2},{4,3},{5,4},{6,5},{7,6},{8,15},{9,8},{10,9... | collective-permute-start | bytes 454664 | tf_op jit(solution)/shard_map/ppermute | solution.py:405
  26.3 85.8 %all-to-all-start = ((f32[8,4,208,128]{3,2,1,0:T(8,128)}), f32[8,4,208,128]{3,2,1,0:T(8,128)S(1)}, u32[]{:S(2)}, u32[]{:S(2)}) async-start(f32[8,4,208,128]{3,2,1,0:T(8,128)} %shard_map.77), calls=%async_computation | async-start | bytes 6815744 | tf_op jit(solution)/shard_map/all_to_all | solution.py:639
  30.1 116.6 %all-gather.3.cloned.1.call-start = ((), (), s32[]{:S(2)}) async-start(), calls=%async_computation.3 | async-start | bytes 1916928 | tf_op jit(solution)/shard_map/all_gather | solution.py:654
  30.4 14.2 %collective-permute-start.4 = (f32[4,8,4736]{2,1,0:T(8,128)}, f32[4,8,4736]{2,1,0:T(8,128)}, u32[]{:S(2)}, u32[]{:S(2)}) collective-permute-start(f32[4,8,4736]{2,1,0:T(8,128)} %pad_maximum_fusion.refs_0_), channel_id=1, source_target_pairs={{0,16},{8,24},{16,0},{24,8},{1,17},{9,25},{17,1},{25,9},{2,18},{10... | collective-permute-start | bytes 1818632 | tf_op jit(solution)/shard_map/ppermute | solution.py:413
  33.2 13.3 %collective-permute-start.3 = (f32[4,8,4736]{2,1,0:T(8,128)}, f32[4,8,4736]{2,1,0:T(8,128)}, u32[]{:S(2)}, u32[]{:S(2)}) collective-permute-start(f32[4,8,4736]{2,1,0:T(8,128)} %pad_maximum_fusion.refs_0_), channel_id=1, source_target_pairs={{0,8},{8,0},{16,24},{24,16},{1,9},{9,1},{17,25},{25,17},{2,10},{10... | collective-permute-start | bytes 1818632 | tf_op jit(solution)/shard_map/ppermute | solution.py:413
  137.4 13.5 %collective-permute-start.10 = (f32[1,192,128]{2,1,0:T(8,128)}, f32[1,192,128]{2,1,0:T(8,128)S(1)}, u32[]{:S(2)}, u32[]{:S(2)}) collective-permute-start(f32[1,192,128]{2,1,0:T(8,128)} %get-tuple-element.121), channel_id=1, source_target_pairs={{0,3},{1,4},{2,5},{3,6},{4,7},{5,0},{6,1},{7,2},{8,11},{9,12},{10,... | collective-permute-start | bytes 294920 | tf_op jit(solution)/shard_map/ppermute | solution.py:405
  140.3 11.2 %collective-permute-start.11 = (f32[1,192,128]{2,1,0:T(8,128)}, f32[1,192,128]{2,1,0:T(8,128)}, u32[]{:S(2)}, u32[]{:S(2)}) collective-permute-start(f32[1,192,128]{2,1,0:T(8,128)} %get-tuple-element.122), channel_id=1, source_target_pairs={{0,4},{1,5},{2,6},{3,7},{4,0},{5,1},{6,2},{7,3},{8,12},{9,13},{10,... | collective-permute-start | bytes 294920 | tf_op jit(solution)/shard_map/ppermute | solution.py:405
  141.3 10.2 %collective-permute-start.12 = (f32[1,192,128]{2,1,0:T(8,128)}, f32[1,192,128]{2,1,0:T(8,128)}, u32[]{:S(2)}, u32[]{:S(2)}) collective-permute-start(f32[1,192,128]{2,1,0:T(8,128)} %get-tuple-element.123), channel_id=1, source_target_pairs={{0,5},{1,6},{2,7},{3,0},{4,1},{5,2},{6,3},{7,4},{8,13},{9,14},{10,... | collective-permute-start | bytes 294920 | tf_op jit(solution)/shard_map/ppermute | solution.py:405
  156.8 19.2 %collective-permute-start.15 = (f32[1,1536,128]{2,1,0:T(8,128)S(1)}, f32[1,1536,128]{2,1,0:T(8,128)S(1)}, u32[]{:S(2)}, u32[]{:S(2)}) collective-permute-start(f32[1,1536,128]{2,1,0:T(8,128)S(1)} %shard_map.81.own_ref.rest_0_), channel_id=1, source_target_pairs={{0,16},{8,24},{16,0},{24,8},{1,17},{9,25},{17,1},{25,9},{2,18},{10... | collective-permute-start | bytes 2359304 | tf_op jit(solution)/shard_map/ppermute | solution.py:413
  158.4 10.9 %collective-permute-start.8 = (f32[1,192,128]{2,1,0:T(8,128)S(1)}, f32[1,192,128]{2,1,0:T(8,128)S(1)}, u32[]{:S(2)}, u32[]{:S(2)}) collective-permute-start(f32[1,192,128]{2,1,0:T(8,128)S(1)} %copy-done.48), channel_id=1, source_target_pairs={{0,1},{1,2},{2,3},{3,4},{4,5},{5,6},{6,7},{7,0},{8,9},{9,10},{10,1... | collective-permute-start | bytes 294920 | tf_op jit(solution)/shard_map/ppermute | solution.py:405
  166.6 16.7 %collective-permute-start.18 = (f32[1,192,128]{2,1,0:T(8,128)S(1)}, f32[1,192,128]{2,1,0:T(8,128)S(1)}, u32[]{:S(2)}, u32[]{:S(2)}) collective-permute-start(f32[1,192,128]{2,1,0:T(8,128)S(1)} %copy-done.46), channel_id=1, source_target_pairs={{0,3},{1,4},{2,5},{3,6},{4,7},{5,0},{6,1},{7,2},{8,11},{9,12},{10,... | collective-permute-start | bytes 294920 | tf_op jit(solution)/shard_map/ppermute | solution.py:405
  168.5 14.8 %collective-permute-start.19 = (f32[1,192,128]{2,1,0:T(8,128)S(1)}, f32[1,192,128]{2,1,0:T(8,128)S(1)}, u32[]{:S(2)}, u32[]{:S(2)}) collective-permute-start(f32[1,192,128]{2,1,0:T(8,128)S(1)} %copy-done.45), channel_id=1, source_target_pairs={{0,4},{1,5},{2,6},{3,7},{4,0},{5,1},{6,2},{7,3},{8,12},{9,13},{10,... | collective-permute-start | bytes 294920 | tf_op jit(solution)/shard_map/ppermute | solution.py:405
  169.3 14.1 %collective-permute-start.20 = (f32[1,192,128]{2,1,0:T(8,128)S(1)}, f32[1,192,128]{2,1,0:T(8,128)S(1)}, u32[]{:S(2)}, u32[]{:S(2)}) collective-permute-start(f32[1,192,128]{2,1,0:T(8,128)S(1)} %copy-done.44), channel_id=1, source_target_pairs={{0,5},{1,6},{2,7},{3,0},{4,1},{5,2},{6,3},{7,4},{8,13},{9,14},{10,... | collective-permute-start | bytes 294920 | tf_op jit(solution)/shard_map/ppermute | solution.py:405
  172.3 11.1 %collective-permute-start.21 = (f32[1,192,128]{2,1,0:T(8,128)S(1)}, f32[1,192,128]{2,1,0:T(8,128)S(1)}, u32[]{:S(2)}, u32[]{:S(2)}) collective-permute-start(f32[1,192,128]{2,1,0:T(8,128)S(1)} %copy-done.43), channel_id=1, source_target_pairs={{0,6},{1,7},{2,0},{3,1},{4,2},{5,3},{6,4},{7,5},{8,14},{9,15},{10,... | collective-permute-start | bytes 294920 | tf_op jit(solution)/shard_map/ppermute | solution.py:405
  187.7 14.4 %collective-permute-start.23 = (f32[1,1536,128]{2,1,0:T(8,128)S(1)}, f32[1,1536,128]{2,1,0:T(8,128)S(1)}, u32[]{:S(2)}, u32[]{:S(2)}) collective-permute-start(f32[1,1536,128]{2,1,0:T(8,128)S(1)} %shard_map.82.own_ref.rest_4_), channel_id=1, source_target_pairs={{0,16},{8,24},{16,0},{24,8},{1,17},{9,25},{17,1},{25,9},{2,18},{10... | collective-permute-start | bytes 2359304 | tf_op jit(solution)/shard_map/ppermute | solution.py:413
  193.9 15.8 %collective-permute-start.35 = (f32[1,192,128]{2,1,0:T(8,128)S(1)}, f32[1,192,128]{2,1,0:T(8,128)S(1)}, u32[]{:S(2)}, u32[]{:S(2)}) collective-permute-start(f32[1,192,128]{2,1,0:T(8,128)S(1)} %copy-done.39), channel_id=1, source_target_pairs={{0,3},{1,4},{2,5},{3,6},{4,7},{5,0},{6,1},{7,2},{8,11},{9,12},{10,... | collective-permute-start | bytes 294920 | tf_op jit(solution)/shard_map/ppermute | solution.py:405
  193.9 15.8 %collective-permute-start.36 = (f32[1,192,128]{2,1,0:T(8,128)S(1)}, f32[1,192,128]{2,1,0:T(8,128)S(1)}, u32[]{:S(2)}, u32[]{:S(2)}) collective-permute-start(f32[1,192,128]{2,1,0:T(8,128)S(1)} %copy-done.38), channel_id=1, source_target_pairs={{0,4},{1,5},{2,6},{3,7},{4,0},{5,1},{6,2},{7,3},{8,12},{9,13},{10,... | collective-permute-start | bytes 294920 | tf_op jit(solution)/shard_map/ppermute | solution.py:405
  197.0 12.6 %collective-permute-start.37 = (f32[1,192,128]{2,1,0:T(8,128)S(1)}, f32[1,192,128]{2,1,0:T(8,128)S(1)}, u32[]{:S(2)}, u32[]{:S(2)}) collective-permute-start(f32[1,192,128]{2,1,0:T(8,128)S(1)} %copy-done.37), channel_id=1, source_target_pairs={{0,5},{1,6},{2,7},{3,0},{4,1},{5,2},{6,3},{7,4},{8,13},{9,14},{10,... | collective-permute-start | bytes 294920 | tf_op jit(solution)/shard_map/ppermute | solution.py:405
  198.4 11.3 %collective-permute-start.38 = (f32[1,192,128]{2,1,0:T(8,128)S(1)}, f32[1,192,128]{2,1,0:T(8,128)S(1)}, u32[]{:S(2)}, u32[]{:S(2)}) collective-permute-start(f32[1,192,128]{2,1,0:T(8,128)S(1)} %copy-done.36), channel_id=1, source_target_pairs={{0,6},{1,7},{2,0},{3,1},{4,2},{5,3},{6,4},{7,5},{8,14},{9,15},{10,... | collective-permute-start | bytes 294920 | tf_op jit(solution)/shard_map/ppermute | solution.py:405
  214.0 32.1 %collective-permute-start.42 = (f32[1,1536,128]{2,1,0:T(8,128)S(1)}, f32[1,1536,128]{2,1,0:T(8,128)S(1)}, u32[]{:S(2)}, u32[]{:S(2)}) collective-permute-start(f32[1,1536,128]{2,1,0:T(8,128)S(1)} %shard_map.85.own_ref.rest_8_), channel_id=1, source_target_pairs={{0,16},{8,24},{16,0},{24,8},{1,17},{9,25},{17,1},{25,9},{2,18},{10... | collective-permute-start | bytes 2359304 | tf_op jit(solution)/shard_map/ppermute | solution.py:413
  214.7 32.0 %collective-permute-start.32 = (f32[1,1536,128]{2,1,0:T(8,128)S(1)}, f32[1,1536,128]{2,1,0:T(8,128)S(1)}, u32[]{:S(2)}, u32[]{:S(2)}) collective-permute-start(f32[1,1536,128]{2,1,0:T(8,128)S(1)} %shard_map.81.own_ref.rest_0_), channel_id=1, source_target_pairs={{0,8},{8,0},{16,24},{24,16},{1,9},{9,1},{17,25},{25,17},{2,10},{10... | collective-permute-start | bytes 2359304 | tf_op jit(solution)/shard_map/ppermute | solution.py:413
  215.0 31.8 %collective-permute-start.33 = (f32[1,1536,128]{2,1,0:T(8,128)S(1)}, f32[1,1536,128]{2,1,0:T(8,128)S(1)}, u32[]{:S(2)}, u32[]{:S(2)}) collective-permute-start(f32[1,1536,128]{2,1,0:T(8,128)S(1)} %collective-permute-done.15.rest_1_.rest_2_), channel_id=1, source_target_pairs={{0,8},{8,0},{16,24},{24,16},{1,9},{9,1},{17,25},{25,17},{2,10},{10... | collective-permute-start | bytes 2359304 | tf_op jit(solution)/shard_map/ppermute | solution.py:413
  246.8 21.4 %collective-permute-start.31 = (f32[1,1536,128]{2,1,0:T(8,128)S(1)}, f32[1,1536,128]{2,1,0:T(8,128)S(1)}, u32[]{:S(2)}, u32[]{:S(2)}) collective-permute-start(f32[1,1536,128]{2,1,0:T(8,128)S(1)} %shard_map.83.own_ref.rest_12_), channel_id=1, source_target_pairs={{0,16},{8,24},{16,0},{24,8},{1,17},{9,25},{17,1},{25,9},{2,18},{10... | collective-permute-start | bytes 2359304 | tf_op jit(solution)/shard_map/ppermute | solution.py:413
  251.4 16.8 %collective-permute-start.44 = (f32[1,1536,128]{2,1,0:T(8,128)S(1)}, f32[1,1536,128]{2,1,0:T(8,128)S(1)}, u32[]{:S(2)}, u32[]{:S(2)}) collective-permute-start(f32[1,1536,128]{2,1,0:T(8,128)S(1)} %shard_map.83.own_ref.rest_12_), channel_id=1, source_target_pairs={{0,8},{8,0},{16,24},{24,16},{1,9},{9,1},{17,25},{25,17},{2,10},{10... | collective-permute-start | bytes 2359304 | tf_op jit(solution)/shard_map/ppermute | solution.py:413
  (76 other events, 1178.7 us)
Sparse Core Ops, SparseCore 0:
  66.5 69.4 all-gather.2

commit v9 on v8

--- a/solution.py
+++ b/solution.py
@@ -110,9 +110,9 @@
 
 
 def swap_out_kernel(me_ref, high_ref, low_ref, weights_ref, *refs):
-    arrived_refs, out_ref = refs[:-1], refs[-1]
+    planes, rows, _ = refs[0].shape
+    arrived_refs, out_refs = refs[:-planes], refs[-planes:]
     count = len(arrived_refs)
-    planes, rows, _ = arrived_refs[0].shape
     weights = side_by_side(weights_ref[...] * (1.0 / 18.0))
     for plane in range(planes):
 
@@ -121,7 +121,7 @@
 
         def write(block, start, size, value):
             at = pl.ds(pl.multiple_of(block * rows + start, 8), size)
-            out_ref[plane, at, :] = value
+            out_refs[plane][at, :] = value
 
         swap_into(read, write, count, rows, after=me_ref[0])
         tile = rows * count // 6
@@ -129,7 +129,7 @@
         def add(index, carry):
             at = pl.ds(pl.multiple_of(index * tile, 8), tile)
             term = folded(dot_halves((high_ref[plane, at, :], low_ref[plane, at, :]), weights))
-            out_ref[plane, at, :] = out_ref[plane, at, :] + term
+            out_refs[plane][at, :] = out_refs[plane][at, :] + term
             return carry
 
         lax.fori_loop(0, 6, add, 0)
@@ -150,8 +150,8 @@
             pl.BlockSpec(weights.shape, lambda i: (0, 0)),
         ]
         + [pl.BlockSpec(arrived[0].shape, lambda i: (0, 0, 0))] * count,
-        out_specs=pl.BlockSpec((planes, cells, LANES), lambda i: (0, 0, 0)),
-        out_shape=jax.ShapeDtypeStruct((planes, cells, LANES), jnp.float32),
+        out_specs=[pl.BlockSpec((None, cells, LANES), lambda i: (0, 0, 0))] * planes,
+        out_shape=[jax.ShapeDtypeStruct((1, cells, LANES), jnp.float32)] * planes,
         compiler_params=params(24),
         cost_estimate=cost(0, 24 * cells * planes * LANES),
     )(me, high, low, weights, *arrived)
@@ -625,6 +625,8 @@
     width = local_orbs // blocks
     norb = local_orbs * bands
     chunks = tuple((plane, 1) for plane in range(planes))
+    half = planes // 2
+    groups = ((0, half), (half, half))
     me = lax.axis_index("dom").astype(jnp.int32).reshape(1)
 
     order = jnp.arange(bands, dtype=jnp.int32) ^ band
@@ -657,25 +659,25 @@
         everyone[:, : 3 * LANES].reshape(blocks, 3, LANES, LANES), everyone[:, 3 * LANES :, :vectors],
     )
 
-    seconds = filter_orbitals(me, arrived, side_y, side_z, width, chunks)
-
-    came, owns, besides, acrosses = exchanged(seconds[0]), [], [], []
-    for index, (begin, size) in enumerate(chunks):
-        if index + 1 < len(chunks):
-            tied = (seconds[index + 1], came[1:3], acrosses[-1:])
-            packed, came[1:3], acrosses[-1:] = lax.optimization_barrier(tied)
-            coming = exchanged(packed)
-        own = swap_out(me, came, high, low, weights, begin)
-        owns.append(own)
-        besides.append(crossed(own, 1))
-        acrosses.append(crossed(own, 2))
-        came = coming
+    seconds = filter_orbitals(me, arrived, side_y, side_z, width, groups)
+
+    tie = lax.optimization_barrier
+    came = exchanged(seconds[0])
+    packed, came[1:3] = tie((seconds[1], came[1:3]))
+    coming = exchanged(packed)
+    owns = list(swap_out(me, came, high, low, weights, 0))
+    acrosses = [crossed(own, 2) for own in owns]
+    besides = [crossed(own, 1) for own in owns]
+    coming, acrosses[0] = tie((coming, acrosses[0]))
+    late = list(swap_out(me, coming, high, low, weights, half))
+    late, acrosses[1:] = tie((late, acrosses[1:]))
+    acrosses += [crossed(own, 2) for own in late]
+    besides += [crossed(own, 1) for own in late]
+    owns += late
     panels, part = [], None
     for index, across in enumerate(acrosses):
-        if index + 1 < len(acrosses):
-            across, owns[index + 1] = lax.optimization_barrier((across, owns[index + 1]))
-        else:
-            across, part = lax.optimization_barrier((across, part))
+        if index >= half:
+            across, part = tie((across, part))
         panels.append([owns[index], besides[index], across, crossed(across, 1)])
         rows_of = gram_rows(panels[-1])
         part = rows_of if part is None else part + rows_of

time: 350 us -> 353 us (level)
  waiting for transfers between devices: 110 us -> 117 us
  starting transfers between devices: 83.8 us -> 79.2 us
    ppermute x18, waiting for transfers between devices: 37.1 us -> 52.2 us  [crossed(): lax.ppermute(value, 'band', [(source, source ^ bit) for source in range(l...]
    ppermute x31 -> x17, waiting for transfers between devices: 27 us -> 19.3 us  [shifted(): lax.ppermute(value, axis, [(source, (source + step) % count) for source i...]
    ppermute x31 -> x17, starting transfers between devices: 69.4 us -> 66.3 us  [shifted(): lax.ppermute(value, axis, [(source, (source + step) % count) for source i...]
    unnamed x101 -> x73, local copies, waits for them, and re-layouts: 6.63 us -> 7.29 us
    pallas_call x4 -> x2, Pallas kernels: 9.93 us -> 10.2 us  [swap_out(): pl.pallas_call(swap_out_kernel, grid=(1,), in_specs=[pl.BlockSpec(memory_...]
  transfers between devices with their start and end apart: 51 -> 37, of which waited for: 19 -> 16; matrix products, arithmetic and copies ran while one was open for 4% -> 4% of each run, Pallas kernels for 14% -> 14%
where the time goes in v9:
time: 353 us
  waiting for transfers between devices  117 us (33%)
  Pallas kernels  91.2 us (26%)
  starting transfers between devices  79.2 us (22%)
  blocking collectives  27.4 us (8%)
  local copies, waits for them, and re-layouts  18.4 us (5%)
  between operations  14.5 us (4%)
  other arithmetic  4.64 us (1%)
    ppermute x17, starting transfers between devices, shifted(): lax.ppermute(value, axis, [(source, (source + step) % count) for source i...  66.3 us
    ppermute x18, waiting for transfers between devices, crossed(): lax.ppermute(value, 'band', [(source, source ^ bit) for source in range(l...  52.2 us
    all_to_all x1, waiting for transfers between devices, shards(): arrived = lax.all_to_all(packed, 'dom', 0, 0, tiled=True)  45.8 us
    pallas_call x1, Pallas kernels, cholesky_inverse(): pl.pallas_call(cholesky_kernel, in_specs=[pl.BlockSpec(memory_space=pltpu...  25.5 us
    pallas_call x1, Pallas kernels, filter_orbitals(): pl.pallas_call(functools.partial(filter_kernel, planes, side_y, side_z, w...  22 us
    ppermute x17, waiting for transfers between devices, shifted(): lax.ppermute(value, axis, [(source, (source + step) % count) for source i...  19.3 us
    all_to_all x1, blocking collectives, shards(): lax.all_to_all(part.reshape(blocks, width, norb), 'dom', 0, 0, tiled=True)  15.5 us
    pallas_call x1, Pallas kernels, build_basis(): pl.pallas_call(functools.partial(basis_kernel, planes, side_y, side_z, le...  13.5 us
  transfers between devices with their start and end apart: 37, of which 16 were waited for; matrix products, arithmetic and copies ran while one was open for 4% of the time, Pallas kernels for 14%

profile of v9, /device:TPU:0, one launch (start us, length us, event | category | flops | bytes accessed | tf_op | source)
XLA Modules:
  0.0 352.6 jit_solution(6151473148073329103)
XLA Ops:
  9.8 6.1 %collective-permute-start.2 = (f32[8,4736]{1,0:T(8,128)S(1)}, f32[8,4736]{1,0:T(8,128)S(1)}, u32[]{:S(2)}, u32[]{:S(2)}) collective-permute-start(f32[8,4736]{1,0:T(8,128)S(1)} %reshape.268), channel_id=1, source_target_pairs={{0,7},{1,0},{2,1},{3,2},{4,3},{5,4},{6,5},{7,6},{8,15},{9,8},{10,9... | collective-permute-start | bytes 454664 | tf_op jit(solution)/shard_map/ppermute | solution.py:405
  17.8 4.2 %shard_map.77 = f32[8,4,208,128]{3,2,1,0:T(8,128)} custom-call(f32[4,16,128]{2,1,0:T(8,128)S(1)} %pad.8.levels_ref, f32[4,8,192,128]{3,2,1,0:T(8,128)S(1)} %bitcast.35), custom_call_target="tpu_custom_call" | custom-call | bytes 6291456 | tf_op jit(solution)/shard_map/pallas_call | solution.py:98
  22.1 3.4 collective-permute-done.1
  26.3 3.8 %all-to-all-start = ((f32[8,4,208,128]{3,2,1,0:T(8,128)}), f32[8,4,208,128]{3,2,1,0:T(8,128)S(1)}, u32[]{:S(2)}, u32[]{:S(2)}) async-start(f32[8,4,208,128]{3,2,1,0:T(8,128)} %shard_map.77), calls=%async_computation | async-start | bytes 6815744 | tf_op jit(solution)/shard_map/all_to_all | solution.py:641
  33.4 11.2 %collective-permute-done.4.refs_2_ = f32[4,8,4736]{2,1,0:T(8,128)} collective-permute-done((f32[4,8,4736]{2,1,0:T(8,128)}, f32[4,8,4736]{2,1,0:T(8,128)}, u32[]{:S(2)}, u32[]{:S(2)}) %collective-permute-start.4) | collective-permute-done | bytes 606240 | tf_op jit(solution)/shard_map/ppermute | solution.py:413
  51.2 13.5 %shard_map.78 = (bf16[4,1536,256]{2,1,0:T(8,128)(2,1)}, bf16[4,1536,256]{2,1,0:T(8,128)(2,1)}, f32[3,128,128]{2,1,0:T(8,128)}) custom-call(f32[4,8,4736]{2,1,0:T(8,128)} %pad_maximum_fusion.refs_0_, f32[4,8,4736]{2,1,0:T(8,128)} %collective-permute-done.3.refs_1_, f32[4,8,4736]{2,1,0:T(8,128)} %collective-permute-done.4.refs_2_, ...), custom_call_target="tpu_custom_call" | custom-call | flops 157286400 | bytes 18874368 | tf_op jit(solution)/shard_map/pallas_call | solution.py:328
  66.3 45.8 %all-to-all-done.arrived_ref = f32[8,4,208,128]{3,2,1,0:T(8,128)S(1)} async-done(((f32[8,4,208,128]{3,2,1,0:T(8,128)}), f32[8,4,208,128]{3,2,1,0:T(8,128)S(1)}, u32[]{:S(2)}, u32[]{:S(2)}) %all-to-all-start) | async-done | bytes 3407904 | tf_op jit(solution)/shard_map/all_to_all | solution.py:641
  113.9 22.0 %shard_map.80 = (f32[2,192,128]{2,1,0:T(8,128)}, f32[2,192,128]{2,1,0:T(8,128)}, f32[2,192,128]{2,1,0:T(8,128)}, f32[2,192,128]{2,1,0:T(8,128)}, f32[2,192,128]{...) custom-call(s32[1]{0:T(128)} %bitcast.1.me_ref, ...), custom_call_target="tpu_custom_call" | custom-call | flops 85196800 | bytes 10223616 | tf_op jit(solution)/shard_map/pallas_call | solution.py:264
  143.2 3.6 %collective-permute-done.6.refs_1_ = f32[2,192,128]{2,1,0:T(8,128)S(1)} collective-permute-done((f32[2,192,128]{2,1,0:T(8,128)}, f32[2,192,128]{2,1,0:T(8,128)S(1)}, u32[]{:S(2)}, u32[]{:S(2)}) %collective-permute-start.6) | collective-permute-done | bytes 196640 | tf_op jit(solution)/shard_map/ppermute | solution.py:405
  148.8 4.4 %collective-permute-start.19 = (f32[2,192,128]{2,1,0:T(8,128)}, f32[2,192,128]{2,1,0:T(8,128)}, u32[]{:S(2)}, u32[]{:S(2)}) collective-permute-start(f32[2,192,128]{2,1,0:T(8,128)} %get-tuple-element.89), channel_id=1, source_target_pairs={{0,7},{1,0},{2,1},{3,2},{4,3},{5,4},{6,5},{7,6},{8,15},{9,8},{10,9... | collective-permute-start | bytes 589832 | tf_op jit(solution)/shard_map/ppermute | solution.py:405
  164.1 5.8 %shard_map.81 = (f32[1,1536,128]{2,1,0:T(8,128)S(1)}, f32[1,1536,128]{2,1,0:T(8,128)S(1)}) custom-call(s32[1]{0:T(128)} %bitcast.1.me_ref, bf16[4,1536,256]{2,1,0:T(8,128)(2,1)S(1)} %copy-done.1, bf16[4,1536,256]{2,1,0:T(8,128)(2,1)S(1)} %copy-done.2, f32[256,128]{1,0:T(8,128)S(1)} %shard_map.79.weights_ref, f32[2,192,128]{2,1,0:T(8,128)S(1)} %copy-done.21, ...), custom_call_target="tpu_custom_call" | custom-call | bytes 9437184 | tf_op jit(solution)/shard_map/pallas_call | solution.py:143
  172.0 5.6 %collective-permute-start.8 = (f32[2,192,128]{2,1,0:T(8,128)S(1)}, f32[2,192,128]{2,1,0:T(8,128)S(1)}, u32[]{:S(2)}, u32[]{:S(2)}) collective-permute-start(f32[2,192,128]{2,1,0:T(8,128)S(1)} %copy-done.34), channel_id=1, source_target_pairs={{0,1},{1,2},{2,3},{3,4},{4,5},{5,6},{6,7},{7,0},{8,9},{9,10},{10,1... | collective-permute-start | bytes 589832 | tf_op jit(solution)/shard_map/ppermute | solution.py:405
  177.6 8.9 %collective-permute-start.9 = (f32[2,192,128]{2,1,0:T(8,128)S(1)}, f32[2,192,128]{2,1,0:T(8,128)S(1)}, u32[]{:S(2)}, u32[]{:S(2)}) collective-permute-start(f32[2,192,128]{2,1,0:T(8,128)S(1)} %copy-done.33), channel_id=1, source_target_pairs={{0,2},{1,3},{2,4},{3,5},{4,6},{5,7},{6,0},{7,1},{8,10},{9,11},{10,... | collective-permute-start | bytes 589832 | tf_op jit(solution)/shard_map/ppermute | solution.py:405
  189.5 5.2 %collective-permute-start.11 = (f32[2,192,128]{2,1,0:T(8,128)S(1)}, f32[2,192,128]{2,1,0:T(8,128)S(1)}, u32[]{:S(2)}, u32[]{:S(2)}) collective-permute-start(f32[2,192,128]{2,1,0:T(8,128)S(1)} %copy-done.31), channel_id=1, source_target_pairs={{0,4},{1,5},{2,6},{3,7},{4,0},{5,1},{6,2},{7,3},{8,12},{9,13},{10,... | collective-permute-start | bytes 589832 | tf_op jit(solution)/shard_map/ppermute | solution.py:405
  194.8 19.5 %collective-permute-start.12 = (f32[2,192,128]{2,1,0:T(8,128)S(1)}, f32[2,192,128]{2,1,0:T(8,128)S(1)}, u32[]{:S(2)}, u32[]{:S(2)}) collective-permute-start(f32[2,192,128]{2,1,0:T(8,128)S(1)} %copy-done.30), channel_id=1, source_target_pairs={{0,5},{1,6},{2,7},{3,0},{4,1},{5,2},{6,3},{7,4},{8,13},{9,14},{10,... | collective-permute-start | bytes 589832 | tf_op jit(solution)/shard_map/ppermute | solution.py:405
  214.2 5.1 %collective-permute-start.13 = (f32[2,192,128]{2,1,0:T(8,128)S(1)}, f32[2,192,128]{2,1,0:T(8,128)S(1)}, u32[]{:S(2)}, u32[]{:S(2)}) collective-permute-start(f32[2,192,128]{2,1,0:T(8,128)S(1)} %copy-done.29), channel_id=1, source_target_pairs={{0,6},{1,7},{2,0},{3,1},{4,2},{5,3},{6,4},{7,5},{8,14},{9,15},{10,... | collective-permute-start | bytes 589832 | tf_op jit(solution)/shard_map/ppermute | solution.py:405
  227.3 4.4 %shard_map.82 = (f32[1,1536,128]{2,1,0:T(8,128)S(1)}, f32[1,1536,128]{2,1,0:T(8,128)S(1)}) custom-call(s32[1]{0:T(128)} %bitcast.1.me_ref, bf16[4,1536,256]{2,1,0:T(8,128)(2,1)S(1)} %copy-done.1, bf16[4,1536,256]{2,1,0:T(8,128)(2,1)S(1)} %copy-done.2, f32[256,128]{1,0:T(8,128)S(1)} %shard_map.79.weights_ref, f32[2,192,128]{2,1,0:T(8,128)S(1)} %copy-done.20, ...), custom_call_target="tpu_custom_call" | custom-call | bytes 9437184 | tf_op jit(solution)/shard_map/pallas_call | solution.py:143
  236.3 15.4 %collective-permute-done.23.rest_1_.rest_10_ = f32[1,1536,128]{2,1,0:T(8,128)S(1)} collective-permute-done((f32[1,1536,128]{2,1,0:T(8,128)S(1)}, f32[1,1536,128]{2,1,0:T(8,128)S(1)}, u32[]{:S(2)}, u32[]{:S(2)}) %collective-permute-start.23) | collective-permute-done | bytes 786464 | tf_op jit(solution)/shard_map/ppermute | solution.py:413
  255.4 16.3 %collective-permute-done.22.rest_1_.rest_14_ = f32[1,1536,128]{2,1,0:T(8,128)S(1)} collective-permute-done((f32[1,1536,128]{2,1,0:T(8,128)S(1)}, f32[1,1536,128]{2,1,0:T(8,128)S(1)}, u32[]{:S(2)}, u32[]{:S(2)}) %collective-permute-start.22) | collective-permute-done | bytes 786464 | tf_op jit(solution)/shard_map/ppermute | solution.py:413
  275.4 15.5 %all_to_all.15 = f32[8,16,512]{2,1,0:T(8,128)S(1)} all-to-all(f32[8,16,512]{2,1,0:T(8,128)S(1)} %bitcast.43), channel_id=1, replica_groups=mesh['band'=4,'dom'=8] {'dom'}, dimensions={0} | all-to-all | bytes 524288 | tf_op jit(solution)/shard_map/all_to_all | solution.py:685
  291.0 12.0 %all_to_all.16 = f32[8,16,512]{2,1,0:T(8,128)S(1)} all-to-all(f32[8,16,512]{2,1,0:T(8,128)S(1)} %broadcast_in_dim.58), channel_id=1, replica_groups=mesh['band'=4,'dom'=8] {'dom'}, dimensions={0} | all-to-all | bytes 524288 | tf_op jit(solution)/shard_map/all_to_all | solution.py:687
  304.4 4.9 %collective-permute-done.33.refs_2_ = f32[128,512]{1,0:T(8,128)S(1)} collective-permute-done((f32[128,512]{1,0:T(8,128)S(1)}, f32[128,512]{1,0:T(8,128)S(1)}, u32[]{:S(2)}, u32[]{:S(2)}) %collective-permute-start.33) | collective-permute-done | bytes 262176 | tf_op jit(solution)/shard_map/ppermute | solution.py:413
  310.8 25.5 %shard_map.87 = (f32[512,512]{1,0:T(8,128)}, f32[128,512]{1,0:T(8,128)S(1)}) custom-call(s32[1]{0:T(128)} %bitcast.band_ref, f32[128,512]{1,0:T(8,128)S(1)} %bitcast.39, f32[128,512]{1,0:T(8,128)S(1)} %collective-permute-done.32.refs_1_, f32[128,512]{1,0:T(8,128)S(1)} %collective-permute-done.33.refs_2_, f32[128,512]{1,0:T(8,128)S(1)} %collective-permute-done.34.refs_3_), custom_call_target="tpu_custom_call" | custom-call | tf_op jit(solution)/shard_map/pallas_call | solution.py:579
  337.0 8.7 %shard_map.88 = f32[4,1536,128]{2,1,0:T(8,128)} custom-call(f32[128,512]{1,0:T(8,128)} %copy-done.19, f32[1,1536,128]{2,1,0:T(8,128)} %copy-done.3, f32[1,1536,128]{2,1,0:T(8,128)} %copy-done.7, f32[1,1536,128]{2,1,0:T(8,128)} %copy-done.5, f32[1,1536,128]{2,1,0:T(8,128)} %copy-done.8, f32[1,1536,128]{2,1,0:T(8,128)} %copy-done.4, ...), custom_call_target="tpu_custom_call" | custom-call | tf_op jit(solution)/shard_map/pallas_call | solution.py:462
  (181 shorter events, 67.4 us)
Async XLA Ops:
  9.8 12.2 %collective-permute-start.2 = (f32[8,4736]{1,0:T(8,128)S(1)}, f32[8,4736]{1,0:T(8,128)S(1)}, u32[]{:S(2)}, u32[]{:S(2)}) collective-permute-start(f32[8,4736]{1,0:T(8,128)S(1)} %reshape.268), channel_id=1, source_target_pairs={{0,7},{1,0},{2,1},{3,2},{4,3},{5,4},{6,5},{7,6},{8,15},{9,8},{10,9... | collective-permute-start | bytes 454664 | tf_op jit(solution)/shard_map/ppermute | solution.py:405
  26.3 85.8 %all-to-all-start = ((f32[8,4,208,128]{3,2,1,0:T(8,128)}), f32[8,4,208,128]{3,2,1,0:T(8,128)S(1)}, u32[]{:S(2)}, u32[]{:S(2)}) async-start(f32[8,4,208,128]{3,2,1,0:T(8,128)} %shard_map.77), calls=%async_computation | async-start | bytes 6815744 | tf_op jit(solution)/shard_map/all_to_all | solution.py:641
  30.1 123.0 %all-gather.3.cloned.1.call-start = ((), (), s32[]{:S(2)}) async-start(), calls=%async_computation.3 | async-start | bytes 1916928 | tf_op jit(solution)/shard_map/all_gather | solution.py:656
  30.4 14.2 %collective-permute-start.4 = (f32[4,8,4736]{2,1,0:T(8,128)}, f32[4,8,4736]{2,1,0:T(8,128)}, u32[]{:S(2)}, u32[]{:S(2)}) collective-permute-start(f32[4,8,4736]{2,1,0:T(8,128)} %pad_maximum_fusion.refs_0_), channel_id=1, source_target_pairs={{0,16},{8,24},{16,0},{24,8},{1,17},{9,25},{17,1},{25,9},{2,18},{10... | collective-permute-start | bytes 1818632 | tf_op jit(solution)/shard_map/ppermute | solution.py:413
  33.2 13.3 %collective-permute-start.3 = (f32[4,8,4736]{2,1,0:T(8,128)}, f32[4,8,4736]{2,1,0:T(8,128)}, u32[]{:S(2)}, u32[]{:S(2)}) collective-permute-start(f32[4,8,4736]{2,1,0:T(8,128)} %pad_maximum_fusion.refs_0_), channel_id=1, source_target_pairs={{0,8},{8,0},{16,24},{24,16},{1,9},{9,1},{17,25},{25,17},{2,10},{10... | collective-permute-start | bytes 1818632 | tf_op jit(solution)/shard_map/ppermute | solution.py:413
  135.9 10.9 %collective-permute-start.6 = (f32[2,192,128]{2,1,0:T(8,128)}, f32[2,192,128]{2,1,0:T(8,128)S(1)}, u32[]{:S(2)}, u32[]{:S(2)}) collective-permute-start(f32[2,192,128]{2,1,0:T(8,128)} %get-tuple-element.72), channel_id=1, source_target_pairs={{0,1},{1,2},{2,3},{3,4},{4,5},{5,6},{6,7},{7,0},{8,9},{9,10},{10,1... | collective-permute-start | bytes 589832 | tf_op jit(solution)/shard_map/ppermute | solution.py:405
  137.4 10.7 %collective-permute-start.7 = (f32[2,192,128]{2,1,0:T(8,128)}, f32[2,192,128]{2,1,0:T(8,128)S(1)}, u32[]{:S(2)}, u32[]{:S(2)}) collective-permute-start(f32[2,192,128]{2,1,0:T(8,128)} %get-tuple-element.73), channel_id=1, source_target_pairs={{0,2},{1,3},{2,4},{3,5},{4,6},{5,7},{6,0},{7,1},{8,10},{9,11},{10,... | collective-permute-start | bytes 589832 | tf_op jit(solution)/shard_map/ppermute | solution.py:405
  137.4 22.8 %collective-permute-start.15 = (f32[2,192,128]{2,1,0:T(8,128)}, f32[2,192,128]{2,1,0:T(8,128)}, u32[]{:S(2)}, u32[]{:S(2)}) collective-permute-start(f32[2,192,128]{2,1,0:T(8,128)} %get-tuple-element.85), channel_id=1, source_target_pairs={{0,3},{1,4},{2,5},{3,6},{4,7},{5,0},{6,1},{7,2},{8,11},{9,12},{10,... | collective-permute-start | bytes 589832 | tf_op jit(solution)/shard_map/ppermute | solution.py:405
  140.3 21.7 %collective-permute-start.16 = (f32[2,192,128]{2,1,0:T(8,128)}, f32[2,192,128]{2,1,0:T(8,128)}, u32[]{:S(2)}, u32[]{:S(2)}) collective-permute-start(f32[2,192,128]{2,1,0:T(8,128)} %get-tuple-element.86), channel_id=1, source_target_pairs={{0,4},{1,5},{2,6},{3,7},{4,0},{5,1},{6,2},{7,3},{8,12},{9,13},{10,... | collective-permute-start | bytes 589832 | tf_op jit(solution)/shard_map/ppermute | solution.py:405
  141.3 20.8 %collective-permute-start.17 = (f32[2,192,128]{2,1,0:T(8,128)}, f32[2,192,128]{2,1,0:T(8,128)}, u32[]{:S(2)}, u32[]{:S(2)}) collective-permute-start(f32[2,192,128]{2,1,0:T(8,128)} %get-tuple-element.87), channel_id=1, source_target_pairs={{0,5},{1,6},{2,7},{3,0},{4,1},{5,2},{6,3},{7,4},{8,13},{9,14},{10,... | collective-permute-start | bytes 589832 | tf_op jit(solution)/shard_map/ppermute | solution.py:405
  146.8 15.3 %collective-permute-start.18 = (f32[2,192,128]{2,1,0:T(8,128)}, f32[2,192,128]{2,1,0:T(8,128)}, u32[]{:S(2)}, u32[]{:S(2)}) collective-permute-start(f32[2,192,128]{2,1,0:T(8,128)} %get-tuple-element.88), channel_id=1, source_target_pairs={{0,6},{1,7},{2,0},{3,1},{4,2},{5,3},{6,4},{7,5},{8,14},{9,15},{10,... | collective-permute-start | bytes 589832 | tf_op jit(solution)/shard_map/ppermute | solution.py:405
  148.8 13.4 %collective-permute-start.19 = (f32[2,192,128]{2,1,0:T(8,128)}, f32[2,192,128]{2,1,0:T(8,128)}, u32[]{:S(2)}, u32[]{:S(2)}) collective-permute-start(f32[2,192,128]{2,1,0:T(8,128)} %get-tuple-element.89), channel_id=1, source_target_pairs={{0,7},{1,0},{2,1},{3,2},{4,3},{5,4},{6,5},{7,6},{8,15},{9,8},{10,9... | collective-permute-start | bytes 589832 | tf_op jit(solution)/shard_map/ppermute | solution.py:405
  170.0 56.8 %collective-permute-start.20 = (f32[1,1536,128]{2,1,0:T(8,128)S(1)}, f32[1,1536,128]{2,1,0:T(8,128)S(1)}, u32[]{:S(2)}, u32[]{:S(2)}) collective-permute-start(f32[1,1536,128]{2,1,0:T(8,128)S(1)} %get-tuple-element.90.own_ref.rest_0_), channel_id=1, source_target_pairs={{0,16},{8,24},{16,0},{24,8},{1,17},{9,25},{17,1},{25,9},{2,18},{10... | collective-permute-start | bytes 2359304 | tf_op jit(solution)/shard_map/ppermute | solution.py:413
  171.5 60.2 %collective-permute-start.21 = (f32[1,1536,128]{2,1,0:T(8,128)S(1)}, f32[1,1536,128]{2,1,0:T(8,128)S(1)}, u32[]{:S(2)}, u32[]{:S(2)}) collective-permute-start(f32[1,1536,128]{2,1,0:T(8,128)S(1)} %get-tuple-element.101.own_ref.rest_4_), channel_id=1, source_target_pairs={{0,16},{8,24},{16,0},{24,8},{1,17},{9,25},{17,1},{25,9},{2,18},{10... | collective-permute-start | bytes 2359304 | tf_op jit(solution)/shard_map/ppermute | solution.py:413
  172.0 17.5 %collective-permute-start.8 = (f32[2,192,128]{2,1,0:T(8,128)S(1)}, f32[2,192,128]{2,1,0:T(8,128)S(1)}, u32[]{:S(2)}, u32[]{:S(2)}) collective-permute-start(f32[2,192,128]{2,1,0:T(8,128)S(1)} %copy-done.34), channel_id=1, source_target_pairs={{0,1},{1,2},{2,3},{3,4},{4,5},{5,6},{6,7},{7,0},{8,9},{9,10},{10,1... | collective-permute-start | bytes 589832 | tf_op jit(solution)/shard_map/ppermute | solution.py:405
  177.6 17.1 %collective-permute-start.9 = (f32[2,192,128]{2,1,0:T(8,128)S(1)}, f32[2,192,128]{2,1,0:T(8,128)S(1)}, u32[]{:S(2)}, u32[]{:S(2)}) collective-permute-start(f32[2,192,128]{2,1,0:T(8,128)S(1)} %copy-done.33), channel_id=1, source_target_pairs={{0,2},{1,3},{2,4},{3,5},{4,6},{5,7},{6,0},{7,1},{8,10},{9,11},{10,... | collective-permute-start | bytes 589832 | tf_op jit(solution)/shard_map/ppermute | solution.py:405
  186.5 27.7 %collective-permute-start.10 = (f32[2,192,128]{2,1,0:T(8,128)S(1)}, f32[2,192,128]{2,1,0:T(8,128)S(1)}, u32[]{:S(2)}, u32[]{:S(2)}) collective-permute-start(f32[2,192,128]{2,1,0:T(8,128)S(1)} %copy-done.32), channel_id=1, source_target_pairs={{0,3},{1,4},{2,5},{3,6},{4,7},{5,0},{6,1},{7,2},{8,11},{9,12},{10,... | collective-permute-start | bytes 589832 | tf_op jit(solution)/shard_map/ppermute | solution.py:405
  189.5 29.8 %collective-permute-start.11 = (f32[2,192,128]{2,1,0:T(8,128)S(1)}, f32[2,192,128]{2,1,0:T(8,128)S(1)}, u32[]{:S(2)}, u32[]{:S(2)}) collective-permute-start(f32[2,192,128]{2,1,0:T(8,128)S(1)} %copy-done.31), channel_id=1, source_target_pairs={{0,4},{1,5},{2,6},{3,7},{4,0},{5,1},{6,2},{7,3},{8,12},{9,13},{10,... | collective-permute-start | bytes 589832 | tf_op jit(solution)/shard_map/ppermute | solution.py:405
  194.8 27.6 %collective-permute-start.12 = (f32[2,192,128]{2,1,0:T(8,128)S(1)}, f32[2,192,128]{2,1,0:T(8,128)S(1)}, u32[]{:S(2)}, u32[]{:S(2)}) collective-permute-start(f32[2,192,128]{2,1,0:T(8,128)S(1)} %copy-done.30), channel_id=1, source_target_pairs={{0,5},{1,6},{2,7},{3,0},{4,1},{5,2},{6,3},{7,4},{8,13},{9,14},{10,... | collective-permute-start | bytes 589832 | tf_op jit(solution)/shard_map/ppermute | solution.py:405
  222.3 11.0 %collective-permute-start.24 = (f32[1,1536,128]{2,1,0:T(8,128)S(1)}, f32[1,1536,128]{2,1,0:T(8,128)S(1)}, u32[]{:S(2)}, u32[]{:S(2)}) collective-permute-start(f32[1,1536,128]{2,1,0:T(8,128)S(1)} %get-tuple-element.90.own_ref.rest_0_), channel_id=1, source_target_pairs={{0,8},{8,0},{16,24},{24,16},{1,9},{9,1},{17,25},{25,17},{2,10},{10... | collective-permute-start | bytes 2359304 | tf_op jit(solution)/shard_map/ppermute | solution.py:413
  231.8 19.9 %collective-permute-start.23 = (f32[1,1536,128]{2,1,0:T(8,128)S(1)}, f32[1,1536,128]{2,1,0:T(8,128)S(1)}, u32[]{:S(2)}, u32[]{:S(2)}) collective-permute-start(f32[1,1536,128]{2,1,0:T(8,128)S(1)} %get-tuple-element.103.own_ref.rest_8_), channel_id=1, source_target_pairs={{0,16},{8,24},{16,0},{24,8},{1,17},{9,25},{17,1},{25,9},{2,18},{10... | collective-permute-start | bytes 2359304 | tf_op jit(solution)/shard_map/ppermute | solution.py:413
  233.3 20.1 %collective-permute-start.28 = (f32[1,1536,128]{2,1,0:T(8,128)S(1)}, f32[1,1536,128]{2,1,0:T(8,128)S(1)}, u32[]{:S(2)}, u32[]{:S(2)}) collective-permute-start(f32[1,1536,128]{2,1,0:T(8,128)S(1)} %get-tuple-element.103.own_ref.rest_8_), channel_id=1, source_target_pairs={{0,8},{8,0},{16,24},{24,16},{1,9},{9,1},{17,25},{25,17},{2,10},{10... | collective-permute-start | bytes 2359304 | tf_op jit(solution)/shard_map/ppermute | solution.py:413
  251.8 20.0 %collective-permute-start.22 = (f32[1,1536,128]{2,1,0:T(8,128)S(1)}, f32[1,1536,128]{2,1,0:T(8,128)S(1)}, u32[]{:S(2)}, u32[]{:S(2)}) collective-permute-start(f32[1,1536,128]{2,1,0:T(8,128)S(1)} %get-tuple-element.102.own_ref.rest_12_), channel_id=1, source_target_pairs={{0,16},{8,24},{16,0},{24,8},{1,17},{9,25},{17,1},{25,9},{2,18},{10... | collective-permute-start | bytes 2359304 | tf_op jit(solution)/shard_map/ppermute | solution.py:413
  253.2 18.5 %collective-permute-start.30 = (f32[1,1536,128]{2,1,0:T(8,128)S(1)}, f32[1,1536,128]{2,1,0:T(8,128)S(1)}, u32[]{:S(2)}, u32[]{:S(2)}) collective-permute-start(f32[1,1536,128]{2,1,0:T(8,128)S(1)} %get-tuple-element.102.own_ref.rest_12_), channel_id=1, source_target_pairs={{0,8},{8,0},{16,24},{24,16},{1,9},{9,1},{17,25},{25,17},{2,10},{10... | collective-permute-start | bytes 2359304 | tf_op jit(solution)/shard_map/ppermute | solution.py:413
  (48 other events, 815.3 us)
Sparse Core Ops, SparseCore 0:
  66.5 69.5 all-gather.2

commit v10 on v9

--- a/solution.py
+++ b/solution.py
@@ -80,50 +80,53 @@
     lax.fori_loop(0, rows // tile, step, 0, unroll=True)
 
 
-def swap_in_kernel(count, rows, levels_ref, in_ref, out_ref):
+def swap_in_kernel(count, rows, me_ref, levels_ref, in_ref, *out_refs):
     def read(block, start, size):
         return in_ref[block, pl.ds(start, size), :]
 
     def write(block, start, size, value):
-        out_ref[block, pl.ds(start, size), :] = value
-
-    swap_into(read, write, count, rows)
-    for block in range(count):
-        out_ref[block, pl.ds(rows, levels_ref.shape[0]), :] = levels_ref[...]
-
-
-def swap_in(levels, value):
+        out_refs[block][pl.ds(start, size), :] = value
+
+    swap_into(read, write, count, rows, before=me_ref[0])
+    for out_ref in out_refs:
+        out_ref[pl.ds(rows, levels_ref.shape[0]), :] = levels_ref[...]
+
+
+def swap_in(me, levels, value):
     planes, count, rows, _ = value.shape
     extra = levels.shape[1]
     return pl.pallas_call(
         functools.partial(swap_in_kernel, count, rows),
         grid=(planes,),
         in_specs=[
+            pl.BlockSpec(memory_space=pltpu.SMEM),
             pl.BlockSpec((None, extra, LANES), lambda p: (p, 0, 0)),
             pl.BlockSpec((None, count, rows, LANES), lambda p: (p, 0, 0, 0)),
         ],
-        out_specs=pl.BlockSpec((count, None, rows + extra, LANES), lambda p: (0, p, 0, 0)),
-        out_shape=jax.ShapeDtypeStruct((count, planes, rows + extra, LANES), jnp.float32),
-        compiler_params=params(12),
+        out_specs=[pl.BlockSpec((None, rows + extra, LANES), lambda p: (p, 0, 0))] * count,
+        out_shape=[jax.ShapeDtypeStruct((planes, rows + extra, LANES), jnp.float32)] * count,
+        compiler_params=params(14),
         cost_estimate=cost(0, 8 * value.size),
-    )(levels, value)
-
-
-def swap_out_kernel(me_ref, high_ref, low_ref, weights_ref, *refs):
-    planes, rows, _ = refs[0].shape
+    )(me, levels, value)
+
+
+def swap_out_kernel(planes, count, me_ref, high_ref, low_ref, weights_ref, *refs):
     arrived_refs, out_refs = refs[:-planes], refs[-planes:]
-    count = len(arrived_refs)
+    rows = arrived_refs[0].shape[-2]
+    by_steps = len(arrived_refs) > 1
     weights = side_by_side(weights_ref[...] * (1.0 / 18.0))
     for plane in range(planes):
 
         def read(block, start, size):
-            return arrived_refs[-block % count][plane, pl.ds(start, size), :]
+            if by_steps:
+                return arrived_refs[-block % count][plane, pl.ds(start, size), :]
+            return arrived_refs[0][block, plane, pl.ds(start, size), :]
 
         def write(block, start, size, value):
             at = pl.ds(pl.multiple_of(block * rows + start, 8), size)
             out_refs[plane][at, :] = value
 
-        swap_into(read, write, count, rows, after=me_ref[0])
+        swap_into(read, write, count, rows, after=me_ref[0] if by_steps else None)
         tile = rows * count // 6
 
         def add(index, carry):
@@ -136,12 +139,12 @@
 
 
 def swap_out(me, arrived, high, low, weights, first_plane):
-    count = len(arrived)
-    planes, rows, _ = arrived[0].shape
+    count = len(arrived) if len(arrived) > 1 else arrived[0].shape[0]
+    planes, rows = arrived[0].shape[-3:-1]
     cells = count * rows
     basis = pl.BlockSpec((planes, cells, 2 * LANES), lambda i: (first_plane // planes, 0, 0))
     return pl.pallas_call(
-        swap_out_kernel,
+        functools.partial(swap_out_kernel, planes, count),
         grid=(1,),
         in_specs=[
             pl.BlockSpec(memory_space=pltpu.SMEM),
@@ -149,7 +152,7 @@
             basis,
             pl.BlockSpec(weights.shape, lambda i: (0, 0)),
         ]
-        + [pl.BlockSpec(arrived[0].shape, lambda i: (0, 0, 0))] * count,
+        + [pl.BlockSpec(arrived[0].shape, lambda i: (0,) * arrived[0].ndim)] * len(arrived),
         out_specs=[pl.BlockSpec((None, cells, LANES), lambda i: (0, 0, 0))] * planes,
         out_shape=[jax.ShapeDtypeStruct((1, cells, LANES), jnp.float32)] * planes,
         compiler_params=params(24),
@@ -190,9 +193,12 @@
     lax.fori_loop(0, side_y, row, 0)
 
 
-def filter_kernel(planes, side_y, side_z, width, chunks, me_ref, arrived_ref, *rest):
-    outs, (field, padded, first, flat, potential) = rest[:-5], rest[-5:]
-    count = arrived_ref.shape[0]
+def filter_kernel(planes, side_y, side_z, count, half, me_ref, *refs):
+    arrived_refs = [refs[-group % count] for group in range(count)]
+    near_refs, late_ref = refs[count : 2 * count], refs[2 * count]
+    field, padded, first, flat, potential = refs[2 * count + 1 :]
+    me = me_ref[0]
+    width = LANES // count
     cells = side_y * side_z
     rows = cells // count
     tile = 16
@@ -201,7 +207,10 @@
     lane = lax.broadcasted_iota(jnp.int32, (2 * count, LANES), 1) // width
     spread = (line == lane).astype(jnp.bfloat16)
     for plane in range(planes):
-        lines = [arrived_ref[:, plane, rows + at, :] for at in range(cells // LANES)]
+        lines = [ref[plane, pl.ds(rows, -(-cells // LANES // GROUP) * GROUP), :] for ref in arrived_refs]
+        lines = [
+            jnp.concatenate([value[at : at + 1] for value in lines], axis=0) for at in range(cells // LANES)
+        ]
         high, low = halves(jnp.concatenate(lines, axis=1))
         both = jnp.concatenate([high.astype(jnp.float32), low.astype(jnp.float32)], axis=0)
         potential[plane] = jnp.dot(both.T.astype(jnp.bfloat16), spread, preferred_element_type=jnp.float32)
@@ -209,7 +218,7 @@
     for plane in range(planes):
 
         def read_in(block, start, size):
-            return arrived_ref[block, plane, pl.ds(start, size), :]
+            return arrived_refs[block][plane, pl.ds(start, size), :]
 
         def write_in(block, start, size, value):
             field[plane, pl.ds(pl.multiple_of(block * rows + start, 8), size), :] = value
@@ -242,35 +251,38 @@
     local_part(padded, potential, planes, 0, side_y, side_z, line_of, finish_first)
     local_part(first, potential, planes, 0, side_y, side_z, line_of, finish_second)
 
-    for index, (begin, size_of) in enumerate(chunks):
-        group = outs[index * count : (index + 1) * count]
-        for plane in range(size_of):
-
-            def read_out(block, start, size):
-                return flat[begin + plane, pl.ds(pl.multiple_of(block * rows + start, 8), size), :]
-
-            def write_out(block, start, size, value):
-                group[block][plane, pl.ds(start, size), :] = value
-
-            swap_into(read_out, write_out, count, rows, before=me_ref[0])
-
-
-def filter_orbitals(me, arrived, side_y, side_z, width, chunks):
-    count, planes = arrived.shape[:2]
+    for plane in range(planes):
+
+        def read_out(block, start, size):
+            return flat[plane, pl.ds(pl.multiple_of(block * rows + start, 8), size), :]
+
+        def write_out(block, start, size, value):
+            if plane < half:
+                near_refs[block][plane, pl.ds(start, size), :] = value
+            else:
+                late_ref[lax.rem(me + block, count), plane - half, pl.ds(start, size), :] = value
+
+        swap_into(read_out, write_out, count, rows)
+
+
+def filter_orbitals(me, arrived, side_y, side_z, half):
+    count, planes = len(arrived), arrived[0].shape[0]
     rows = side_y * side_z // count
+    size = planes * side_y * side_z * LANES
     flat = pltpu.VMEM((planes, side_y * side_z, LANES), jnp.float32)
     padded = pltpu.VMEM((planes, side_y, side_z + 2 * PAD, LANES), jnp.float32)
-    shapes = [jax.ShapeDtypeStruct((size, rows, LANES), jnp.float32) for _, size in chunks for _ in range(count)]
+    shapes = [jax.ShapeDtypeStruct((half, rows, LANES), jnp.float32)] * count
+    shapes += [jax.ShapeDtypeStruct((count, planes - half, rows, LANES), jnp.float32)]
     outs = pl.pallas_call(
-        functools.partial(filter_kernel, planes, side_y, side_z, width, chunks),
-        in_specs=[pl.BlockSpec(memory_space=pltpu.SMEM), WHOLE],
+        functools.partial(filter_kernel, planes, side_y, side_z, count, half),
+        in_specs=[pl.BlockSpec(memory_space=pltpu.SMEM)] + [WHOLE] * count,
         out_specs=[WHOLE] * len(shapes),
         out_shape=shapes,
         scratch_shapes=[flat, padded, padded, flat, flat],
         compiler_params=params(56),
-        cost_estimate=cost(100 * arrived.size, 12 * arrived.size),
-    )(me, arrived)
-    return [outs[index * count : (index + 1) * count] for index in range(len(chunks))]
+        cost_estimate=cost(100 * size, 12 * size),
+    )(me, *arrived)
+    return list(outs[:count]), outs[count]
 
 
 def basis_kernel(planes, side_y, side_z, bands, *refs):
@@ -608,12 +620,10 @@
     return jnp.stack([mine if step == BEFORE else shifted(mine, "dom", BEFORE - step) for step in range(NEAR)])
 
 
-def near_projectors(near, planes):
-    across = crossed(near, 2)
-    raw = [near, crossed(near, 1), across, crossed(across, 1)]
+def first_planes(raw, planes):
     moved = (planes * (jnp.arange(NEAR, dtype=jnp.float32) - BEFORE))[:, None]
     first = jnp.stack([member[:, :, -1] + moved for member in raw]).reshape(1, LANES)
-    return raw, jnp.broadcast_to(first, (GROUP, LANES))
+    return jnp.broadcast_to(first, (GROUP, LANES))
 
 
 def shards(orbitals, potential, projectors, coupling, atom_plane, projector_count):
@@ -626,7 +636,7 @@
     norb = local_orbs * bands
     chunks = tuple((plane, 1) for plane in range(planes))
     half = planes // 2
-    groups = ((0, half), (half, half))
+    tie = lax.optimization_barrier
     me = lax.axis_index("dom").astype(jnp.int32).reshape(1)
 
     order = jnp.arange(bands, dtype=jnp.int32) ^ band
@@ -635,10 +645,13 @@
     mine, levels = lax.optimization_barrier((mine, potential.reshape(planes, cells // LANES, LANES)))
     near = near_shares(mine)
     levels = jnp.pad(levels, ((0, 0), (0, -levels.shape[1] % GROUP), (0, 0)))
-    packed = swap_in(levels, orbitals.reshape(planes, blocks, rows, local_orbs))
-    packed, near = lax.optimization_barrier((packed, near))
-    raw, first = near_projectors(near, planes)
-    arrived = lax.all_to_all(packed, "dom", 0, 0, tiled=True)
+    packed = list(swap_in(me, levels, orbitals.reshape(planes, blocks, rows, local_orbs)))
+    packed, near = tie((packed, near))
+    across = crossed(near, 2)
+    arrived = exchanged(packed)
+    raw = [near, crossed(near, 1), across, crossed(across, 1)]
+    raw, arrived[1:-1] = tie((raw, arrived[1:-1]))
+    first = first_planes(raw, planes)
 
     own_levels = jnp.broadcast_to(potential.reshape(planes, cells, 1), (planes, cells, LANES))
     high, low, parts = build_basis(raw, first, own_levels, orbitals.reshape(planes, cells, LANES), side_y, side_z)
@@ -659,17 +672,16 @@
         everyone[:, : 3 * LANES].reshape(blocks, 3, LANES, LANES), everyone[:, 3 * LANES :, :vectors],
     )
 
-    seconds = filter_orbitals(me, arrived, side_y, side_z, width, groups)
-
-    tie = lax.optimization_barrier
-    came = exchanged(seconds[0])
-    packed, came[1:3] = tie((seconds[1], came[1:3]))
-    coming = exchanged(packed)
+    early, late = filter_orbitals(me, arrived, side_y, side_z, half)
+
+    came = exchanged(early)
+    late, came = tie((late, came))
+    coming = lax.all_to_all(late, "dom", 0, 0, tiled=True)
     owns = list(swap_out(me, came, high, low, weights, 0))
     acrosses = [crossed(own, 2) for own in owns]
     besides = [crossed(own, 1) for own in owns]
     coming, acrosses[0] = tie((coming, acrosses[0]))
-    late = list(swap_out(me, coming, high, low, weights, half))
+    late = list(swap_out(me, [coming], high, low, weights, half))
     late, acrosses[1:] = tie((late, acrosses[1:]))
     acrosses += [crossed(own, 2) for own in late]
     besides += [crossed(own, 1) for own in late]

time: 353 us -> 374 us (1.059)
  waiting for transfers between devices: 117 us -> 132 us
  local copies, waits for them, and re-layouts: 18.4 us -> 22.8 us
    ppermute x17, waiting for transfers between devices: 19.3 us -> 62.1 us  [shifted(): lax.ppermute(value, axis, [(source, (source + step) % count) for source i...]
    all_to_all x1, waiting for transfers between devices: 45.8 us -> 22.5 us  [shards(): coming = lax.all_to_all(late, 'dom', 0, 0, tiled=True)]
    ppermute x17, starting transfers between devices: 66.3 us -> 54.2 us  [shifted(): lax.ppermute(value, axis, [(source, (source + step) % count) for source i...]
    all_to_all x1, starting transfers between devices: 3.79 us -> 14.2 us  [shards(): coming = lax.all_to_all(late, 'dom', 0, 0, tiled=True)]
    unnamed x73 -> x83, local copies, waits for them, and re-layouts: 7.29 us -> 13 us
    ppermute x18, waiting for transfers between devices: 52.2 us -> 47.9 us  [crossed(): lax.ppermute(value, 'band', [(source, source ^ bit) for source in range(l...]
  transfers between devices with their start and end apart: 37 -> 37, of which waited for: 16 -> 17; matrix products, arithmetic and copies ran while one was open for 4% -> 1% of each run, Pallas kernels for 14% -> 12%
where the time goes in v10:
time: 374 us; the launch traced here: 373 us
  waiting for transfers between devices  132 us (35%)
  Pallas kernels  94.3 us (25%)
  starting transfers between devices  77.3 us (21%)
  blocking collectives  26.7 us (7%)
  local copies, waits for them, and re-layouts  22.8 us (6%)
  between operations  14.6 us (4%)
  other arithmetic  5.29 us (1%)
    ppermute x17, waiting for transfers between devices, shifted(): lax.ppermute(value, axis, [(source, (source + step) % count) for source i...  62.1 us
    ppermute x17, starting transfers between devices, shifted(): lax.ppermute(value, axis, [(source, (source + step) % count) for source i...  54.2 us
    ppermute x18, waiting for transfers between devices, crossed(): lax.ppermute(value, 'band', [(source, source ^ bit) for source in range(l...  47.9 us
    pallas_call x1, Pallas kernels, cholesky_inverse(): pl.pallas_call(cholesky_kernel, in_specs=[pl.BlockSpec(memory_space=pltpu...  25.5 us
    all_to_all x1, waiting for transfers between devices, shards(): coming = lax.all_to_all(late, 'dom', 0, 0, tiled=True)  22.5 us
    pallas_call x1, Pallas kernels, filter_orbitals(): pl.pallas_call(functools.partial(filter_kernel, planes, side_y, side_z, c...  22 us
    all_to_all x1, blocking collectives, shards(): lax.all_to_all(part.reshape(blocks, width, norb), 'dom', 0, 0, tiled=True)  14.7 us
    all_to_all x1, starting transfers between devices, shards(): coming = lax.all_to_all(late, 'dom', 0, 0, tiled=True)  14.2 us
  transfers between devices with their start and end apart: 37, of which 17 were waited for; matrix products, arithmetic and copies ran while one was open for 1% of the time, Pallas kernels for 12%

profile of v10, /device:TPU:0, one launch (start us, length us, event | category | flops | bytes accessed | tf_op | source)
XLA Modules:
  0.0 373.4 jit_solution(8115498672304764204)
XLA Ops:
  9.9 6.1 %collective-permute-start.2 = (f32[8,4736]{1,0:T(8,128)S(1)}, f32[8,4736]{1,0:T(8,128)S(1)}, u32[]{:S(2)}, u32[]{:S(2)}) collective-permute-start(f32[8,4736]{1,0:T(8,128)S(1)} %reshape.268), channel_id=1, source_target_pairs={{0,7},{1,0},{2,1},{3,2},{4,3},{5,4},{6,5},{7,6},{8,15},{9,8},{10,9... | collective-permute-start | bytes 454664 | tf_op jit(solution)/shard_map/ppermute | solution.py:417
  32.5 7.0 %collective-permute-done.4.refs_2_ = f32[4,8,4736]{2,1,0:T(8,128)} collective-permute-done((f32[4,8,4736]{2,1,0:T(8,128)}, f32[4,8,4736]{2,1,0:T(8,128)}, u32[]{:S(2)}, u32[]{:S(2)}) %collective-permute-start.4) | collective-permute-done | bytes 606240 | tf_op jit(solution)/shard_map/ppermute | solution.py:425
  45.7 6.5 %collective-permute-start.10 = (f32[4,208,128]{2,1,0:T(8,128)S(1)}, f32[4,208,128]{2,1,0:T(8,128)S(1)}, u32[]{:S(2)}, u32[]{:S(2)}) collective-permute-start(f32[4,208,128]{2,1,0:T(8,128)S(1)} %get-tuple-element.82), channel_id=1, source_target_pairs={{0,5},{1,6},{2,7},{3,0},{4,1},{5,2},{6,3},{7,4},{8,13},{9,14},{10,... | collective-permute-start | bytes 1277960 | tf_op jit(solution)/shard_map/ppermute | solution.py:417
  52.2 24.4 %collective-permute-done.8.refs_3_ = f32[4,208,128]{2,1,0:T(8,128)} collective-permute-done((f32[4,208,128]{2,1,0:T(8,128)S(1)}, f32[4,208,128]{2,1,0:T(8,128)}, u32[]{:S(2)}, u32[]{:S(2)}) %collective-permute-start.8) | collective-permute-done | bytes 426016 | tf_op jit(solution)/shard_map/ppermute | solution.py:417
  76.6 20.3 %collective-permute-start.11 = (f32[4,208,128]{2,1,0:T(8,128)S(1)}, f32[4,208,128]{2,1,0:T(8,128)S(1)}, u32[]{:S(2)}, u32[]{:S(2)}) collective-permute-start(f32[4,208,128]{2,1,0:T(8,128)S(1)} %get-tuple-element.83), channel_id=1, source_target_pairs={{0,6},{1,7},{2,0},{3,1},{4,2},{5,3},{6,4},{7,5},{8,14},{9,15},{10,... | collective-permute-start | bytes 1277960 | tf_op jit(solution)/shard_map/ppermute | solution.py:417
  97.1 5.4 %collective-permute-done.11.refs_6_ = f32[4,208,128]{2,1,0:T(8,128)S(1)} collective-permute-done((f32[4,208,128]{2,1,0:T(8,128)S(1)}, f32[4,208,128]{2,1,0:T(8,128)S(1)}, u32[]{:S(2)}, u32[]{:S(2)}) %collective-permute-start.11) | collective-permute-done | bytes 426016 | tf_op jit(solution)/shard_map/ppermute | solution.py:417
  107.3 13.5 %shard_map.78 = (bf16[4,1536,256]{2,1,0:T(8,128)(2,1)}, bf16[4,1536,256]{2,1,0:T(8,128)(2,1)}, f32[3,128,128]{2,1,0:T(8,128)}) custom-call(f32[4,8,4736]{2,1,0:T(8,128)} %pad_maximum_fusion.refs_0_, f32[4,8,4736]{2,1,0:T(8,128)} %collective-permute-done.3.refs_1_, f32[4,8,4736]{2,1,0:T(8,128)} %collective-permute-done.4.refs_2_, ...), custom_call_target="tpu_custom_call" | custom-call | flops 157286400 | bytes 18874368 | tf_op jit(solution)/shard_map/pallas_call | solution.py:340
  123.6 7.1 %collective-permute-done.12.refs_7_ = f32[4,208,128]{2,1,0:T(8,128)S(1)} collective-permute-done((f32[4,208,128]{2,1,0:T(8,128)S(1)}, f32[4,208,128]{2,1,0:T(8,128)S(1)}, u32[]{:S(2)}, u32[]{:S(2)}) %collective-permute-start.12) | collective-permute-done | bytes 426016 | tf_op jit(solution)/shard_map/ppermute | solution.py:417
  131.4 22.0 %shard_map.80 = (f32[2,192,128]{2,1,0:T(8,128)}, f32[2,192,128]{2,1,0:T(8,128)}, f32[2,192,128]{2,1,0:T(8,128)}, f32[2,192,128]{2,1,0:T(8,128)}, f32[2,192,128]{...) custom-call(s32[1]{0:T(128)} %bitcast.1.me_ref, ...), custom_call_target="tpu_custom_call" | custom-call | flops 78643200 | bytes 9437184 | tf_op jit(solution)/shard_map/pallas_call | solution.py:276
  153.4 4.7 %collective-permute-start.14 = (f32[2,192,128]{2,1,0:T(8,128)}, f32[2,192,128]{2,1,0:T(8,128)S(1)}, u32[]{:S(2)}, u32[]{:S(2)}) collective-permute-start(f32[2,192,128]{2,1,0:T(8,128)} %get-tuple-element.102), channel_id=1, source_target_pairs={{0,2},{1,3},{2,4},{3,5},{4,6},{5,7},{6,0},{7,1},{8,10},{9,11},{10,... | collective-permute-start | bytes 589832 | tf_op jit(solution)/shard_map/ppermute | solution.py:417
  163.4 5.0 %collective-permute-done.13.refs_1_ = f32[2,192,128]{2,1,0:T(8,128)S(1)} collective-permute-done((f32[2,192,128]{2,1,0:T(8,128)}, f32[2,192,128]{2,1,0:T(8,128)S(1)}, u32[]{:S(2)}, u32[]{:S(2)}) %collective-permute-start.13) | collective-permute-done | bytes 196640 | tf_op jit(solution)/shard_map/ppermute | solution.py:417
  170.5 6.5 %collective-permute-start.19 = (f32[2,192,128]{2,1,0:T(8,128)}, f32[2,192,128]{2,1,0:T(8,128)S(1)}, u32[]{:S(2)}, u32[]{:S(2)}) collective-permute-start(f32[2,192,128]{2,1,0:T(8,128)} %get-tuple-element.107), channel_id=1, source_target_pairs={{0,7},{1,0},{2,1},{3,2},{4,3},{5,4},{6,5},{7,6},{8,15},{9,8},{10,9... | collective-permute-start | bytes 589832 | tf_op jit(solution)/shard_map/ppermute | solution.py:417
  177.0 11.0 %collective-permute-done.15.refs_3_ = f32[2,192,128]{2,1,0:T(8,128)S(1)} collective-permute-done((f32[2,192,128]{2,1,0:T(8,128)}, f32[2,192,128]{2,1,0:T(8,128)S(1)}, u32[]{:S(2)}, u32[]{:S(2)}) %collective-permute-start.15) | collective-permute-done | bytes 196640 | tf_op jit(solution)/shard_map/ppermute | solution.py:417
  191.5 14.2 %all-to-all-start = ((f32[8,2,192,128]{3,2,1,0:T(8,128)}), f32[8,2,192,128]{3,2,1,0:T(8,128)}, u32[]{:S(2)}, u32[]{:S(2)}) async-start(f32[8,2,192,128]{3,2,1,0:T(8,128)} %get-tuple-element.108), calls=%async_computation | async-start | bytes 3145728 | tf_op jit(solution)/shard_map/all_to_all | solution.py:679
  212.4 5.4 %shard_map.81 = (f32[1,1536,128]{2,1,0:T(8,128)}, f32[1,1536,128]{2,1,0:T(8,128)}) custom-call(s32[1]{0:T(128)} %bitcast.1.me_ref, bf16[4,1536,256]{2,1,0:T(8,128)(2,1)S(1)} %copy-done.1, bf16[4,1536,256]{2,1,0:T(8,128)(2,1)S(1)} %copy-done.2, f32[256,128]{1,0:T(8,128)S(1)} %shard_map.79.weights_ref, f32[2,192,128]{2,1,0:T(8,128)S(1)} %copy-done.17, ...), custom_call_target="tpu_custom_call" | custom-call | bytes 9437184 | tf_op jit(solution)/shard_map/pallas_call | solution.py:146
  219.8 22.5 %all-to-all-done.refs_0_ = f32[8,2,192,128]{3,2,1,0:T(8,128)} async-done(((f32[8,2,192,128]{3,2,1,0:T(8,128)}), f32[8,2,192,128]{3,2,1,0:T(8,128)}, u32[]{:S(2)}, u32[]{:S(2)}) %all-to-all-start) | async-done | bytes 1572896 | tf_op jit(solution)/shard_map/all_to_all | solution.py:679
  244.7 5.8 %shard_map.82 = (f32[1,1536,128]{2,1,0:T(8,128)S(1)}, f32[1,1536,128]{2,1,0:T(8,128)S(1)}) custom-call(s32[1]{0:T(128)} %bitcast.1.me_ref, bf16[4,1536,256]{2,1,0:T(8,128)(2,1)S(1)} %copy-done.1, bf16[4,1536,256]{2,1,0:T(8,128)(2,1)S(1)} %copy-done.3, f32[256,128]{1,0:T(8,128)S(1)} %shard_map.79.weights_ref, f32[8,2,192,128]{3,2,1,0:T(8,128)} %all-to-all-done.refs_0_), custom_call_target="tpu_custom_call" | custom-call | bytes 9437184 | tf_op jit(solution)/shard_map/pallas_call | solution.py:146
  261.0 12.3 %collective-permute-done.23.rest_1_.rest_10_ = f32[1,1536,128]{2,1,0:T(8,128)S(1)} collective-permute-done((f32[1,1536,128]{2,1,0:T(8,128)S(1)}, f32[1,1536,128]{2,1,0:T(8,128)S(1)}, u32[]{:S(2)}, u32[]{:S(2)}) %collective-permute-start.23) | collective-permute-done | bytes 786464 | tf_op jit(solution)/shard_map/ppermute | solution.py:425
  277.0 16.3 %collective-permute-done.22.rest_1_.rest_14_ = f32[1,1536,128]{2,1,0:T(8,128)S(1)} collective-permute-done((f32[1,1536,128]{2,1,0:T(8,128)S(1)}, f32[1,1536,128]{2,1,0:T(8,128)S(1)}, u32[]{:S(2)}, u32[]{:S(2)}) %collective-permute-start.22) | collective-permute-done | bytes 786464 | tf_op jit(solution)/shard_map/ppermute | solution.py:425
  297.0 14.7 %all_to_all.15 = f32[8,16,512]{2,1,0:T(8,128)S(1)} all-to-all(f32[8,16,512]{2,1,0:T(8,128)S(1)} %bitcast.43), channel_id=1, replica_groups=mesh['band'=4,'dom'=8] {'dom'}, dimensions={0} | all-to-all | bytes 524288 | tf_op jit(solution)/shard_map/all_to_all | solution.py:697
  311.8 12.0 %all_to_all.16 = f32[8,16,512]{2,1,0:T(8,128)S(1)} all-to-all(f32[8,16,512]{2,1,0:T(8,128)S(1)} %broadcast_in_dim.58), channel_id=1, replica_groups=mesh['band'=4,'dom'=8] {'dom'}, dimensions={0} | all-to-all | bytes 524288 | tf_op jit(solution)/shard_map/all_to_all | solution.py:699
  325.2 5.0 %collective-permute-done.33.refs_2_ = f32[128,512]{1,0:T(8,128)S(1)} collective-permute-done((f32[128,512]{1,0:T(8,128)S(1)}, f32[128,512]{1,0:T(8,128)S(1)}, u32[]{:S(2)}, u32[]{:S(2)}) %collective-permute-start.33) | collective-permute-done | bytes 262176 | tf_op jit(solution)/shard_map/ppermute | solution.py:425
  331.7 25.5 %shard_map.87 = (f32[512,512]{1,0:T(8,128)}, f32[128,512]{1,0:T(8,128)S(1)}) custom-call(s32[1]{0:T(128)} %bitcast.band_ref, f32[128,512]{1,0:T(8,128)S(1)} %bitcast.39, f32[128,512]{1,0:T(8,128)S(1)} %collective-permute-done.32.refs_1_, f32[128,512]{1,0:T(8,128)S(1)} %collective-permute-done.33.refs_2_, f32[128,512]{1,0:T(8,128)S(1)} %collective-permute-done.34.refs_3_), custom_call_target="tpu_custom_call" | custom-call | tf_op jit(solution)/shard_map/pallas_call | solution.py:591
  357.8 8.7 %shard_map.88 = f32[4,1536,128]{2,1,0:T(8,128)} custom-call(f32[128,512]{1,0:T(8,128)} %copy-done.16, f32[1,1536,128]{2,1,0:T(8,128)} %get-tuple-element.117.own_ref.rest_0_, f32[1,1536,128]{2,1,0:T(8,128)} %collective-permute-done.24.rest_0_.rest_1_, f32[1,1536,128]{2,1,0:T(8,128)} %collective-permute-done.20.rest_1_.rest_2_, f32[1,1536,128]{2,1,0:T(8,128)} %copy-done.4, ...), custom_call_target="tpu_custom_call" | custom-call | tf_op jit(solution)/shard_map/pallas_call | solution.py:474
  (189 shorter events, 77.0 us)
Async XLA Ops:
  7.2 198.5 %all-gather.3.cloned.1.call-start = ((), (), s32[]{:S(2)}) async-start(), calls=%async_computation.3 | async-start | bytes 1916928 | tf_op jit(solution)/shard_map/all_gather | solution.py:669
  28.6 15.6 %collective-permute-start.6 = (f32[4,208,128]{2,1,0:T(8,128)S(1)}, f32[4,208,128]{2,1,0:T(8,128)S(1)}, u32[]{:S(2)}, u32[]{:S(2)}) collective-permute-start(f32[4,208,128]{2,1,0:T(8,128)S(1)} %get-tuple-element.78), channel_id=1, source_target_pairs={{0,1},{1,2},{2,3},{3,4},{4,5},{5,6},{6,7},{7,0},{8,9},{9,10},{10,1... | collective-permute-start | bytes 1277960 | tf_op jit(solution)/shard_map/ppermute | solution.py:417
  30.9 45.7 %collective-permute-start.8 = (f32[4,208,128]{2,1,0:T(8,128)S(1)}, f32[4,208,128]{2,1,0:T(8,128)}, u32[]{:S(2)}, u32[]{:S(2)}) collective-permute-start(f32[4,208,128]{2,1,0:T(8,128)S(1)} %get-tuple-element.80), channel_id=1, source_target_pairs={{0,3},{1,4},{2,5},{3,6},{4,7},{5,0},{6,1},{7,2},{8,11},{9,12},{10,... | collective-permute-start | bytes 1277960 | tf_op jit(solution)/shard_map/ppermute | solution.py:417
  32.5 70.0 %collective-permute-start.3 = (f32[4,8,4736]{2,1,0:T(8,128)}, f32[4,8,4736]{2,1,0:T(8,128)}, u32[]{:S(2)}, u32[]{:S(2)}) collective-permute-start(f32[4,8,4736]{2,1,0:T(8,128)} %pad_maximum_fusion.refs_0_), channel_id=1, source_target_pairs={{0,8},{8,0},{16,24},{24,16},{1,9},{9,1},{17,25},{25,17},{2,10},{10... | collective-permute-start | bytes 1818632 | tf_op jit(solution)/shard_map/ppermute | solution.py:425
  39.5 63.0 %collective-permute-start.5 = (f32[4,8,4736]{2,1,0:T(8,128)}, f32[4,8,4736]{2,1,0:T(8,128)}, u32[]{:S(2)}, u32[]{:S(2)}) collective-permute-start(f32[4,8,4736]{2,1,0:T(8,128)} %collective-permute-done.4.refs_2_), channel_id=1, source_target_pairs={{0,8},{8,0},{16,24},{24,16},{1,9},{9,1},{17,25},{25,17},{2,10},{10... | collective-permute-start | bytes 1818632 | tf_op jit(solution)/shard_map/ppermute | solution.py:425
  44.1 52.9 %collective-permute-start.9 = (f32[4,208,128]{2,1,0:T(8,128)S(1)}, f32[4,208,128]{2,1,0:T(8,128)S(1)}, u32[]{:S(2)}, u32[]{:S(2)}) collective-permute-start(f32[4,208,128]{2,1,0:T(8,128)S(1)} %get-tuple-element.81), channel_id=1, source_target_pairs={{0,4},{1,5},{2,6},{3,7},{4,0},{5,1},{6,2},{7,3},{8,12},{9,13},{10,... | collective-permute-start | bytes 1277960 | tf_op jit(solution)/shard_map/ppermute | solution.py:417
  45.7 51.4 %collective-permute-start.10 = (f32[4,208,128]{2,1,0:T(8,128)S(1)}, f32[4,208,128]{2,1,0:T(8,128)S(1)}, u32[]{:S(2)}, u32[]{:S(2)}) collective-permute-start(f32[4,208,128]{2,1,0:T(8,128)S(1)} %get-tuple-element.82), channel_id=1, source_target_pairs={{0,5},{1,6},{2,7},{3,0},{4,1},{5,2},{6,3},{7,4},{8,13},{9,14},{10,... | collective-permute-start | bytes 1277960 | tf_op jit(solution)/shard_map/ppermute | solution.py:417
  76.6 25.9 %collective-permute-start.11 = (f32[4,208,128]{2,1,0:T(8,128)S(1)}, f32[4,208,128]{2,1,0:T(8,128)S(1)}, u32[]{:S(2)}, u32[]{:S(2)}) collective-permute-start(f32[4,208,128]{2,1,0:T(8,128)S(1)} %get-tuple-element.83), channel_id=1, source_target_pairs={{0,6},{1,7},{2,0},{3,1},{4,2},{5,3},{6,4},{7,5},{8,14},{9,15},{10,... | collective-permute-start | bytes 1277960 | tf_op jit(solution)/shard_map/ppermute | solution.py:417
  153.4 15.0 %collective-permute-start.13 = (f32[2,192,128]{2,1,0:T(8,128)}, f32[2,192,128]{2,1,0:T(8,128)S(1)}, u32[]{:S(2)}, u32[]{:S(2)}) collective-permute-start(f32[2,192,128]{2,1,0:T(8,128)} %get-tuple-element.101), channel_id=1, source_target_pairs={{0,1},{1,2},{2,3},{3,4},{4,5},{5,6},{6,7},{7,0},{8,9},{9,10},{10,1... | collective-permute-start | bytes 589832 | tf_op jit(solution)/shard_map/ppermute | solution.py:417
  153.4 16.5 %collective-permute-start.14 = (f32[2,192,128]{2,1,0:T(8,128)}, f32[2,192,128]{2,1,0:T(8,128)S(1)}, u32[]{:S(2)}, u32[]{:S(2)}) collective-permute-start(f32[2,192,128]{2,1,0:T(8,128)} %get-tuple-element.102), channel_id=1, source_target_pairs={{0,2},{1,3},{2,4},{3,5},{4,6},{5,7},{6,0},{7,1},{8,10},{9,11},{10,... | collective-permute-start | bytes 589832 | tf_op jit(solution)/shard_map/ppermute | solution.py:417
  158.1 30.0 %collective-permute-start.15 = (f32[2,192,128]{2,1,0:T(8,128)}, f32[2,192,128]{2,1,0:T(8,128)S(1)}, u32[]{:S(2)}, u32[]{:S(2)}) collective-permute-start(f32[2,192,128]{2,1,0:T(8,128)} %get-tuple-element.103), channel_id=1, source_target_pairs={{0,3},{1,4},{2,5},{3,6},{4,7},{5,0},{6,1},{7,2},{8,11},{9,12},{10,... | collective-permute-start | bytes 589832 | tf_op jit(solution)/shard_map/ppermute | solution.py:417
  159.7 29.1 %collective-permute-start.16 = (f32[2,192,128]{2,1,0:T(8,128)}, f32[2,192,128]{2,1,0:T(8,128)S(1)}, u32[]{:S(2)}, u32[]{:S(2)}) collective-permute-start(f32[2,192,128]{2,1,0:T(8,128)} %get-tuple-element.104), channel_id=1, source_target_pairs={{0,4},{1,5},{2,6},{3,7},{4,0},{5,1},{6,2},{7,3},{8,12},{9,13},{10,... | collective-permute-start | bytes 589832 | tf_op jit(solution)/shard_map/ppermute | solution.py:417
  160.7 28.7 %collective-permute-start.17 = (f32[2,192,128]{2,1,0:T(8,128)}, f32[2,192,128]{2,1,0:T(8,128)S(1)}, u32[]{:S(2)}, u32[]{:S(2)}) collective-permute-start(f32[2,192,128]{2,1,0:T(8,128)} %get-tuple-element.105), channel_id=1, source_target_pairs={{0,5},{1,6},{2,7},{3,0},{4,1},{5,2},{6,3},{7,4},{8,13},{9,14},{10,... | collective-permute-start | bytes 589832 | tf_op jit(solution)/shard_map/ppermute | solution.py:417
  169.1 21.1 %collective-permute-start.18 = (f32[2,192,128]{2,1,0:T(8,128)}, f32[2,192,128]{2,1,0:T(8,128)S(1)}, u32[]{:S(2)}, u32[]{:S(2)}) collective-permute-start(f32[2,192,128]{2,1,0:T(8,128)} %get-tuple-element.106), channel_id=1, source_target_pairs={{0,6},{1,7},{2,0},{3,1},{4,2},{5,3},{6,4},{7,5},{8,14},{9,15},{10,... | collective-permute-start | bytes 589832 | tf_op jit(solution)/shard_map/ppermute | solution.py:417
  170.5 20.2 %collective-permute-start.19 = (f32[2,192,128]{2,1,0:T(8,128)}, f32[2,192,128]{2,1,0:T(8,128)S(1)}, u32[]{:S(2)}, u32[]{:S(2)}) collective-permute-start(f32[2,192,128]{2,1,0:T(8,128)} %get-tuple-element.107), channel_id=1, source_target_pairs={{0,7},{1,0},{2,1},{3,2},{4,3},{5,4},{6,5},{7,6},{8,15},{9,8},{10,9... | collective-permute-start | bytes 589832 | tf_op jit(solution)/shard_map/ppermute | solution.py:417
  191.5 50.8 %all-to-all-start = ((f32[8,2,192,128]{3,2,1,0:T(8,128)}), f32[8,2,192,128]{3,2,1,0:T(8,128)}, u32[]{:S(2)}, u32[]{:S(2)}) async-start(f32[8,2,192,128]{3,2,1,0:T(8,128)} %get-tuple-element.108), calls=%async_computation | async-start | bytes 3145728 | tf_op jit(solution)/shard_map/all_to_all | solution.py:679
  217.7 24.6 %collective-permute-start.20 = (f32[1,1536,128]{2,1,0:T(8,128)}, f32[1,1536,128]{2,1,0:T(8,128)}, u32[]{:S(2)}, u32[]{:S(2)}) collective-permute-start(f32[1,1536,128]{2,1,0:T(8,128)} %get-tuple-element.117.own_ref.rest_0_), channel_id=1, source_target_pairs={{0,16},{8,24},{16,0},{24,8},{1,17},{9,25},{17,1},{25,9},{2,18},{10... | collective-permute-start | bytes 2359304 | tf_op jit(solution)/shard_map/ppermute | solution.py:425
  219.2 34.2 %collective-permute-start.21 = (f32[1,1536,128]{2,1,0:T(8,128)}, f32[1,1536,128]{2,1,0:T(8,128)}, u32[]{:S(2)}, u32[]{:S(2)}) collective-permute-start(f32[1,1536,128]{2,1,0:T(8,128)} %get-tuple-element.121.own_ref.rest_4_), channel_id=1, source_target_pairs={{0,16},{8,24},{16,0},{24,8},{1,17},{9,25},{17,1},{25,9},{2,18},{10... | collective-permute-start | bytes 2359304 | tf_op jit(solution)/shard_map/ppermute | solution.py:425
  219.7 35.1 %collective-permute-start.24 = (f32[1,1536,128]{2,1,0:T(8,128)}, f32[1,1536,128]{2,1,0:T(8,128)}, u32[]{:S(2)}, u32[]{:S(2)}) collective-permute-start(f32[1,1536,128]{2,1,0:T(8,128)} %get-tuple-element.117.own_ref.rest_0_), channel_id=1, source_target_pairs={{0,8},{8,0},{16,24},{24,16},{1,9},{9,1},{17,25},{25,17},{2,10},{10... | collective-permute-start | bytes 2359304 | tf_op jit(solution)/shard_map/ppermute | solution.py:425
  242.3 15.6 %collective-permute-start.26 = (f32[1,1536,128]{2,1,0:T(8,128)}, f32[1,1536,128]{2,1,0:T(8,128)S(1)}, u32[]{:S(2)}, u32[]{:S(2)}) collective-permute-start(f32[1,1536,128]{2,1,0:T(8,128)} %get-tuple-element.121.own_ref.rest_4_), channel_id=1, source_target_pairs={{0,8},{8,0},{16,24},{24,16},{1,9},{9,1},{17,25},{25,17},{2,10},{10... | collective-permute-start | bytes 2359304 | tf_op jit(solution)/shard_map/ppermute | solution.py:425
  253.4 20.0 %collective-permute-start.23 = (f32[1,1536,128]{2,1,0:T(8,128)S(1)}, f32[1,1536,128]{2,1,0:T(8,128)S(1)}, u32[]{:S(2)}, u32[]{:S(2)}) collective-permute-start(f32[1,1536,128]{2,1,0:T(8,128)S(1)} %get-tuple-element.123.own_ref.rest_8_), channel_id=1, source_target_pairs={{0,16},{8,24},{16,0},{24,8},{1,17},{9,25},{17,1},{25,9},{2,18},{10... | collective-permute-start | bytes 2359304 | tf_op jit(solution)/shard_map/ppermute | solution.py:425
  254.8 20.2 %collective-permute-start.28 = (f32[1,1536,128]{2,1,0:T(8,128)S(1)}, f32[1,1536,128]{2,1,0:T(8,128)S(1)}, u32[]{:S(2)}, u32[]{:S(2)}) collective-permute-start(f32[1,1536,128]{2,1,0:T(8,128)S(1)} %get-tuple-element.123.own_ref.rest_8_), channel_id=1, source_target_pairs={{0,8},{8,0},{16,24},{24,16},{1,9},{9,1},{17,25},{25,17},{2,10},{10... | collective-permute-start | bytes 2359304 | tf_op jit(solution)/shard_map/ppermute | solution.py:425
  273.3 20.0 %collective-permute-start.22 = (f32[1,1536,128]{2,1,0:T(8,128)S(1)}, f32[1,1536,128]{2,1,0:T(8,128)S(1)}, u32[]{:S(2)}, u32[]{:S(2)}) collective-permute-start(f32[1,1536,128]{2,1,0:T(8,128)S(1)} %get-tuple-element.122.own_ref.rest_12_), channel_id=1, source_target_pairs={{0,16},{8,24},{16,0},{24,8},{1,17},{9,25},{17,1},{25,9},{2,18},{10... | collective-permute-start | bytes 2359304 | tf_op jit(solution)/shard_map/ppermute | solution.py:425
  274.8 18.5 %collective-permute-start.30 = (f32[1,1536,128]{2,1,0:T(8,128)S(1)}, f32[1,1536,128]{2,1,0:T(8,128)S(1)}, u32[]{:S(2)}, u32[]{:S(2)}) collective-permute-start(f32[1,1536,128]{2,1,0:T(8,128)S(1)} %get-tuple-element.122.own_ref.rest_12_), channel_id=1, source_target_pairs={{0,8},{8,0},{16,24},{24,16},{1,9},{9,1},{17,25},{25,17},{2,10},{10... | collective-permute-start | bytes 2359304 | tf_op jit(solution)/shard_map/ppermute | solution.py:425
  (53 other events, 612.9 us)
Sparse Core Ops, SparseCore 0:
  122.6 63.9 all-gather.2

commit v11 on v9

--- a/solution.py
+++ b/solution.py
@@ -109,21 +109,23 @@
     )(levels, value)
 
 
-def swap_out_kernel(me_ref, high_ref, low_ref, weights_ref, *refs):
-    planes, rows, _ = refs[0].shape
+def swap_out_kernel(planes, count, me_ref, high_ref, low_ref, weights_ref, *refs):
     arrived_refs, out_refs = refs[:-planes], refs[-planes:]
-    count = len(arrived_refs)
+    rows = arrived_refs[0].shape[-2]
+    by_steps = len(arrived_refs) > 1
     weights = side_by_side(weights_ref[...] * (1.0 / 18.0))
     for plane in range(planes):
 
         def read(block, start, size):
-            return arrived_refs[-block % count][plane, pl.ds(start, size), :]
+            if by_steps:
+                return arrived_refs[-block % count][plane, pl.ds(start, size), :]
+            return arrived_refs[0][block, plane, pl.ds(start, size), :]
 
         def write(block, start, size, value):
             at = pl.ds(pl.multiple_of(block * rows + start, 8), size)
             out_refs[plane][at, :] = value
 
-        swap_into(read, write, count, rows, after=me_ref[0])
+        swap_into(read, write, count, rows, after=me_ref[0] if by_steps else None)
         tile = rows * count // 6
 
         def add(index, carry):
@@ -136,12 +138,12 @@
 
 
 def swap_out(me, arrived, high, low, weights, first_plane):
-    count = len(arrived)
-    planes, rows, _ = arrived[0].shape
+    count = len(arrived) if len(arrived) > 1 else arrived[0].shape[0]
+    planes, rows = arrived[0].shape[-3:-1]
     cells = count * rows
     basis = pl.BlockSpec((planes, cells, 2 * LANES), lambda i: (first_plane // planes, 0, 0))
     return pl.pallas_call(
-        swap_out_kernel,
+        functools.partial(swap_out_kernel, planes, count),
         grid=(1,),
         in_specs=[
             pl.BlockSpec(memory_space=pltpu.SMEM),
@@ -149,7 +151,7 @@
             basis,
             pl.BlockSpec(weights.shape, lambda i: (0, 0)),
         ]
-        + [pl.BlockSpec(arrived[0].shape, lambda i: (0, 0, 0))] * count,
+        + [pl.BlockSpec(arrived[0].shape, lambda i: (0,) * arrived[0].ndim)] * len(arrived),
         out_specs=[pl.BlockSpec((None, cells, LANES), lambda i: (0, 0, 0))] * planes,
         out_shape=[jax.ShapeDtypeStruct((1, cells, LANES), jnp.float32)] * planes,
         compiler_params=params(24),
@@ -190,8 +192,8 @@
     lax.fori_loop(0, side_y, row, 0)
 
 
-def filter_kernel(planes, side_y, side_z, width, chunks, me_ref, arrived_ref, *rest):
-    outs, (field, padded, first, flat, potential) = rest[:-5], rest[-5:]
+def filter_kernel(planes, side_y, side_z, width, half, me_ref, arrived_ref, *rest):
+    near_refs, late_ref, (field, padded, first, flat, potential) = rest[:-6], rest[-6], rest[-5:]
     count = arrived_ref.shape[0]
     cells = side_y * side_z
     rows = cells // count
@@ -242,27 +244,29 @@
     local_part(padded, potential, planes, 0, side_y, side_z, line_of, finish_first)
     local_part(first, potential, planes, 0, side_y, side_z, line_of, finish_second)
 
-    for index, (begin, size_of) in enumerate(chunks):
-        group = outs[index * count : (index + 1) * count]
-        for plane in range(size_of):
-
-            def read_out(block, start, size):
-                return flat[begin + plane, pl.ds(pl.multiple_of(block * rows + start, 8), size), :]
-
-            def write_out(block, start, size, value):
-                group[block][plane, pl.ds(start, size), :] = value
-
-            swap_into(read_out, write_out, count, rows, before=me_ref[0])
-
-
-def filter_orbitals(me, arrived, side_y, side_z, width, chunks):
+    for plane in range(planes):
+
+        def read_out(block, start, size):
+            return flat[plane, pl.ds(pl.multiple_of(block * rows + start, 8), size), :]
+
+        def write_out(block, start, size, value):
+            if plane < half:
+                near_refs[block][plane, pl.ds(start, size), :] = value
+            else:
+                late_ref[block, plane - half, pl.ds(start, size), :] = value
+
+        swap_into(read_out, write_out, count, rows, before=me_ref[0] if plane < half else None)
+
+
+def filter_orbitals(me, arrived, side_y, side_z, width, half):
     count, planes = arrived.shape[:2]
     rows = side_y * side_z // count
     flat = pltpu.VMEM((planes, side_y * side_z, LANES), jnp.float32)
     padded = pltpu.VMEM((planes, side_y, side_z + 2 * PAD, LANES), jnp.float32)
-    shapes = [jax.ShapeDtypeStruct((size, rows, LANES), jnp.float32) for _, size in chunks for _ in range(count)]
+    shapes = [jax.ShapeDtypeStruct((half, rows, LANES), jnp.float32)] * count
+    shapes += [jax.ShapeDtypeStruct((count, planes - half, rows, LANES), jnp.float32)]
     outs = pl.pallas_call(
-        functools.partial(filter_kernel, planes, side_y, side_z, width, chunks),
+        functools.partial(filter_kernel, planes, side_y, side_z, width, half),
         in_specs=[pl.BlockSpec(memory_space=pltpu.SMEM), WHOLE],
         out_specs=[WHOLE] * len(shapes),
         out_shape=shapes,
@@ -270,7 +274,7 @@
         compiler_params=params(56),
         cost_estimate=cost(100 * arrived.size, 12 * arrived.size),
     )(me, arrived)
-    return [outs[index * count : (index + 1) * count] for index in range(len(chunks))]
+    return list(outs[:count]), outs[count]
 
 
 def basis_kernel(planes, side_y, side_z, bands, *refs):
@@ -626,7 +630,7 @@
     norb = local_orbs * bands
     chunks = tuple((plane, 1) for plane in range(planes))
     half = planes // 2
-    groups = ((0, half), (half, half))
+    tie = lax.optimization_barrier
     me = lax.axis_index("dom").astype(jnp.int32).reshape(1)
 
     order = jnp.arange(bands, dtype=jnp.int32) ^ band
@@ -659,17 +663,16 @@
         everyone[:, : 3 * LANES].reshape(blocks, 3, LANES, LANES), everyone[:, 3 * LANES :, :vectors],
     )
 
-    seconds = filter_orbitals(me, arrived, side_y, side_z, width, groups)
-
-    tie = lax.optimization_barrier
-    came = exchanged(seconds[0])
-    packed, came[1:3] = tie((seconds[1], came[1:3]))
-    coming = exchanged(packed)
+    early, late = filter_orbitals(me, arrived, side_y, side_z, width, half)
+
+    came = exchanged(early)
+    late, came = tie((late, came))
+    coming = lax.all_to_all(late, "dom", 0, 0, tiled=True)
     owns = list(swap_out(me, came, high, low, weights, 0))
     acrosses = [crossed(own, 2) for own in owns]
     besides = [crossed(own, 1) for own in owns]
     coming, acrosses[0] = tie((coming, acrosses[0]))
-    late = list(swap_out(me, coming, high, low, weights, half))
+    late = list(swap_out(me, [coming], high, low, weights, half))
     late, acrosses[1:] = tie((late, acrosses[1:]))
     acrosses += [crossed(own, 2) for own in late]
     besides += [crossed(own, 1) for own in late]

time: 353 us -> 347 us (0.983)
  starting transfers between devices: 79.2 us -> 44.6 us
  waiting for transfers between devices: 117 us -> 136 us
  local copies, waits for them, and re-layouts: 18.4 us -> 24.6 us
  Pallas kernels: 91.2 us -> 95.3 us
    ppermute x17 -> x10, starting transfers between devices: 66.3 us -> 18.3 us  [shifted(): lax.ppermute(value, axis, [(source, (source + step) % count) for source i...]
    ppermute x18, waiting for transfers between devices: 52.2 us -> 70.4 us  [crossed(): lax.ppermute(value, 'band', [(source, source ^ bit) for source in range(l...]
    all_to_all x0 -> x1, starting transfers between devices: none -> 13.2 us  [shards(): coming = lax.all_to_all(late, 'dom', 0, 0, tiled=True)]
    unnamed x73, local copies, waits for them, and re-layouts: 7.29 us -> 13.2 us
    all_to_all x0 -> x1, waiting for transfers between devices: none -> 4.55 us  [shards(): coming = lax.all_to_all(late, 'dom', 0, 0, tiled=True)]
    ppermute x17 -> x10, waiting for transfers between devices: 19.3 us -> 15.1 us  [shifted(): lax.ppermute(value, axis, [(source, (source + step) % count) for source i...]
  transfers between devices with their start and end apart: 37 -> 31, of which waited for: 16 -> 15; matrix products, arithmetic and copies ran while one was open for 4% -> 4% of each run, Pallas kernels for 14% -> 17%
where the time goes in v11:
time: 347 us; the launch traced here: 346 us
  waiting for transfers between devices  136 us (39%)
  Pallas kernels  95.3 us (27%)
  starting transfers between devices  44.6 us (13%)
  blocking collectives  26.7 us (8%)
  local copies, waits for them, and re-layouts  24.6 us (7%)
  between operations  14.5 us (4%)
  other arithmetic  4.64 us (1%)
    ppermute x18, waiting for transfers between devices, crossed(): lax.ppermute(value, 'band', [(source, source ^ bit) for source in range(l...  70.4 us
    all_to_all x1, waiting for transfers between devices, shards(): arrived = lax.all_to_all(packed, 'dom', 0, 0, tiled=True)  45.8 us
    pallas_call x1, Pallas kernels, cholesky_inverse(): pl.pallas_call(cholesky_kernel, in_specs=[pl.BlockSpec(memory_space=pltpu...  25.5 us
    pallas_call x1, Pallas kernels, filter_orbitals(): pl.pallas_call(functools.partial(filter_kernel, planes, side_y, side_z, w...  22.1 us
    ppermute x10, starting transfers between devices, shifted(): lax.ppermute(value, axis, [(source, (source + step) % count) for source i...  18.3 us
    ppermute x10, waiting for transfers between devices, shifted(): lax.ppermute(value, axis, [(source, (source + step) % count) for source i...  15.1 us
    all_to_all x1, blocking collectives, shards(): lax.all_to_all(part.reshape(blocks, width, norb), 'dom', 0, 0, tiled=True)  14.7 us
    pallas_call x1, Pallas kernels, build_basis(): pl.pallas_call(functools.partial(basis_kernel, planes, side_y, side_z, le...  13.5 us
  transfers between devices with their start and end apart: 31, of which 15 were waited for; matrix products, arithmetic and copies ran while one was open for 4% of the time, Pallas kernels for 17%

profile of v11, /device:TPU:0, one launch (start us, length us, event | category | flops | bytes accessed | tf_op | source)
XLA Modules:
  0.0 346.2 jit_solution(6107829402212075788)
XLA Ops:
  9.8 6.1 %collective-permute-start.2 = (f32[8,4736]{1,0:T(8,128)S(1)}, f32[8,4736]{1,0:T(8,128)S(1)}, u32[]{:S(2)}, u32[]{:S(2)}) collective-permute-start(f32[8,4736]{1,0:T(8,128)S(1)} %reshape.268), channel_id=1, source_target_pairs={{0,7},{1,0},{2,1},{3,2},{4,3},{5,4},{6,5},{7,6},{8,15},{9,8},{10,9... | collective-permute-start | bytes 454664 | tf_op jit(solution)/shard_map/ppermute | solution.py:409
  17.8 4.2 %shard_map.77 = f32[8,4,208,128]{3,2,1,0:T(8,128)} custom-call(f32[4,16,128]{2,1,0:T(8,128)S(1)} %pad.8.levels_ref, f32[4,8,192,128]{3,2,1,0:T(8,128)S(1)} %bitcast.35), custom_call_target="tpu_custom_call" | custom-call | bytes 6291456 | tf_op jit(solution)/shard_map/pallas_call | solution.py:98
  22.1 3.4 collective-permute-done.1
  26.3 3.8 %all-to-all-start = ((f32[8,4,208,128]{3,2,1,0:T(8,128)}), f32[8,4,208,128]{3,2,1,0:T(8,128)S(1)}, u32[]{:S(2)}, u32[]{:S(2)}) async-start(f32[8,4,208,128]{3,2,1,0:T(8,128)} %shard_map.77), calls=%async_computation | async-start | bytes 6815744 | tf_op jit(solution)/shard_map/all_to_all | solution.py:645
  33.4 11.2 %collective-permute-done.4.refs_2_ = f32[4,8,4736]{2,1,0:T(8,128)} collective-permute-done((f32[4,8,4736]{2,1,0:T(8,128)}, f32[4,8,4736]{2,1,0:T(8,128)}, u32[]{:S(2)}, u32[]{:S(2)}) %collective-permute-start.4) | collective-permute-done | bytes 606240 | tf_op jit(solution)/shard_map/ppermute | solution.py:417
  51.2 13.5 %shard_map.78 = (bf16[4,1536,256]{2,1,0:T(8,128)(2,1)}, bf16[4,1536,256]{2,1,0:T(8,128)(2,1)}, f32[3,128,128]{2,1,0:T(8,128)}) custom-call(f32[4,8,4736]{2,1,0:T(8,128)} %pad_maximum_fusion.refs_0_, f32[4,8,4736]{2,1,0:T(8,128)} %collective-permute-done.3.refs_1_, f32[4,8,4736]{2,1,0:T(8,128)} %collective-permute-done.4.refs_2_, ...), custom_call_target="tpu_custom_call" | custom-call | flops 157286400 | bytes 18874368 | tf_op jit(solution)/shard_map/pallas_call | solution.py:332
  66.3 45.8 %all-to-all-done.arrived_ref = f32[8,4,208,128]{3,2,1,0:T(8,128)S(1)} async-done(((f32[8,4,208,128]{3,2,1,0:T(8,128)}), f32[8,4,208,128]{3,2,1,0:T(8,128)S(1)}, u32[]{:S(2)}, u32[]{:S(2)}) %all-to-all-start) | async-done | bytes 3407904 | tf_op jit(solution)/shard_map/all_to_all | solution.py:645
  113.8 22.1 %shard_map.80 = (f32[2,192,128]{2,1,0:T(8,128)}, f32[2,192,128]{2,1,0:T(8,128)}, f32[2,192,128]{2,1,0:T(8,128)}, f32[2,192,128]{2,1,0:T(8,128)}, f32[2,192,128]{...) custom-call(s32[1]{0:T(128)} %bitcast.1.me_ref, ...), custom_call_target="tpu_custom_call" | custom-call | flops 85196800 | bytes 10223616 | tf_op jit(solution)/shard_map/pallas_call | solution.py:268
  143.2 3.6 %collective-permute-done.6.refs_1_ = f32[2,192,128]{2,1,0:T(8,128)S(1)} collective-permute-done((f32[2,192,128]{2,1,0:T(8,128)}, f32[2,192,128]{2,1,0:T(8,128)S(1)}, u32[]{:S(2)}, u32[]{:S(2)}) %collective-permute-start.6) | collective-permute-done | bytes 196640 | tf_op jit(solution)/shard_map/ppermute | solution.py:409
  149.4 3.7 %collective-permute-start.12 = (f32[2,192,128]{2,1,0:T(8,128)}, f32[2,192,128]{2,1,0:T(8,128)S(1)}, u32[]{:S(2)}, u32[]{:S(2)}) collective-permute-start(f32[2,192,128]{2,1,0:T(8,128)} %get-tuple-element.57), channel_id=1, source_target_pairs={{0,7},{1,0},{2,1},{3,2},{4,3},{5,4},{6,5},{7,6},{8,15},{9,8},{10,9... | collective-permute-start | bytes 589832 | tf_op jit(solution)/shard_map/ppermute | solution.py:409
  153.1 6.9 %collective-permute-done.8.refs_3_ = f32[2,192,128]{2,1,0:T(8,128)S(1)} collective-permute-done((f32[2,192,128]{2,1,0:T(8,128)}, f32[2,192,128]{2,1,0:T(8,128)S(1)}, u32[]{:S(2)}, u32[]{:S(2)}) %collective-permute-start.8) | collective-permute-done | bytes 196640 | tf_op jit(solution)/shard_map/ppermute | solution.py:409
  164.6 13.2 %all-to-all-start.1 = ((f32[8,2,192,128]{3,2,1,0:T(8,128)}), f32[8,2,192,128]{3,2,1,0:T(8,128)}, u32[]{:S(2)}, u32[]{:S(2)}) async-start(f32[8,2,192,128]{3,2,1,0:T(8,128)} %get-tuple-element.58), calls=%async_computation.1 | async-start | bytes 3145728 | tf_op jit(solution)/shard_map/all_to_all | solution.py:670
  184.5 5.3 %shard_map.81 = (f32[1,1536,128]{2,1,0:T(8,128)}, f32[1,1536,128]{2,1,0:T(8,128)}) custom-call(s32[1]{0:T(128)} %bitcast.1.me_ref, bf16[4,1536,256]{2,1,0:T(8,128)(2,1)S(1)} %copy-done.1, bf16[4,1536,256]{2,1,0:T(8,128)(2,1)S(1)} %copy-done.2, f32[256,128]{1,0:T(8,128)S(1)} %shard_map.79.weights_ref, f32[2,192,128]{2,1,0:T(8,128)S(1)} %copy-done.16, ...), custom_call_target="tpu_custom_call" | custom-call | bytes 9437184 | tf_op jit(solution)/shard_map/pallas_call | solution.py:145
  191.9 18.7 %collective-permute-done.13.rest_1_.rest_2_ = f32[1,1536,128]{2,1,0:T(8,128)} collective-permute-done((f32[1,1536,128]{2,1,0:T(8,128)}, f32[1,1536,128]{2,1,0:T(8,128)}, u32[]{:S(2)}, u32[]{:S(2)}) %collective-permute-start.13) | collective-permute-done | bytes 786464 | tf_op jit(solution)/shard_map/ppermute | solution.py:417
  210.6 4.5 %all-to-all-done.1.refs_0_ = f32[8,2,192,128]{3,2,1,0:T(8,128)} async-done(((f32[8,2,192,128]{3,2,1,0:T(8,128)}), f32[8,2,192,128]{3,2,1,0:T(8,128)}, u32[]{:S(2)}, u32[]{:S(2)}) %all-to-all-start.1) | async-done | bytes 1572896 | tf_op jit(solution)/shard_map/all_to_all | solution.py:670
  217.5 5.8 %shard_map.82 = (f32[1,1536,128]{2,1,0:T(8,128)S(1)}, f32[1,1536,128]{2,1,0:T(8,128)S(1)}) custom-call(s32[1]{0:T(128)} %bitcast.1.me_ref, bf16[4,1536,256]{2,1,0:T(8,128)(2,1)S(1)} %copy-done.1, bf16[4,1536,256]{2,1,0:T(8,128)(2,1)S(1)} %copy-done.3, f32[256,128]{1,0:T(8,128)S(1)} %shard_map.79.weights_ref, f32[8,2,192,128]{3,2,1,0:T(8,128)} %all-to-all-done.1.refs_0_), custom_call_target="tpu_custom_call" | custom-call | bytes 9437184 | tf_op jit(solution)/shard_map/pallas_call | solution.py:145
  230.8 3.0 shard_map.84
  233.9 12.2 %collective-permute-done.16.rest_1_.rest_10_ = f32[1,1536,128]{2,1,0:T(8,128)S(1)} collective-permute-done((f32[1,1536,128]{2,1,0:T(8,128)S(1)}, f32[1,1536,128]{2,1,0:T(8,128)S(1)}, u32[]{:S(2)}, u32[]{:S(2)}) %collective-permute-start.16) | collective-permute-done | bytes 786464 | tf_op jit(solution)/shard_map/ppermute | solution.py:417
  249.8 16.3 %collective-permute-done.15.rest_1_.rest_14_ = f32[1,1536,128]{2,1,0:T(8,128)S(1)} collective-permute-done((f32[1,1536,128]{2,1,0:T(8,128)S(1)}, f32[1,1536,128]{2,1,0:T(8,128)S(1)}, u32[]{:S(2)}, u32[]{:S(2)}) %collective-permute-start.15) | collective-permute-done | bytes 786464 | tf_op jit(solution)/shard_map/ppermute | solution.py:417
  269.8 14.7 %all_to_all.20 = f32[8,16,512]{2,1,0:T(8,128)S(1)} all-to-all(f32[8,16,512]{2,1,0:T(8,128)S(1)} %bitcast.43), channel_id=1, replica_groups=mesh['band'=4,'dom'=8] {'dom'}, dimensions={0} | all-to-all | bytes 524288 | tf_op jit(solution)/shard_map/all_to_all | solution.py:688
  284.6 12.0 %all_to_all.21 = f32[8,16,512]{2,1,0:T(8,128)S(1)} all-to-all(f32[8,16,512]{2,1,0:T(8,128)S(1)} %broadcast_in_dim.58), channel_id=1, replica_groups=mesh['band'=4,'dom'=8] {'dom'}, dimensions={0} | all-to-all | bytes 524288 | tf_op jit(solution)/shard_map/all_to_all | solution.py:690
  298.1 4.8 %collective-permute-done.26.refs_2_ = f32[128,512]{1,0:T(8,128)S(1)} collective-permute-done((f32[128,512]{1,0:T(8,128)S(1)}, f32[128,512]{1,0:T(8,128)S(1)}, u32[]{:S(2)}, u32[]{:S(2)}) %collective-permute-start.26) | collective-permute-done | bytes 262176 | tf_op jit(solution)/shard_map/ppermute | solution.py:417
  304.4 25.5 %shard_map.87 = (f32[512,512]{1,0:T(8,128)}, f32[128,512]{1,0:T(8,128)S(1)}) custom-call(s32[1]{0:T(128)} %bitcast.band_ref, f32[128,512]{1,0:T(8,128)S(1)} %bitcast.39, f32[128,512]{1,0:T(8,128)S(1)} %collective-permute-done.25.refs_1_, f32[128,512]{1,0:T(8,128)S(1)} %collective-permute-done.26.refs_2_, f32[128,512]{1,0:T(8,128)S(1)} %collective-permute-done.27.refs_3_), custom_call_target="tpu_custom_call" | custom-call | tf_op jit(solution)/shard_map/pallas_call | solution.py:583
  330.6 8.7 %shard_map.88 = f32[4,1536,128]{2,1,0:T(8,128)} custom-call(f32[128,512]{1,0:T(8,128)} %copy-done.15, f32[1,1536,128]{2,1,0:T(8,128)} %get-tuple-element.67.own_ref.rest_0_, f32[1,1536,128]{2,1,0:T(8,128)} %collective-permute-done.17.rest_0_.rest_1_, f32[1,1536,128]{2,1,0:T(8,128)} %collective-permute-done.13.rest_1_.rest_2_, f32[1,1536,128]{2,1,0:T(8,128)} %copy-done.4, ...), custom_call_target="tpu_custom_call" | custom-call | tf_op jit(solution)/shard_map/pallas_call | solution.py:466
  (169 shorter events, 62.6 us)
Async XLA Ops:
  9.8 12.2 %collective-permute-start.2 = (f32[8,4736]{1,0:T(8,128)S(1)}, f32[8,4736]{1,0:T(8,128)S(1)}, u32[]{:S(2)}, u32[]{:S(2)}) collective-permute-start(f32[8,4736]{1,0:T(8,128)S(1)} %reshape.268), channel_id=1, source_target_pairs={{0,7},{1,0},{2,1},{3,2},{4,3},{5,4},{6,5},{7,6},{8,15},{9,8},{10,9... | collective-permute-start | bytes 454664 | tf_op jit(solution)/shard_map/ppermute | solution.py:409
  15.9 9.6 %collective-permute-start.1 = (f32[8,4736]{1,0:T(8,128)S(1)}, f32[8,4736]{1,0:T(8,128)S(1)}, u32[]{:S(2)}, u32[]{:S(2)}) collective-permute-start(f32[8,4736]{1,0:T(8,128)S(1)} %reshape.268), channel_id=1, source_target_pairs={{0,1},{1,2},{2,3},{3,4},{4,5},{5,6},{6,7},{7,0},{8,9},{9,10},{10,1... | collective-permute-start | bytes 454664 | tf_op jit(solution)/shard_map/ppermute | solution.py:409
  15.9 9.6 %collective-permute-start = (f32[8,4736]{1,0:T(8,128)S(1)}, f32[8,4736]{1,0:T(8,128)S(1)}, u32[]{:S(2)}, u32[]{:S(2)}) collective-permute-start(f32[8,4736]{1,0:T(8,128)S(1)} %reshape.268), channel_id=1, source_target_pairs={{0,2},{1,3},{2,4},{3,5},{4,6},{5,7},{6,0},{7,1},{8,10},{9,11},{10,... | collective-permute-start | bytes 454664 | tf_op jit(solution)/shard_map/ppermute | solution.py:409
  26.3 85.8 %all-to-all-start = ((f32[8,4,208,128]{3,2,1,0:T(8,128)}), f32[8,4,208,128]{3,2,1,0:T(8,128)S(1)}, u32[]{:S(2)}, u32[]{:S(2)}) async-start(f32[8,4,208,128]{3,2,1,0:T(8,128)} %shard_map.77), calls=%async_computation | async-start | bytes 6815744 | tf_op jit(solution)/shard_map/all_to_all | solution.py:645
  30.1 147.7 %all-gather.3.cloned.1.call-start = ((), (), s32[]{:S(2)}) async-start(), calls=%async_computation.4 | async-start | bytes 1916928 | tf_op jit(solution)/shard_map/all_gather | solution.py:660
  30.4 14.2 %collective-permute-start.4 = (f32[4,8,4736]{2,1,0:T(8,128)}, f32[4,8,4736]{2,1,0:T(8,128)}, u32[]{:S(2)}, u32[]{:S(2)}) collective-permute-start(f32[4,8,4736]{2,1,0:T(8,128)} %pad_maximum_fusion.refs_0_), channel_id=1, source_target_pairs={{0,16},{8,24},{16,0},{24,8},{1,17},{9,25},{17,1},{25,9},{2,18},{10... | collective-permute-start | bytes 1818632 | tf_op jit(solution)/shard_map/ppermute | solution.py:417
  33.2 13.3 %collective-permute-start.3 = (f32[4,8,4736]{2,1,0:T(8,128)}, f32[4,8,4736]{2,1,0:T(8,128)}, u32[]{:S(2)}, u32[]{:S(2)}) collective-permute-start(f32[4,8,4736]{2,1,0:T(8,128)} %pad_maximum_fusion.refs_0_), channel_id=1, source_target_pairs={{0,8},{8,0},{16,24},{24,16},{1,9},{9,1},{17,25},{25,17},{2,10},{10... | collective-permute-start | bytes 1818632 | tf_op jit(solution)/shard_map/ppermute | solution.py:417
  135.9 10.8 %collective-permute-start.6 = (f32[2,192,128]{2,1,0:T(8,128)}, f32[2,192,128]{2,1,0:T(8,128)S(1)}, u32[]{:S(2)}, u32[]{:S(2)}) collective-permute-start(f32[2,192,128]{2,1,0:T(8,128)} %get-tuple-element.51), channel_id=1, source_target_pairs={{0,1},{1,2},{2,3},{3,4},{4,5},{5,6},{6,7},{7,0},{8,9},{9,10},{10,1... | collective-permute-start | bytes 589832 | tf_op jit(solution)/shard_map/ppermute | solution.py:409
  137.3 11.4 %collective-permute-start.7 = (f32[2,192,128]{2,1,0:T(8,128)}, f32[2,192,128]{2,1,0:T(8,128)S(1)}, u32[]{:S(2)}, u32[]{:S(2)}) collective-permute-start(f32[2,192,128]{2,1,0:T(8,128)} %get-tuple-element.52), channel_id=1, source_target_pairs={{0,2},{1,3},{2,4},{3,5},{4,6},{5,7},{6,0},{7,1},{8,10},{9,11},{10,... | collective-permute-start | bytes 589832 | tf_op jit(solution)/shard_map/ppermute | solution.py:409
  137.3 22.7 %collective-permute-start.8 = (f32[2,192,128]{2,1,0:T(8,128)}, f32[2,192,128]{2,1,0:T(8,128)S(1)}, u32[]{:S(2)}, u32[]{:S(2)}) collective-permute-start(f32[2,192,128]{2,1,0:T(8,128)} %get-tuple-element.53), channel_id=1, source_target_pairs={{0,3},{1,4},{2,5},{3,6},{4,7},{5,0},{6,1},{7,2},{8,11},{9,12},{10,... | collective-permute-start | bytes 589832 | tf_op jit(solution)/shard_map/ppermute | solution.py:409
  140.3 21.6 %collective-permute-start.9 = (f32[2,192,128]{2,1,0:T(8,128)}, f32[2,192,128]{2,1,0:T(8,128)S(1)}, u32[]{:S(2)}, u32[]{:S(2)}) collective-permute-start(f32[2,192,128]{2,1,0:T(8,128)} %get-tuple-element.54), channel_id=1, source_target_pairs={{0,4},{1,5},{2,6},{3,7},{4,0},{5,1},{6,2},{7,3},{8,12},{9,13},{10,... | collective-permute-start | bytes 589832 | tf_op jit(solution)/shard_map/ppermute | solution.py:409
  141.2 21.4 %collective-permute-start.10 = (f32[2,192,128]{2,1,0:T(8,128)}, f32[2,192,128]{2,1,0:T(8,128)S(1)}, u32[]{:S(2)}, u32[]{:S(2)}) collective-permute-start(f32[2,192,128]{2,1,0:T(8,128)} %get-tuple-element.55), channel_id=1, source_target_pairs={{0,5},{1,6},{2,7},{3,0},{4,1},{5,2},{6,3},{7,4},{8,13},{9,14},{10,... | collective-permute-start | bytes 589832 | tf_op jit(solution)/shard_map/ppermute | solution.py:409
  147.4 15.9 %collective-permute-start.11 = (f32[2,192,128]{2,1,0:T(8,128)}, f32[2,192,128]{2,1,0:T(8,128)S(1)}, u32[]{:S(2)}, u32[]{:S(2)}) collective-permute-start(f32[2,192,128]{2,1,0:T(8,128)} %get-tuple-element.56), channel_id=1, source_target_pairs={{0,6},{1,7},{2,0},{3,1},{4,2},{5,3},{6,4},{7,5},{8,14},{9,15},{10,... | collective-permute-start | bytes 589832 | tf_op jit(solution)/shard_map/ppermute | solution.py:409
  149.4 14.5 %collective-permute-start.12 = (f32[2,192,128]{2,1,0:T(8,128)}, f32[2,192,128]{2,1,0:T(8,128)S(1)}, u32[]{:S(2)}, u32[]{:S(2)}) collective-permute-start(f32[2,192,128]{2,1,0:T(8,128)} %get-tuple-element.57), channel_id=1, source_target_pairs={{0,7},{1,0},{2,1},{3,2},{4,3},{5,4},{6,5},{7,6},{8,15},{9,8},{10,9... | collective-permute-start | bytes 589832 | tf_op jit(solution)/shard_map/ppermute | solution.py:409
  164.6 50.5 %all-to-all-start.1 = ((f32[8,2,192,128]{3,2,1,0:T(8,128)}), f32[8,2,192,128]{3,2,1,0:T(8,128)}, u32[]{:S(2)}, u32[]{:S(2)}) async-start(f32[8,2,192,128]{3,2,1,0:T(8,128)} %get-tuple-element.58), calls=%async_computation.1 | async-start | bytes 3145728 | tf_op jit(solution)/shard_map/all_to_all | solution.py:670
  189.8 20.8 %collective-permute-start.13 = (f32[1,1536,128]{2,1,0:T(8,128)}, f32[1,1536,128]{2,1,0:T(8,128)}, u32[]{:S(2)}, u32[]{:S(2)}) collective-permute-start(f32[1,1536,128]{2,1,0:T(8,128)} %get-tuple-element.67.own_ref.rest_0_), channel_id=1, source_target_pairs={{0,16},{8,24},{16,0},{24,8},{1,17},{9,25},{17,1},{25,9},{2,18},{10... | collective-permute-start | bytes 2359304 | tf_op jit(solution)/shard_map/ppermute | solution.py:417
  191.3 34.9 %collective-permute-start.14 = (f32[1,1536,128]{2,1,0:T(8,128)}, f32[1,1536,128]{2,1,0:T(8,128)}, u32[]{:S(2)}, u32[]{:S(2)}) collective-permute-start(f32[1,1536,128]{2,1,0:T(8,128)} %get-tuple-element.71.own_ref.rest_4_), channel_id=1, source_target_pairs={{0,16},{8,24},{16,0},{24,8},{1,17},{9,25},{17,1},{25,9},{2,18},{10... | collective-permute-start | bytes 2359304 | tf_op jit(solution)/shard_map/ppermute | solution.py:417
  191.9 35.9 %collective-permute-start.17 = (f32[1,1536,128]{2,1,0:T(8,128)}, f32[1,1536,128]{2,1,0:T(8,128)}, u32[]{:S(2)}, u32[]{:S(2)}) collective-permute-start(f32[1,1536,128]{2,1,0:T(8,128)} %get-tuple-element.67.own_ref.rest_0_), channel_id=1, source_target_pairs={{0,8},{8,0},{16,24},{24,16},{1,9},{9,1},{17,25},{25,17},{2,10},{10... | collective-permute-start | bytes 2359304 | tf_op jit(solution)/shard_map/ppermute | solution.py:417
  215.1 12.8 %collective-permute-start.18 = (f32[1,1536,128]{2,1,0:T(8,128)}, f32[1,1536,128]{2,1,0:T(8,128)S(1)}, u32[]{:S(2)}, u32[]{:S(2)}) collective-permute-start(f32[1,1536,128]{2,1,0:T(8,128)} %collective-permute-done.13.rest_1_.rest_2_), channel_id=1, source_target_pairs={{0,8},{8,0},{16,24},{24,16},{1,9},{9,1},{17,25},{25,17},{2,10},{10... | collective-permute-start | bytes 2359304 | tf_op jit(solution)/shard_map/ppermute | solution.py:417
  215.1 15.7 %collective-permute-start.19 = (f32[1,1536,128]{2,1,0:T(8,128)}, f32[1,1536,128]{2,1,0:T(8,128)S(1)}, u32[]{:S(2)}, u32[]{:S(2)}) collective-permute-start(f32[1,1536,128]{2,1,0:T(8,128)} %get-tuple-element.71.own_ref.rest_4_), channel_id=1, source_target_pairs={{0,8},{8,0},{16,24},{24,16},{1,9},{9,1},{17,25},{25,17},{2,10},{10... | collective-permute-start | bytes 2359304 | tf_op jit(solution)/shard_map/ppermute | solution.py:417
  226.2 20.0 %collective-permute-start.16 = (f32[1,1536,128]{2,1,0:T(8,128)S(1)}, f32[1,1536,128]{2,1,0:T(8,128)S(1)}, u32[]{:S(2)}, u32[]{:S(2)}) collective-permute-start(f32[1,1536,128]{2,1,0:T(8,128)S(1)} %get-tuple-element.73.own_ref.rest_8_), channel_id=1, source_target_pairs={{0,16},{8,24},{16,0},{24,8},{1,17},{9,25},{17,1},{25,9},{2,18},{10... | collective-permute-start | bytes 2359304 | tf_op jit(solution)/shard_map/ppermute | solution.py:417
  227.7 20.2 %collective-permute-start.21 = (f32[1,1536,128]{2,1,0:T(8,128)S(1)}, f32[1,1536,128]{2,1,0:T(8,128)S(1)}, u32[]{:S(2)}, u32[]{:S(2)}) collective-permute-start(f32[1,1536,128]{2,1,0:T(8,128)S(1)} %get-tuple-element.73.own_ref.rest_8_), channel_id=1, source_target_pairs={{0,8},{8,0},{16,24},{24,16},{1,9},{9,1},{17,25},{25,17},{2,10},{10... | collective-permute-start | bytes 2359304 | tf_op jit(solution)/shard_map/ppermute | solution.py:417
  246.2 20.0 %collective-permute-start.15 = (f32[1,1536,128]{2,1,0:T(8,128)S(1)}, f32[1,1536,128]{2,1,0:T(8,128)S(1)}, u32[]{:S(2)}, u32[]{:S(2)}) collective-permute-start(f32[1,1536,128]{2,1,0:T(8,128)S(1)} %get-tuple-element.72.own_ref.rest_12_), channel_id=1, source_target_pairs={{0,16},{8,24},{16,0},{24,8},{1,17},{9,25},{17,1},{25,9},{2,18},{10... | collective-permute-start | bytes 2359304 | tf_op jit(solution)/shard_map/ppermute | solution.py:417
  247.7 18.4 %collective-permute-start.23 = (f32[1,1536,128]{2,1,0:T(8,128)S(1)}, f32[1,1536,128]{2,1,0:T(8,128)S(1)}, u32[]{:S(2)}, u32[]{:S(2)}) collective-permute-start(f32[1,1536,128]{2,1,0:T(8,128)S(1)} %get-tuple-element.72.own_ref.rest_12_), channel_id=1, source_target_pairs={{0,8},{8,0},{16,24},{24,16},{1,9},{9,1},{17,25},{25,17},{2,10},{10... | collective-permute-start | bytes 2359304 | tf_op jit(solution)/shard_map/ppermute | solution.py:417
  (42 other events, 345.6 us)
Sparse Core Ops, SparseCore 0:
  66.5 69.4 all-gather.2

commit v12 on v11

--- a/solution.py
+++ b/solution.py
@@ -109,11 +109,10 @@
     )(levels, value)
 
 
-def swap_out_kernel(planes, count, me_ref, high_ref, low_ref, weights_ref, *refs):
+def swap_out_kernel(planes, count, me_ref, added_ref, *refs):
     arrived_refs, out_refs = refs[:-planes], refs[-planes:]
     rows = arrived_refs[0].shape[-2]
     by_steps = len(arrived_refs) > 1
-    weights = side_by_side(weights_ref[...] * (1.0 / 18.0))
     for plane in range(planes):
 
         def read(block, start, size):
@@ -123,40 +122,54 @@
 
         def write(block, start, size, value):
             at = pl.ds(pl.multiple_of(block * rows + start, 8), size)
-            out_refs[plane][at, :] = value
+            out_refs[plane][at, :] = value + added_ref[plane, at, :]
 
         swap_into(read, write, count, rows, after=me_ref[0] if by_steps else None)
-        tile = rows * count // 6
-
-        def add(index, carry):
-            at = pl.ds(pl.multiple_of(index * tile, 8), tile)
-            term = folded(dot_halves((high_ref[plane, at, :], low_ref[plane, at, :]), weights))
-            out_refs[plane][at, :] = out_refs[plane][at, :] + term
-            return carry
-
-        lax.fori_loop(0, 6, add, 0)
-
-
-def swap_out(me, arrived, high, low, weights, first_plane):
+
+
+def swap_out(me, arrived, added, first_plane):
     count = len(arrived) if len(arrived) > 1 else arrived[0].shape[0]
     planes, rows = arrived[0].shape[-3:-1]
     cells = count * rows
-    basis = pl.BlockSpec((planes, cells, 2 * LANES), lambda i: (first_plane // planes, 0, 0))
     return pl.pallas_call(
         functools.partial(swap_out_kernel, planes, count),
         grid=(1,),
         in_specs=[
             pl.BlockSpec(memory_space=pltpu.SMEM),
-            basis,
-            basis,
-            pl.BlockSpec(weights.shape, lambda i: (0, 0)),
+            pl.BlockSpec((planes, cells, LANES), lambda i: (first_plane // planes, 0, 0)),
         ]
         + [pl.BlockSpec(arrived[0].shape, lambda i: (0,) * arrived[0].ndim)] * len(arrived),
         out_specs=[pl.BlockSpec((None, cells, LANES), lambda i: (0, 0, 0))] * planes,
         out_shape=[jax.ShapeDtypeStruct((1, cells, LANES), jnp.float32)] * planes,
         compiler_params=params(24),
         cost_estimate=cost(0, 24 * cells * planes * LANES),
-    )(me, high, low, weights, *arrived)
+    )(me, added, *arrived)
+
+
+def spread_kernel(high_ref, low_ref, weights_ref, out_ref):
+    weights = side_by_side(weights_ref[...] * (1.0 / 18.0))
+    tile = out_ref.shape[0] // 6
+
+    def step(index, carry):
+        at = pl.ds(pl.multiple_of(index * tile, 8), tile)
+        out_ref[at, :] = folded(dot_halves((high_ref[at, :], low_ref[at, :]), weights))
+        return carry
+
+    lax.fori_loop(0, 6, step, 0)
+
+
+def spread(high, low, weights):
+    planes, cells, _ = high.shape
+    basis = pl.BlockSpec((None, cells, 2 * LANES), lambda i: (i, 0, 0))
+    return pl.pallas_call(
+        spread_kernel,
+        grid=(planes,),
+        in_specs=[basis, basis, pl.BlockSpec(weights.shape, lambda i: (0, 0))],
+        out_specs=pl.BlockSpec((None, cells, LANES), lambda i: (i, 0, 0)),
+        out_shape=jax.ShapeDtypeStruct((planes, cells, LANES), jnp.float32),
+        compiler_params=params(24),
+        cost_estimate=cost(0, 8 * high.size),
+    )(high, low, weights)
 
 
 def fill_row(target, plane, y, row, side_z):
@@ -193,7 +206,7 @@
 
 
 def filter_kernel(planes, side_y, side_z, width, half, me_ref, arrived_ref, *rest):
-    near_refs, late_ref, (field, padded, first, flat, potential) = rest[:-6], rest[-6], rest[-5:]
+    near_refs, late_refs, (field, padded, first, flat, potential) = rest[: -5 - planes + half], rest[-5 - planes + half : -5], rest[-5:]
     count = arrived_ref.shape[0]
     cells = side_y * side_z
     rows = cells // count
@@ -253,7 +266,7 @@
             if plane < half:
                 near_refs[block][plane, pl.ds(start, size), :] = value
             else:
-                late_ref[block, plane - half, pl.ds(start, size), :] = value
+                late_refs[plane - half][block, 0, pl.ds(start, size), :] = value
 
         swap_into(read_out, write_out, count, rows, before=me_ref[0] if plane < half else None)
 
@@ -264,7 +277,7 @@
     flat = pltpu.VMEM((planes, side_y * side_z, LANES), jnp.float32)
     padded = pltpu.VMEM((planes, side_y, side_z + 2 * PAD, LANES), jnp.float32)
     shapes = [jax.ShapeDtypeStruct((half, rows, LANES), jnp.float32)] * count
-    shapes += [jax.ShapeDtypeStruct((count, planes - half, rows, LANES), jnp.float32)]
+    shapes += [jax.ShapeDtypeStruct((count, 1, rows, LANES), jnp.float32)] * (planes - half)
     outs = pl.pallas_call(
         functools.partial(filter_kernel, planes, side_y, side_z, width, half),
         in_specs=[pl.BlockSpec(memory_space=pltpu.SMEM), WHOLE],
@@ -274,7 +287,7 @@
         compiler_params=params(56),
         cost_estimate=cost(100 * arrived.size, 12 * arrived.size),
     )(me, arrived)
-    return list(outs[:count]), outs[count]
+    return list(outs[:count]), list(outs[count:])
 
 
 def basis_kernel(planes, side_y, side_z, bands, *refs):
@@ -666,17 +679,25 @@
     early, late = filter_orbitals(me, arrived, side_y, side_z, width, half)
 
     came = exchanged(early)
-    late, came = tie((late, came))
-    coming = lax.all_to_all(late, "dom", 0, 0, tiled=True)
-    owns = list(swap_out(me, came, high, low, weights, 0))
+    added = spread(high, low, weights)
+    owns = list(swap_out(me, came, added, 0))
     acrosses = [crossed(own, 2) for own in owns]
     besides = [crossed(own, 1) for own in owns]
-    coming, acrosses[0] = tie((coming, acrosses[0]))
-    late = list(swap_out(me, [coming], high, low, weights, half))
-    late, acrosses[1:] = tie((late, acrosses[1:]))
-    acrosses += [crossed(own, 2) for own in late]
-    besides += [crossed(own, 1) for own in late]
-    owns += late
+    for index, packed in enumerate(late):
+        if index:
+            packed, coming = tie((packed, coming))
+            own = swap_out(me, [coming], added, half + index - 1)[0]
+            own, acrosses[index] = tie((own, acrosses[index]))
+            owns.append(own)
+            acrosses.append(crossed(own, 2))
+            besides.append(crossed(own, 1))
+        else:
+            packed, owns = tie((packed, owns))
+        coming = lax.all_to_all(packed, "dom", 0, 0, tiled=True)
+        coming, acrosses[index] = tie((coming, acrosses[index]))
+    owns.append(swap_out(me, [coming], added, planes - 1)[0])
+    acrosses.append(crossed(owns[-1], 2))
+    besides.append(crossed(owns[-1], 1))
     panels, part = [], None
     for index, across in enumerate(acrosses):
         if index >= half:

time: 347 us -> 349 us (level)
  starting transfers between devices: 44.6 us -> 48.6 us
    ppermute x18, waiting for transfers between devices: 70.4 us -> 80 us  [crossed(): lax.ppermute(value, 'band', [(source, source ^ bit) for source in range(l...]
    ppermute x10, waiting for transfers between devices: 15.1 us -> 6.97 us  [shifted(): lax.ppermute(value, axis, [(source, (source + step) % count) for source i...]
    pallas_call x0 -> x1, Pallas kernels: none -> 5.66 us  [spread(): pl.pallas_call(spread_kernel, grid=(planes,), in_specs=[basis, basis, pl....]
    pallas_call x2 -> x3, Pallas kernels: 11.1 us -> 6.97 us  [swap_out(): pl.pallas_call(functools.partial(swap_out_kernel, planes, count), grid=(1...]
    all_to_all x1 -> x2, starting transfers between devices: 13.2 us -> 15.9 us  [shards(): coming = lax.all_to_all(packed, 'dom', 0, 0, tiled=True)]
    unnamed x73 -> x49, local copies, waits for them, and re-layouts: 13.2 us -> 12.2 us
  transfers between devices with their start and end apart: 31 -> 32, of which waited for: 15 -> 13; matrix products, arithmetic and copies ran while one was open for 4% -> 4% of each run, Pallas kernels for 17% -> 17%
where the time goes in v12:
time: 349 us; the launch traced here: 348 us
  waiting for transfers between devices  135 us (39%)
  Pallas kernels  96.3 us (28%)
  starting transfers between devices  48.6 us (14%)
  blocking collectives  25.7 us (7%)
  local copies, waits for them, and re-layouts  23.2 us (7%)
  between operations  14.5 us (4%)
  other arithmetic  4.63 us (1%)
    ppermute x18, waiting for transfers between devices, crossed(): lax.ppermute(value, 'band', [(source, source ^ bit) for source in range(l...  80 us
    all_to_all x1, waiting for transfers between devices, shards(): arrived = lax.all_to_all(packed, 'dom', 0, 0, tiled=True)  45.8 us
    pallas_call x1, Pallas kernels, cholesky_inverse(): pl.pallas_call(cholesky_kernel, in_specs=[pl.BlockSpec(memory_space=pltpu...  25.5 us
    pallas_call x1, Pallas kernels, filter_orbitals(): pl.pallas_call(functools.partial(filter_kernel, planes, side_y, side_z, w...  22 us
    ppermute x10, starting transfers between devices, shifted(): lax.ppermute(value, axis, [(source, (source + step) % count) for source i...  19 us
    all_to_all x2, starting transfers between devices, shards(): coming = lax.all_to_all(packed, 'dom', 0, 0, tiled=True)  15.9 us
    all_to_all x1, blocking collectives, shards(): lax.all_to_all(part.reshape(blocks, width, norb), 'dom', 0, 0, tiled=True)  13.7 us
    pallas_call x1, Pallas kernels, build_basis(): pl.pallas_call(functools.partial(basis_kernel, planes, side_y, side_z, le...  13.5 us
  transfers between devices with their start and end apart: 32, of which 13 were waited for; matrix products, arithmetic and copies ran while one was open for 4% of the time, Pallas kernels for 17%

profile of v12, /device:TPU:0, one launch (start us, length us, event | category | flops | bytes accessed | tf_op | source)
XLA Modules:
  0.0 347.7 jit_solution(7111368277783677052)
XLA Ops:
  9.8 6.1 %collective-permute-start.2 = (f32[8,4736]{1,0:T(8,128)S(1)}, f32[8,4736]{1,0:T(8,128)S(1)}, u32[]{:S(2)}, u32[]{:S(2)}) collective-permute-start(f32[8,4736]{1,0:T(8,128)S(1)} %reshape.268), channel_id=1, source_target_pairs={{0,7},{1,0},{2,1},{3,2},{4,3},{5,4},{6,5},{7,6},{8,15},{9,8},{10,9... | collective-permute-start | bytes 454664 | tf_op jit(solution)/shard_map/ppermute | solution.py:422
  17.8 4.3 %shard_map.77 = f32[8,4,208,128]{3,2,1,0:T(8,128)} custom-call(f32[4,16,128]{2,1,0:T(8,128)S(1)} %pad.8.levels_ref, f32[4,8,192,128]{3,2,1,0:T(8,128)S(1)} %bitcast.35), custom_call_target="tpu_custom_call" | custom-call | bytes 6291456 | tf_op jit(solution)/shard_map/pallas_call | solution.py:98
  22.1 3.4 collective-permute-done.1
  26.3 3.8 %all-to-all-start = ((f32[8,4,208,128]{3,2,1,0:T(8,128)}), f32[8,4,208,128]{3,2,1,0:T(8,128)S(1)}, u32[]{:S(2)}, u32[]{:S(2)}) async-start(f32[8,4,208,128]{3,2,1,0:T(8,128)} %shard_map.77), calls=%async_computation | async-start | bytes 6815744 | tf_op jit(solution)/shard_map/all_to_all | solution.py:658
  33.4 11.2 %collective-permute-done.4.refs_2_ = f32[4,8,4736]{2,1,0:T(8,128)} collective-permute-done((f32[4,8,4736]{2,1,0:T(8,128)}, f32[4,8,4736]{2,1,0:T(8,128)}, u32[]{:S(2)}, u32[]{:S(2)}) %collective-permute-start.4) | collective-permute-done | bytes 606240 | tf_op jit(solution)/shard_map/ppermute | solution.py:430
  51.2 13.5 %shard_map.78 = (bf16[4,1536,256]{2,1,0:T(8,128)(2,1)}, bf16[4,1536,256]{2,1,0:T(8,128)(2,1)}, f32[3,128,128]{2,1,0:T(8,128)}) custom-call(f32[4,8,4736]{2,1,0:T(8,128)} %pad_maximum_fusion.refs_0_, f32[4,8,4736]{2,1,0:T(8,128)} %collective-permute-done.3.refs_1_, f32[4,8,4736]{2,1,0:T(8,128)} %collective-permute-done.4.refs_2_, ...), custom_call_target="tpu_custom_call" | custom-call | flops 157286400 | bytes 18874368 | tf_op jit(solution)/shard_map/pallas_call | solution.py:345
  66.3 45.8 %all-to-all-done.arrived_ref = f32[8,4,208,128]{3,2,1,0:T(8,128)S(1)} async-done(((f32[8,4,208,128]{3,2,1,0:T(8,128)}), f32[8,4,208,128]{3,2,1,0:T(8,128)S(1)}, u32[]{:S(2)}, u32[]{:S(2)}) %all-to-all-start) | async-done | bytes 3407904 | tf_op jit(solution)/shard_map/all_to_all | solution.py:658
  113.8 22.0 %shard_map.81 = (f32[2,192,128]{2,1,0:T(8,128)}, f32[2,192,128]{2,1,0:T(8,128)}, f32[2,192,128]{2,1,0:T(8,128)}, f32[2,192,128]{2,1,0:T(8,128)}, f32[2,192,128]{...) custom-call(s32[1]{0:T(128)} %bitcast.1.me_ref, ...), custom_call_target="tpu_custom_call" | custom-call | flops 85196800 | bytes 10223616 | tf_op jit(solution)/shard_map/pallas_call | solution.py:281
  137.3 2.9 collective-permute-start.8
  143.1 3.6 %collective-permute-done.6.refs_1_ = f32[2,192,128]{2,1,0:T(8,128)S(1)} collective-permute-done((f32[2,192,128]{2,1,0:T(8,128)}, f32[2,192,128]{2,1,0:T(8,128)S(1)}, u32[]{:S(2)}, u32[]{:S(2)}) %collective-permute-start.6) | collective-permute-done | bytes 196640 | tf_op jit(solution)/shard_map/ppermute | solution.py:422
  148.0 4.4 %collective-permute-start.12 = (f32[2,192,128]{2,1,0:T(8,128)}, f32[2,192,128]{2,1,0:T(8,128)}, u32[]{:S(2)}, u32[]{:S(2)}) collective-permute-start(f32[2,192,128]{2,1,0:T(8,128)} %get-tuple-element.54), channel_id=1, source_target_pairs={{0,7},{1,0},{2,1},{3,2},{4,3},{5,4},{6,5},{7,6},{8,15},{9,8},{10,9... | collective-permute-start | bytes 589832 | tf_op jit(solution)/shard_map/ppermute | solution.py:422
  160.3 5.7 %shard_map.80.added_ref = f32[4,1536,128]{2,1,0:T(8,128)S(1)} custom-call(bf16[4,1536,256]{2,1,0:T(8,128)(2,1)S(1)} %copy-done.15, bf16[4,1536,256]{2,1,0:T(8,128)(2,1)S(1)} %copy-done.16, f32[256,128]{1,0:T(8,128)S(1)} %shard_map.79.weights_ref), custom_call_target="tpu_custom_call" | custom-call | bytes 12582912 | tf_op jit(solution)/shard_map/pallas_call | solution.py:164
  166.0 2.9 shard_map.82
  170.7 11.2 %all-to-all-start.1 = ((f32[8,1,192,128]{3,2,1,0:T(8,128)}), f32[8,1,192,128]{3,2,1,0:T(8,128)}, u32[]{:S(2)}, u32[]{:S(2)}) async-start(f32[8,1,192,128]{3,2,1,0:T(8,128)} %get-tuple-element.57), calls=%async_computation.1 | async-start | bytes 1572864 | tf_op jit(solution)/shard_map/all_to_all | solution.py:696
  183.4 18.0 %collective-permute-done.13.rest_1_.rest_2_ = f32[1,1536,128]{2,1,0:T(8,128)} collective-permute-done((f32[1,1536,128]{2,1,0:T(8,128)}, f32[1,1536,128]{2,1,0:T(8,128)}, u32[]{:S(2)}, u32[]{:S(2)}) %collective-permute-start.13) | collective-permute-done | bytes 786464 | tf_op jit(solution)/shard_map/ppermute | solution.py:430
  202.4 4.7 %all-to-all-start.2 = ((f32[8,1,192,128]{3,2,1,0:T(8,128)}), f32[8,1,192,128]{3,2,1,0:T(8,128)}, u32[]{:S(2)}, u32[]{:S(2)}) async-start(f32[8,1,192,128]{3,2,1,0:T(8,128)} %get-tuple-element.59), calls=%async_computation.2 | async-start | bytes 1572864 | tf_op jit(solution)/shard_map/all_to_all | solution.py:696
  211.9 13.5 %collective-permute-done.14.rest_1_.rest_6_ = f32[1,1536,128]{2,1,0:T(8,128)} collective-permute-done((f32[1,1536,128]{2,1,0:T(8,128)}, f32[1,1536,128]{2,1,0:T(8,128)}, u32[]{:S(2)}, u32[]{:S(2)}) %collective-permute-start.14) | collective-permute-done | bytes 786464 | tf_op jit(solution)/shard_map/ppermute | solution.py:430
  234.8 11.8 %collective-permute-done.16.rest_1_.rest_10_ = f32[1,1536,128]{2,1,0:T(8,128)S(1)} collective-permute-done((f32[1,1536,128]{2,1,0:T(8,128)}, f32[1,1536,128]{2,1,0:T(8,128)S(1)}, u32[]{:S(2)}, u32[]{:S(2)}) %collective-permute-start.16) | collective-permute-done | bytes 786464 | tf_op jit(solution)/shard_map/ppermute | solution.py:430
  251.8 16.7 %collective-permute-done.15.rest_1_.rest_14_ = f32[1,1536,128]{2,1,0:T(8,128)S(1)} collective-permute-done((f32[1,1536,128]{2,1,0:T(8,128)S(1)}, f32[1,1536,128]{2,1,0:T(8,128)S(1)}, u32[]{:S(2)}, u32[]{:S(2)}) %collective-permute-start.15) | collective-permute-done | bytes 786464 | tf_op jit(solution)/shard_map/ppermute | solution.py:430
  272.3 13.7 %all_to_all.25 = f32[8,16,512]{2,1,0:T(8,128)S(1)} all-to-all(f32[8,16,512]{2,1,0:T(8,128)S(1)} %bitcast.43), channel_id=1, replica_groups=mesh['band'=4,'dom'=8] {'dom'}, dimensions={0} | all-to-all | bytes 524288 | tf_op jit(solution)/shard_map/all_to_all | solution.py:709
  286.0 12.0 %all_to_all.26 = f32[8,16,512]{2,1,0:T(8,128)S(1)} all-to-all(f32[8,16,512]{2,1,0:T(8,128)S(1)} %broadcast_in_dim.58), channel_id=1, replica_groups=mesh['band'=4,'dom'=8] {'dom'}, dimensions={0} | all-to-all | bytes 524288 | tf_op jit(solution)/shard_map/all_to_all | solution.py:711
  299.5 4.9 %collective-permute-done.26.refs_2_ = f32[128,512]{1,0:T(8,128)S(1)} collective-permute-done((f32[128,512]{1,0:T(8,128)S(1)}, f32[128,512]{1,0:T(8,128)S(1)}, u32[]{:S(2)}, u32[]{:S(2)}) %collective-permute-start.26) | collective-permute-done | bytes 262176 | tf_op jit(solution)/shard_map/ppermute | solution.py:430
  305.9 25.5 %shard_map.89 = (f32[512,512]{1,0:T(8,128)}, f32[128,512]{1,0:T(8,128)S(1)}) custom-call(s32[1]{0:T(128)} %bitcast.band_ref, f32[128,512]{1,0:T(8,128)S(1)} %bitcast.39, f32[128,512]{1,0:T(8,128)S(1)} %collective-permute-done.25.refs_1_, f32[128,512]{1,0:T(8,128)S(1)} %collective-permute-done.26.refs_2_, f32[128,512]{1,0:T(8,128)S(1)} %collective-permute-done.27.refs_3_), custom_call_target="tpu_custom_call" | custom-call | tf_op jit(solution)/shard_map/pallas_call | solution.py:596
  332.1 8.7 %shard_map.90 = f32[4,1536,128]{2,1,0:T(8,128)} custom-call(f32[128,512]{1,0:T(8,128)} %copy-done.17, f32[1,1536,128]{2,1,0:T(8,128)} %copy-done.4, f32[1,1536,128]{2,1,0:T(8,128)} %collective-permute-done.17.rest_0_.rest_1_, f32[1,1536,128]{2,1,0:T(8,128)} %collective-permute-done.13.rest_1_.rest_2_, ...), custom_call_target="tpu_custom_call" | custom-call | tf_op jit(solution)/shard_map/pallas_call | solution.py:479
  (149 shorter events, 63.0 us)
Async XLA Ops:
  9.8 12.2 %collective-permute-start.2 = (f32[8,4736]{1,0:T(8,128)S(1)}, f32[8,4736]{1,0:T(8,128)S(1)}, u32[]{:S(2)}, u32[]{:S(2)}) collective-permute-start(f32[8,4736]{1,0:T(8,128)S(1)} %reshape.268), channel_id=1, source_target_pairs={{0,7},{1,0},{2,1},{3,2},{4,3},{5,4},{6,5},{7,6},{8,15},{9,8},{10,9... | collective-permute-start | bytes 454664 | tf_op jit(solution)/shard_map/ppermute | solution.py:422
  15.9 9.6 %collective-permute-start.1 = (f32[8,4736]{1,0:T(8,128)S(1)}, f32[8,4736]{1,0:T(8,128)S(1)}, u32[]{:S(2)}, u32[]{:S(2)}) collective-permute-start(f32[8,4736]{1,0:T(8,128)S(1)} %reshape.268), channel_id=1, source_target_pairs={{0,1},{1,2},{2,3},{3,4},{4,5},{5,6},{6,7},{7,0},{8,9},{9,10},{10,1... | collective-permute-start | bytes 454664 | tf_op jit(solution)/shard_map/ppermute | solution.py:422
  26.3 85.8 %all-to-all-start = ((f32[8,4,208,128]{3,2,1,0:T(8,128)}), f32[8,4,208,128]{3,2,1,0:T(8,128)S(1)}, u32[]{:S(2)}, u32[]{:S(2)}) async-start(f32[8,4,208,128]{3,2,1,0:T(8,128)} %shard_map.77), calls=%async_computation | async-start | bytes 6815744 | tf_op jit(solution)/shard_map/all_to_all | solution.py:658
  30.1 122.2 %all-gather.3.cloned.1.call-start = ((), (), s32[]{:S(2)}) async-start(), calls=%async_computation.5 | async-start | bytes 1916928 | tf_op jit(solution)/shard_map/all_gather | solution.py:673
  30.4 14.2 %collective-permute-start.4 = (f32[4,8,4736]{2,1,0:T(8,128)}, f32[4,8,4736]{2,1,0:T(8,128)}, u32[]{:S(2)}, u32[]{:S(2)}) collective-permute-start(f32[4,8,4736]{2,1,0:T(8,128)} %pad_maximum_fusion.refs_0_), channel_id=1, source_target_pairs={{0,16},{8,24},{16,0},{24,8},{1,17},{9,25},{17,1},{25,9},{2,18},{10... | collective-permute-start | bytes 1818632 | tf_op jit(solution)/shard_map/ppermute | solution.py:430
  33.2 13.3 %collective-permute-start.3 = (f32[4,8,4736]{2,1,0:T(8,128)}, f32[4,8,4736]{2,1,0:T(8,128)}, u32[]{:S(2)}, u32[]{:S(2)}) collective-permute-start(f32[4,8,4736]{2,1,0:T(8,128)} %pad_maximum_fusion.refs_0_), channel_id=1, source_target_pairs={{0,8},{8,0},{16,24},{24,16},{1,9},{9,1},{17,25},{25,17},{2,10},{10... | collective-permute-start | bytes 1818632 | tf_op jit(solution)/shard_map/ppermute | solution.py:430
  135.8 10.8 %collective-permute-start.6 = (f32[2,192,128]{2,1,0:T(8,128)}, f32[2,192,128]{2,1,0:T(8,128)S(1)}, u32[]{:S(2)}, u32[]{:S(2)}) collective-permute-start(f32[2,192,128]{2,1,0:T(8,128)} %get-tuple-element.48), channel_id=1, source_target_pairs={{0,1},{1,2},{2,3},{3,4},{4,5},{5,6},{6,7},{7,0},{8,9},{9,10},{10,1... | collective-permute-start | bytes 589832 | tf_op jit(solution)/shard_map/ppermute | solution.py:422
  137.2 10.7 %collective-permute-start.7 = (f32[2,192,128]{2,1,0:T(8,128)}, f32[2,192,128]{2,1,0:T(8,128)S(1)}, u32[]{:S(2)}, u32[]{:S(2)}) collective-permute-start(f32[2,192,128]{2,1,0:T(8,128)} %get-tuple-element.49), channel_id=1, source_target_pairs={{0,2},{1,3},{2,4},{3,5},{4,6},{5,7},{6,0},{7,1},{8,10},{9,11},{10,... | collective-permute-start | bytes 589832 | tf_op jit(solution)/shard_map/ppermute | solution.py:422
  137.3 28.7 %collective-permute-start.8 = (f32[2,192,128]{2,1,0:T(8,128)}, f32[2,192,128]{2,1,0:T(8,128)}, u32[]{:S(2)}, u32[]{:S(2)}) collective-permute-start(f32[2,192,128]{2,1,0:T(8,128)} %get-tuple-element.50), channel_id=1, source_target_pairs={{0,3},{1,4},{2,5},{3,6},{4,7},{5,0},{6,1},{7,2},{8,11},{9,12},{10,... | collective-permute-start | bytes 589832 | tf_op jit(solution)/shard_map/ppermute | solution.py:422
  140.2 25.8 %collective-permute-start.9 = (f32[2,192,128]{2,1,0:T(8,128)}, f32[2,192,128]{2,1,0:T(8,128)}, u32[]{:S(2)}, u32[]{:S(2)}) collective-permute-start(f32[2,192,128]{2,1,0:T(8,128)} %get-tuple-element.51), channel_id=1, source_target_pairs={{0,4},{1,5},{2,6},{3,7},{4,0},{5,1},{6,2},{7,3},{8,12},{9,13},{10,... | collective-permute-start | bytes 589832 | tf_op jit(solution)/shard_map/ppermute | solution.py:422
  141.1 24.9 %collective-permute-start.10 = (f32[2,192,128]{2,1,0:T(8,128)}, f32[2,192,128]{2,1,0:T(8,128)}, u32[]{:S(2)}, u32[]{:S(2)}) collective-permute-start(f32[2,192,128]{2,1,0:T(8,128)} %get-tuple-element.52), channel_id=1, source_target_pairs={{0,5},{1,6},{2,7},{3,0},{4,1},{5,2},{6,3},{7,4},{8,13},{9,14},{10,... | collective-permute-start | bytes 589832 | tf_op jit(solution)/shard_map/ppermute | solution.py:422
  146.7 19.3 %collective-permute-start.11 = (f32[2,192,128]{2,1,0:T(8,128)}, f32[2,192,128]{2,1,0:T(8,128)}, u32[]{:S(2)}, u32[]{:S(2)}) collective-permute-start(f32[2,192,128]{2,1,0:T(8,128)} %get-tuple-element.53), channel_id=1, source_target_pairs={{0,6},{1,7},{2,0},{3,1},{4,2},{5,3},{6,4},{7,5},{8,14},{9,15},{10,... | collective-permute-start | bytes 589832 | tf_op jit(solution)/shard_map/ppermute | solution.py:422
  148.0 18.0 %collective-permute-start.12 = (f32[2,192,128]{2,1,0:T(8,128)}, f32[2,192,128]{2,1,0:T(8,128)}, u32[]{:S(2)}, u32[]{:S(2)}) collective-permute-start(f32[2,192,128]{2,1,0:T(8,128)} %get-tuple-element.54), channel_id=1, source_target_pairs={{0,7},{1,0},{2,1},{3,2},{4,3},{5,4},{6,5},{7,6},{8,15},{9,8},{10,9... | collective-permute-start | bytes 589832 | tf_op jit(solution)/shard_map/ppermute | solution.py:422
  170.7 31.7 %all-to-all-start.1 = ((f32[8,1,192,128]{3,2,1,0:T(8,128)}), f32[8,1,192,128]{3,2,1,0:T(8,128)}, u32[]{:S(2)}, u32[]{:S(2)}) async-start(f32[8,1,192,128]{3,2,1,0:T(8,128)} %get-tuple-element.57), calls=%async_computation.1 | async-start | bytes 1572864 | tf_op jit(solution)/shard_map/all_to_all | solution.py:696
  181.9 19.5 %collective-permute-start.13 = (f32[1,1536,128]{2,1,0:T(8,128)}, f32[1,1536,128]{2,1,0:T(8,128)}, u32[]{:S(2)}, u32[]{:S(2)}) collective-permute-start(f32[1,1536,128]{2,1,0:T(8,128)} %copy-done.4), channel_id=1, source_target_pairs={{0,16},{8,24},{16,0},{24,8},{1,17},{9,25},{17,1},{25,9},{2,18},{10... | collective-permute-start | bytes 2359304 | tf_op jit(solution)/shard_map/ppermute | solution.py:430
  202.4 24.1 %all-to-all-start.2 = ((f32[8,1,192,128]{3,2,1,0:T(8,128)}), f32[8,1,192,128]{3,2,1,0:T(8,128)}, u32[]{:S(2)}, u32[]{:S(2)}) async-start(f32[8,1,192,128]{3,2,1,0:T(8,128)} %get-tuple-element.59), calls=%async_computation.2 | async-start | bytes 1572864 | tf_op jit(solution)/shard_map/all_to_all | solution.py:696
  207.1 18.3 %collective-permute-start.14 = (f32[1,1536,128]{2,1,0:T(8,128)}, f32[1,1536,128]{2,1,0:T(8,128)}, u32[]{:S(2)}, u32[]{:S(2)}) collective-permute-start(f32[1,1536,128]{2,1,0:T(8,128)} %copy-done.6), channel_id=1, source_target_pairs={{0,16},{8,24},{16,0},{24,8},{1,17},{9,25},{17,1},{25,9},{2,18},{10... | collective-permute-start | bytes 2359304 | tf_op jit(solution)/shard_map/ppermute | solution.py:430
  208.6 19.4 %collective-permute-start.17 = (f32[1,1536,128]{2,1,0:T(8,128)}, f32[1,1536,128]{2,1,0:T(8,128)}, u32[]{:S(2)}, u32[]{:S(2)}) collective-permute-start(f32[1,1536,128]{2,1,0:T(8,128)} %copy-done.4), channel_id=1, source_target_pairs={{0,8},{8,0},{16,24},{24,16},{1,9},{9,1},{17,25},{25,17},{2,10},{10... | collective-permute-start | bytes 2359304 | tf_op jit(solution)/shard_map/ppermute | solution.py:430
  208.6 19.6 %collective-permute-start.18 = (f32[1,1536,128]{2,1,0:T(8,128)}, f32[1,1536,128]{2,1,0:T(8,128)}, u32[]{:S(2)}, u32[]{:S(2)}) collective-permute-start(f32[1,1536,128]{2,1,0:T(8,128)} %collective-permute-done.13.rest_1_.rest_2_), channel_id=1, source_target_pairs={{0,8},{8,0},{16,24},{24,16},{1,9},{9,1},{17,25},{25,17},{2,10},{10... | collective-permute-start | bytes 2359304 | tf_op jit(solution)/shard_map/ppermute | solution.py:430
  209.1 22.9 %collective-permute-start.19 = (f32[1,1536,128]{2,1,0:T(8,128)}, f32[1,1536,128]{2,1,0:T(8,128)}, u32[]{:S(2)}, u32[]{:S(2)}) collective-permute-start(f32[1,1536,128]{2,1,0:T(8,128)} %copy-done.6), channel_id=1, source_target_pairs={{0,8},{8,0},{16,24},{24,16},{1,9},{9,1},{17,25},{25,17},{2,10},{10... | collective-permute-start | bytes 2359304 | tf_op jit(solution)/shard_map/ppermute | solution.py:430
  226.5 20.2 %collective-permute-start.16 = (f32[1,1536,128]{2,1,0:T(8,128)}, f32[1,1536,128]{2,1,0:T(8,128)S(1)}, u32[]{:S(2)}, u32[]{:S(2)}) collective-permute-start(f32[1,1536,128]{2,1,0:T(8,128)} %copy-done.1), channel_id=1, source_target_pairs={{0,16},{8,24},{16,0},{24,8},{1,17},{9,25},{17,1},{25,9},{2,18},{10... | collective-permute-start | bytes 2359304 | tf_op jit(solution)/shard_map/ppermute | solution.py:430
  228.0 22.5 %collective-permute-start.21 = (f32[1,1536,128]{2,1,0:T(8,128)}, f32[1,1536,128]{2,1,0:T(8,128)S(1)}, u32[]{:S(2)}, u32[]{:S(2)}) collective-permute-start(f32[1,1536,128]{2,1,0:T(8,128)} %copy-done.1), channel_id=1, source_target_pairs={{0,8},{8,0},{16,24},{24,16},{1,9},{9,1},{17,25},{25,17},{2,10},{10... | collective-permute-start | bytes 2359304 | tf_op jit(solution)/shard_map/ppermute | solution.py:430
  248.9 19.7 %collective-permute-start.15 = (f32[1,1536,128]{2,1,0:T(8,128)S(1)}, f32[1,1536,128]{2,1,0:T(8,128)S(1)}, u32[]{:S(2)}, u32[]{:S(2)}) collective-permute-start(f32[1,1536,128]{2,1,0:T(8,128)S(1)} %shard_map.84.own_ref.rest_12_), channel_id=1, source_target_pairs={{0,16},{8,24},{16,0},{24,8},{1,17},{9,25},{17,1},{25,9},{2,18},{10... | collective-permute-start | bytes 2359304 | tf_op jit(solution)/shard_map/ppermute | solution.py:430
  250.4 18.2 %collective-permute-start.23 = (f32[1,1536,128]{2,1,0:T(8,128)S(1)}, f32[1,1536,128]{2,1,0:T(8,128)S(1)}, u32[]{:S(2)}, u32[]{:S(2)}) collective-permute-start(f32[1,1536,128]{2,1,0:T(8,128)S(1)} %shard_map.84.own_ref.rest_12_), channel_id=1, source_target_pairs={{0,8},{8,0},{16,24},{24,16},{1,9},{9,1},{17,25},{25,17},{2,10},{10... | collective-permute-start | bytes 2359304 | tf_op jit(solution)/shard_map/ppermute | solution.py:430
  (31 other events, 362.0 us)
Sparse Core Ops, SparseCore 0:
  66.4 69.5 all-gather.2

commit v13 on v12

--- a/solution.py
+++ b/solution.py
@@ -550,7 +550,7 @@
 
 
 def cholesky_kernel(band_ref, *refs):
-    rows_refs, (gram_ref, own_ref, inverse, matrix, work, corner, scaled) = refs[:-7], refs[-7:]
+    rows_refs, (gram_ref, own_ref, matrix, work, corner, scaled) = refs[:-6], refs[-6:]
     size = gram_ref.shape[0]
     bands = len(rows_refs)
     band = band_ref[0]
@@ -572,15 +572,17 @@
     def block(index, carry):
         start = pl.multiple_of(index * LANES, LANES)
         at = pl.ds(start, LANES)
+        live = pl.ds(pl.multiple_of(start + LANES, LANES), size)
         work[:, :LANES] = matrix[at, at]
         work[:, LANES:] = identity
         eliminate(work, corner)
-        scaled[...] = dot(corner[...], matrix[at, :])
-        inverse[at, :] = scaled[:, size:]
+        scaled[...] = dot(corner[...], matrix[at, live])
+        matrix[at, live] = scaled[...]
 
         def below(other, carry):
             rows = pl.ds(pl.multiple_of(other * LANES, LANES), LANES)
-            matrix[rows, :] = matrix[rows, :] - dot(scaled[:, rows].T, scaled[...])
+            columns = pl.ds(pl.multiple_of((other - index - 1) * LANES, LANES), LANES)
+            matrix[rows, live] = matrix[rows, live] - dot(scaled[:, columns].T, scaled[...])
             return carry
 
         lax.fori_loop(index + 1, size // LANES, below, 0)
@@ -588,7 +590,8 @@
 
     lax.fori_loop(0, size // LANES, block, 0)
     for member in range(bands):
-        own_ref[:, member * LANES : (member + 1) * LANES] = inverse[block_of(0), block_of(member)]
+        columns = pl.ds(pl.multiple_of(size + (band ^ member) * LANES, LANES), LANES)
+        own_ref[:, member * LANES : (member + 1) * LANES] = matrix[block_of(0), columns]
 
 
 def cholesky_inverse(band, rows):
@@ -602,11 +605,10 @@
             jax.ShapeDtypeStruct((LANES, size), jnp.float32),
         ],
         scratch_shapes=[
-            pltpu.VMEM((size, size), jnp.float32),
             pltpu.VMEM((size, 2 * size), jnp.float32),
             pltpu.VMEM((LANES, 2 * LANES), jnp.float32),
             pltpu.VMEM((LANES, LANES), jnp.float32),
-            pltpu.VMEM((LANES, 2 * size), jnp.float32),
+            pltpu.VMEM((LANES, size), jnp.float32),
         ],
         compiler_params=params(14),
     )(band.astype(jnp.int32).reshape(1), *rows)
@@ -686,15 +688,14 @@
     for index, packed in enumerate(late):
         if index:
             packed, coming = tie((packed, coming))
-            own = swap_out(me, [coming], added, half + index - 1)[0]
-            own, acrosses[index] = tie((own, acrosses[index]))
-            owns.append(own)
-            acrosses.append(crossed(own, 2))
-            besides.append(crossed(own, 1))
         else:
-            packed, owns = tie((packed, owns))
-        coming = lax.all_to_all(packed, "dom", 0, 0, tiled=True)
-        coming, acrosses[index] = tie((coming, acrosses[index]))
+            packed, acrosses[0] = tie((packed, acrosses[0]))
+        arriving = lax.all_to_all(packed, "dom", 0, 0, tiled=True)
+        if index:
+            owns.append(swap_out(me, [coming], added, half + index - 1)[0])
+            acrosses.append(crossed(owns[-1], 2))
+            besides.append(crossed(owns[-1], 1))
+        coming, acrosses[index + 1] = tie((arriving, acrosses[index + 1]))
     owns.append(swap_out(me, [coming], added, planes - 1)[0])
     acrosses.append(crossed(owns[-1], 2))
     besides.append(crossed(owns[-1], 1))

time: 349 us -> 352 us (level)
    unnamed x49 -> x51, local copies, waits for them, and re-layouts: 12.2 us -> 11.1 us
  transfers between devices with their start and end apart: 32 -> 32, of which waited for: 13 -> 12; matrix products, arithmetic and copies ran while one was open for 4% -> 4% of each run, Pallas kernels for 17% -> 17%
where the time goes in v13:
time: 352 us; the launch traced here: 351 us
  waiting for transfers between devices  137 us (39%)
  Pallas kernels  95 us (27%)
  starting transfers between devices  50.3 us (14%)
  blocking collectives  26.9 us (8%)
  local copies, waits for them, and re-layouts  22.1 us (6%)
  between operations  14.5 us (4%)
  other arithmetic  4.63 us (1%)
    ppermute x18, waiting for transfers between devices, crossed(): lax.ppermute(value, 'band', [(source, source ^ bit) for source in range(l...  83.3 us
    all_to_all x1, waiting for transfers between devices, shards(): arrived = lax.all_to_all(packed, 'dom', 0, 0, tiled=True)  45.8 us
    pallas_call x1, Pallas kernels, cholesky_inverse(): pl.pallas_call(cholesky_kernel, in_specs=[pl.BlockSpec(memory_space=pltpu...  23.5 us
    pallas_call x1, Pallas kernels, filter_orbitals(): pl.pallas_call(functools.partial(filter_kernel, planes, side_y, side_z, w...  22 us
    ppermute x10, starting transfers between devices, shifted(): lax.ppermute(value, axis, [(source, (source + step) % count) for source i...  19 us
    all_to_all x2, starting transfers between devices, shards(): arriving = lax.all_to_all(packed, 'dom', 0, 0, tiled=True)  16.9 us
    all_to_all x1, blocking collectives, shards(): lax.all_to_all(part.reshape(blocks, width, norb), 'dom', 0, 0, tiled=True)  15 us
    pallas_call x1, Pallas kernels, build_basis(): pl.pallas_call(functools.partial(basis_kernel, planes, side_y, side_z, le...  13.5 us
  transfers between devices with their start and end apart: 32, of which 12 were waited for; matrix products, arithmetic and copies ran while one was open for 4% of the time, Pallas kernels for 17%

profile of v13, /device:TPU:0, one launch (start us, length us, event | category | flops | bytes accessed | tf_op | source)
XLA Modules:
  0.0 350.7 jit_solution(12994250579254383385)
XLA Ops:
  9.8 6.1 %collective-permute-start.2 = (f32[8,4736]{1,0:T(8,128)S(1)}, f32[8,4736]{1,0:T(8,128)S(1)}, u32[]{:S(2)}, u32[]{:S(2)}) collective-permute-start(f32[8,4736]{1,0:T(8,128)S(1)} %reshape.268), channel_id=1, source_target_pairs={{0,7},{1,0},{2,1},{3,2},{4,3},{5,4},{6,5},{7,6},{8,15},{9,8},{10,9... | collective-permute-start | bytes 454664 | tf_op jit(solution)/shard_map/ppermute | solution.py:422
  17.8 4.2 %shard_map.77 = f32[8,4,208,128]{3,2,1,0:T(8,128)} custom-call(f32[4,16,128]{2,1,0:T(8,128)S(1)} %pad.8.levels_ref, f32[4,8,192,128]{3,2,1,0:T(8,128)S(1)} %bitcast.35), custom_call_target="tpu_custom_call" | custom-call | bytes 6291456 | tf_op jit(solution)/shard_map/pallas_call | solution.py:98
  22.1 3.4 collective-permute-done.1
  26.3 3.8 %all-to-all-start = ((f32[8,4,208,128]{3,2,1,0:T(8,128)}), f32[8,4,208,128]{3,2,1,0:T(8,128)S(1)}, u32[]{:S(2)}, u32[]{:S(2)}) async-start(f32[8,4,208,128]{3,2,1,0:T(8,128)} %shard_map.77), calls=%async_computation | async-start | bytes 6815744 | tf_op jit(solution)/shard_map/all_to_all | solution.py:660
  33.4 11.2 %collective-permute-done.4.refs_2_ = f32[4,8,4736]{2,1,0:T(8,128)} collective-permute-done((f32[4,8,4736]{2,1,0:T(8,128)}, f32[4,8,4736]{2,1,0:T(8,128)}, u32[]{:S(2)}, u32[]{:S(2)}) %collective-permute-start.4) | collective-permute-done | bytes 606240 | tf_op jit(solution)/shard_map/ppermute | solution.py:430
  51.2 13.5 %shard_map.78 = (bf16[4,1536,256]{2,1,0:T(8,128)(2,1)}, bf16[4,1536,256]{2,1,0:T(8,128)(2,1)}, f32[3,128,128]{2,1,0:T(8,128)}) custom-call(f32[4,8,4736]{2,1,0:T(8,128)} %pad_maximum_fusion.refs_0_, f32[4,8,4736]{2,1,0:T(8,128)} %collective-permute-done.3.refs_1_, f32[4,8,4736]{2,1,0:T(8,128)} %collective-permute-done.4.refs_2_, ...), custom_call_target="tpu_custom_call" | custom-call | flops 157286400 | bytes 18874368 | tf_op jit(solution)/shard_map/pallas_call | solution.py:345
  66.3 45.8 %all-to-all-done.arrived_ref = f32[8,4,208,128]{3,2,1,0:T(8,128)S(1)} async-done(((f32[8,4,208,128]{3,2,1,0:T(8,128)}), f32[8,4,208,128]{3,2,1,0:T(8,128)S(1)}, u32[]{:S(2)}, u32[]{:S(2)}) %all-to-all-start) | async-done | bytes 3407904 | tf_op jit(solution)/shard_map/all_to_all | solution.py:660
  113.8 22.0 %shard_map.81 = (f32[2,192,128]{2,1,0:T(8,128)}, f32[2,192,128]{2,1,0:T(8,128)}, f32[2,192,128]{2,1,0:T(8,128)}, f32[2,192,128]{2,1,0:T(8,128)}, f32[2,192,128]{...) custom-call(s32[1]{0:T(128)} %bitcast.1.me_ref, ...), custom_call_target="tpu_custom_call" | custom-call | flops 85196800 | bytes 10223616 | tf_op jit(solution)/shard_map/pallas_call | solution.py:281
  137.3 2.9 collective-permute-start.8
  143.1 3.6 %collective-permute-done.6.refs_1_ = f32[2,192,128]{2,1,0:T(8,128)S(1)} collective-permute-done((f32[2,192,128]{2,1,0:T(8,128)}, f32[2,192,128]{2,1,0:T(8,128)S(1)}, u32[]{:S(2)}, u32[]{:S(2)}) %collective-permute-start.6) | collective-permute-done | bytes 196640 | tf_op jit(solution)/shard_map/ppermute | solution.py:422
  148.0 4.4 %collective-permute-start.12 = (f32[2,192,128]{2,1,0:T(8,128)}, f32[2,192,128]{2,1,0:T(8,128)}, u32[]{:S(2)}, u32[]{:S(2)}) collective-permute-start(f32[2,192,128]{2,1,0:T(8,128)} %get-tuple-element.51), channel_id=1, source_target_pairs={{0,7},{1,0},{2,1},{3,2},{4,3},{5,4},{6,5},{7,6},{8,15},{9,8},{10,9... | collective-permute-start | bytes 589832 | tf_op jit(solution)/shard_map/ppermute | solution.py:422
  160.3 5.7 %shard_map.80.added_ref = f32[4,1536,128]{2,1,0:T(8,128)S(1)} custom-call(bf16[4,1536,256]{2,1,0:T(8,128)(2,1)S(1)} %copy-done.16, bf16[4,1536,256]{2,1,0:T(8,128)(2,1)S(1)} %copy-done.17, f32[256,128]{1,0:T(8,128)S(1)} %shard_map.79.weights_ref), custom_call_target="tpu_custom_call" | custom-call | bytes 12582912 | tf_op jit(solution)/shard_map/pallas_call | solution.py:164
  166.1 2.9 shard_map.82
  172.2 16.9 %collective-permute-done.13.rest_1_.rest_2_ = f32[1,1536,128]{2,1,0:T(8,128)S(1)} collective-permute-done((f32[1,1536,128]{2,1,0:T(8,128)S(1)}, f32[1,1536,128]{2,1,0:T(8,128)S(1)}, u32[]{:S(2)}, u32[]{:S(2)}) %collective-permute-start.13) | collective-permute-done | bytes 786464 | tf_op jit(solution)/shard_map/ppermute | solution.py:430
  190.0 12.2 %all-to-all-start.1 = ((f32[8,1,192,128]{3,2,1,0:T(8,128)}), f32[8,1,192,128]{3,2,1,0:T(8,128)}, u32[]{:S(2)}, u32[]{:S(2)}) async-start(f32[8,1,192,128]{3,2,1,0:T(8,128)} %get-tuple-element.53), calls=%async_computation.1 | async-start | bytes 1572864 | tf_op jit(solution)/shard_map/all_to_all | solution.py:693
  203.7 17.2 %collective-permute-done.14.rest_1_.rest_6_ = f32[1,1536,128]{2,1,0:T(8,128)} collective-permute-done((f32[1,1536,128]{2,1,0:T(8,128)}, f32[1,1536,128]{2,1,0:T(8,128)}, u32[]{:S(2)}, u32[]{:S(2)}) %collective-permute-start.14) | collective-permute-done | bytes 786464 | tf_op jit(solution)/shard_map/ppermute | solution.py:430
  221.9 4.7 %all-to-all-start.2 = ((f32[8,1,192,128]{3,2,1,0:T(8,128)}), f32[8,1,192,128]{3,2,1,0:T(8,128)}, u32[]{:S(2)}, u32[]{:S(2)}) async-start(f32[8,1,192,128]{3,2,1,0:T(8,128)} %get-tuple-element.56), calls=%async_computation.2 | async-start | bytes 1572864 | tf_op jit(solution)/shard_map/all_to_all | solution.py:693
  236.2 14.1 %collective-permute-done.15.rest_1_.rest_10_ = f32[1,1536,128]{2,1,0:T(8,128)} collective-permute-done((f32[1,1536,128]{2,1,0:T(8,128)}, f32[1,1536,128]{2,1,0:T(8,128)}, u32[]{:S(2)}, u32[]{:S(2)}) %collective-permute-start.15) | collective-permute-done | bytes 786464 | tf_op jit(solution)/shard_map/ppermute | solution.py:430
  257.0 15.3 %collective-permute-done.16.rest_1_.rest_14_ = f32[1,1536,128]{2,1,0:T(8,128)S(1)} collective-permute-done((f32[1,1536,128]{2,1,0:T(8,128)S(1)}, f32[1,1536,128]{2,1,0:T(8,128)S(1)}, u32[]{:S(2)}, u32[]{:S(2)}) %collective-permute-start.16) | collective-permute-done | bytes 786464 | tf_op jit(solution)/shard_map/ppermute | solution.py:430
  276.0 15.0 %all_to_all.25 = f32[8,16,512]{2,1,0:T(8,128)S(1)} all-to-all(f32[8,16,512]{2,1,0:T(8,128)S(1)} %bitcast.43), channel_id=1, replica_groups=mesh['band'=4,'dom'=8] {'dom'}, dimensions={0} | all-to-all | bytes 524288 | tf_op jit(solution)/shard_map/all_to_all | solution.py:710
  291.1 12.0 %all_to_all.26 = f32[8,16,512]{2,1,0:T(8,128)S(1)} all-to-all(f32[8,16,512]{2,1,0:T(8,128)S(1)} %broadcast_in_dim.58), channel_id=1, replica_groups=mesh['band'=4,'dom'=8] {'dom'}, dimensions={0} | all-to-all | bytes 524288 | tf_op jit(solution)/shard_map/all_to_all | solution.py:712
  304.5 4.9 %collective-permute-done.26.refs_2_ = f32[128,512]{1,0:T(8,128)S(1)} collective-permute-done((f32[128,512]{1,0:T(8,128)S(1)}, f32[128,512]{1,0:T(8,128)S(1)}, u32[]{:S(2)}, u32[]{:S(2)}) %collective-permute-start.26) | collective-permute-done | bytes 262176 | tf_op jit(solution)/shard_map/ppermute | solution.py:430
  310.9 23.5 %shard_map.89 = (f32[512,512]{1,0:T(8,128)}, f32[128,512]{1,0:T(8,128)S(1)}) custom-call(s32[1]{0:T(128)} %bitcast.band_ref, f32[128,512]{1,0:T(8,128)S(1)} %bitcast.39, f32[128,512]{1,0:T(8,128)S(1)} %collective-permute-done.25.refs_1_, f32[128,512]{1,0:T(8,128)S(1)} %collective-permute-done.26.refs_2_, f32[128,512]{1,0:T(8,128)S(1)} %collective-permute-done.27.refs_3_), custom_call_target="tpu_custom_call" | custom-call | tf_op jit(solution)/shard_map/pallas_call | solution.py:599
  335.1 8.7 %shard_map.90 = f32[4,1536,128]{2,1,0:T(8,128)} custom-call(f32[128,512]{1,0:T(8,128)} %copy-done.18, f32[1,1536,128]{2,1,0:T(8,128)} %copy-done.2, f32[1,1536,128]{2,1,0:T(8,128)} %copy-done.8, f32[1,1536,128]{2,1,0:T(8,128)} %copy-done.6, f32[1,1536,128]{2,1,0:T(8,128)} %copy-done.9, f32[1,1536,128]{2,1,0:T(8,128)} %copy-done.4, ...), custom_call_target="tpu_custom_call" | custom-call | tf_op jit(solution)/shard_map/pallas_call | solution.py:479
  (151 shorter events, 62.3 us)
Async XLA Ops:
  9.8 12.2 %collective-permute-start.2 = (f32[8,4736]{1,0:T(8,128)S(1)}, f32[8,4736]{1,0:T(8,128)S(1)}, u32[]{:S(2)}, u32[]{:S(2)}) collective-permute-start(f32[8,4736]{1,0:T(8,128)S(1)} %reshape.268), channel_id=1, source_target_pairs={{0,7},{1,0},{2,1},{3,2},{4,3},{5,4},{6,5},{7,6},{8,15},{9,8},{10,9... | collective-permute-start | bytes 454664 | tf_op jit(solution)/shard_map/ppermute | solution.py:422
  15.9 9.6 %collective-permute-start.1 = (f32[8,4736]{1,0:T(8,128)S(1)}, f32[8,4736]{1,0:T(8,128)S(1)}, u32[]{:S(2)}, u32[]{:S(2)}) collective-permute-start(f32[8,4736]{1,0:T(8,128)S(1)} %reshape.268), channel_id=1, source_target_pairs={{0,1},{1,2},{2,3},{3,4},{4,5},{5,6},{6,7},{7,0},{8,9},{9,10},{10,1... | collective-permute-start | bytes 454664 | tf_op jit(solution)/shard_map/ppermute | solution.py:422
  15.9 9.6 %collective-permute-start = (f32[8,4736]{1,0:T(8,128)S(1)}, f32[8,4736]{1,0:T(8,128)S(1)}, u32[]{:S(2)}, u32[]{:S(2)}) collective-permute-start(f32[8,4736]{1,0:T(8,128)S(1)} %reshape.268), channel_id=1, source_target_pairs={{0,2},{1,3},{2,4},{3,5},{4,6},{5,7},{6,0},{7,1},{8,10},{9,11},{10,... | collective-permute-start | bytes 454664 | tf_op jit(solution)/shard_map/ppermute | solution.py:422
  26.3 85.8 %all-to-all-start = ((f32[8,4,208,128]{3,2,1,0:T(8,128)}), f32[8,4,208,128]{3,2,1,0:T(8,128)S(1)}, u32[]{:S(2)}, u32[]{:S(2)}) async-start(f32[8,4,208,128]{3,2,1,0:T(8,128)} %shard_map.77), calls=%async_computation | async-start | bytes 6815744 | tf_op jit(solution)/shard_map/all_to_all | solution.py:660
  30.1 122.2 %all-gather.3.cloned.1.call-start = ((), (), s32[]{:S(2)}) async-start(), calls=%async_computation.5 | async-start | bytes 1916928 | tf_op jit(solution)/shard_map/all_gather | solution.py:675
  30.4 14.2 %collective-permute-start.4 = (f32[4,8,4736]{2,1,0:T(8,128)}, f32[4,8,4736]{2,1,0:T(8,128)}, u32[]{:S(2)}, u32[]{:S(2)}) collective-permute-start(f32[4,8,4736]{2,1,0:T(8,128)} %pad_maximum_fusion.refs_0_), channel_id=1, source_target_pairs={{0,16},{8,24},{16,0},{24,8},{1,17},{9,25},{17,1},{25,9},{2,18},{10... | collective-permute-start | bytes 1818632 | tf_op jit(solution)/shard_map/ppermute | solution.py:430
  33.2 13.3 %collective-permute-start.3 = (f32[4,8,4736]{2,1,0:T(8,128)}, f32[4,8,4736]{2,1,0:T(8,128)}, u32[]{:S(2)}, u32[]{:S(2)}) collective-permute-start(f32[4,8,4736]{2,1,0:T(8,128)} %pad_maximum_fusion.refs_0_), channel_id=1, source_target_pairs={{0,8},{8,0},{16,24},{24,16},{1,9},{9,1},{17,25},{25,17},{2,10},{10... | collective-permute-start | bytes 1818632 | tf_op jit(solution)/shard_map/ppermute | solution.py:430
  135.9 10.8 %collective-permute-start.6 = (f32[2,192,128]{2,1,0:T(8,128)}, f32[2,192,128]{2,1,0:T(8,128)S(1)}, u32[]{:S(2)}, u32[]{:S(2)}) collective-permute-start(f32[2,192,128]{2,1,0:T(8,128)} %get-tuple-element.45), channel_id=1, source_target_pairs={{0,1},{1,2},{2,3},{3,4},{4,5},{5,6},{6,7},{7,0},{8,9},{9,10},{10,1... | collective-permute-start | bytes 589832 | tf_op jit(solution)/shard_map/ppermute | solution.py:422
  137.3 10.7 %collective-permute-start.7 = (f32[2,192,128]{2,1,0:T(8,128)}, f32[2,192,128]{2,1,0:T(8,128)S(1)}, u32[]{:S(2)}, u32[]{:S(2)}) collective-permute-start(f32[2,192,128]{2,1,0:T(8,128)} %get-tuple-element.46), channel_id=1, source_target_pairs={{0,2},{1,3},{2,4},{3,5},{4,6},{5,7},{6,0},{7,1},{8,10},{9,11},{10,... | collective-permute-start | bytes 589832 | tf_op jit(solution)/shard_map/ppermute | solution.py:422
  137.3 28.7 %collective-permute-start.8 = (f32[2,192,128]{2,1,0:T(8,128)}, f32[2,192,128]{2,1,0:T(8,128)}, u32[]{:S(2)}, u32[]{:S(2)}) collective-permute-start(f32[2,192,128]{2,1,0:T(8,128)} %get-tuple-element.47), channel_id=1, source_target_pairs={{0,3},{1,4},{2,5},{3,6},{4,7},{5,0},{6,1},{7,2},{8,11},{9,12},{10,... | collective-permute-start | bytes 589832 | tf_op jit(solution)/shard_map/ppermute | solution.py:422
  140.2 25.8 %collective-permute-start.9 = (f32[2,192,128]{2,1,0:T(8,128)}, f32[2,192,128]{2,1,0:T(8,128)}, u32[]{:S(2)}, u32[]{:S(2)}) collective-permute-start(f32[2,192,128]{2,1,0:T(8,128)} %get-tuple-element.48), channel_id=1, source_target_pairs={{0,4},{1,5},{2,6},{3,7},{4,0},{5,1},{6,2},{7,3},{8,12},{9,13},{10,... | collective-permute-start | bytes 589832 | tf_op jit(solution)/shard_map/ppermute | solution.py:422
  141.1 24.9 %collective-permute-start.10 = (f32[2,192,128]{2,1,0:T(8,128)}, f32[2,192,128]{2,1,0:T(8,128)}, u32[]{:S(2)}, u32[]{:S(2)}) collective-permute-start(f32[2,192,128]{2,1,0:T(8,128)} %get-tuple-element.49), channel_id=1, source_target_pairs={{0,5},{1,6},{2,7},{3,0},{4,1},{5,2},{6,3},{7,4},{8,13},{9,14},{10,... | collective-permute-start | bytes 589832 | tf_op jit(solution)/shard_map/ppermute | solution.py:422
  146.7 19.3 %collective-permute-start.11 = (f32[2,192,128]{2,1,0:T(8,128)}, f32[2,192,128]{2,1,0:T(8,128)}, u32[]{:S(2)}, u32[]{:S(2)}) collective-permute-start(f32[2,192,128]{2,1,0:T(8,128)} %get-tuple-element.50), channel_id=1, source_target_pairs={{0,6},{1,7},{2,0},{3,1},{4,2},{5,3},{6,4},{7,5},{8,14},{9,15},{10,... | collective-permute-start | bytes 589832 | tf_op jit(solution)/shard_map/ppermute | solution.py:422
  148.0 18.1 %collective-permute-start.12 = (f32[2,192,128]{2,1,0:T(8,128)}, f32[2,192,128]{2,1,0:T(8,128)}, u32[]{:S(2)}, u32[]{:S(2)}) collective-permute-start(f32[2,192,128]{2,1,0:T(8,128)} %get-tuple-element.51), channel_id=1, source_target_pairs={{0,7},{1,0},{2,1},{3,2},{4,3},{5,4},{6,5},{7,6},{8,15},{9,8},{10,9... | collective-permute-start | bytes 589832 | tf_op jit(solution)/shard_map/ppermute | solution.py:422
  170.7 18.4 %collective-permute-start.13 = (f32[1,1536,128]{2,1,0:T(8,128)S(1)}, f32[1,1536,128]{2,1,0:T(8,128)S(1)}, u32[]{:S(2)}, u32[]{:S(2)}) collective-permute-start(f32[1,1536,128]{2,1,0:T(8,128)S(1)} %get-tuple-element.52.own_ref.rest_0_), channel_id=1, source_target_pairs={{0,16},{8,24},{16,0},{24,8},{1,17},{9,25},{17,1},{25,9},{2,18},{10... | collective-permute-start | bytes 2359304 | tf_op jit(solution)/shard_map/ppermute | solution.py:430
  190.0 31.9 %all-to-all-start.1 = ((f32[8,1,192,128]{3,2,1,0:T(8,128)}), f32[8,1,192,128]{3,2,1,0:T(8,128)}, u32[]{:S(2)}, u32[]{:S(2)}) async-start(f32[8,1,192,128]{3,2,1,0:T(8,128)} %get-tuple-element.53), calls=%async_computation.1 | async-start | bytes 1572864 | tf_op jit(solution)/shard_map/all_to_all | solution.py:693
  202.2 18.7 %collective-permute-start.14 = (f32[1,1536,128]{2,1,0:T(8,128)}, f32[1,1536,128]{2,1,0:T(8,128)}, u32[]{:S(2)}, u32[]{:S(2)}) collective-permute-start(f32[1,1536,128]{2,1,0:T(8,128)} %copy-done.4), channel_id=1, source_target_pairs={{0,16},{8,24},{16,0},{24,8},{1,17},{9,25},{17,1},{25,9},{2,18},{10... | collective-permute-start | bytes 2359304 | tf_op jit(solution)/shard_map/ppermute | solution.py:430
  221.9 28.4 %all-to-all-start.2 = ((f32[8,1,192,128]{3,2,1,0:T(8,128)}), f32[8,1,192,128]{3,2,1,0:T(8,128)}, u32[]{:S(2)}, u32[]{:S(2)}) async-start(f32[8,1,192,128]{3,2,1,0:T(8,128)} %get-tuple-element.56), calls=%async_computation.2 | async-start | bytes 1572864 | tf_op jit(solution)/shard_map/all_to_all | solution.py:693
  227.2 6.3 %collective-permute-start.19 = (f32[1,1536,128]{2,1,0:T(8,128)}, f32[1,1536,128]{2,1,0:T(8,128)S(1)}, u32[]{:S(2)}, u32[]{:S(2)}) collective-permute-start(f32[1,1536,128]{2,1,0:T(8,128)} %copy-done.4), channel_id=1, source_target_pairs={{0,8},{8,0},{16,24},{24,16},{1,9},{9,1},{17,25},{25,17},{2,10},{10... | collective-permute-start | bytes 2359304 | tf_op jit(solution)/shard_map/ppermute | solution.py:430
  230.5 19.8 %collective-permute-start.15 = (f32[1,1536,128]{2,1,0:T(8,128)}, f32[1,1536,128]{2,1,0:T(8,128)}, u32[]{:S(2)}, u32[]{:S(2)}) collective-permute-start(f32[1,1536,128]{2,1,0:T(8,128)} %shard_map.83.own_ref.rest_8_), channel_id=1, source_target_pairs={{0,16},{8,24},{16,0},{24,8},{1,17},{9,25},{17,1},{25,9},{2,18},{10... | collective-permute-start | bytes 2359304 | tf_op jit(solution)/shard_map/ppermute | solution.py:430
  233.4 20.7 %collective-permute-start.21 = (f32[1,1536,128]{2,1,0:T(8,128)}, f32[1,1536,128]{2,1,0:T(8,128)}, u32[]{:S(2)}, u32[]{:S(2)}) collective-permute-start(f32[1,1536,128]{2,1,0:T(8,128)} %shard_map.83.own_ref.rest_8_), channel_id=1, source_target_pairs={{0,8},{8,0},{16,24},{24,16},{1,9},{9,1},{17,25},{25,17},{2,10},{10... | collective-permute-start | bytes 2359304 | tf_op jit(solution)/shard_map/ppermute | solution.py:430
  252.3 20.0 %collective-permute-start.16 = (f32[1,1536,128]{2,1,0:T(8,128)S(1)}, f32[1,1536,128]{2,1,0:T(8,128)S(1)}, u32[]{:S(2)}, u32[]{:S(2)}) collective-permute-start(f32[1,1536,128]{2,1,0:T(8,128)S(1)} %shard_map.84.own_ref.rest_12_), channel_id=1, source_target_pairs={{0,16},{8,24},{16,0},{24,8},{1,17},{9,25},{17,1},{25,9},{2,18},{10... | collective-permute-start | bytes 2359304 | tf_op jit(solution)/shard_map/ppermute | solution.py:430
  253.9 18.5 %collective-permute-start.23 = (f32[1,1536,128]{2,1,0:T(8,128)S(1)}, f32[1,1536,128]{2,1,0:T(8,128)S(1)}, u32[]{:S(2)}, u32[]{:S(2)}) collective-permute-start(f32[1,1536,128]{2,1,0:T(8,128)S(1)} %shard_map.84.own_ref.rest_12_), channel_id=1, source_target_pairs={{0,8},{8,0},{16,24},{24,16},{1,9},{9,1},{17,25},{25,17},{2,10},{10... | collective-permute-start | bytes 2359304 | tf_op jit(solution)/shard_map/ppermute | solution.py:430
  303.0 6.4 %collective-permute-start.26 = (f32[128,512]{1,0:T(8,128)S(1)}, f32[128,512]{1,0:T(8,128)S(1)}, u32[]{:S(2)}, u32[]{:S(2)}) collective-permute-start(f32[128,512]{1,0:T(8,128)S(1)} %bitcast.37), channel_id=1, source_target_pairs={{0,16},{8,24},{16,0},{24,8},{1,17},{9,25},{17,1},{25,9},{2,18},{10... | collective-permute-start | bytes 786440 | tf_op jit(solution)/shard_map/ppermute | solution.py:430
  (32 other events, 325.9 us)
Sparse Core Ops, SparseCore 0:
  66.5 69.5 all-gather.2

commit v14 on v13

--- a/solution.py
+++ b/solution.py
@@ -110,7 +110,7 @@
 
 
 def swap_out_kernel(planes, count, me_ref, added_ref, *refs):
-    arrived_refs, out_refs = refs[:-planes], refs[-planes:]
+    arrived_refs, out_ref = refs[:-1], refs[-1]
     rows = arrived_refs[0].shape[-2]
     by_steps = len(arrived_refs) > 1
     for plane in range(planes):
@@ -122,7 +122,7 @@
 
         def write(block, start, size, value):
             at = pl.ds(pl.multiple_of(block * rows + start, 8), size)
-            out_refs[plane][at, :] = value + added_ref[plane, at, :]
+            out_ref[plane, at, :] = value + added_ref[plane, at, :]
 
         swap_into(read, write, count, rows, after=me_ref[0] if by_steps else None)
 
@@ -139,8 +139,8 @@
             pl.BlockSpec((planes, cells, LANES), lambda i: (first_plane // planes, 0, 0)),
         ]
         + [pl.BlockSpec(arrived[0].shape, lambda i: (0,) * arrived[0].ndim)] * len(arrived),
-        out_specs=[pl.BlockSpec((None, cells, LANES), lambda i: (0, 0, 0))] * planes,
-        out_shape=[jax.ShapeDtypeStruct((1, cells, LANES), jnp.float32)] * planes,
+        out_specs=pl.BlockSpec((planes, cells, LANES), lambda i: (0, 0, 0)),
+        out_shape=jax.ShapeDtypeStruct((planes, cells, LANES), jnp.float32),
         compiler_params=params(24),
         cost_estimate=cost(0, 24 * cells * planes * LANES),
     )(me, added, *arrived)
@@ -206,7 +206,7 @@
 
 
 def filter_kernel(planes, side_y, side_z, width, half, me_ref, arrived_ref, *rest):
-    near_refs, late_refs, (field, padded, first, flat, potential) = rest[: -5 - planes + half], rest[-5 - planes + half : -5], rest[-5:]
+    near_refs, late_ref, (field, padded, first, flat, potential) = rest[:-6], rest[-6], rest[-5:]
     count = arrived_ref.shape[0]
     cells = side_y * side_z
     rows = cells // count
@@ -266,7 +266,7 @@
             if plane < half:
                 near_refs[block][plane, pl.ds(start, size), :] = value
             else:
-                late_refs[plane - half][block, 0, pl.ds(start, size), :] = value
+                late_ref[block, plane - half, pl.ds(start, size), :] = value
 
         swap_into(read_out, write_out, count, rows, before=me_ref[0] if plane < half else None)
 
@@ -277,7 +277,7 @@
     flat = pltpu.VMEM((planes, side_y * side_z, LANES), jnp.float32)
     padded = pltpu.VMEM((planes, side_y, side_z + 2 * PAD, LANES), jnp.float32)
     shapes = [jax.ShapeDtypeStruct((half, rows, LANES), jnp.float32)] * count
-    shapes += [jax.ShapeDtypeStruct((count, 1, rows, LANES), jnp.float32)] * (planes - half)
+    shapes += [jax.ShapeDtypeStruct((count, planes - half, rows, LANES), jnp.float32)]
     outs = pl.pallas_call(
         functools.partial(filter_kernel, planes, side_y, side_z, width, half),
         in_specs=[pl.BlockSpec(memory_space=pltpu.SMEM), WHOLE],
@@ -287,7 +287,7 @@
         compiler_params=params(56),
         cost_estimate=cost(100 * arrived.size, 12 * arrived.size),
     )(me, arrived)
-    return list(outs[:count]), list(outs[count:])
+    return list(outs[:count]), outs[count]
 
 
 def basis_kernel(planes, side_y, side_z, bands, *refs):
@@ -643,8 +643,8 @@
     rows = cells // blocks
     width = local_orbs // blocks
     norb = local_orbs * bands
-    chunks = tuple((plane, 1) for plane in range(planes))
     half = planes // 2
+    chunks = ((0, half), (half, half))
     tie = lax.optimization_barrier
     me = lax.axis_index("dom").astype(jnp.int32).reshape(1)
 
@@ -682,30 +682,18 @@
 
     came = exchanged(early)
     added = spread(high, low, weights)
-    owns = list(swap_out(me, came, added, 0))
-    acrosses = [crossed(own, 2) for own in owns]
-    besides = [crossed(own, 1) for own in owns]
-    for index, packed in enumerate(late):
-        if index:
-            packed, coming = tie((packed, coming))
-        else:
-            packed, acrosses[0] = tie((packed, acrosses[0]))
-        arriving = lax.all_to_all(packed, "dom", 0, 0, tiled=True)
-        if index:
-            owns.append(swap_out(me, [coming], added, half + index - 1)[0])
-            acrosses.append(crossed(owns[-1], 2))
-            besides.append(crossed(owns[-1], 1))
-        coming, acrosses[index + 1] = tie((arriving, acrosses[index + 1]))
-    owns.append(swap_out(me, [coming], added, planes - 1)[0])
-    acrosses.append(crossed(owns[-1], 2))
-    besides.append(crossed(owns[-1], 1))
-    panels, part = [], None
-    for index, across in enumerate(acrosses):
-        if index >= half:
-            across, part = tie((across, part))
-        panels.append([owns[index], besides[index], across, crossed(across, 1)])
-        rows_of = gram_rows(panels[-1])
-        part = rows_of if part is None else part + rows_of
+    own = swap_out(me, came, added, 0)
+    late, own = tie((late, own))
+    coming = lax.all_to_all(late, "dom", 0, 0, tiled=True)
+    across, beside = crossed(own, 2), crossed(own, 1)
+    last = swap_out(me, [coming], added, half)
+    across, last = tie((across, last))
+    panels = [[own, beside, across, crossed(across, 1)]]
+    part = gram_rows(panels[0])
+    across, beside = crossed(last, 2), crossed(last, 1)
+    across, part = tie((across, part))
+    panels.append([last, beside, across, crossed(across, 1)])
+    part = part + gram_rows(panels[1])
 
     pieces = lax.all_to_all(part.reshape(blocks, width, norb), "dom", 0, 0, tiled=True)
     piece = jnp.sum(pieces, axis=0) * (1.0 / (planes * cells * blocks))

time: 352 us -> 338 us (0.960)
  starting transfers between devices: 50.3 us -> 42.1 us
    all_to_all x2 -> x1, waiting for transfers between devices: 1.03 us -> 35.8 us  [shards(): coming = lax.all_to_all(late, 'dom', 0, 0, tiled=True)]
    ppermute x18 -> x12, waiting for transfers between devices: 83.3 us -> 51.9 us  [crossed(): lax.ppermute(value, 'band', [(source, source ^ bit) for source in range(l...]
    ppermute x18 -> x12, starting transfers between devices: 10.5 us -> 6.36 us  [crossed(): lax.ppermute(value, 'band', [(source, source ^ bit) for source in range(l...]
    all_to_all x2 -> x1, starting transfers between devices: 16.9 us -> 12.9 us  [shards(): coming = lax.all_to_all(late, 'dom', 0, 0, tiled=True)]
    unnamed x51 -> x35, local copies, waits for them, and re-layouts: 11.1 us -> 7.71 us
    pallas_call x3 -> x2, Pallas kernels: 7.58 us -> 5.91 us  [swap_out(): pl.pallas_call(functools.partial(swap_out_kernel, planes, count), grid=(1...]
    pallas_call x4 -> x2, Pallas kernels: 8.12 us -> 6.74 us  [gram_rows(): pl.pallas_call(gram_kernel, grid=(cells // tile,), in_specs=[pl.BlockSpec...]
  transfers between devices with their start and end apart: 32 -> 25, of which waited for: 12 -> 10; matrix products, arithmetic and copies ran while one was open for 4% -> 4% of each run, Pallas kernels for 17% -> 16%
where the time goes in v14:
time: 338 us; the launch traced here: 337 us
  waiting for transfers between devices  140 us (41%)
  Pallas kernels  91.8 us (27%)
  starting transfers between devices  42.1 us (12%)
  blocking collectives  24.6 us (7%)
  local copies, waits for them, and re-layouts  18.9 us (6%)
  between operations  14.4 us (4%)
  other arithmetic  4.57 us (1%)
    ppermute x12, waiting for transfers between devices, crossed(): lax.ppermute(value, 'band', [(source, source ^ bit) for source in range(l...  51.9 us
    all_to_all x1, waiting for transfers between devices, shards(): arrived = lax.all_to_all(packed, 'dom', 0, 0, tiled=True)  45.8 us
    all_to_all x1, waiting for transfers between devices, shards(): coming = lax.all_to_all(late, 'dom', 0, 0, tiled=True)  35.8 us
    pallas_call x1, Pallas kernels, cholesky_inverse(): pl.pallas_call(cholesky_kernel, in_specs=[pl.BlockSpec(memory_space=pltpu...  23.5 us
    pallas_call x1, Pallas kernels, filter_orbitals(): pl.pallas_call(functools.partial(filter_kernel, planes, side_y, side_z, w...  22.1 us
    ppermute x10, starting transfers between devices, shifted(): lax.ppermute(value, axis, [(source, (source + step) % count) for source i...  19 us
    pallas_call x1, Pallas kernels, build_basis(): pl.pallas_call(functools.partial(basis_kernel, planes, side_y, side_z, le...  13.5 us
    all_to_all x1, starting transfers between devices, shards(): coming = lax.all_to_all(late, 'dom', 0, 0, tiled=True)  12.9 us
  transfers between devices with their start and end apart: 25, of which 10 were waited for; matrix products, arithmetic and copies ran while one was open for 4% of the time, Pallas kernels for 16%

profile of v14, /device:TPU:0, one launch (start us, length us, event | category | flops | bytes accessed | tf_op | source)
XLA Modules:
  0.0 336.8 jit_solution(764404835337891374)
XLA Ops:
  9.8 6.1 %collective-permute-start.2 = (f32[8,4736]{1,0:T(8,128)S(1)}, f32[8,4736]{1,0:T(8,128)S(1)}, u32[]{:S(2)}, u32[]{:S(2)}) collective-permute-start(f32[8,4736]{1,0:T(8,128)S(1)} %reshape.268), channel_id=1, source_target_pairs={{0,7},{1,0},{2,1},{3,2},{4,3},{5,4},{6,5},{7,6},{8,15},{9,8},{10,9... | collective-permute-start | bytes 454664 | tf_op jit(solution)/shard_map/ppermute | solution.py:422
  17.8 4.2 %shard_map.77 = f32[8,4,208,128]{3,2,1,0:T(8,128)} custom-call(f32[4,16,128]{2,1,0:T(8,128)S(1)} %pad.8.levels_ref, f32[4,8,192,128]{3,2,1,0:T(8,128)S(1)} %bitcast.35), custom_call_target="tpu_custom_call" | custom-call | bytes 6291456 | tf_op jit(solution)/shard_map/pallas_call | solution.py:98
  22.1 3.4 %collective-permute-done.1 = f32[8,4736]{1,0:T(8,128)S(1)} collective-permute-done((f32[8,4736]{1,0:T(8,128)S(1)}, f32[8,4736]{1,0:T(8,128)S(1)}, u32[]{:S(2)}, u32[]{:S(2)}) %collective-permute-start.1) | collective-permute-done | bytes 151584 | tf_op jit(solution)/shard_map/ppermute | solution.py:422
  26.3 3.8 %all-to-all-start = ((f32[8,4,208,128]{3,2,1,0:T(8,128)}), f32[8,4,208,128]{3,2,1,0:T(8,128)S(1)}, u32[]{:S(2)}, u32[]{:S(2)}) async-start(f32[8,4,208,128]{3,2,1,0:T(8,128)} %shard_map.77), calls=%async_computation | async-start | bytes 6815744 | tf_op jit(solution)/shard_map/all_to_all | solution.py:660
  33.4 11.2 %collective-permute-done.4.refs_2_ = f32[4,8,4736]{2,1,0:T(8,128)} collective-permute-done((f32[4,8,4736]{2,1,0:T(8,128)}, f32[4,8,4736]{2,1,0:T(8,128)}, u32[]{:S(2)}, u32[]{:S(2)}) %collective-permute-start.4) | collective-permute-done | bytes 606240 | tf_op jit(solution)/shard_map/ppermute | solution.py:430
  51.2 13.5 %shard_map.79 = (bf16[4,1536,256]{2,1,0:T(8,128)(2,1)}, bf16[4,1536,256]{2,1,0:T(8,128)(2,1)}, f32[3,128,128]{2,1,0:T(8,128)}) custom-call(f32[4,8,4736]{2,1,0:T(8,128)} %pad_maximum_fusion.refs_0_, f32[4,8,4736]{2,1,0:T(8,128)} %collective-permute-done.3.refs_1_, f32[4,8,4736]{2,1,0:T(8,128)} %collective-permute-done.4.refs_2_, ...), custom_call_target="tpu_custom_call" | custom-call | flops 157286400 | bytes 18874368 | tf_op jit(solution)/shard_map/pallas_call | solution.py:345
  66.3 45.8 %all-to-all-done.arrived_ref = f32[8,4,208,128]{3,2,1,0:T(8,128)S(1)} async-done(((f32[8,4,208,128]{3,2,1,0:T(8,128)}), f32[8,4,208,128]{3,2,1,0:T(8,128)S(1)}, u32[]{:S(2)}, u32[]{:S(2)}) %all-to-all-start) | async-done | bytes 3407904 | tf_op jit(solution)/shard_map/all_to_all | solution.py:660
  113.8 22.1 %shard_map.78 = (f32[2,192,128]{2,1,0:T(8,128)}, f32[2,192,128]{2,1,0:T(8,128)}, f32[2,192,128]{2,1,0:T(8,128)}, f32[2,192,128]{2,1,0:T(8,128)}, f32[2,192,128]{...) custom-call(s32[1]{0:T(128)} %bitcast.1.me_ref, ...), custom_call_target="tpu_custom_call" | custom-call | flops 85196800 | bytes 10223616 | tf_op jit(solution)/shard_map/pallas_call | solution.py:281
  137.3 2.9 collective-permute-start.8
  143.2 3.6 %collective-permute-done.6.refs_1_ = f32[2,192,128]{2,1,0:T(8,128)S(1)} collective-permute-done((f32[2,192,128]{2,1,0:T(8,128)}, f32[2,192,128]{2,1,0:T(8,128)S(1)}, u32[]{:S(2)}, u32[]{:S(2)}) %collective-permute-start.6) | collective-permute-done | bytes 196640 | tf_op jit(solution)/shard_map/ppermute | solution.py:422
  148.0 4.4 %collective-permute-start.12 = (f32[2,192,128]{2,1,0:T(8,128)}, f32[2,192,128]{2,1,0:T(8,128)}, u32[]{:S(2)}, u32[]{:S(2)}) collective-permute-start(f32[2,192,128]{2,1,0:T(8,128)} %get-tuple-element.41), channel_id=1, source_target_pairs={{0,7},{1,0},{2,1},{3,2},{4,3},{5,4},{6,5},{7,6},{8,15},{9,8},{10,9... | collective-permute-start | bytes 589832 | tf_op jit(solution)/shard_map/ppermute | solution.py:422
  158.6 5.7 %shard_map.81.added_ref = f32[4,1536,128]{2,1,0:T(8,128)S(1)} custom-call(bf16[4,1536,256]{2,1,0:T(8,128)(2,1)S(1)} %copy-done.8, bf16[4,1536,256]{2,1,0:T(8,128)(2,1)S(1)} %copy-done.9, f32[256,128]{1,0:T(8,128)S(1)} %shard_map.80.weights_ref), custom_call_target="tpu_custom_call" | custom-call | bytes 12582912 | tf_op jit(solution)/shard_map/pallas_call | solution.py:164
  164.4 2.9 shard_map.82.own_ref.rest_0_
  168.4 12.9 %all-to-all-start.1 = ((f32[8,2,192,128]{3,2,1,0:T(8,128)}), f32[8,2,192,128]{3,2,1,0:T(8,128)}, u32[]{:S(2)}, u32[]{:S(2)}) async-start(f32[8,2,192,128]{3,2,1,0:T(8,128)} %get-tuple-element.43), calls=%async_computation.1 | async-start | bytes 3145728 | tf_op jit(solution)/shard_map/all_to_all | solution.py:687
  182.8 35.8 %all-to-all-done.1.refs_0_ = f32[8,2,192,128]{3,2,1,0:T(8,128)} async-done(((f32[8,2,192,128]{3,2,1,0:T(8,128)}), f32[8,2,192,128]{3,2,1,0:T(8,128)}, u32[]{:S(2)}, u32[]{:S(2)}) %all-to-all-start.1) | async-done | bytes 1572896 | tf_op jit(solution)/shard_map/all_to_all | solution.py:687
  218.6 3.0 shard_map.83.own_ref.rest_4_
  225.4 4.1 %shard_map.84 = f32[128,512]{1,0:T(8,128)S(1)} custom-call(f32[2,1536,128]{2,1,0:T(8,128)S(1)} %copy-done.1, f32[2,1536,128]{2,1,0:T(8,128)} %collective-permute-done.15.rest_0_.rest_1_, f32[2,1536,128]{2,1,0:T(8,128)} %collective-permute-done.13.rest_1_.rest_2_, f32[2,1536,128]{2,1,0:T(8,128)S(1)} %collective-permute-done.16.rest_2_.rest_3_), custom_call_target="tpu_custom_call" | custom-call | flops 1610612736 | bytes 6291456 | tf_op jit(solution)/shard_map/pallas_call | solution.py:452
  229.5 29.0 %collective-permute-done.14.rest_1_.rest_6_ = f32[2,1536,128]{2,1,0:T(8,128)S(1)} collective-permute-done((f32[2,1536,128]{2,1,0:T(8,128)S(1)}, f32[2,1536,128]{2,1,0:T(8,128)S(1)}, u32[]{:S(2)}, u32[]{:S(2)}) %collective-permute-start.14) | collective-permute-done | bytes 1572896 | tf_op jit(solution)/shard_map/ppermute | solution.py:430
  258.6 3.4 %collective-permute-done.18.rest_2_.rest_7_ = f32[2,1536,128]{2,1,0:T(8,128)S(1)} collective-permute-done((f32[2,1536,128]{2,1,0:T(8,128)S(1)}, f32[2,1536,128]{2,1,0:T(8,128)S(1)}, u32[]{:S(2)}, u32[]{:S(2)}) %collective-permute-start.18) | collective-permute-done | bytes 1572896 | tf_op jit(solution)/shard_map/ppermute | solution.py:430
  264.7 12.7 %all_to_all.20 = f32[8,16,512]{2,1,0:T(8,128)S(1)} all-to-all(f32[8,16,512]{2,1,0:T(8,128)S(1)} %bitcast.43), channel_id=1, replica_groups=mesh['band'=4,'dom'=8] {'dom'}, dimensions={0} | all-to-all | bytes 524288 | tf_op jit(solution)/shard_map/all_to_all | solution.py:698
  277.4 12.0 %all_to_all.21 = f32[8,16,512]{2,1,0:T(8,128)S(1)} all-to-all(f32[8,16,512]{2,1,0:T(8,128)S(1)} %broadcast_in_dim.58), channel_id=1, replica_groups=mesh['band'=4,'dom'=8] {'dom'}, dimensions={0} | all-to-all | bytes 524288 | tf_op jit(solution)/shard_map/all_to_all | solution.py:700
  290.9 4.9 %collective-permute-done.20.refs_2_ = f32[128,512]{1,0:T(8,128)S(1)} collective-permute-done((f32[128,512]{1,0:T(8,128)S(1)}, f32[128,512]{1,0:T(8,128)S(1)}, u32[]{:S(2)}, u32[]{:S(2)}) %collective-permute-start.20) | collective-permute-done | bytes 262176 | tf_op jit(solution)/shard_map/ppermute | solution.py:430
  297.3 23.5 %shard_map.86 = (f32[512,512]{1,0:T(8,128)}, f32[128,512]{1,0:T(8,128)S(1)}) custom-call(s32[1]{0:T(128)} %bitcast.band_ref, f32[128,512]{1,0:T(8,128)S(1)} %bitcast.39, f32[128,512]{1,0:T(8,128)S(1)} %collective-permute-done.19.refs_1_, f32[128,512]{1,0:T(8,128)S(1)} %collective-permute-done.20.refs_2_, f32[128,512]{1,0:T(8,128)S(1)} %collective-permute-done.21.refs_3_), custom_call_target="tpu_custom_call" | custom-call | tf_op jit(solution)/shard_map/pallas_call | solution.py:599
  321.5 8.5 %shard_map.87 = f32[4,1536,128]{2,1,0:T(8,128)} custom-call(f32[128,512]{1,0:T(8,128)} %copy-done.10, f32[2,1536,128]{2,1,0:T(8,128)} %copy-done, f32[2,1536,128]{2,1,0:T(8,128)} %collective-permute-done.15.rest_0_.rest_1_, f32[2,1536,128]{2,1,0:T(8,128)} %collective-permute-done.13.rest_1_.rest_2_, f32[2,1536,128]{2,1,0:T(8,128)} %copy-done.4, ...), custom_call_target="tpu_custom_call" | custom-call | tf_op jit(solution)/shard_map/pallas_call | solution.py:479
  (116 shorter events, 43.2 us)
Async XLA Ops:
  9.8 12.2 %collective-permute-start.2 = (f32[8,4736]{1,0:T(8,128)S(1)}, f32[8,4736]{1,0:T(8,128)S(1)}, u32[]{:S(2)}, u32[]{:S(2)}) collective-permute-start(f32[8,4736]{1,0:T(8,128)S(1)} %reshape.268), channel_id=1, source_target_pairs={{0,7},{1,0},{2,1},{3,2},{4,3},{5,4},{6,5},{7,6},{8,15},{9,8},{10,9... | collective-permute-start | bytes 454664 | tf_op jit(solution)/shard_map/ppermute | solution.py:422
  15.9 9.6 %collective-permute-start.1 = (f32[8,4736]{1,0:T(8,128)S(1)}, f32[8,4736]{1,0:T(8,128)S(1)}, u32[]{:S(2)}, u32[]{:S(2)}) collective-permute-start(f32[8,4736]{1,0:T(8,128)S(1)} %reshape.268), channel_id=1, source_target_pairs={{0,1},{1,2},{2,3},{3,4},{4,5},{5,6},{6,7},{7,0},{8,9},{9,10},{10,1... | collective-permute-start | bytes 454664 | tf_op jit(solution)/shard_map/ppermute | solution.py:422
  15.9 9.6 %collective-permute-start = (f32[8,4736]{1,0:T(8,128)S(1)}, f32[8,4736]{1,0:T(8,128)S(1)}, u32[]{:S(2)}, u32[]{:S(2)}) collective-permute-start(f32[8,4736]{1,0:T(8,128)S(1)} %reshape.268), channel_id=1, source_target_pairs={{0,2},{1,3},{2,4},{3,5},{4,6},{5,7},{6,0},{7,1},{8,10},{9,11},{10,... | collective-permute-start | bytes 454664 | tf_op jit(solution)/shard_map/ppermute | solution.py:422
  26.3 85.8 %all-to-all-start = ((f32[8,4,208,128]{3,2,1,0:T(8,128)}), f32[8,4,208,128]{3,2,1,0:T(8,128)S(1)}, u32[]{:S(2)}, u32[]{:S(2)}) async-start(f32[8,4,208,128]{3,2,1,0:T(8,128)} %shard_map.77), calls=%async_computation | async-start | bytes 6815744 | tf_op jit(solution)/shard_map/all_to_all | solution.py:660
  30.1 122.3 %all-gather.3.cloned.1.call-start = ((), (), s32[]{:S(2)}) async-start(), calls=%async_computation.4 | async-start | bytes 1916928 | tf_op jit(solution)/shard_map/all_gather | solution.py:675
  30.4 14.2 %collective-permute-start.4 = (f32[4,8,4736]{2,1,0:T(8,128)}, f32[4,8,4736]{2,1,0:T(8,128)}, u32[]{:S(2)}, u32[]{:S(2)}) collective-permute-start(f32[4,8,4736]{2,1,0:T(8,128)} %pad_maximum_fusion.refs_0_), channel_id=1, source_target_pairs={{0,16},{8,24},{16,0},{24,8},{1,17},{9,25},{17,1},{25,9},{2,18},{10... | collective-permute-start | bytes 1818632 | tf_op jit(solution)/shard_map/ppermute | solution.py:430
  33.2 13.3 %collective-permute-start.3 = (f32[4,8,4736]{2,1,0:T(8,128)}, f32[4,8,4736]{2,1,0:T(8,128)}, u32[]{:S(2)}, u32[]{:S(2)}) collective-permute-start(f32[4,8,4736]{2,1,0:T(8,128)} %pad_maximum_fusion.refs_0_), channel_id=1, source_target_pairs={{0,8},{8,0},{16,24},{24,16},{1,9},{9,1},{17,25},{25,17},{2,10},{10... | collective-permute-start | bytes 1818632 | tf_op jit(solution)/shard_map/ppermute | solution.py:430
  44.6 2.8 collective-permute-start.5
  135.9 10.8 %collective-permute-start.6 = (f32[2,192,128]{2,1,0:T(8,128)}, f32[2,192,128]{2,1,0:T(8,128)S(1)}, u32[]{:S(2)}, u32[]{:S(2)}) collective-permute-start(f32[2,192,128]{2,1,0:T(8,128)} %get-tuple-element.35), channel_id=1, source_target_pairs={{0,1},{1,2},{2,3},{3,4},{4,5},{5,6},{6,7},{7,0},{8,9},{9,10},{10,1... | collective-permute-start | bytes 589832 | tf_op jit(solution)/shard_map/ppermute | solution.py:422
  137.3 10.7 %collective-permute-start.7 = (f32[2,192,128]{2,1,0:T(8,128)}, f32[2,192,128]{2,1,0:T(8,128)S(1)}, u32[]{:S(2)}, u32[]{:S(2)}) collective-permute-start(f32[2,192,128]{2,1,0:T(8,128)} %get-tuple-element.36), channel_id=1, source_target_pairs={{0,2},{1,3},{2,4},{3,5},{4,6},{5,7},{6,0},{7,1},{8,10},{9,11},{10,... | collective-permute-start | bytes 589832 | tf_op jit(solution)/shard_map/ppermute | solution.py:422
  137.3 27.0 %collective-permute-start.8 = (f32[2,192,128]{2,1,0:T(8,128)}, f32[2,192,128]{2,1,0:T(8,128)}, u32[]{:S(2)}, u32[]{:S(2)}) collective-permute-start(f32[2,192,128]{2,1,0:T(8,128)} %get-tuple-element.37), channel_id=1, source_target_pairs={{0,3},{1,4},{2,5},{3,6},{4,7},{5,0},{6,1},{7,2},{8,11},{9,12},{10,... | collective-permute-start | bytes 589832 | tf_op jit(solution)/shard_map/ppermute | solution.py:422
  140.3 24.1 %collective-permute-start.9 = (f32[2,192,128]{2,1,0:T(8,128)}, f32[2,192,128]{2,1,0:T(8,128)}, u32[]{:S(2)}, u32[]{:S(2)}) collective-permute-start(f32[2,192,128]{2,1,0:T(8,128)} %get-tuple-element.38), channel_id=1, source_target_pairs={{0,4},{1,5},{2,6},{3,7},{4,0},{5,1},{6,2},{7,3},{8,12},{9,13},{10,... | collective-permute-start | bytes 589832 | tf_op jit(solution)/shard_map/ppermute | solution.py:422
  141.2 23.1 %collective-permute-start.10 = (f32[2,192,128]{2,1,0:T(8,128)}, f32[2,192,128]{2,1,0:T(8,128)}, u32[]{:S(2)}, u32[]{:S(2)}) collective-permute-start(f32[2,192,128]{2,1,0:T(8,128)} %get-tuple-element.39), channel_id=1, source_target_pairs={{0,5},{1,6},{2,7},{3,0},{4,1},{5,2},{6,3},{7,4},{8,13},{9,14},{10,... | collective-permute-start | bytes 589832 | tf_op jit(solution)/shard_map/ppermute | solution.py:422
  146.7 17.6 %collective-permute-start.11 = (f32[2,192,128]{2,1,0:T(8,128)}, f32[2,192,128]{2,1,0:T(8,128)}, u32[]{:S(2)}, u32[]{:S(2)}) collective-permute-start(f32[2,192,128]{2,1,0:T(8,128)} %get-tuple-element.40), channel_id=1, source_target_pairs={{0,6},{1,7},{2,0},{3,1},{4,2},{5,3},{6,4},{7,5},{8,14},{9,15},{10,... | collective-permute-start | bytes 589832 | tf_op jit(solution)/shard_map/ppermute | solution.py:422
  148.0 16.3 %collective-permute-start.12 = (f32[2,192,128]{2,1,0:T(8,128)}, f32[2,192,128]{2,1,0:T(8,128)}, u32[]{:S(2)}, u32[]{:S(2)}) collective-permute-start(f32[2,192,128]{2,1,0:T(8,128)} %get-tuple-element.41), channel_id=1, source_target_pairs={{0,7},{1,0},{2,1},{3,2},{4,3},{5,4},{6,5},{7,6},{8,15},{9,8},{10,9... | collective-permute-start | bytes 589832 | tf_op jit(solution)/shard_map/ppermute | solution.py:422
  168.4 50.2 %all-to-all-start.1 = ((f32[8,2,192,128]{3,2,1,0:T(8,128)}), f32[8,2,192,128]{3,2,1,0:T(8,128)}, u32[]{:S(2)}, u32[]{:S(2)}) async-start(f32[8,2,192,128]{3,2,1,0:T(8,128)} %get-tuple-element.43), calls=%async_computation.1 | async-start | bytes 3145728 | tf_op jit(solution)/shard_map/all_to_all | solution.py:687
  181.3 40.4 %collective-permute-start.13 = (f32[2,1536,128]{2,1,0:T(8,128)}, f32[2,1536,128]{2,1,0:T(8,128)}, u32[]{:S(2)}, u32[]{:S(2)}) collective-permute-start(f32[2,1536,128]{2,1,0:T(8,128)} %copy-done), channel_id=1, source_target_pairs={{0,16},{8,24},{16,0},{24,8},{1,17},{9,25},{17,1},{25,9},{2,18},{10... | collective-permute-start | bytes 4718600 | tf_op jit(solution)/shard_map/ppermute | solution.py:430
  182.8 40.7 %collective-permute-start.15 = (f32[2,1536,128]{2,1,0:T(8,128)}, f32[2,1536,128]{2,1,0:T(8,128)}, u32[]{:S(2)}, u32[]{:S(2)}) collective-permute-start(f32[2,1536,128]{2,1,0:T(8,128)} %copy-done), channel_id=1, source_target_pairs={{0,8},{8,0},{16,24},{24,16},{1,9},{9,1},{17,25},{25,17},{2,10},{10... | collective-permute-start | bytes 4718600 | tf_op jit(solution)/shard_map/ppermute | solution.py:430
  221.7 3.7 %collective-permute-start.16 = (f32[2,1536,128]{2,1,0:T(8,128)}, f32[2,1536,128]{2,1,0:T(8,128)S(1)}, u32[]{:S(2)}, u32[]{:S(2)}) collective-permute-start(f32[2,1536,128]{2,1,0:T(8,128)} %collective-permute-done.13.rest_1_.rest_2_), channel_id=1, source_target_pairs={{0,8},{8,0},{16,24},{24,16},{1,9},{9,1},{17,25},{25,17},{2,10},{10... | collective-permute-start | bytes 4718600 | tf_op jit(solution)/shard_map/ppermute | solution.py:430
  221.8 36.8 %collective-permute-start.14 = (f32[2,1536,128]{2,1,0:T(8,128)S(1)}, f32[2,1536,128]{2,1,0:T(8,128)S(1)}, u32[]{:S(2)}, u32[]{:S(2)}) collective-permute-start(f32[2,1536,128]{2,1,0:T(8,128)S(1)} %shard_map.83.own_ref.rest_4_), channel_id=1, source_target_pairs={{0,16},{8,24},{16,0},{24,8},{1,17},{9,25},{17,1},{25,9},{2,18},{10... | collective-permute-start | bytes 4718600 | tf_op jit(solution)/shard_map/ppermute | solution.py:430
  223.3 35.3 %collective-permute-start.17 = (f32[2,1536,128]{2,1,0:T(8,128)S(1)}, f32[2,1536,128]{2,1,0:T(8,128)S(1)}, u32[]{:S(2)}, u32[]{:S(2)}) collective-permute-start(f32[2,1536,128]{2,1,0:T(8,128)S(1)} %shard_map.83.own_ref.rest_4_), channel_id=1, source_target_pairs={{0,8},{8,0},{16,24},{24,16},{1,9},{9,1},{17,25},{25,17},{2,10},{10... | collective-permute-start | bytes 4718600 | tf_op jit(solution)/shard_map/ppermute | solution.py:430
  258.6 3.4 %collective-permute-start.18 = (f32[2,1536,128]{2,1,0:T(8,128)S(1)}, f32[2,1536,128]{2,1,0:T(8,128)S(1)}, u32[]{:S(2)}, u32[]{:S(2)}) collective-permute-start(f32[2,1536,128]{2,1,0:T(8,128)S(1)} %collective-permute-done.14.rest_1_.rest_6_), channel_id=1, source_target_pairs={{0,8},{8,0},{16,24},{24,16},{1,9},{9,1},{17,25},{25,17},{2,10},{10... | collective-permute-start | bytes 4718600 | tf_op jit(solution)/shard_map/ppermute | solution.py:430
  289.4 6.4 %collective-permute-start.20 = (f32[128,512]{1,0:T(8,128)S(1)}, f32[128,512]{1,0:T(8,128)S(1)}, u32[]{:S(2)}, u32[]{:S(2)}) collective-permute-start(f32[128,512]{1,0:T(8,128)S(1)} %bitcast.37), channel_id=1, source_target_pairs={{0,16},{8,24},{16,0},{24,8},{1,17},{9,25},{17,1},{25,9},{2,18},{10... | collective-permute-start | bytes 786440 | tf_op jit(solution)/shard_map/ppermute | solution.py:430
  290.9 4.9 %collective-permute-start.19 = (f32[128,512]{1,0:T(8,128)S(1)}, f32[128,512]{1,0:T(8,128)S(1)}, u32[]{:S(2)}, u32[]{:S(2)}) collective-permute-start(f32[128,512]{1,0:T(8,128)S(1)} %bitcast.38), channel_id=1, source_target_pairs={{0,8},{8,0},{16,24},{24,16},{1,9},{9,1},{17,25},{25,17},{2,10},{10... | collective-permute-start | bytes 786440 | tf_op jit(solution)/shard_map/ppermute | solution.py:430
  (17 other events, 100.4 us)
Sparse Core Ops, SparseCore 0:
  66.5 69.5 all-gather.2

commit v15 on v14

--- a/solution.py
+++ b/solution.py
@@ -474,7 +474,7 @@
     bands = len(panels[0])
     planes = sum(size for _, size in chunks)
     cells = panels[0][0].shape[1]
-    tile = cells // 4
+    tile = cells // 6
     specs = [pl.BlockSpec((size, tile, LANES), lambda i: (0, i, 0)) for _, size in chunks for _ in range(bands)]
     return pl.pallas_call(
         functools.partial(rotate_kernel, chunks, bands),
@@ -682,9 +682,9 @@
 
     came = exchanged(early)
     added = spread(high, low, weights)
+    late, came, added = tie((late, came, added))
+    coming = lax.all_to_all(late, "dom", 0, 0, tiled=True)
     own = swap_out(me, came, added, 0)
-    late, own = tie((late, own))
-    coming = lax.all_to_all(late, "dom", 0, 0, tiled=True)
     across, beside = crossed(own, 2), crossed(own, 1)
     last = swap_out(me, [coming], added, half)
     across, last = tie((across, last))

time: 338 us -> 339 us (level)
  waiting for transfers between devices: 140 us -> 136 us
    all_to_all x1, waiting for transfers between devices: 35.8 us -> 30 us  [shards(): coming = lax.all_to_all(late, 'dom', 0, 0, tiled=True)]
    unnamed x35 -> x39, local copies, waits for them, and re-layouts: 7.71 us -> 9.75 us
  transfers between devices with their start and end apart: 25 -> 25, of which waited for: 10 -> 11; matrix products, arithmetic and copies ran while one was open for 4% -> 4% of each run, Pallas kernels for 16% -> 17%
where the time goes in v15:
time: 339 us; the launch traced here: 338 us
  waiting for transfers between devices  136 us (40%)
  Pallas kernels  94 us (28%)
  starting transfers between devices  40.8 us (12%)
  blocking collectives  26.7 us (8%)
  local copies, waits for them, and re-layouts  20.9 us (6%)
  between operations  14.3 us (4%)
  other arithmetic  4.57 us (1%)
    ppermute x12, waiting for transfers between devices, crossed(): lax.ppermute(value, 'band', [(source, source ^ bit) for source in range(l...  53.6 us
    all_to_all x1, waiting for transfers between devices, shards(): arrived = lax.all_to_all(packed, 'dom', 0, 0, tiled=True)  45.8 us
    all_to_all x1, waiting for transfers between devices, shards(): coming = lax.all_to_all(late, 'dom', 0, 0, tiled=True)  30 us
    pallas_call x1, Pallas kernels, cholesky_inverse(): pl.pallas_call(cholesky_kernel, in_specs=[pl.BlockSpec(memory_space=pltpu...  23.5 us
    pallas_call x1, Pallas kernels, filter_orbitals(): pl.pallas_call(functools.partial(filter_kernel, planes, side_y, side_z, w...  22.1 us
    ppermute x10, starting transfers between devices, shifted(): lax.ppermute(value, axis, [(source, (source + step) % count) for source i...  19 us
    all_to_all x1, blocking collectives, shards(): lax.all_to_all(part.reshape(blocks, width, norb), 'dom', 0, 0, tiled=True)  14.7 us
    pallas_call x1, Pallas kernels, build_basis(): pl.pallas_call(functools.partial(basis_kernel, planes, side_y, side_z, le...  13.5 us
  transfers between devices with their start and end apart: 25, of which 11 were waited for; matrix products, arithmetic and copies ran while one was open for 4% of the time, Pallas kernels for 17%

profile of v15, /device:TPU:0, one launch (start us, length us, event | category | flops | bytes accessed | tf_op | source)
XLA Modules:
  0.0 337.6 jit_solution(1558916865934904275)
XLA Ops:
  9.8 6.1 %collective-permute-start.2 = (f32[8,4736]{1,0:T(8,128)S(1)}, f32[8,4736]{1,0:T(8,128)S(1)}, u32[]{:S(2)}, u32[]{:S(2)}) collective-permute-start(f32[8,4736]{1,0:T(8,128)S(1)} %reshape.268), channel_id=1, source_target_pairs={{0,7},{1,0},{2,1},{3,2},{4,3},{5,4},{6,5},{7,6},{8,15},{9,8},{10,9... | collective-permute-start | bytes 454664 | tf_op jit(solution)/shard_map/ppermute | solution.py:422
  17.8 4.3 %shard_map.77 = f32[8,4,208,128]{3,2,1,0:T(8,128)} custom-call(f32[4,16,128]{2,1,0:T(8,128)S(1)} %pad.8.levels_ref, f32[4,8,192,128]{3,2,1,0:T(8,128)S(1)} %bitcast.35), custom_call_target="tpu_custom_call" | custom-call | bytes 6291456 | tf_op jit(solution)/shard_map/pallas_call | solution.py:98
  22.1 3.4 collective-permute-done.1
  26.3 3.8 %all-to-all-start = ((f32[8,4,208,128]{3,2,1,0:T(8,128)}), f32[8,4,208,128]{3,2,1,0:T(8,128)S(1)}, u32[]{:S(2)}, u32[]{:S(2)}) async-start(f32[8,4,208,128]{3,2,1,0:T(8,128)} %shard_map.77), calls=%async_computation | async-start | bytes 6815744 | tf_op jit(solution)/shard_map/all_to_all | solution.py:660
  33.4 11.2 %collective-permute-done.11.refs_2_ = f32[4,8,4736]{2,1,0:T(8,128)} collective-permute-done((f32[4,8,4736]{2,1,0:T(8,128)}, f32[4,8,4736]{2,1,0:T(8,128)}, u32[]{:S(2)}, u32[]{:S(2)}) %collective-permute-start.11) | collective-permute-done | bytes 606240 | tf_op jit(solution)/shard_map/ppermute | solution.py:430
  51.2 13.5 %shard_map.79 = (bf16[4,1536,256]{2,1,0:T(8,128)(2,1)}, bf16[4,1536,256]{2,1,0:T(8,128)(2,1)}, f32[3,128,128]{2,1,0:T(8,128)}) custom-call(f32[4,8,4736]{2,1,0:T(8,128)} %pad_maximum_fusion.refs_0_, f32[4,8,4736]{2,1,0:T(8,128)} %collective-permute-done.10.refs_1_, f32[4,8,4736]{2,1,0:T(8,128)} %collective-permute-done.11.refs_2_, ...), custom_call_target="tpu_custom_call" | custom-call | flops 157286400 | bytes 18874368 | tf_op jit(solution)/shard_map/pallas_call | solution.py:345
  66.3 45.8 %all-to-all-done.arrived_ref = f32[8,4,208,128]{3,2,1,0:T(8,128)S(1)} async-done(((f32[8,4,208,128]{3,2,1,0:T(8,128)}), f32[8,4,208,128]{3,2,1,0:T(8,128)S(1)}, u32[]{:S(2)}, u32[]{:S(2)}) %all-to-all-start) | async-done | bytes 3407904 | tf_op jit(solution)/shard_map/all_to_all | solution.py:660
  113.8 22.1 %shard_map.78 = (f32[2,192,128]{2,1,0:T(8,128)}, f32[2,192,128]{2,1,0:T(8,128)}, f32[2,192,128]{2,1,0:T(8,128)}, f32[2,192,128]{2,1,0:T(8,128)}, f32[2,192,128]{...) custom-call(s32[1]{0:T(128)} %bitcast.1.me_ref, ...), custom_call_target="tpu_custom_call" | custom-call | flops 85196800 | bytes 10223616 | tf_op jit(solution)/shard_map/pallas_call | solution.py:281
  137.3 2.9 collective-permute-start.5
  143.2 3.6 %collective-permute-done.3.refs_1_ = f32[2,192,128]{2,1,0:T(8,128)S(1)} collective-permute-done((f32[2,192,128]{2,1,0:T(8,128)}, f32[2,192,128]{2,1,0:T(8,128)S(1)}, u32[]{:S(2)}, u32[]{:S(2)}) %collective-permute-start.3) | collective-permute-done | bytes 196640 | tf_op jit(solution)/shard_map/ppermute | solution.py:422
  148.7 4.4 %collective-permute-start.9 = (f32[2,192,128]{2,1,0:T(8,128)}, f32[2,192,128]{2,1,0:T(8,128)}, u32[]{:S(2)}, u32[]{:S(2)}) collective-permute-start(f32[2,192,128]{2,1,0:T(8,128)} %get-tuple-element.45), channel_id=1, source_target_pairs={{0,7},{1,0},{2,1},{3,2},{4,3},{5,4},{6,5},{7,6},{8,15},{9,8},{10,9... | collective-permute-start | bytes 589832 | tf_op jit(solution)/shard_map/ppermute | solution.py:422
  159.3 5.7 %shard_map.81.added_ref = f32[4,1536,128]{2,1,0:T(8,128)S(1)} custom-call(bf16[4,1536,256]{2,1,0:T(8,128)(2,1)S(1)} %copy-done.6, bf16[4,1536,256]{2,1,0:T(8,128)(2,1)S(1)} %copy-done.7, f32[256,128]{1,0:T(8,128)S(1)} %shard_map.80.weights_ref), custom_call_target="tpu_custom_call" | custom-call | bytes 12582912 | tf_op jit(solution)/shard_map/pallas_call | solution.py:164
  165.7 11.7 %all-to-all-start.1 = ((f32[8,2,192,128]{3,2,1,0:T(8,128)}), f32[8,2,192,128]{3,2,1,0:T(8,128)}, u32[]{:S(2)}, u32[]{:S(2)}) async-start(f32[8,2,192,128]{3,2,1,0:T(8,128)} %get-tuple-element.59), calls=%async_computation.1 | async-start | bytes 3145728 | tf_op jit(solution)/shard_map/all_to_all | solution.py:686
  179.3 4.0 %shard_map.82.own_ref.rest_0_ = f32[2,1536,128]{2,1,0:T(8,128)} custom-call(s32[1]{0:T(128)} %bitcast.1.me_ref, f32[4,1536,128]{2,1,0:T(8,128)S(1)} %shard_map.81.added_ref, f32[2,192,128]{2,1,0:T(8,128)S(1)} %copy-done.9, f32[2,192,128]{2,1,0:T(8,128)S(1)} %collective-permute-done.3.refs_1_, f32[2,192,128]{2,1,0:T(8,128)S(1)} %copy-done.11, ...), custom_call_target="tpu_custom_call" | custom-call | bytes 9437184 | tf_op jit(solution)/shard_map/pallas_call | solution.py:134
  184.7 30.0 %all-to-all-done.1.refs_0_ = f32[8,2,192,128]{3,2,1,0:T(8,128)} async-done(((f32[8,2,192,128]{3,2,1,0:T(8,128)}), f32[8,2,192,128]{3,2,1,0:T(8,128)}, u32[]{:S(2)}, u32[]{:S(2)}) %all-to-all-start.1) | async-done | bytes 1572896 | tf_op jit(solution)/shard_map/all_to_all | solution.py:686
  214.7 2.9 shard_map.83.own_ref.rest_4_
  223.2 4.4 %shard_map.84 = f32[128,512]{1,0:T(8,128)S(1)} custom-call(f32[2,1536,128]{2,1,0:T(8,128)} %shard_map.82.own_ref.rest_0_, f32[2,1536,128]{2,1,0:T(8,128)} %collective-permute-done.15.rest_0_.rest_1_, f32[2,1536,128]{2,1,0:T(8,128)} %collective-permute-done.13.rest_1_.rest_2_, f32[2,1536,128]{2,1,0:T(8,128)S(1)} %collective-permute-done.16.rest_2_.rest_3_), custom_call_target="tpu_custom_call" | custom-call | flops 1610612736 | bytes 6291456 | tf_op jit(solution)/shard_map/pallas_call | solution.py:452
  227.6 28.8 %collective-permute-done.14.rest_1_.rest_6_ = f32[2,1536,128]{2,1,0:T(8,128)S(1)} collective-permute-done((f32[2,1536,128]{2,1,0:T(8,128)S(1)}, f32[2,1536,128]{2,1,0:T(8,128)S(1)}, u32[]{:S(2)}, u32[]{:S(2)}) %collective-permute-start.14) | collective-permute-done | bytes 1572896 | tf_op jit(solution)/shard_map/ppermute | solution.py:430
  256.4 3.4 %collective-permute-done.18.rest_2_.rest_7_ = f32[2,1536,128]{2,1,0:T(8,128)S(1)} collective-permute-done((f32[2,1536,128]{2,1,0:T(8,128)S(1)}, f32[2,1536,128]{2,1,0:T(8,128)S(1)}, u32[]{:S(2)}, u32[]{:S(2)}) %collective-permute-start.18) | collective-permute-done | bytes 1572896 | tf_op jit(solution)/shard_map/ppermute | solution.py:430
  262.5 14.7 %all_to_all.20 = f32[8,16,512]{2,1,0:T(8,128)S(1)} all-to-all(f32[8,16,512]{2,1,0:T(8,128)S(1)} %bitcast.43), channel_id=1, replica_groups=mesh['band'=4,'dom'=8] {'dom'}, dimensions={0} | all-to-all | bytes 524288 | tf_op jit(solution)/shard_map/all_to_all | solution.py:698
  277.3 12.0 %all_to_all.21 = f32[8,16,512]{2,1,0:T(8,128)S(1)} all-to-all(f32[8,16,512]{2,1,0:T(8,128)S(1)} %broadcast_in_dim.58), channel_id=1, replica_groups=mesh['band'=4,'dom'=8] {'dom'}, dimensions={0} | all-to-all | bytes 524288 | tf_op jit(solution)/shard_map/all_to_all | solution.py:700
  290.7 4.9 %collective-permute-done.20.refs_2_ = f32[128,512]{1,0:T(8,128)S(1)} collective-permute-done((f32[128,512]{1,0:T(8,128)S(1)}, f32[128,512]{1,0:T(8,128)S(1)}, u32[]{:S(2)}, u32[]{:S(2)}) %collective-permute-start.20) | collective-permute-done | bytes 262176 | tf_op jit(solution)/shard_map/ppermute | solution.py:430
  297.2 23.5 %shard_map.86 = (f32[512,512]{1,0:T(8,128)}, f32[128,512]{1,0:T(8,128)S(1)}) custom-call(s32[1]{0:T(128)} %bitcast.band_ref, f32[128,512]{1,0:T(8,128)S(1)} %bitcast.39, f32[128,512]{1,0:T(8,128)S(1)} %collective-permute-done.19.refs_1_, f32[128,512]{1,0:T(8,128)S(1)} %collective-permute-done.20.refs_2_, f32[128,512]{1,0:T(8,128)S(1)} %collective-permute-done.21.refs_3_), custom_call_target="tpu_custom_call" | custom-call | tf_op jit(solution)/shard_map/pallas_call | solution.py:599
  321.4 9.4 %shard_map.87 = f32[4,1536,128]{2,1,0:T(8,128)} custom-call(f32[128,512]{1,0:T(8,128)} %copy-done.8, f32[2,1536,128]{2,1,0:T(8,128)} %shard_map.82.own_ref.rest_0_, f32[2,1536,128]{2,1,0:T(8,128)} %collective-permute-done.15.rest_0_.rest_1_, f32[2,1536,128]{2,1,0:T(8,128)} %collective-permute-done.13.rest_1_.rest_2_, f32[2,1536,128]{2,1,0:T(8,128)} %copy-done.2, ...), custom_call_target="tpu_custom_call" | custom-call | tf_op jit(solution)/shard_map/pallas_call | solution.py:479
  (120 shorter events, 47.1 us)
Async XLA Ops:
  9.8 12.2 %collective-permute-start.2 = (f32[8,4736]{1,0:T(8,128)S(1)}, f32[8,4736]{1,0:T(8,128)S(1)}, u32[]{:S(2)}, u32[]{:S(2)}) collective-permute-start(f32[8,4736]{1,0:T(8,128)S(1)} %reshape.268), channel_id=1, source_target_pairs={{0,7},{1,0},{2,1},{3,2},{4,3},{5,4},{6,5},{7,6},{8,15},{9,8},{10,9... | collective-permute-start | bytes 454664 | tf_op jit(solution)/shard_map/ppermute | solution.py:422
  15.9 9.6 %collective-permute-start.1 = (f32[8,4736]{1,0:T(8,128)S(1)}, f32[8,4736]{1,0:T(8,128)S(1)}, u32[]{:S(2)}, u32[]{:S(2)}) collective-permute-start(f32[8,4736]{1,0:T(8,128)S(1)} %reshape.268), channel_id=1, source_target_pairs={{0,1},{1,2},{2,3},{3,4},{4,5},{5,6},{6,7},{7,0},{8,9},{9,10},{10,1... | collective-permute-start | bytes 454664 | tf_op jit(solution)/shard_map/ppermute | solution.py:422
  15.9 9.6 %collective-permute-start = (f32[8,4736]{1,0:T(8,128)S(1)}, f32[8,4736]{1,0:T(8,128)S(1)}, u32[]{:S(2)}, u32[]{:S(2)}) collective-permute-start(f32[8,4736]{1,0:T(8,128)S(1)} %reshape.268), channel_id=1, source_target_pairs={{0,2},{1,3},{2,4},{3,5},{4,6},{5,7},{6,0},{7,1},{8,10},{9,11},{10,... | collective-permute-start | bytes 454664 | tf_op jit(solution)/shard_map/ppermute | solution.py:422
  26.3 85.8 %all-to-all-start = ((f32[8,4,208,128]{3,2,1,0:T(8,128)}), f32[8,4,208,128]{3,2,1,0:T(8,128)S(1)}, u32[]{:S(2)}, u32[]{:S(2)}) async-start(f32[8,4,208,128]{3,2,1,0:T(8,128)} %shard_map.77), calls=%async_computation | async-start | bytes 6815744 | tf_op jit(solution)/shard_map/all_to_all | solution.py:660
  30.1 123.0 %all-gather.3.cloned.1.call-start = ((), (), s32[]{:S(2)}) async-start(), calls=%async_computation.4 | async-start | bytes 1916928 | tf_op jit(solution)/shard_map/all_gather | solution.py:675
  30.4 14.2 %collective-permute-start.11 = (f32[4,8,4736]{2,1,0:T(8,128)}, f32[4,8,4736]{2,1,0:T(8,128)}, u32[]{:S(2)}, u32[]{:S(2)}) collective-permute-start(f32[4,8,4736]{2,1,0:T(8,128)} %pad_maximum_fusion.refs_0_), channel_id=1, source_target_pairs={{0,16},{8,24},{16,0},{24,8},{1,17},{9,25},{17,1},{25,9},{2,18},{10... | collective-permute-start | bytes 1818632 | tf_op jit(solution)/shard_map/ppermute | solution.py:430
  33.2 13.3 %collective-permute-start.10 = (f32[4,8,4736]{2,1,0:T(8,128)}, f32[4,8,4736]{2,1,0:T(8,128)}, u32[]{:S(2)}, u32[]{:S(2)}) collective-permute-start(f32[4,8,4736]{2,1,0:T(8,128)} %pad_maximum_fusion.refs_0_), channel_id=1, source_target_pairs={{0,8},{8,0},{16,24},{24,16},{1,9},{9,1},{17,25},{25,17},{2,10},{10... | collective-permute-start | bytes 1818632 | tf_op jit(solution)/shard_map/ppermute | solution.py:430
  44.6 2.8 collective-permute-start.12
  135.9 10.8 %collective-permute-start.3 = (f32[2,192,128]{2,1,0:T(8,128)}, f32[2,192,128]{2,1,0:T(8,128)S(1)}, u32[]{:S(2)}, u32[]{:S(2)}) collective-permute-start(f32[2,192,128]{2,1,0:T(8,128)} %get-tuple-element.39), channel_id=1, source_target_pairs={{0,1},{1,2},{2,3},{3,4},{4,5},{5,6},{6,7},{7,0},{8,9},{9,10},{10,1... | collective-permute-start | bytes 589832 | tf_op jit(solution)/shard_map/ppermute | solution.py:422
  137.3 10.7 %collective-permute-start.4 = (f32[2,192,128]{2,1,0:T(8,128)}, f32[2,192,128]{2,1,0:T(8,128)S(1)}, u32[]{:S(2)}, u32[]{:S(2)}) collective-permute-start(f32[2,192,128]{2,1,0:T(8,128)} %get-tuple-element.40), channel_id=1, source_target_pairs={{0,2},{1,3},{2,4},{3,5},{4,6},{5,7},{6,0},{7,1},{8,10},{9,11},{10,... | collective-permute-start | bytes 589832 | tf_op jit(solution)/shard_map/ppermute | solution.py:422
  137.3 27.7 %collective-permute-start.5 = (f32[2,192,128]{2,1,0:T(8,128)}, f32[2,192,128]{2,1,0:T(8,128)S(1)}, u32[]{:S(2)}, u32[]{:S(2)}) collective-permute-start(f32[2,192,128]{2,1,0:T(8,128)} %get-tuple-element.41), channel_id=1, source_target_pairs={{0,3},{1,4},{2,5},{3,6},{4,7},{5,0},{6,1},{7,2},{8,11},{9,12},{10,... | collective-permute-start | bytes 589832 | tf_op jit(solution)/shard_map/ppermute | solution.py:422
  140.2 25.5 %collective-permute-start.6 = (f32[2,192,128]{2,1,0:T(8,128)}, f32[2,192,128]{2,1,0:T(8,128)}, u32[]{:S(2)}, u32[]{:S(2)}) collective-permute-start(f32[2,192,128]{2,1,0:T(8,128)} %get-tuple-element.42), channel_id=1, source_target_pairs={{0,4},{1,5},{2,6},{3,7},{4,0},{5,1},{6,2},{7,3},{8,12},{9,13},{10,... | collective-permute-start | bytes 589832 | tf_op jit(solution)/shard_map/ppermute | solution.py:422
  141.2 24.5 %collective-permute-start.7 = (f32[2,192,128]{2,1,0:T(8,128)}, f32[2,192,128]{2,1,0:T(8,128)}, u32[]{:S(2)}, u32[]{:S(2)}) collective-permute-start(f32[2,192,128]{2,1,0:T(8,128)} %get-tuple-element.43), channel_id=1, source_target_pairs={{0,5},{1,6},{2,7},{3,0},{4,1},{5,2},{6,3},{7,4},{8,13},{9,14},{10,... | collective-permute-start | bytes 589832 | tf_op jit(solution)/shard_map/ppermute | solution.py:422
  146.7 19.0 %collective-permute-start.8 = (f32[2,192,128]{2,1,0:T(8,128)}, f32[2,192,128]{2,1,0:T(8,128)}, u32[]{:S(2)}, u32[]{:S(2)}) collective-permute-start(f32[2,192,128]{2,1,0:T(8,128)} %get-tuple-element.44), channel_id=1, source_target_pairs={{0,6},{1,7},{2,0},{3,1},{4,2},{5,3},{6,4},{7,5},{8,14},{9,15},{10,... | collective-permute-start | bytes 589832 | tf_op jit(solution)/shard_map/ppermute | solution.py:422
  148.7 17.0 %collective-permute-start.9 = (f32[2,192,128]{2,1,0:T(8,128)}, f32[2,192,128]{2,1,0:T(8,128)}, u32[]{:S(2)}, u32[]{:S(2)}) collective-permute-start(f32[2,192,128]{2,1,0:T(8,128)} %get-tuple-element.45), channel_id=1, source_target_pairs={{0,7},{1,0},{2,1},{3,2},{4,3},{5,4},{6,5},{7,6},{8,15},{9,8},{10,9... | collective-permute-start | bytes 589832 | tf_op jit(solution)/shard_map/ppermute | solution.py:422
  165.7 48.9 %all-to-all-start.1 = ((f32[8,2,192,128]{3,2,1,0:T(8,128)}), f32[8,2,192,128]{3,2,1,0:T(8,128)}, u32[]{:S(2)}, u32[]{:S(2)}) async-start(f32[8,2,192,128]{3,2,1,0:T(8,128)} %get-tuple-element.59), calls=%async_computation.1 | async-start | bytes 3145728 | tf_op jit(solution)/shard_map/all_to_all | solution.py:686
  183.2 36.4 %collective-permute-start.13 = (f32[2,1536,128]{2,1,0:T(8,128)}, f32[2,1536,128]{2,1,0:T(8,128)}, u32[]{:S(2)}, u32[]{:S(2)}) collective-permute-start(f32[2,1536,128]{2,1,0:T(8,128)} %shard_map.82.own_ref.rest_0_), channel_id=1, source_target_pairs={{0,16},{8,24},{16,0},{24,8},{1,17},{9,25},{17,1},{25,9},{2,18},{10... | collective-permute-start | bytes 4718600 | tf_op jit(solution)/shard_map/ppermute | solution.py:430
  184.7 36.6 %collective-permute-start.15 = (f32[2,1536,128]{2,1,0:T(8,128)}, f32[2,1536,128]{2,1,0:T(8,128)}, u32[]{:S(2)}, u32[]{:S(2)}) collective-permute-start(f32[2,1536,128]{2,1,0:T(8,128)} %shard_map.82.own_ref.rest_0_), channel_id=1, source_target_pairs={{0,8},{8,0},{16,24},{24,16},{1,9},{9,1},{17,25},{25,17},{2,10},{10... | collective-permute-start | bytes 4718600 | tf_op jit(solution)/shard_map/ppermute | solution.py:430
  219.6 3.6 %collective-permute-start.16 = (f32[2,1536,128]{2,1,0:T(8,128)}, f32[2,1536,128]{2,1,0:T(8,128)S(1)}, u32[]{:S(2)}, u32[]{:S(2)}) collective-permute-start(f32[2,1536,128]{2,1,0:T(8,128)} %collective-permute-done.13.rest_1_.rest_2_), channel_id=1, source_target_pairs={{0,8},{8,0},{16,24},{24,16},{1,9},{9,1},{17,25},{25,17},{2,10},{10... | collective-permute-start | bytes 4718600 | tf_op jit(solution)/shard_map/ppermute | solution.py:430
  219.6 36.8 %collective-permute-start.14 = (f32[2,1536,128]{2,1,0:T(8,128)S(1)}, f32[2,1536,128]{2,1,0:T(8,128)S(1)}, u32[]{:S(2)}, u32[]{:S(2)}) collective-permute-start(f32[2,1536,128]{2,1,0:T(8,128)S(1)} %shard_map.83.own_ref.rest_4_), channel_id=1, source_target_pairs={{0,16},{8,24},{16,0},{24,8},{1,17},{9,25},{17,1},{25,9},{2,18},{10... | collective-permute-start | bytes 4718600 | tf_op jit(solution)/shard_map/ppermute | solution.py:430
  221.1 35.3 %collective-permute-start.17 = (f32[2,1536,128]{2,1,0:T(8,128)S(1)}, f32[2,1536,128]{2,1,0:T(8,128)S(1)}, u32[]{:S(2)}, u32[]{:S(2)}) collective-permute-start(f32[2,1536,128]{2,1,0:T(8,128)S(1)} %shard_map.83.own_ref.rest_4_), channel_id=1, source_target_pairs={{0,8},{8,0},{16,24},{24,16},{1,9},{9,1},{17,25},{25,17},{2,10},{10... | collective-permute-start | bytes 4718600 | tf_op jit(solution)/shard_map/ppermute | solution.py:430
  256.4 3.4 %collective-permute-start.18 = (f32[2,1536,128]{2,1,0:T(8,128)S(1)}, f32[2,1536,128]{2,1,0:T(8,128)S(1)}, u32[]{:S(2)}, u32[]{:S(2)}) collective-permute-start(f32[2,1536,128]{2,1,0:T(8,128)S(1)} %collective-permute-done.14.rest_1_.rest_6_), channel_id=1, source_target_pairs={{0,8},{8,0},{16,24},{24,16},{1,9},{9,1},{17,25},{25,17},{2,10},{10... | collective-permute-start | bytes 4718600 | tf_op jit(solution)/shard_map/ppermute | solution.py:430
  289.2 6.4 %collective-permute-start.20 = (f32[128,512]{1,0:T(8,128)S(1)}, f32[128,512]{1,0:T(8,128)S(1)}, u32[]{:S(2)}, u32[]{:S(2)}) collective-permute-start(f32[128,512]{1,0:T(8,128)S(1)} %bitcast.37), channel_id=1, source_target_pairs={{0,16},{8,24},{16,0},{24,8},{1,17},{9,25},{17,1},{25,9},{2,18},{10... | collective-permute-start | bytes 786440 | tf_op jit(solution)/shard_map/ppermute | solution.py:430
  290.7 4.9 %collective-permute-start.19 = (f32[128,512]{1,0:T(8,128)S(1)}, f32[128,512]{1,0:T(8,128)S(1)}, u32[]{:S(2)}, u32[]{:S(2)}) collective-permute-start(f32[128,512]{1,0:T(8,128)S(1)} %bitcast.38), channel_id=1, source_target_pairs={{0,8},{8,0},{16,24},{24,16},{1,9},{9,1},{17,25},{25,17},{2,10},{10... | collective-permute-start | bytes 786440 | tf_op jit(solution)/shard_map/ppermute | solution.py:430
  (19 other events, 103.7 us)
Sparse Core Ops, SparseCore 0:
  66.5 69.5 all-gather.2

commit v16 on v14

--- a/solution.py
+++ b/solution.py
@@ -672,6 +672,7 @@
     matrix = jnp.where(row[:, None] == row[None, :], matrix, 0.0)
     matrix = jnp.pad(matrix, ((0, 0), (0, LANES - vectors)))
     payload = jnp.concatenate([parts.reshape(3 * LANES, LANES), matrix], axis=0)
+    arrived, payload = tie((arrived, payload))
     everyone = lax.all_gather(payload, "dom")
     weights = near_weights(
         me,

time: 338 us -> 349 us (1.033)
  waiting for transfers between devices: 140 us -> 154 us
    all_gather x1, waiting for transfers between devices: 0.01 us -> 16.5 us  [shards(): everyone = lax.all_gather(payload, 'dom')]
    all_to_all x1, starting transfers between devices: 12.9 us -> 5.57 us  [shards(): coming = lax.all_to_all(late, 'dom', 0, 0, tiled=True)]
    all_to_all x1, waiting for transfers between devices: 45.8 us -> 38.9 us  [shards(): arrived = lax.all_to_all(packed, 'dom', 0, 0, tiled=True)]
    ppermute x10, starting transfers between devices: 19 us -> 23.9 us  [shifted(): lax.ppermute(value, axis, [(source, (source + step) % count) for source i...]
    ppermute x10, waiting for transfers between devices: 6.99 us -> 11.1 us  [shifted(): lax.ppermute(value, axis, [(source, (source + step) % count) for source i...]
  transfers between devices with their start and end apart: 25 -> 25, of which waited for: 10 -> 11; matrix products, arithmetic and copies ran while one was open for 4% -> 4% of each run, Pallas kernels for 16% -> 16%
where the time goes in v16:
time: 349 us; the launch traced here: 348 us
  waiting for transfers between devices  154 us (44%)
  Pallas kernels  91.9 us (26%)
  starting transfers between devices  39.7 us (11%)
  blocking collectives  24.6 us (7%)
  local copies, waits for them, and re-layouts  18.8 us (5%)
  between operations  14.4 us (4%)
  other arithmetic  4.57 us (1%)
    ppermute x12, waiting for transfers between devices, crossed(): lax.ppermute(value, 'band', [(source, source ^ bit) for source in range(l...  51.8 us
    all_to_all x1, waiting for transfers between devices, shards(): arrived = lax.all_to_all(packed, 'dom', 0, 0, tiled=True)  38.9 us
    all_to_all x1, waiting for transfers between devices, shards(): coming = lax.all_to_all(late, 'dom', 0, 0, tiled=True)  35.8 us
    ppermute x10, starting transfers between devices, shifted(): lax.ppermute(value, axis, [(source, (source + step) % count) for source i...  23.9 us
    pallas_call x1, Pallas kernels, cholesky_inverse(): pl.pallas_call(cholesky_kernel, in_specs=[pl.BlockSpec(memory_space=pltpu...  23.5 us
    pallas_call x1, Pallas kernels, filter_orbitals(): pl.pallas_call(functools.partial(filter_kernel, planes, side_y, side_z, w...  22.1 us
    all_gather x1, waiting for transfers between devices, shards(): everyone = lax.all_gather(payload, 'dom')  16.5 us
    pallas_call x1, Pallas kernels, build_basis(): pl.pallas_call(functools.partial(basis_kernel, planes, side_y, side_z, le...  13.5 us
  transfers between devices with their start and end apart: 25, of which 11 were waited for; matrix products, arithmetic and copies ran while one was open for 4% of the time, Pallas kernels for 16%

profile of v16, /device:TPU:0, one launch (start us, length us, event | category | flops | bytes accessed | tf_op | source)
XLA Modules:
  0.0 348.2 jit_solution(1847487652589001967)
XLA Ops:
  9.8 6.1 %collective-permute-start.2 = (f32[8,4736]{1,0:T(8,128)S(1)}, f32[8,4736]{1,0:T(8,128)S(1)}, u32[]{:S(2)}, u32[]{:S(2)}) collective-permute-start(f32[8,4736]{1,0:T(8,128)S(1)} %reshape.268), channel_id=1, source_target_pairs={{0,7},{1,0},{2,1},{3,2},{4,3},{5,4},{6,5},{7,6},{8,15},{9,8},{10,9... | collective-permute-start | bytes 454664 | tf_op jit(solution)/shard_map/ppermute | solution.py:422
  17.8 4.2 %shard_map.77 = f32[8,4,208,128]{3,2,1,0:T(8,128)} custom-call(f32[4,16,128]{2,1,0:T(8,128)S(1)} %pad.8.levels_ref, f32[4,8,192,128]{3,2,1,0:T(8,128)S(1)} %bitcast.35), custom_call_target="tpu_custom_call" | custom-call | bytes 6291456 | tf_op jit(solution)/shard_map/pallas_call | solution.py:98
  22.1 3.4 collective-permute-done.1
  26.3 3.8 %all-to-all-start = ((f32[8,4,208,128]{3,2,1,0:T(8,128)}), f32[8,4,208,128]{3,2,1,0:T(8,128)S(1)}, u32[]{:S(2)}, u32[]{:S(2)}) async-start(f32[8,4,208,128]{3,2,1,0:T(8,128)} %shard_map.77), calls=%async_computation | async-start | bytes 6815744 | tf_op jit(solution)/shard_map/all_to_all | solution.py:660
  33.4 11.2 %collective-permute-done.4.refs_2_ = f32[4,8,4736]{2,1,0:T(8,128)} collective-permute-done((f32[4,8,4736]{2,1,0:T(8,128)}, f32[4,8,4736]{2,1,0:T(8,128)}, u32[]{:S(2)}, u32[]{:S(2)}) %collective-permute-start.4) | collective-permute-done | bytes 606240 | tf_op jit(solution)/shard_map/ppermute | solution.py:430
  51.2 13.5 %shard_map.78 = (bf16[4,1536,256]{2,1,0:T(8,128)(2,1)}, bf16[4,1536,256]{2,1,0:T(8,128)(2,1)}, f32[3,128,128]{2,1,0:T(8,128)}) custom-call(f32[4,8,4736]{2,1,0:T(8,128)} %pad_maximum_fusion.refs_0_, f32[4,8,4736]{2,1,0:T(8,128)} %collective-permute-done.3.refs_1_, f32[4,8,4736]{2,1,0:T(8,128)} %collective-permute-done.4.refs_2_, ...), custom_call_target="tpu_custom_call" | custom-call | flops 157286400 | bytes 18874368 | tf_op jit(solution)/shard_map/pallas_call | solution.py:345
  66.3 38.9 %all-to-all-done.arrived_ref = f32[8,4,208,128]{3,2,1,0:T(8,128)S(1)} async-done(((f32[8,4,208,128]{3,2,1,0:T(8,128)}), f32[8,4,208,128]{3,2,1,0:T(8,128)S(1)}, u32[]{:S(2)}, u32[]{:S(2)}) %all-to-all-start) | async-done | bytes 3407904 | tf_op jit(solution)/shard_map/all_to_all | solution.py:660
  106.9 22.1 %shard_map.79 = (f32[2,192,128]{2,1,0:T(8,128)}, f32[2,192,128]{2,1,0:T(8,128)}, f32[2,192,128]{2,1,0:T(8,128)}, f32[2,192,128]{2,1,0:T(8,128)}, f32[2,192,128]{...) custom-call(s32[1]{0:T(128)} %bitcast.1.me_ref, ...), custom_call_target="tpu_custom_call" | custom-call | flops 85196800 | bytes 10223616 | tf_op jit(solution)/shard_map/pallas_call | solution.py:281
  136.3 7.7 %collective-permute-done.6.refs_1_ = f32[2,192,128]{2,1,0:T(8,128)S(1)} collective-permute-done((f32[2,192,128]{2,1,0:T(8,128)}, f32[2,192,128]{2,1,0:T(8,128)S(1)}, u32[]{:S(2)}, u32[]{:S(2)}) %collective-permute-start.6) | collective-permute-done | bytes 196640 | tf_op jit(solution)/shard_map/ppermute | solution.py:422
  144.0 4.4 %collective-permute-start.11 = (f32[2,192,128]{2,1,0:T(8,128)}, f32[2,192,128]{2,1,0:T(8,128)}, u32[]{:S(2)}, u32[]{:S(2)}) collective-permute-start(f32[2,192,128]{2,1,0:T(8,128)} %get-tuple-element.44), channel_id=1, source_target_pairs={{0,6},{1,7},{2,0},{3,1},{4,2},{5,3},{6,4},{7,5},{8,14},{9,15},{10,... | collective-permute-start | bytes 589832 | tf_op jit(solution)/shard_map/ppermute | solution.py:422
  148.4 6.1 %collective-permute-start.12 = (f32[2,192,128]{2,1,0:T(8,128)}, f32[2,192,128]{2,1,0:T(8,128)}, u32[]{:S(2)}, u32[]{:S(2)}) collective-permute-start(f32[2,192,128]{2,1,0:T(8,128)} %get-tuple-element.45), channel_id=1, source_target_pairs={{0,7},{1,0},{2,1},{3,2},{4,3},{5,4},{6,5},{7,6},{8,15},{9,8},{10,9... | collective-permute-start | bytes 589832 | tf_op jit(solution)/shard_map/ppermute | solution.py:422
  154.5 16.5 %all-gather.3.cloned.1.call-done = f32[3328,128]{1,0:T(8,128)} async-done(((f32[416,128]{1,0:T(8,128)}), f32[3328,128]{1,0:T(8,128)}) %all-gather.3.cloned.1.call-update) | async-done | bytes 1703952 | tf_op jit(solution)/shard_map/all_gather | solution.py:676
  177.3 5.7 %shard_map.81.added_ref = f32[4,1536,128]{2,1,0:T(8,128)S(1)} custom-call(bf16[4,1536,256]{2,1,0:T(8,128)(2,1)S(1)} %copy-done.8, bf16[4,1536,256]{2,1,0:T(8,128)(2,1)S(1)} %copy-done.9, f32[256,128]{1,0:T(8,128)S(1)} %shard_map.80.weights_ref), custom_call_target="tpu_custom_call" | custom-call | bytes 12582912 | tf_op jit(solution)/shard_map/pallas_call | solution.py:164
  187.1 5.6 %all-to-all-start.1 = ((f32[8,2,192,128]{3,2,1,0:T(8,128)}), f32[8,2,192,128]{3,2,1,0:T(8,128)}, u32[]{:S(2)}, u32[]{:S(2)}) async-start(f32[8,2,192,128]{3,2,1,0:T(8,128)} %get-tuple-element.47), calls=%async_computation.1 | async-start | bytes 3145728 | tf_op jit(solution)/shard_map/all_to_all | solution.py:688
  194.2 35.8 %all-to-all-done.1.refs_0_ = f32[8,2,192,128]{3,2,1,0:T(8,128)} async-done(((f32[8,2,192,128]{3,2,1,0:T(8,128)}), f32[8,2,192,128]{3,2,1,0:T(8,128)}, u32[]{:S(2)}, u32[]{:S(2)}) %all-to-all-start.1) | async-done | bytes 1572896 | tf_op jit(solution)/shard_map/all_to_all | solution.py:688
  230.0 3.0 shard_map.83.own_ref.rest_4_
  236.8 4.1 %shard_map.84 = f32[128,512]{1,0:T(8,128)S(1)} custom-call(f32[2,1536,128]{2,1,0:T(8,128)S(1)} %copy-done.1, f32[2,1536,128]{2,1,0:T(8,128)} %collective-permute-done.15.rest_0_.rest_1_, f32[2,1536,128]{2,1,0:T(8,128)} %collective-permute-done.13.rest_1_.rest_2_, f32[2,1536,128]{2,1,0:T(8,128)S(1)} %collective-permute-done.16.rest_2_.rest_3_), custom_call_target="tpu_custom_call" | custom-call | flops 1610612736 | bytes 6291456 | tf_op jit(solution)/shard_map/pallas_call | solution.py:452
  240.9 29.0 %collective-permute-done.14.rest_1_.rest_6_ = f32[2,1536,128]{2,1,0:T(8,128)S(1)} collective-permute-done((f32[2,1536,128]{2,1,0:T(8,128)S(1)}, f32[2,1536,128]{2,1,0:T(8,128)S(1)}, u32[]{:S(2)}, u32[]{:S(2)}) %collective-permute-start.14) | collective-permute-done | bytes 1572896 | tf_op jit(solution)/shard_map/ppermute | solution.py:430
  270.0 3.4 collective-permute-done.18.rest_2_.rest_7_
  276.1 12.7 %all_to_all.20 = f32[8,16,512]{2,1,0:T(8,128)S(1)} all-to-all(f32[8,16,512]{2,1,0:T(8,128)S(1)} %bitcast.43), channel_id=1, replica_groups=mesh['band'=4,'dom'=8] {'dom'}, dimensions={0} | all-to-all | bytes 524288 | tf_op jit(solution)/shard_map/all_to_all | solution.py:699
  288.8 12.0 %all_to_all.21 = f32[8,16,512]{2,1,0:T(8,128)S(1)} all-to-all(f32[8,16,512]{2,1,0:T(8,128)S(1)} %broadcast_in_dim.58), channel_id=1, replica_groups=mesh['band'=4,'dom'=8] {'dom'}, dimensions={0} | all-to-all | bytes 524288 | tf_op jit(solution)/shard_map/all_to_all | solution.py:701
  302.3 4.8 %collective-permute-done.20.refs_2_ = f32[128,512]{1,0:T(8,128)S(1)} collective-permute-done((f32[128,512]{1,0:T(8,128)S(1)}, f32[128,512]{1,0:T(8,128)S(1)}, u32[]{:S(2)}, u32[]{:S(2)}) %collective-permute-start.20) | collective-permute-done | bytes 262176 | tf_op jit(solution)/shard_map/ppermute | solution.py:430
  308.6 23.5 %shard_map.86 = (f32[512,512]{1,0:T(8,128)}, f32[128,512]{1,0:T(8,128)S(1)}) custom-call(s32[1]{0:T(128)} %bitcast.band_ref, f32[128,512]{1,0:T(8,128)S(1)} %bitcast.39, f32[128,512]{1,0:T(8,128)S(1)} %collective-permute-done.19.refs_1_, f32[128,512]{1,0:T(8,128)S(1)} %collective-permute-done.20.refs_2_, f32[128,512]{1,0:T(8,128)S(1)} %collective-permute-done.21.refs_3_), custom_call_target="tpu_custom_call" | custom-call | tf_op jit(solution)/shard_map/pallas_call | solution.py:599
  332.8 8.5 %shard_map.87 = f32[4,1536,128]{2,1,0:T(8,128)} custom-call(f32[128,512]{1,0:T(8,128)} %copy-done.10, f32[2,1536,128]{2,1,0:T(8,128)} %copy-done, f32[2,1536,128]{2,1,0:T(8,128)} %collective-permute-done.15.rest_0_.rest_1_, f32[2,1536,128]{2,1,0:T(8,128)} %collective-permute-done.13.rest_1_.rest_2_, f32[2,1536,128]{2,1,0:T(8,128)} %copy-done.4, ...), custom_call_target="tpu_custom_call" | custom-call | tf_op jit(solution)/shard_map/pallas_call | solution.py:479
  (116 shorter events, 47.8 us)
Async XLA Ops:
  9.8 12.2 %collective-permute-start.2 = (f32[8,4736]{1,0:T(8,128)S(1)}, f32[8,4736]{1,0:T(8,128)S(1)}, u32[]{:S(2)}, u32[]{:S(2)}) collective-permute-start(f32[8,4736]{1,0:T(8,128)S(1)} %reshape.268), channel_id=1, source_target_pairs={{0,7},{1,0},{2,1},{3,2},{4,3},{5,4},{6,5},{7,6},{8,15},{9,8},{10,9... | collective-permute-start | bytes 454664 | tf_op jit(solution)/shard_map/ppermute | solution.py:422
  15.9 9.6 %collective-permute-start.1 = (f32[8,4736]{1,0:T(8,128)S(1)}, f32[8,4736]{1,0:T(8,128)S(1)}, u32[]{:S(2)}, u32[]{:S(2)}) collective-permute-start(f32[8,4736]{1,0:T(8,128)S(1)} %reshape.268), channel_id=1, source_target_pairs={{0,1},{1,2},{2,3},{3,4},{4,5},{5,6},{6,7},{7,0},{8,9},{9,10},{10,1... | collective-permute-start | bytes 454664 | tf_op jit(solution)/shard_map/ppermute | solution.py:422
  15.9 9.6 %collective-permute-start = (f32[8,4736]{1,0:T(8,128)S(1)}, f32[8,4736]{1,0:T(8,128)S(1)}, u32[]{:S(2)}, u32[]{:S(2)}) collective-permute-start(f32[8,4736]{1,0:T(8,128)S(1)} %reshape.268), channel_id=1, source_target_pairs={{0,2},{1,3},{2,4},{3,5},{4,6},{5,7},{6,0},{7,1},{8,10},{9,11},{10,... | collective-permute-start | bytes 454664 | tf_op jit(solution)/shard_map/ppermute | solution.py:422
  26.3 78.9 %all-to-all-start = ((f32[8,4,208,128]{3,2,1,0:T(8,128)}), f32[8,4,208,128]{3,2,1,0:T(8,128)S(1)}, u32[]{:S(2)}, u32[]{:S(2)}) async-start(f32[8,4,208,128]{3,2,1,0:T(8,128)} %shard_map.77), calls=%async_computation | async-start | bytes 6815744 | tf_op jit(solution)/shard_map/all_to_all | solution.py:660
  30.1 140.9 %all-gather.3.cloned.1.call-start = ((), (), s32[]{:S(2)}) async-start(), calls=%async_computation.4 | async-start | bytes 1916928 | tf_op jit(solution)/shard_map/all_gather | solution.py:676
  30.4 14.2 %collective-permute-start.4 = (f32[4,8,4736]{2,1,0:T(8,128)}, f32[4,8,4736]{2,1,0:T(8,128)}, u32[]{:S(2)}, u32[]{:S(2)}) collective-permute-start(f32[4,8,4736]{2,1,0:T(8,128)} %pad_maximum_fusion.refs_0_), channel_id=1, source_target_pairs={{0,16},{8,24},{16,0},{24,8},{1,17},{9,25},{17,1},{25,9},{2,18},{10... | collective-permute-start | bytes 1818632 | tf_op jit(solution)/shard_map/ppermute | solution.py:430
  33.2 13.3 %collective-permute-start.3 = (f32[4,8,4736]{2,1,0:T(8,128)}, f32[4,8,4736]{2,1,0:T(8,128)}, u32[]{:S(2)}, u32[]{:S(2)}) collective-permute-start(f32[4,8,4736]{2,1,0:T(8,128)} %pad_maximum_fusion.refs_0_), channel_id=1, source_target_pairs={{0,8},{8,0},{16,24},{24,16},{1,9},{9,1},{17,25},{25,17},{2,10},{10... | collective-permute-start | bytes 1818632 | tf_op jit(solution)/shard_map/ppermute | solution.py:430
  44.6 2.8 collective-permute-start.5
  129.0 15.0 %collective-permute-start.6 = (f32[2,192,128]{2,1,0:T(8,128)}, f32[2,192,128]{2,1,0:T(8,128)S(1)}, u32[]{:S(2)}, u32[]{:S(2)}) collective-permute-start(f32[2,192,128]{2,1,0:T(8,128)} %get-tuple-element.39), channel_id=1, source_target_pairs={{0,1},{1,2},{2,3},{3,4},{4,5},{5,6},{6,7},{7,0},{8,9},{9,10},{10,1... | collective-permute-start | bytes 589832 | tf_op jit(solution)/shard_map/ppermute | solution.py:422
  130.5 17.9 %collective-permute-start.7 = (f32[2,192,128]{2,1,0:T(8,128)}, f32[2,192,128]{2,1,0:T(8,128)S(1)}, u32[]{:S(2)}, u32[]{:S(2)}) collective-permute-start(f32[2,192,128]{2,1,0:T(8,128)} %get-tuple-element.40), channel_id=1, source_target_pairs={{0,2},{1,3},{2,4},{3,5},{4,6},{5,7},{6,0},{7,1},{8,10},{9,11},{10,... | collective-permute-start | bytes 589832 | tf_op jit(solution)/shard_map/ppermute | solution.py:422
  130.5 52.5 %collective-permute-start.8 = (f32[2,192,128]{2,1,0:T(8,128)}, f32[2,192,128]{2,1,0:T(8,128)}, u32[]{:S(2)}, u32[]{:S(2)}) collective-permute-start(f32[2,192,128]{2,1,0:T(8,128)} %get-tuple-element.41), channel_id=1, source_target_pairs={{0,3},{1,4},{2,5},{3,6},{4,7},{5,0},{6,1},{7,2},{8,11},{9,12},{10,... | collective-permute-start | bytes 589832 | tf_op jit(solution)/shard_map/ppermute | solution.py:422
  133.3 49.7 %collective-permute-start.9 = (f32[2,192,128]{2,1,0:T(8,128)}, f32[2,192,128]{2,1,0:T(8,128)}, u32[]{:S(2)}, u32[]{:S(2)}) collective-permute-start(f32[2,192,128]{2,1,0:T(8,128)} %get-tuple-element.42), channel_id=1, source_target_pairs={{0,4},{1,5},{2,6},{3,7},{4,0},{5,1},{6,2},{7,3},{8,12},{9,13},{10,... | collective-permute-start | bytes 589832 | tf_op jit(solution)/shard_map/ppermute | solution.py:422
  134.3 48.7 %collective-permute-start.10 = (f32[2,192,128]{2,1,0:T(8,128)}, f32[2,192,128]{2,1,0:T(8,128)}, u32[]{:S(2)}, u32[]{:S(2)}) collective-permute-start(f32[2,192,128]{2,1,0:T(8,128)} %get-tuple-element.43), channel_id=1, source_target_pairs={{0,5},{1,6},{2,7},{3,0},{4,1},{5,2},{6,3},{7,4},{8,13},{9,14},{10,... | collective-permute-start | bytes 589832 | tf_op jit(solution)/shard_map/ppermute | solution.py:422
  144.0 39.0 %collective-permute-start.11 = (f32[2,192,128]{2,1,0:T(8,128)}, f32[2,192,128]{2,1,0:T(8,128)}, u32[]{:S(2)}, u32[]{:S(2)}) collective-permute-start(f32[2,192,128]{2,1,0:T(8,128)} %get-tuple-element.44), channel_id=1, source_target_pairs={{0,6},{1,7},{2,0},{3,1},{4,2},{5,3},{6,4},{7,5},{8,14},{9,15},{10,... | collective-permute-start | bytes 589832 | tf_op jit(solution)/shard_map/ppermute | solution.py:422
  148.4 34.6 %collective-permute-start.12 = (f32[2,192,128]{2,1,0:T(8,128)}, f32[2,192,128]{2,1,0:T(8,128)}, u32[]{:S(2)}, u32[]{:S(2)}) collective-permute-start(f32[2,192,128]{2,1,0:T(8,128)} %get-tuple-element.45), channel_id=1, source_target_pairs={{0,7},{1,0},{2,1},{3,2},{4,3},{5,4},{6,5},{7,6},{8,15},{9,8},{10,9... | collective-permute-start | bytes 589832 | tf_op jit(solution)/shard_map/ppermute | solution.py:422
  187.1 42.9 %all-to-all-start.1 = ((f32[8,2,192,128]{3,2,1,0:T(8,128)}), f32[8,2,192,128]{3,2,1,0:T(8,128)}, u32[]{:S(2)}, u32[]{:S(2)}) async-start(f32[8,2,192,128]{3,2,1,0:T(8,128)} %get-tuple-element.47), calls=%async_computation.1 | async-start | bytes 3145728 | tf_op jit(solution)/shard_map/all_to_all | solution.py:688
  192.6 40.4 %collective-permute-start.13 = (f32[2,1536,128]{2,1,0:T(8,128)}, f32[2,1536,128]{2,1,0:T(8,128)}, u32[]{:S(2)}, u32[]{:S(2)}) collective-permute-start(f32[2,1536,128]{2,1,0:T(8,128)} %copy-done), channel_id=1, source_target_pairs={{0,16},{8,24},{16,0},{24,8},{1,17},{9,25},{17,1},{25,9},{2,18},{10... | collective-permute-start | bytes 4718600 | tf_op jit(solution)/shard_map/ppermute | solution.py:430
  194.2 40.8 %collective-permute-start.15 = (f32[2,1536,128]{2,1,0:T(8,128)}, f32[2,1536,128]{2,1,0:T(8,128)}, u32[]{:S(2)}, u32[]{:S(2)}) collective-permute-start(f32[2,1536,128]{2,1,0:T(8,128)} %copy-done), channel_id=1, source_target_pairs={{0,8},{8,0},{16,24},{24,16},{1,9},{9,1},{17,25},{25,17},{2,10},{10... | collective-permute-start | bytes 4718600 | tf_op jit(solution)/shard_map/ppermute | solution.py:430
  233.1 3.7 %collective-permute-start.16 = (f32[2,1536,128]{2,1,0:T(8,128)}, f32[2,1536,128]{2,1,0:T(8,128)S(1)}, u32[]{:S(2)}, u32[]{:S(2)}) collective-permute-start(f32[2,1536,128]{2,1,0:T(8,128)} %collective-permute-done.13.rest_1_.rest_2_), channel_id=1, source_target_pairs={{0,8},{8,0},{16,24},{24,16},{1,9},{9,1},{17,25},{25,17},{2,10},{10... | collective-permute-start | bytes 4718600 | tf_op jit(solution)/shard_map/ppermute | solution.py:430
  233.1 36.8 %collective-permute-start.14 = (f32[2,1536,128]{2,1,0:T(8,128)S(1)}, f32[2,1536,128]{2,1,0:T(8,128)S(1)}, u32[]{:S(2)}, u32[]{:S(2)}) collective-permute-start(f32[2,1536,128]{2,1,0:T(8,128)S(1)} %shard_map.83.own_ref.rest_4_), channel_id=1, source_target_pairs={{0,16},{8,24},{16,0},{24,8},{1,17},{9,25},{17,1},{25,9},{2,18},{10... | collective-permute-start | bytes 4718600 | tf_op jit(solution)/shard_map/ppermute | solution.py:430
  234.7 35.2 %collective-permute-start.17 = (f32[2,1536,128]{2,1,0:T(8,128)S(1)}, f32[2,1536,128]{2,1,0:T(8,128)S(1)}, u32[]{:S(2)}, u32[]{:S(2)}) collective-permute-start(f32[2,1536,128]{2,1,0:T(8,128)S(1)} %shard_map.83.own_ref.rest_4_), channel_id=1, source_target_pairs={{0,8},{8,0},{16,24},{24,16},{1,9},{9,1},{17,25},{25,17},{2,10},{10... | collective-permute-start | bytes 4718600 | tf_op jit(solution)/shard_map/ppermute | solution.py:430
  270.0 3.4 collective-permute-start.18
  300.7 6.4 %collective-permute-start.20 = (f32[128,512]{1,0:T(8,128)S(1)}, f32[128,512]{1,0:T(8,128)S(1)}, u32[]{:S(2)}, u32[]{:S(2)}) collective-permute-start(f32[128,512]{1,0:T(8,128)S(1)} %bitcast.37), channel_id=1, source_target_pairs={{0,16},{8,24},{16,0},{24,8},{1,17},{9,25},{17,1},{25,9},{2,18},{10... | collective-permute-start | bytes 786440 | tf_op jit(solution)/shard_map/ppermute | solution.py:430
  302.3 4.8 %collective-permute-start.19 = (f32[128,512]{1,0:T(8,128)S(1)}, f32[128,512]{1,0:T(8,128)S(1)}, u32[]{:S(2)}, u32[]{:S(2)}) collective-permute-start(f32[128,512]{1,0:T(8,128)S(1)} %bitcast.38), channel_id=1, source_target_pairs={{0,8},{8,0},{16,24},{24,16},{1,9},{9,1},{17,25},{25,17},{2,10},{10... | collective-permute-start | bytes 786440 | tf_op jit(solution)/shard_map/ppermute | solution.py:430
  (17 other events, 100.4 us)
Sparse Core Ops, SparseCore 0:
  105.4 65.6 all-gather.2
